TPU v7x, 32 devices: a whole 2x2x4 slice. The times are simulated.
32 devices in a mesh: dp: 2 (over y), seq: 16 (over z, x, core).
Axes of the slice: x: 2, y: 2, z: 4, core: 2. Of those that a mesh axis runs over, the one named last changes fastest.
Arguments:
- queries: bfloat16 [4096, 3072], P('seq', 'dp'), may hold values from -6 to 6
- keys: bfloat16 [4096, 3072], P('seq', 'dp'), may hold values from -6 to 6
- values: bfloat16 [4096, 3072], P('seq', 'dp'), may hold values from -6 to 6
- out_grad: bfloat16 [4096, 3072], P('seq', 'dp'), may hold values from -6 to 6
- log_decay: float32 [4096, 24], P('seq', 'dp'), may hold values from -0.61 to 0
- norm_gain: float32 [3072], P('dp'), may hold values from 0.1 to 1.9
- doc_ids: int32 [32], P('seq'), may hold values from 0 to 3, never falling along the last dimension, each value on 1 to 16 neighbouring positions
Outputs:
- key_grad: bfloat16 [4096, 3072], P('seq', 'dp')
- value_grad: bfloat16 [4096, 3072], P('seq', 'dp')
- gain_grad: float32 [3072], P('dp')
Inputs may be any that keep to these rules, and one draw needn't show every extreme that they name: `doc_ids`: document numbers never fall along the sequence; every number from 0 to 3 occurs.
All inputs are finite; a program needn't handle non-finite values.
Results may differ from a plain program's by a relative error of at most 0.0052.
Values sent between devices are 32-bit elements; how exact they have to be, the bound alone decides.
No kernel may reach another device: no remote copies, remote signals or barrier semaphores. Data moves between devices by JAX's collectives and lax.ppermute only.
A program may use at most 64 MiB of HBM per device.

v0:
```python
import jax
import jax.numpy as jnp
from jax import lax
from jax.sharding import PartitionSpec as P

C = 128


EPSILON = 1e-06


def from_behind(value, axis, steps):
    count = lax.axis_size(axis)
    leading, last = (max(0, -steps), min(count, count - steps))
    return lax.ppermute(value, axis, [(source, source + steps) for source in range(leading, last)])


def carried_in(part, axis, combine, identity, reverse):
    count = lax.axis_size(axis)
    place = lax.axis_index(axis)
    ahead = count - 1 - place if reverse else place
    gathered = jax.tree.map(lambda a: lax.all_gather(a, axis), part)
    state = jax.tree.map(lambda a, e: jnp.zeros_like(a) + jnp.asarray(e, a.dtype), part, identity)

    def one(lap, state):
        source = count - 1 - lap if reverse else lap
        return combine(
            state, jax.tree.map(lambda a: lax.dynamic_index_in_dim(a, source, 0, False), gathered)
        )

    return lax.fori_loop(0, ahead, one, state)


def combine_pairs(earlier, later):
    return (earlier[0] * later[0], later[0][..., None, None] * earlier[1] + later[1])


def far_grads(value_blocks, key_blocks, end_decay, later_grad):
    value_end = value_blocks.astype(jnp.float32) * end_decay[..., None]
    key_end = key_blocks.astype(jnp.float32) * end_decay[..., None]
    key_far = jnp.einsum("nshe,nhde->nshd", value_end, later_grad, precision=lax.Precision.HIGHEST)
    value_far = jnp.einsum("nshd,nhde->nshe", key_end, later_grad, precision=lax.Precision.HIGHEST)
    return (key_far, value_far)


def per_device(queries, keys, values, out_grad, log_decay, norm_gain, doc_ids):
    tokens = queries.shape[0]
    features = queries.shape[1]
    head_count = log_decay.shape[1]
    head_width = features // head_count
    all_features = features * lax.axis_size("dp")
    block_len = C
    nblocks = tokens // block_len
    block_shape = (nblocks, block_len, head_count, head_width)
    query_blocks = queries.reshape(block_shape)
    key_blocks = keys.reshape(block_shape)
    value_blocks = values.reshape(block_shape)
    cumulative = jnp.cumsum(log_decay.reshape(nblocks, block_len, head_count), axis=1)
    block_total = cumulative[:, -1, :]
    marked = from_behind(doc_ids[-1:] + 1, "seq", 1)
    before = marked - 1
    prev_ids = jnp.concatenate([before, doc_ids[:-1]])
    carried = (prev_ids == doc_ids).astype(jnp.float32)
    causal = (jnp.arange(block_len)[:, None] >= jnp.arange(block_len)[None, :]).astype(jnp.float32)
    log_gap = jnp.swapaxes(cumulative, 1, 2)
    decay_mask = jnp.exp(jnp.minimum(log_gap[:, :, :, None] - log_gap[:, :, None, :], 0.0)) * causal
    scores = jnp.einsum(
        "nthd,nshd->nhts", query_blocks, key_blocks, preferred_element_type=jnp.float32
    )
    weights = (scores * decay_mask).astype(jnp.bfloat16)
    local_out = jnp.einsum(
        "nhts,nshd->nthd", weights, value_blocks, preferred_element_type=jnp.float32
    )
    end_decay = jnp.exp(block_total[:, None, :] - cumulative)
    key_scaled = (key_blocks.astype(jnp.float32) * end_decay[..., None]).astype(jnp.bfloat16)
    update = jnp.einsum(
        "nshd,nshe->nhde", key_scaled, value_blocks, preferred_element_type=jnp.float32
    )
    factor = carried[:, None] * jnp.exp(block_total)

    def forward_step(carry_pair, block_item):
        acc_factor, acc_state = carry_pair
        blk_factor, blk_update = block_item
        nxt = (acc_factor * blk_factor, blk_factor[:, None, None] * acc_state + blk_update)
        return (nxt, (acc_factor, acc_state))

    identity = (
        jnp.ones((head_count,), jnp.float32),
        jnp.zeros((head_count, head_width, head_width), jnp.float32),
    )
    summary, (lead_factor, lead_state) = lax.scan(forward_step, identity, (factor, update))
    prefix = carried_in(summary, "seq", combine_pairs, identity, False)
    state_in = lead_factor[:, :, None, None] * prefix[1][None] + lead_state
    query_scaled = (
        query_blocks.astype(jnp.float32) * (jnp.exp(cumulative) * carried[:, None, None])[..., None]
    )
    far_out = jnp.einsum("nthd,nhde->nthe", query_scaled, state_in, precision=lax.Precision.HIGHEST)
    attention = (local_out + far_out).reshape(tokens, features)
    out_cot = out_grad.astype(jnp.float32)
    weighted = out_cot * norm_gain
    square_part = jnp.sum(attention * attention, axis=1)
    inner_part = jnp.sum(weighted * attention, axis=1)
    square_total, inner_total = lax.psum((square_part, inner_part), "dp")
    inverse = lax.rsqrt(square_total[:, None] / all_features + EPSILON)
    inner = inner_total[:, None] / all_features
    attn_grad = ((weighted - attention * inner * inverse * inverse) * inverse).astype(jnp.bfloat16)
    gain_part = jnp.sum(out_cot * attention * inverse, axis=0)
    grad_attn = attn_grad.reshape(block_shape)
    query_weighted = (query_blocks.astype(jnp.float32) * jnp.exp(cumulative)[..., None]).astype(
        jnp.bfloat16
    )
    back_term = jnp.einsum(
        "nthd,nthe->nhde", query_weighted, grad_attn, preferred_element_type=jnp.float32
    )
    back_term = back_term * carried[:, None, None, None]

    def backward_step(carry_pair, block_item):
        acc_factor, acc_term = carry_pair
        blk_factor, blk_term = block_item
        nxt = (acc_factor * blk_factor, blk_term + blk_factor[:, None, None] * acc_term)
        return (nxt, (acc_factor, acc_term))

    back_summary, (trail_factor, trail_term) = lax.scan(
        backward_step, identity, (factor, back_term), reverse=True
    )
    value_local = jnp.einsum(
        "nhts,nthd->nshd", weights, grad_attn, preferred_element_type=jnp.float32
    )
    grad_dot = jnp.einsum(
        "nthd,nshd->nhts", grad_attn, value_blocks, preferred_element_type=jnp.float32
    )
    grad_weights = (grad_dot * decay_mask).astype(jnp.bfloat16)
    key_local = jnp.einsum(
        "nhts,nthd->nshd", grad_weights, query_blocks, preferred_element_type=jnp.float32
    )
    suffix = carried_in(back_summary, "seq", combine_pairs, identity, True)
    later_grad = trail_factor[:, :, None, None] * suffix[1][None] + trail_term
    key_far, value_far = far_grads(value_blocks, key_blocks, end_decay, later_grad)
    gain_grad = lax.psum(gain_part, "seq")
    key_grad = (key_local + key_far).reshape(tokens, features).astype(jnp.bfloat16)
    value_grad = (value_local + value_far).reshape(tokens, features).astype(jnp.bfloat16)
    return (key_grad, value_grad, gain_grad)


def solution(mesh):
    placed = (
        P("seq", "dp"),
        P("seq", "dp"),
        P("seq", "dp"),
        P("seq", "dp"),
        P("seq", "dp"),
        P("dp"),
        P("seq"),
    )
    return jax.shard_map(
        per_device,
        mesh=mesh,
        in_specs=placed,
        out_specs=(P("seq", "dp"), P("seq", "dp"), P("dp")),
        check_vma=False,
    )
```

profile of v0, /device:TPU:0, one launch (start us, length us, event | category | flops | bytes accessed | tf_op | source)
XLA Modules:
  0.0 333.0 jit_solution(6070772191970306350)
XLA Ops:
  7.2 1.3 fusion.64
  9.2 3.2 collective-permute-start
  13.4 1.6 reshape.100
  15.0 1.5 reshape.99
  19.4 2.3 fusion.26
  21.7 1.4 broadcast.42.clone
  23.6 7.2 %while.66 = (s32[]{:T(128)}, f32[12]{0:T(128)}, f32[12,128,128]{2,1,0:T(8,128)S(1)}, f32[2,12]{1,0:T(2,128)}, f32[2,12,128,128]{3,2,1,0:T(8,128)}, /*index=5*/f3...) while((s32[]{:T(128)}, f32[12]{0:T(128)}, f32[12,128,128]{2,1,0:T(8,128)S(1)}, ...), condition=%wide.region_2.3_spmd.clone, body=%wide.region_1.2_spmd.clone.sunk | while | flops 786459 | bytes 3933173 | solution.py:91
  25.9 1.3 dynamic_update_slice.37
  29.5 1.3 dynamic_update_slice.37
  31.8 2.5 reshape.98
  34.4 2.3 copy.96
  38.0 2.9 multiply_convert_fusion.1
  41.2 34.1 %all-reduce = f32[192]{0:T(256)S(1)} all-reduce(f32[192]{0:T(256)S(1)} %dynamic-update-slice), channel_id=2, replica_groups=mesh['dp'=2,'seq'=16] {'seq'}, use_global_device_ids=true, to_apply=%add | all-reduce | flops 192 | bytes 1536
  75.6 59.9 %all-gather.7.cloned.1.call-done = f32[192,128,128]{2,1,0:T(8,128)} async-done(((f32[12,128,128]{2,1,0:T(8,128)}), f32[192,128,128]{2,1,0:T(8,128)}) %all-gather.7.cloned.1.call-update) | async-done | bytes 12582928 | tf_op jit(solution)/shard_map/all_gather | solution.py:22
  136.2 4.9 %fusion.13 = f32[2,12,128,128]{3,2,1,0:T(8,128)S(1)} fusion(f32[2,12,128,128]{3,2,1,0:T(8,128)} %get-tuple-element.319, f32[2,128,12]{1,2,0:T(8,128)S(1)} %copy.111, f32[12,128,128]{2,1,0:T(8,128)S(1)} %get-tuple-element.318, f32[2,12]{1,0:T(2,128)S(1)} %copy-done.21, bf16[2,128,12,128]{3,2,1,0:T(8,128)(2,1)} %reshape.98), kind=kOutput, calls=%fused_computation.29 | convolution fusion | flops 605552640 | bytes 4730976 | tf_op jit(solution)/shard_map/nthd,nhde->nthe/dot_general | solution.py:97
  143.1 5.0 %psum.22 = f32[256]{0:T(256)S(1)} all-reduce(f32[256]{0:T(256)S(1)} %bitcast.97), channel_id=1, replica_groups=mesh['dp'=2,'seq'=16] {'dp'}, use_global_device_ids=true, to_apply=%region_8.9 | all-reduce | flops 256 | bytes 2048 | tf_op jit(solution)/shard_map/psum | solution.py:103
  148.1 1.8 fusion.12
  149.9 5.1 %psum.21 = f32[256]{0:T(256)S(1)} all-reduce(f32[256]{0:T(256)S(1)} %get-tuple-element.383), channel_id=1, replica_groups=mesh['dp'=2,'seq'=16] {'dp'}, use_global_device_ids=true, to_apply=%region_6.7 | all-reduce | flops 256 | bytes 2048 | tf_op jit(solution)/shard_map/psum | solution.py:103
  155.0 2.4 fusion.10
  157.4 2.7 reshape.81
  160.1 2.6 convolution_multiply_fusion
  162.7 1.4 broadcast.42
  164.1 2.4 while.67
  167.7 51.6 %all-reduce.2 = (f32[192]{0:T(256)S(1)}, f32[1536]{0:T(1024)}) all-reduce(f32[192]{0:T(256)S(1)} %dynamic-update-slice.1, f32[1536]{0:T(1024)S(1)} %get-tuple-element.382), channel_id=4, replica_groups=mesh['dp'=2,'seq'=16] {'seq'}, use_global_device_ids=true, to_apply=%add.1 | all-reduce | flops 1728 | bytes 13824
  219.3 66.3 %all-gather.9.cloned.1.call-done = f32[192,128,128]{2,1,0:T(8,128)} async-done(((f32[12,128,128]{2,1,0:T(8,128)}), f32[192,128,128]{2,1,0:T(8,128)}) %all-gather.9.cloned.1.call-update) | async-done | bytes 12582928 | tf_op jit(solution)/shard_map/all_gather | solution.py:22
  285.7 20.6 %while.65 = (s32[]{:T(128)}, f32[12,128,128]{2,1,0:T(8,128)S(1)}, s32[]{:T(128)}, f32[16,12]{1,0:T(8,128)S(1)}, f32[16,12,128,128]{3,2,1,0:T(8,128)}, /*index=5*/s32[]{:T(128)}, s32[]{:T(128)}, s32[]{:T(128)}, s32[]{:T(128)}) while((s32[]{:T(128)}, f32[12,128,128]{2,1,0:T(8,128)S(1)}, s32[]{:T(128)}, f32[16,12]{1,0:T(8,128)S(1)}, ...), condition=%wide.region_12.13_spmd, body=%wide.region_11.12_spmd.sunk | while | flops 393222 | bytes 2359587 | solution.py:31
  285.7 1.4 bitcast_add_fusion.11
  287.2 1.3 bitcast_add_fusion.11
  288.6 1.3 bitcast_add_fusion.11
  289.9 1.3 bitcast_add_fusion.11
  291.3 1.3 bitcast_add_fusion.11
  292.7 1.3 bitcast_add_fusion.11
  294.0 1.3 bitcast_add_fusion.11
  295.4 1.3 bitcast_add_fusion.11
  296.8 1.3 bitcast_add_fusion.11
  298.1 1.3 bitcast_add_fusion.11
  299.5 1.3 bitcast_add_fusion.11
  300.9 1.3 bitcast_add_fusion.11
  302.2 1.3 bitcast_add_fusion.11
  303.6 1.3 bitcast_add_fusion.11
  305.0 1.3 bitcast_add_fusion.11
  306.3 4.9 %fusion.18 = f32[2,12,128,128]{2,3,1,0:T(8,128)} fusion(f32[2,12,128,128]{3,2,1,0:T(8,128)S(1)} %copy-done.2, f32[12,128,128]{2,1,0:T(8,128)S(1)} %get-tuple-element.323, f32[2,12]{1,0:T(2,128)S(1)} %get-tuple-element.320, f32[2,128,12]{1,2,0:T(8,128)S(1)} %copy.107, bf16[2,128,12,128]{3,2,1,0:T(8,128)(2,1)S(1)} %reshape.100), kind=kOutput, calls=%fused_computation.38 | convolution fusion | flops 605552640 | bytes 4730976 | tf_op jit(solution)/shard_map/nshe,nhde->nshd/dot_general | solution.py:41
  311.2 4.2 %fusion.23 = f32[2,12,128,128]{3,2,1,0:T(8,128)} fusion(f32[2,12,128,128]{3,2,1,0:T(8,128)S(1)} %copy-done.2, f32[12,128,128]{2,1,0:T(8,128)S(1)} %get-tuple-element.323, f32[2,12]{1,0:T(2,128)S(1)} %get-tuple-element.320, f32[2,128,12]{1,2,0:T(8,128)S(1)} %copy.107, bf16[2,128,12,128]{3,2,1,0:T(8,128)(2,1)S(1)} %copy-done.5), kind=kOutput, calls=%fused_computation.47 | convolution fusion | flops 605552640 | bytes 4730976 | tf_op jit(solution)/shard_map/nshd,nhde->nshe/dot_general | solution.py:42
  315.5 4.2 %fusion.17 = bf16[2,128,12,128]{3,1,2,0:T(8,128)(2,1)} fusion(f32[2,12,128,128]{2,3,1,0:T(8,128)} %fusion.18, f32[128,128]{1,0:T(8,128)S(1)} %fusion.60, f32[2,12,128]{2,1,0:T(8,128)S(1)} %copy-done.15, bf16[2,128,12,128]{1,0,3,2:T(2,128)(2,1)} %reshape.81, bf16[2,128,12,128]{3,2,1,0:T(8,128)(2,1)S(1)} %reshape.100, bf16[2,128,12,128]{3,2,1,0:T(8,128)(2,1)} %reshape.98), kind=kOutput, calls=%fused_computation.35 | convolution fusion | flops 204079104 | bytes 4796416 | tf_op jit(solution)/shard_map/nhts,nthd->nshd/dot_general | solution.py:133
  319.7 1.8 copy.136
  321.5 1.3 fusion.25
  322.8 1.9 copy.137
  324.7 1.5 copy_bitcast_fusion
  (111 shorter events, 17.2 us)
Async XLA Ops:
  7.2 7.9 %copy-start.9 = (bf16[256,1536]{1,0:T(8,128)(2,1)S(1)}, bf16[256,1536]{1,0:T(8,128)(2,1)}, u32[]{:S(2)}) copy-start(bf16[256,1536]{1,0:T(8,128)(2,1)} %param.16) | copy-start | bytes 2359300
  7.2 128.3 %all-gather.7.cloned.1.call-start = ((), (), s32[]{:S(2)}) async-start(), calls=%async_computation | async-start | bytes 13369344 | tf_op jit(solution)/shard_map/all_gather | solution.py:22
  9.2 7.4 %collective-permute-start = (s32[1]{0:T(128)}, s32[1]{0:T(128)}, u32[]{:S(2)}, u32[]{:S(2)}) collective-permute-start(s32[1]{0:T(128)} %add.103), channel_id=1, source_target_pairs={{0,1},{1,2},{2,3},{3,4},{4,5},{5,6},{6,7},{7,8},{8,9},{9,10},{10,1... | collective-permute-start | bytes 20 | tf_op jit(solution)/shard_map/ppermute | solution.py:15
  13.4 3.8 %copy-start.20 = (s32[2]{0:T(128)S(1)}, s32[2]{0:T(128)}, u32[]{:S(2)}) copy-start(s32[2]{0:T(128)} %param.21) | copy-start | bytes 28
  17.9 1.4 copy-start.18
  30.8 0.9 copy-start.1
  31.7 253.9 %all-gather.9.cloned.1.call-start = ((), (), s32[]{:S(2)}) async-start(), calls=%async_computation.1 | async-start | bytes 13369344 | tf_op jit(solution)/shard_map/all_gather | solution.py:22
  31.8 4.9 %copy-start.22 = (u32[32]{0:T(128)S(1)}, u32[32]{0:T(128)}, u32[]{:S(2)}) copy-start(u32[32]{0:T(128)} %constant.127) | copy-start | bytes 388
  31.8 6.2 %copy-start.4 = (bf16[2,128,12,128]{3,2,1,0:T(8,128)(2,1)S(1)}, bf16[2,128,12,128]{3,2,1,0:T(8,128)(2,1)}, u32[]{:S(2)}) copy-start(bf16[2,128,12,128]{3,2,1,0:T(8,128)(2,1)} %reshape.99) | copy-start | bytes 2359300
  34.4 6.6 %copy-start.14 = (f32[2,12,128]{2,1,0:T(8,128)}, f32[2,12,128]{2,1,0:T(8,128)S(1)}, u32[]{:S(2)}) copy-start(f32[2,12,128]{2,1,0:T(8,128)S(1)} %copy.102) | copy-start | bytes 36868
  38.0 3.0 copy-start.17
  38.0 37.4 %copy-start.11 = (f32[2,128,12]{2,1,0:T(8,128)S(1)}, f32[2,128,12]{2,1,0:T(8,128)}, u32[]{:S(2)}) copy-start(f32[2,128,12]{2,1,0:T(8,128)} %get-tuple-element.440) | copy-start | bytes 36868
  38.0 37.5 %copy-start.10 = (f32[2,128,12]{2,1,0:T(8,128)S(1)}, f32[2,128,12]{2,1,0:T(8,128)}, u32[]{:S(2)}) copy-start(f32[2,128,12]{2,1,0:T(8,128)} %get-tuple-element.441) | copy-start | bytes 36868
  135.5 0.7 copy-start.21
  136.2 4.9 %copy-start.7 = (bf16[2,12,128,128]{3,2,1,0:T(8,128)(2,1)S(1)}, bf16[2,12,128,128]{3,2,1,0:T(8,128)(2,1)}, u32[]{:S(2)}) copy-start(bf16[2,12,128,128]{3,2,1,0:T(8,128)(2,1)} %multiply_convert_fusion.1) | copy-start | bytes 2359300
  141.9 6.2 %copy-start.13 = (f32[1536]{0:T(1024)S(1)}, f32[1536]{0:T(1024)}, u32[]{:S(2)}) copy-start(f32[1536]{0:T(1024)} %param.20) | copy-start | bytes 18436
  157.4 2.7 copy-start.19
  162.7 1.4 copy-start.12
  162.7 1.4 copy-start.16
  166.5 0.9 copy-start
  285.7 20.6 %copy-start.2 = (f32[2,12,128,128]{3,2,1,0:T(8,128)S(1)}, f32[2,12,128,128]{3,2,1,0:T(8,128)}, u32[]{:S(2)}) copy-start(f32[2,12,128,128]{3,2,1,0:T(8,128)} %get-tuple-element.324) | copy-start | bytes 4718596
  306.3 4.9 %copy-start.5 = (bf16[2,128,12,128]{3,2,1,0:T(8,128)(2,1)S(1)}, bf16[2,128,12,128]{3,2,1,0:T(8,128)(2,1)}, u32[]{:S(2)}) copy-start(bf16[2,128,12,128]{3,2,1,0:T(8,128)(2,1)} %reshape.99) | copy-start | bytes 2359300
  311.2 4.2 %copy-start.15 = (f32[2,12,128]{2,1,0:T(8,128)S(1)}, f32[2,12,128]{2,1,0:T(8,128)}, u32[]{:S(2)}) copy-start(f32[2,12,128]{2,1,0:T(8,128)} %copy-done.14) | copy-start | bytes 36868
  315.4 6.0 %copy-start.6 = (f32[2,12,128,128]{3,2,1,0:T(8,128)S(1)}, f32[2,12,128,128]{3,2,1,0:T(8,128)}, u32[]{:S(2)}) copy-start(f32[2,12,128,128]{3,2,1,0:T(8,128)} %fusion.23) | copy-start | bytes 4718596
  319.7 1.8 copy-start.3
  319.7 1.8 copy-start.8
Sparse Core Ops, SparseCore 0:
  31.8 103.6 all-gather.6
  167.5 118.0 all-gather.8
where the time goes:
time: 334 us; the launch traced here: 333 us
  waiting for transfers between devices  126 us (38%)
  blocking collectives  95.8 us (29%)
  other arithmetic  33.4 us (10%)
  local copies, waits for them, and re-layouts  29.5 us (9%)
  matrix products  28 us (8%)
  between operations  16.3 us (5%)
    all_gather x2, waiting for transfers between devices, carried_in(): gathered = jax.tree.map(lambda a: lax.all_gather(a, axis), part)  126 us
    unnamed x2, blocking collectives  85.7 us
    add x15, other arithmetic, combine_pairs(): later[0][..., None, None] * earlier[1] + later[1]  19.9 us
    unnamed x55, local copies, waits for them, and re-layouts  11.1 us
    psum x2, blocking collectives, per_device(): square_total, inner_total = lax.psum((square_part, inner_part), 'dp')  10.1 us
  transfers between devices with their start and end apart: 3, of which 2 were waited for; matrix products, arithmetic and copies ran while one was open for 4% of the time, Pallas kernels for 0%

commit v1 on v0

v1 whole, which is shorter than its diff:
```python
import functools

import jax
import jax.numpy as jnp
from jax import lax
from jax.experimental import pallas as pl
from jax.experimental.pallas import tpu as pltpu
from jax.sharding import PartitionSpec as P

C = 128
EPSILON = 1e-06
PLANE = 4
F32 = jnp.float32
BF16 = jnp.bfloat16
HIGHEST = lax.Precision.HIGHEST


def dot(a, b, contract_a, contract_b, precision=None):
    return lax.dot_general(
        a,
        b,
        (((contract_a,), (contract_b,)), ((), ())),
        precision=precision,
        preferred_element_type=F32,
    )


def two_parts(a):
    high = a.astype(BF16)
    return high, (a - high.astype(F32)).astype(BF16)


def far_dot(a, state, contract_state):
    high, low = two_parts(state)
    return dot(a, high, 1, contract_state) + dot(a, low, 1, contract_state)


def equal(a, b):
    return (a == b).astype(F32)


def place_bits(count, reverse):
    place = lax.axis_index("seq")
    place = count - 1 - place if reverse else place
    return lax.rem(place, 2), lax.rem(place // 2, 2), place // PLANE


def triangle():
    row = lax.broadcasted_iota(jnp.int32, (C, C), 0)
    column = lax.broadcasted_iota(jnp.int32, (C, C), 1)
    return row, column


def decay_columns(log_block):
    row, column = triangle()
    return dot((row >= column).astype(F32), log_block, 1, 0, HIGHEST)


def decay_rows(log_block):
    row, column = triangle()
    return dot(log_block, (row <= column).astype(F32), 0, 0, HIGHEST)


def total_rows(log_block):
    return dot(log_block, jnp.ones((C, C), F32), 0, 0, HIGHEST)


class Sizes:
    def __init__(self, tokens, features, heads, count):
        self.tokens, self.features, self.heads, self.count = tokens, features, heads, count
        self.blocks = tokens // C
        self.width = features // heads
        self.half = self.width // 2
        self.quarter = self.width // 4
        self.planes = count // PLANE
        longest = self.blocks * count // 2
        per_plane = self.blocks * PLANE
        self.window = max(1, min(self.planes - 1, 1 + (longest - 2) // per_plane))
        self.tail = -(-(2 * heads + 2) // 8) * 8
        self.start, self.end, self.gain = heads, heads + 1, heads + 2

    def head(self, h):
        return slice(h * self.width, (h + 1) * self.width)

    def block(self, j):
        return slice(j * C, (j + 1) * C)

    def rows(self, h, size):
        return slice(h * size, (h + 1) * size)

    def carry(self, j):
        return 2 * self.heads + 2 + j


def call(kernel, outs, *args, flops=0, name=None):
    moved = sum(a.size * a.dtype.itemsize for a in args) + sum(
        o.size * o.dtype.itemsize for o in outs
    )
    return pl.pallas_call(
        kernel,
        out_shape=outs,
        in_specs=[pl.BlockSpec(memory_space=pltpu.VMEM)] * len(args),
        out_specs=[pl.BlockSpec(memory_space=pltpu.VMEM)] * len(outs),
        compiler_params=pltpu.CompilerParams(vmem_limit_bytes=20 * 1024 * 1024),
        cost_estimate=pl.CostEstimate(flops=flops, bytes_accessed=moved, transcendentals=0),
        name=name,
    )(*args)


def shape(rows, columns, dtype=F32):
    return jax.ShapeDtypeStruct((rows, columns), dtype)


def put_tail(s, tail_ref, base, factors, start, end):
    tail_ref[base : base + s.heads, :] = factors
    tail_ref[base + s.start : base + s.start + 1, :] = start
    tail_ref[base + s.end : base + s.end + 1, :] = end


def put_parts(first, own, size, h, whole, keep_ref, send_ref):
    low, high = whole[:size], whole[size:]
    rows = slice(h * size, (h + 1) * size)
    keep_ref[rows, :] = lax.select(first, low, high)
    send_ref[rows, :] = lax.select(first, high, low)


def state_kernel(s, keys, values, log_decay, doc_rows, keep, send, tail, first_update):
    core, _, _ = place_bits(s.count, False)
    lower = core == 0
    docs = [doc_rows[j : j + 1, :] for j in range(s.blocks)]
    carries = [None] + [equal(docs[j - 1], docs[j]) for j in range(1, s.blocks)]
    logs = [log_decay[s.block(j), :] for j in range(s.blocks)]
    totals = [total_rows(a) for a in logs]
    factors = [jnp.exp(t) for t in totals]
    whole_factor = factors[0]
    for j in range(1, s.blocks):
        whole_factor = whole_factor * factors[j] * carries[j]
    base = s.heads * s.half
    send[base:, :] = jnp.zeros((s.tail, s.width), F32)
    put_tail(s, send, base, whole_factor, docs[0], docs[-1])
    tail[...] = jnp.zeros(tail.shape, F32)
    put_tail(s, tail, 0, whole_factor, docs[0], docs[-1])
    for j in range(1, s.blocks):
        tail[s.carry(j) : s.carry(j) + 1, :] = carries[j]
    columns = [decay_columns(a) for a in logs]
    ends = [jnp.exp(a[C - 1 : C, :] - a) for a in columns]
    for h in range(s.heads):
        state = None
        for j in range(s.blocks):
            scaled = keys[s.block(j), s.head(h)].astype(F32) * ends[j][:, h : h + 1]
            update = dot(scaled.astype(BF16), values[s.block(j), s.head(h)], 0, 0)
            if j < s.blocks - 1:
                first_update[s.rows(j * s.heads + h, s.width), :] = update
            if state is None:
                state = update
            else:
                state = (carries[j] * factors[j][h : h + 1, :]) * state + update
        put_parts(lower, None, s.half, h, state, keep, send)


def chip_kernel(s, reverse, keep, received, tail, out_keep, out_send):
    core, chip, _ = place_bits(s.count, reverse)
    lower, left = core == 0, chip == 0
    base = s.heads * s.half
    other = received[base:, :]
    own = tail[: s.tail, :]
    far, near = lax.select(lower, own, other), lax.select(lower, other, own)
    link = equal(far[s.end : s.end + 1, :], near[s.start : s.start + 1, :])
    factor = near[: s.heads, :] * link
    top = s.heads * s.quarter
    out_send[top:, :] = far + near
    put_tail(
        s,
        out_send,
        top,
        far[: s.heads, :] * factor,
        far[s.start : s.start + 1, :],
        near[s.end : s.end + 1, :],
    )
    for h in range(s.heads):
        rows = s.rows(h, s.half)
        a, b = keep[rows, :], received[rows, :]
        far_state, near_state = lax.select(lower, a, b), lax.select(lower, b, a)
        total = near_state + factor[h : h + 1, :] * far_state
        put_parts(left, None, s.quarter, h, total, out_keep, out_send)


def plane_kernel(s, reverse, keep, sent, received, out):
    _, chip, _ = place_bits(s.count, reverse)
    left = chip == 0
    top = s.heads * s.quarter
    own, other = sent[top:, :], received[top:, :]
    far, near = lax.select(left, own, other), lax.select(left, other, own)
    link = equal(far[s.end : s.end + 1, :], near[s.start : s.start + 1, :])
    factor = near[: s.heads, :] * link
    out[top:, :] = far + near
    put_tail(
        s,
        out,
        top,
        far[: s.heads, :] * factor,
        far[s.start : s.start + 1, :],
        near[s.end : s.end + 1, :],
    )
    for h in range(s.heads):
        rows = s.rows(h, s.quarter)
        a, b = keep[rows, :], received[rows, :]
        far_state, near_state = lax.select(left, a, b), lax.select(left, b, a)
        out[rows, :] = near_state + factor[h : h + 1, :] * far_state


def spread_kernel(s, reverse, keep, sent, received, *rest):
    earlier, (out_keep, out_send) = rest[:-2], rest[-2:]
    _, chip, plane = place_bits(s.count, reverse)
    left = chip == 0
    top = s.heads * s.quarter
    own, other = sent[top:, :], received[top:, :]
    far, near = lax.select(left, own, other), lax.select(left, other, own)
    start, end = slice(s.start, s.start + 1), slice(s.end, s.end + 1)
    tails = [ref[top:, :] for ref in earlier]
    reach = [(plane >= w + 1).astype(F32) for w in range(len(earlier))]
    entry = equal(tails[0][end], far[start]) * reach[0]
    inner = [
        equal(tails[w + 1][end], tails[w][start]) * reach[w + 1] * tails[w][: s.heads, :]
        for w in range(len(earlier) - 1)
    ]
    link = equal(far[end], near[start])
    far_factor = far[: s.heads, :]
    for h in range(s.heads):
        rows, one = s.rows(h, s.quarter), slice(h, h + 1)
        state = earlier[-1][rows, :]
        for w in reversed(range(len(earlier) - 1)):
            state = earlier[w][rows, :] + inner[w][one] * state
        into_far = entry * state
        far_state = lax.select(left, keep[rows, :], received[rows, :])
        into_near = link * (far_state + far_factor[one] * into_far)
        out_keep[rows, :] = lax.select(left, into_far, into_near)
        out_send[rows, :] = lax.select(left, into_near, into_far)


def entry_kernel(s, reverse, chip_keep, chip_received, keep, received, tail, out_keep, out_send):
    core, chip, _ = place_bits(s.count, reverse)
    lower, left = core == 0, chip == 0
    base = s.heads * s.half
    other = received[base:, :]
    own = tail[: s.tail, :]
    far, near = lax.select(lower, own, other), lax.select(lower, other, own)
    link = equal(far[s.end : s.end + 1, :], near[s.start : s.start + 1, :])
    far_factor = far[: s.heads, :]
    for h in range(s.heads):
        rows, quarter = s.rows(h, s.half), s.rows(h, s.quarter)
        a, b = chip_keep[quarter, :], chip_received[quarter, :]
        into_far = jnp.concatenate([lax.select(left, a, b), lax.select(left, b, a)], axis=0)
        far_state = lax.select(lower, keep[rows, :], received[rows, :])
        into_near = link * (far_state + far_factor[h : h + 1, :] * into_far)
        out_keep[rows, :] = lax.select(lower, into_far, into_near)
        out_send[rows, :] = lax.select(lower, into_near, into_far)


def joined(s, lower, keep, received, h):
    rows = s.rows(h, s.half)
    a, b = keep[rows, :], received[rows, :]
    return jnp.concatenate([lax.select(lower, a, b), lax.select(lower, b, a)], axis=0)


def decay_mask(column, row):
    at, other = triangle()
    gap = jnp.minimum(column - row, 0.0)
    return jnp.where(at >= other, jnp.exp(gap), 0.0)


def local_kernel(s, queries, keys, values, log_decay, out, weights):
    for j in range(s.blocks):
        logs = log_decay[s.block(j), :]
        columns, rows = decay_columns(logs), decay_rows(logs)
        for h in range(s.heads):
            mask = decay_mask(columns[:, h : h + 1], rows[h : h + 1, :])
            part = (s.block(j), s.head(h))
            scores = dot(queries[part], keys[part], 1, 1)
            weight = (scores * mask).astype(BF16)
            weights[s.rows(j * s.heads + h, C), :] = weight
            out[part] = dot(weight, values[part], 1, 0)


def attention_kernel(
    s, queries, out_grad, gain, log_decay, tail, local, first_update, keep, received, out, sums
):
    core, _, _ = place_bits(s.count, False)
    lower = core == 0
    logs = [log_decay[s.block(j), :] for j in range(s.blocks)]
    factors = [jnp.exp(total_rows(a)) for a in logs]
    decays = [jnp.exp(decay_columns(a)) for a in logs]
    squares = [jnp.zeros((C, s.width), F32) for _ in logs]
    inners = [jnp.zeros((C, s.width), F32) for _ in logs]
    for h in range(s.heads):
        state = joined(s, lower, keep, received, h)
        for j in range(s.blocks):
            part = (s.block(j), s.head(h))
            far = far_dot(queries[part], state, 0)
            attention = local[part] + decays[j][:, h : h + 1] * far
            out[part] = attention
            squares[j] = squares[j] + attention * attention
            inners[j] = inners[j] + out_grad[part].astype(F32) * gain[:, s.head(h)] * attention
            if j < s.blocks - 1:
                update = first_update[s.rows(j * s.heads + h, s.width), :]
                carried = tail[s.carry(j + 1) : s.carry(j + 1) + 1, :]
                state = carried * (factors[j][h : h + 1, :] * state + update)
    sums[...] = jnp.zeros(sums.shape, F32)
    for j in range(s.blocks):
        sums[0:1, s.block(j)] = jnp.sum(squares[j].T, axis=0, keepdims=True)
        sums[1:2, s.block(j)] = jnp.sum(inners[j].T, axis=0, keepdims=True)


def grad_kernel(
    s, all_features, queries, out_grad, gain, log_decay, tail, attention, sums,
    attn_grad, keep, send, out_tail, back_terms,
):
    core, _, _ = place_bits(s.count, True)
    lower = core == 0
    logs = [log_decay[s.block(j), :] for j in range(s.blocks)]
    factors = [jnp.exp(total_rows(a)) for a in logs]
    decays = [jnp.exp(decay_columns(a)) for a in logs]
    totals = sums[...] / all_features
    spread = lambda row: jnp.broadcast_to(row, (C, C)).T
    inverses, slopes = [], []
    for j in range(s.blocks):
        inverse = lax.rsqrt(totals[0:1, s.block(j)] + EPSILON)
        inverses.append(spread(inverse))
        slopes.append(spread(totals[1:2, s.block(j)] * inverse * inverse))
    base = s.heads * s.half
    out_tail[...] = jnp.zeros(out_tail.shape, F32)
    own = tail[...]
    put_tail(
        s, out_tail, 0, own[: s.heads], own[s.end : s.end + 1], own[s.start : s.start + 1]
    )
    for h in range(s.heads):
        gain_row = gain[:, s.head(h)]
        gain_part = jnp.zeros((1, s.width), F32)
        terms = []
        for j in range(s.blocks):
            part = (s.block(j), s.head(h))
            cot = out_grad[part].astype(F32)
            att = attention[part]
            grad = ((cot * gain_row - att * slopes[j]) * inverses[j]).astype(BF16)
            attn_grad[part] = grad
            gain_part = gain_part + jnp.sum(cot * att * inverses[j], axis=0, keepdims=True)
            weighted = (queries[part].astype(F32) * decays[j][:, h : h + 1]).astype(BF16)
            term = dot(weighted, grad, 0, 0)
            terms.append(term)
            if j > 0:
                back_terms[s.rows((j - 1) * s.heads + h, s.width), :] = term
        state = terms[-1]
        for j in reversed(range(s.blocks - 1)):
            carried = tail[s.carry(j + 1) : s.carry(j + 1) + 1, :]
            state = terms[j] + (carried * factors[j][h : h + 1, :]) * state
        put_parts(lower, None, s.half, h, state, keep, send)
        out_tail[s.gain + h : s.gain + h + 1, :] = gain_part
    send[base:, :] = out_tail[...]


def local_grad_kernel(s, queries, values, log_decay, weights, attn_grad, key_out, value_out):
    for j in range(s.blocks):
        logs = log_decay[s.block(j), :]
        columns, rows = decay_columns(logs), decay_rows(logs)
        for h in range(s.heads):
            mask = decay_mask(columns[:, h : h + 1], rows[h : h + 1, :])
            part = (s.block(j), s.head(h))
            grad = attn_grad[part]
            grad_weight = (dot(grad, values[part], 1, 1) * mask).astype(BF16)
            key_out[part] = dot(grad_weight, queries[part], 0, 0)
            value_out[part] = dot(weights[s.rows(j * s.heads + h, C), :], grad, 0, 0)


def final_kernel(
    s, keys, values, log_decay, tail, key_local, value_local, back_terms, keep, received,
    key_out, value_out,
):
    core, _, _ = place_bits(s.count, True)
    lower = core == 0
    logs = [log_decay[s.block(j), :] for j in range(s.blocks)]
    factors = [jnp.exp(total_rows(a)) for a in logs]
    columns = [decay_columns(a) for a in logs]
    ends = [jnp.exp(a[C - 1 : C, :] - a) for a in columns]
    for h in range(s.heads):
        state = joined(s, lower, keep, received, h)
        for j in reversed(range(s.blocks)):
            part = (s.block(j), s.head(h))
            end = ends[j][:, h : h + 1]
            key_far = end * far_dot(values[part], state, 1)
            value_far = end * far_dot(keys[part], state, 0)
            key_out[part] = (key_local[part] + key_far).astype(BF16)
            value_out[part] = (value_local[part] + value_far).astype(BF16)
            if j > 0:
                carried = tail[s.carry(j) : s.carry(j) + 1, :]
                term = back_terms[s.rows((j - 1) * s.heads + h, s.width), :]
                state = carried * (term + factors[j][h : h + 1, :] * state)


def swap(value, axis, bit):
    count = lax.axis_size(axis)
    return lax.ppermute(value, axis, [(i, i ^ bit) for i in range(count)])


def next_plane(value, count, reverse):
    step = -PLANE if reverse else PLANE
    return lax.ppermute(value, "seq", [(i, (i + step) % count) for i in range(count)])


def scan_in(s, keep, send, tail, reverse, beside):
    quarter = shape(s.heads * s.quarter, s.width)
    quarter_tail = shape(s.heads * s.quarter + s.tail, s.width)
    half = shape(s.heads * s.half, s.width)
    with_args = functools.partial
    received = swap(send, "seq", 1)
    chip_keep, chip_sent = call(
        with_args(chip_kernel, s, reverse), [quarter, quarter_tail], keep, received, tail
    )
    chip_received = swap(chip_sent, "seq", 2)
    (plane,) = call(
        with_args(plane_kernel, s, reverse), [quarter_tail], chip_keep, chip_sent, chip_received
    )
    earlier = []
    passed = plane
    for _ in range(s.window):
        passed = next_plane(passed, s.count, reverse)
        earlier.append(passed)
    plane, local = beside(plane)
    into_keep, into_sent = call(
        with_args(spread_kernel, s, reverse),
        [quarter, quarter],
        chip_keep,
        chip_sent,
        chip_received,
        *earlier,
    )
    into_received = swap(into_sent, "seq", 2)
    out_keep, out_sent = call(
        with_args(entry_kernel, s, reverse),
        [half, half],
        into_keep,
        into_received,
        keep,
        received,
        tail,
    )
    out_received = swap(out_sent, "seq", 1)
    return out_keep, out_received, local, [plane] + earlier


def per_device(queries, keys, values, out_grad, log_decay, norm_gain, doc_ids):
    tokens, features = queries.shape
    heads = log_decay.shape[1]
    s = Sizes(tokens, features, heads, lax.axis_size("seq"))
    dp = lax.axis_size("dp")
    bind = functools.partial
    unit = 2 * C * C * C * s.blocks * heads
    doc_rows = jnp.broadcast_to(doc_ids.astype(F32)[:, None], (s.blocks, s.width))
    gain = norm_gain.reshape(1, features)
    half = shape(heads * s.half, s.width)
    half_tail = shape(heads * s.half + s.tail, s.width)
    rest = shape(max(1, s.blocks - 1) * heads * s.width, s.width)
    tail_rows = -(-s.carry(s.blocks) // 8) * 8
    keep, send, tail, first_update = call(
        bind(state_kernel, s),
        [half, half_tail, shape(tail_rows, s.width), rest],
        keys,
        values,
        log_decay,
        doc_rows,
        flops=unit,
    )

    def beside_forward(plane):
        local = call(
            bind(local_kernel, s),
            [shape(tokens, features), shape(s.blocks * heads * C, C, BF16)],
            queries,
            keys,
            values,
            log_decay,
            flops=2 * unit,
        )
        return plane, local

    state_keep, state_received, (local_out, weights), _ = scan_in(
        s, keep, send, tail, False, beside_forward
    )
    attention, sums = call(
        bind(attention_kernel, s),
        [shape(tokens, features), shape(8, tokens)],
        queries,
        out_grad,
        gain,
        log_decay,
        tail,
        local_out,
        first_update,
        state_keep,
        state_received,
        flops=2 * unit,
    )
    if dp & (dp - 1):
        sums = lax.psum(sums, "dp")
    else:
        bit = 1
        while bit < dp:
            sums = sums + swap(sums, "dp", bit)
            bit *= 2
    attn_grad, keep, send, back_tail, back_terms = call(
        bind(grad_kernel, s, features * dp),
        [shape(tokens, features, BF16), half, half_tail, shape(s.tail, s.width), rest],
        queries,
        out_grad,
        gain,
        log_decay,
        tail,
        attention,
        sums,
        flops=unit,
    )

    def beside_backward(plane):
        local = call(
            bind(local_grad_kernel, s),
            [shape(tokens, features), shape(tokens, features)],
            queries,
            values,
            log_decay,
            weights,
            attn_grad,
            flops=3 * unit,
        )
        return plane, local

    grad_keep, grad_received, (key_local, value_local), parts = scan_in(
        s, keep, send, back_tail, True, beside_backward
    )
    top = heads * s.quarter
    gains = [a[top + s.gain : top + s.gain + heads] for a in parts]
    while len(gains) < s.planes:
        gains.append(next_plane(gains[-1], s.count, True))
    gain_grad = sum(gains[1:], gains[0]).reshape(features)
    key_grad, value_grad = call(
        bind(final_kernel, s),
        [shape(tokens, features, BF16), shape(tokens, features, BF16)],
        keys,
        values,
        log_decay,
        tail,
        key_local,
        value_local,
        back_terms,
        grad_keep,
        grad_received,
        flops=4 * unit,
    )
    return (key_grad, value_grad, gain_grad)


def solution(mesh):
    placed = (
        P("seq", "dp"),
        P("seq", "dp"),
        P("seq", "dp"),
        P("seq", "dp"),
        P("seq", "dp"),
        P("dp"),
        P("seq"),
    )
    return jax.shard_map(
        per_device,
        mesh=mesh,
        in_specs=placed,
        out_specs=(P("seq", "dp"), P("seq", "dp"), P("dp")),
        check_vma=False,
    )
```

time: 334 us -> 86.8 us (0.26)
  blocking collectives: 95.8 us -> 0 us
  waiting for transfers between devices: 126 us -> 49.6 us
  other arithmetic: 33.4 us -> 1.27 us
  matrix products: 28 us -> 0 us
  local copies, waits for them, and re-layouts: 29.5 us -> 3.2 us
  between operations: 16.3 us -> 0.85 us
  starting transfers between devices: 3.25 us -> 17.9 us
  Pallas kernels: 0 us -> 13.8 us
    all_gather x2 -> x0, waiting for transfers between devices: 126 us -> none  [carried_in(): gathered = jax.tree.map(lambda a: lax.all_gather(a, axis), part)]
    unnamed x2 -> x0, blocking collectives: 85.7 us -> none
    ppermute x1 -> x14, waiting for transfers between devices: 0.01 us -> 49.6 us  [the longest x9 25 us: swap(): return lax.ppermute(value, axis, [(i, i ^ bit) for i in range(count)])]
    dot_general x9 -> x0, matrix products: 28 us -> none  [the longest x1 4.9 us: far_grads(): jnp.einsum('nshe,nhde->nshd', value_end, later_grad, precision=lax.Precis...]
    add x19 -> x1, other arithmetic: 20.5 us -> 0.01 us  [per_device(): sums = sums + swap(sums, 'dp', bit)]
    ppermute x1 -> x14, starting transfers between devices: 3.17 us -> 17.9 us  [the longest x9 9.91 us: swap(): return lax.ppermute(value, axis, [(i, i ^ bit) for i in range(count)])]
    pallas_call x0 -> x14, Pallas kernels: none -> 13.8 us  [call(): pl.pallas_call(kernel, out_shape=outs, in_specs=[pl.BlockSpec(memory_spac...]
    psum x2 -> x0, blocking collectives: 10.1 us -> none  [per_device(): square_total, inner_total = lax.psum((square_part, inner_part), 'dp')]
  transfers between devices with their start and end apart: 3 -> 14, of which waited for: 2 -> 11; matrix products, arithmetic and copies ran while one was open for 4% -> 1% of each run, Pallas kernels for 0% -> 7%
where the time goes in v1:
time: 86.8 us; the launch traced here: 86.5 us
  waiting for transfers between devices  49.6 us (57%)
  starting transfers between devices  17.9 us (21%)
  Pallas kernels  13.8 us (16%)
  local copies, waits for them, and re-layouts  3.2 us (4%)
  other arithmetic  1.27 us (1%)
    ppermute x9, waiting for transfers between devices, swap(): return lax.ppermute(value, axis, [(i, i ^ bit) for i in range(count)])  25 us
    ppermute x5, waiting for transfers between devices, next_plane(): lax.ppermute(value, 'seq', [(i, (i + step) % count) for i in range(count)])  24.6 us
    pallas_call x14, Pallas kernels, call(): pl.pallas_call(kernel, out_shape=outs, in_specs=[pl.BlockSpec(memory_spac...  13.8 us
    ppermute x9, starting transfers between devices, swap(): return lax.ppermute(value, axis, [(i, i ^ bit) for i in range(count)])  9.91 us
    ppermute x5, starting transfers between devices, next_plane(): lax.ppermute(value, 'seq', [(i, (i + step) % count) for i in range(count)])  7.96 us
    unnamed x15, local copies, waits for them, and re-layouts  3.12 us
  transfers between devices with their start and end apart: 14, of which 11 were waited for; matrix products, arithmetic and copies ran while one was open for 1% of the time, Pallas kernels for 7%

profile of v1, /device:TPU:0, one launch (start us, length us, event | category | flops | bytes accessed | tf_op | source)
XLA Modules:
  0.0 86.5 jit_solution(11420066740287120520)
XLA Ops:
  0.6 0.7 convert_element_type.3
  1.3 0.8 copy.15.log_decay
  2.1 0.1 broadcast_in_dim.2.doc_rows
  2.2 1.1 %copy-done.1 = bf16[256,1536]{1,0:T(8,128)(2,1)S(1)} copy-done((bf16[256,1536]{1,0:T(8,128)(2,1)S(1)}, bf16[256,1536]{1,0:T(8,128)(2,1)}, u32[]{:S(2)}) %copy-start.1) | copy-done | bytes 786456
  3.3 1.1 %copy-done.3 = bf16[256,1536]{1,0:T(8,128)(2,1)S(1)} copy-done((bf16[256,1536]{1,0:T(8,128)(2,1)S(1)}, bf16[256,1536]{1,0:T(8,128)(2,1)}, u32[]{:S(2)}) %copy-start.3) | copy-done | bytes 786456
  4.5 1.5 %shard_map.94 = (f32[768,128]{1,0:T(8,128)S(1)}, f32[800,128]{1,0:T(8,128)S(1)}, f32[32,128]{1,0:T(8,128)S(1)}, f32[1536,128]{1,0:T(8,128)S(1)}) custom-call(bf16[256,1536]{1,0:T(8,128)(2,1)S(1)} %copy-done.3, bf16[256,1536]{1,0:T(8,128)(2,1)S(1)} %copy-done.1, f32[256,12]{1,0:T(8,128)S(1)} %copy.15.log_decay, f32[2,128]{1,0:T(2,128)S(1)} %broadcast_in_dim.2.doc_rows), custom_call_target="tpu_custom_call" | custom-call | flops 100663296 | bytes 3191808 | tf_op jit(solution)/shard_map/pallas_call | solution.py:99
  5.9 0.5 collective-permute-start
  6.4 1.4 %collective-permute-done.received = f32[800,128]{1,0:T(8,128)S(1)} collective-permute-done((f32[800,128]{1,0:T(8,128)S(1)}, f32[800,128]{1,0:T(8,128)S(1)}, u32[]{:S(2)}, u32[]{:S(2)}) %collective-permute-start) | collective-permute-done | bytes 409632 | tf_op jit(solution)/shard_map/ppermute | solution.py:401
  7.8 0.1 shard_map.96
  7.9 0.0 copy-start.6
  7.9 0.0 copy-start
  7.9 0.0 copy-start.2
  7.9 0.0 copy-start.4
  7.9 2.9 %collective-permute-start.1 = (f32[416,128]{1,0:T(8,128)S(1)}, f32[416,128]{1,0:T(8,128)S(1)}, u32[]{:S(2)}, u32[]{:S(2)}) collective-permute-start(f32[416,128]{1,0:T(8,128)S(1)} %get-tuple-element.39.sent), channel_id=1, source_target_pairs={{0,2},{1,3},{2,0},{3,1},{4,6},{5,7},{6,4},{7,5},{8,10},{9,11},{10,... | collective-permute-start | bytes 638984 | tf_op jit(solution)/shard_map/ppermute | solution.py:401
  10.9 5.6 %collective-permute-done.1.received = f32[416,128]{1,0:T(8,128)S(1)} collective-permute-done((f32[416,128]{1,0:T(8,128)S(1)}, f32[416,128]{1,0:T(8,128)S(1)}, u32[]{:S(2)}, u32[]{:S(2)}) %collective-permute-start.1) | collective-permute-done | bytes 213024 | tf_op jit(solution)/shard_map/ppermute | solution.py:401
  16.5 1.9 %collective-permute-start.2 = (f32[416,128]{1,0:T(8,128)S(1)}, f32[416,128]{1,0:T(8,128)S(1)}, u32[]{:S(2)}, u32[]{:S(2)}) collective-permute-start(f32[416,128]{1,0:T(8,128)S(1)} %shard_map.97), channel_id=1, source_target_pairs={{0,4},{1,5},{2,6},{3,7},{4,8},{5,9},{6,10},{7,11},{8,12},{9,13},{1... | collective-permute-start | bytes 638984 | tf_op jit(solution)/shard_map/ppermute | solution.py:406
  18.4 6.8 %collective-permute-done.2.rest_0_ = f32[416,128]{1,0:T(8,128)S(1)} collective-permute-done((f32[416,128]{1,0:T(8,128)S(1)}, f32[416,128]{1,0:T(8,128)S(1)}, u32[]{:S(2)}, u32[]{:S(2)}) %collective-permute-start.2) | collective-permute-done | bytes 213024 | tf_op jit(solution)/shard_map/ppermute | solution.py:406
  25.1 0.0 collective-permute-start.3
  25.1 7.6 %collective-permute-done.3.rest_1_ = f32[416,128]{1,0:T(8,128)S(1)} collective-permute-done((f32[416,128]{1,0:T(8,128)S(1)}, f32[416,128]{1,0:T(8,128)S(1)}, u32[]{:S(2)}, u32[]{:S(2)}) %collective-permute-start.3) | collective-permute-done | bytes 213024 | tf_op jit(solution)/shard_map/ppermute | solution.py:406
  32.8 0.1 shard_map.98
  32.8 1.6 %collective-permute-start.4 = (f32[384,128]{1,0:T(8,128)S(1)}, f32[384,128]{1,0:T(8,128)S(1)}, u32[]{:S(2)}, u32[]{:S(2)}) collective-permute-start(f32[384,128]{1,0:T(8,128)S(1)} %get-tuple-element.41), channel_id=1, source_target_pairs={{0,2},{1,3},{2,0},{3,1},{4,6},{5,7},{6,4},{7,5},{8,10},{9,11},{10,... | collective-permute-start | bytes 589832 | tf_op jit(solution)/shard_map/ppermute | solution.py:401
  34.4 4.2 %collective-permute-done.4.chip_received = f32[384,128]{1,0:T(8,128)S(1)} collective-permute-done((f32[384,128]{1,0:T(8,128)S(1)}, f32[384,128]{1,0:T(8,128)S(1)}, u32[]{:S(2)}, u32[]{:S(2)}) %collective-permute-start.4) | collective-permute-done | bytes 196640 | tf_op jit(solution)/shard_map/ppermute | solution.py:401
  38.6 0.1 shard_map.99
  38.7 0.1 collective-permute-start.5
  38.8 4.1 %shard_map.95 = (f32[256,1536]{1,0:T(8,128)S(1)}, bf16[3072,128]{1,0:T(8,128)(2,1)S(1)}) custom-call(bf16[256,1536]{1,0:T(8,128)(2,1)S(1)} %copy-done, bf16[256,1536]{1,0:T(8,128)(2,1)S(1)} %copy-done.4, bf16[256,1536]{1,0:T(8,128)(2,1)S(1)} %copy-done.2, f32[256,12]{1,0:T(8,128)S(1)} %copy.15.log_decay), custom_call_target="tpu_custom_call" | custom-call | flops 201326592 | bytes 4730880 | tf_op jit(solution)/shard_map/pallas_call | solution.py:99
  43.0 1.2 %shard_map.100 = (f32[256,1536]{1,0:T(8,128)S(1)}, f32[8,256]{1,0:T(8,128)S(1)}) custom-call(bf16[256,1536]{1,0:T(8,128)(2,1)S(1)} %copy-done, bf16[256,1536]{1,0:T(8,128)(2,1)S(1)} %copy-done.5, f32[1,1536]{1,0:T(1,128)S(1)} %reshape.13.gain, f32[256,12]{1,0:T(8,128)S(1)} %copy.15.log_decay, f32[32,128]{1,0:T(8,128)S(1)} %get-tuple-element.32.tail, ...), custom_call_target="tpu_custom_call" | custom-call | flops 201326592 | bytes 6334464 | tf_op jit(solution)/shard_map/pallas_call | solution.py:99
  44.2 1.6 %collective-permute-start.6 = (f32[8,256]{1,0:T(8,128)S(1)}, f32[8,256]{1,0:T(8,128)S(1)}, u32[]{:S(2)}, u32[]{:S(2)}) collective-permute-start(f32[8,256]{1,0:T(8,128)S(1)} %get-tuple-element.45), channel_id=1, source_target_pairs={{0,16},{16,0},{1,17},{17,1},{2,18},{18,2},{3,19},{19,3},{4,20},{20... | collective-permute-start | bytes 24584 | tf_op jit(solution)/shard_map/ppermute | solution.py:401
  45.8 2.1 %collective-permute-done.6 = f32[8,256]{1,0:T(8,128)S(1)} collective-permute-done((f32[8,256]{1,0:T(8,128)S(1)}, f32[8,256]{1,0:T(8,128)S(1)}, u32[]{:S(2)}, u32[]{:S(2)}) %collective-permute-start.6) | collective-permute-done | bytes 8224 | tf_op jit(solution)/shard_map/ppermute | solution.py:401
  47.9 1.5 %shard_map.101 = (bf16[256,1536]{1,0:T(8,128)(2,1)S(1)}, f32[768,128]{1,0:T(8,128)S(1)}, f32[800,128]{1,0:T(8,128)S(1)}, f32[32,128]{1,0:T(8,128)S(1)}, f32[1536,128]{1,0:T(8,128)S(1)}) custom-call(bf16[256,1536]{1,0:T(8,128)(2,1)S(1)} %copy-done, bf16[256,1536]{1,0:T(8,128)(2,1)S(1)} %copy-done.5, f32[1,1536]{1,0:T(1,128)S(1)} %reshape.13.gain, ...), custom_call_target="tpu_custom_call" | custom-call | flops 100663296 | bytes 5580800 | tf_op jit(solution)/shard_map/pallas_call | solution.py:99
  49.4 0.1 collective-permute-start.7
  49.5 1.7 %collective-permute-done.7.received = f32[800,128]{1,0:T(8,128)S(1)} collective-permute-done((f32[800,128]{1,0:T(8,128)S(1)}, f32[800,128]{1,0:T(8,128)S(1)}, u32[]{:S(2)}, u32[]{:S(2)}) %collective-permute-start.7) | collective-permute-done | bytes 409632 | tf_op jit(solution)/shard_map/ppermute | solution.py:401
  51.2 0.1 shard_map.103
  51.3 1.6 %collective-permute-start.8 = (f32[416,128]{1,0:T(8,128)S(1)}, f32[416,128]{1,0:T(8,128)S(1)}, u32[]{:S(2)}, u32[]{:S(2)}) collective-permute-start(f32[416,128]{1,0:T(8,128)S(1)} %get-tuple-element.54.sent), channel_id=1, source_target_pairs={{0,2},{1,3},{2,0},{3,1},{4,6},{5,7},{6,4},{7,5},{8,10},{9,11},{10,... | collective-permute-start | bytes 638984 | tf_op jit(solution)/shard_map/ppermute | solution.py:401
  52.9 5.8 %collective-permute-done.8.received = f32[416,128]{1,0:T(8,128)S(1)} collective-permute-done((f32[416,128]{1,0:T(8,128)S(1)}, f32[416,128]{1,0:T(8,128)S(1)}, u32[]{:S(2)}, u32[]{:S(2)}) %collective-permute-start.8) | collective-permute-done | bytes 213024 | tf_op jit(solution)/shard_map/ppermute | solution.py:401
  58.7 0.1 collective-permute-start.9
  58.8 6.5 %collective-permute-done.9.rest_0_ = f32[416,128]{1,0:T(8,128)S(1)} collective-permute-done((f32[416,128]{1,0:T(8,128)S(1)}, f32[416,128]{1,0:T(8,128)S(1)}, u32[]{:S(2)}, u32[]{:S(2)}) %collective-permute-start.9) | collective-permute-done | bytes 213024 | tf_op jit(solution)/shard_map/ppermute | solution.py:406
  65.2 2.1 %collective-permute-start.10 = (f32[416,128]{1,0:T(8,128)S(1)}, f32[416,128]{1,0:T(8,128)S(1)}, u32[]{:S(2)}, u32[]{:S(2)}) collective-permute-start(f32[416,128]{1,0:T(8,128)S(1)} %collective-permute-done.9.rest_0_), channel_id=1, source_target_pairs={{0,12},{1,13},{2,14},{3,15},{4,0},{5,1},{6,2},{7,3},{8,4},{9,5},{1... | collective-permute-start | bytes 638984 | tf_op jit(solution)/shard_map/ppermute | solution.py:406
  67.3 3.8 %collective-permute-done.10.rest_1_ = f32[416,128]{1,0:T(8,128)S(1)} collective-permute-done((f32[416,128]{1,0:T(8,128)S(1)}, f32[416,128]{1,0:T(8,128)S(1)}, u32[]{:S(2)}, u32[]{:S(2)}) %collective-permute-start.10) | collective-permute-done | bytes 213024 | tf_op jit(solution)/shard_map/ppermute | solution.py:406
  71.1 0.1 shard_map.105
  71.2 1.6 %collective-permute-start.11 = (f32[384,128]{1,0:T(8,128)S(1)}, f32[384,128]{1,0:T(8,128)S(1)}, u32[]{:S(2)}, u32[]{:S(2)}) collective-permute-start(f32[384,128]{1,0:T(8,128)S(1)} %get-tuple-element.56), channel_id=1, source_target_pairs={{0,2},{1,3},{2,0},{3,1},{4,6},{5,7},{6,4},{7,5},{8,10},{9,11},{10,... | collective-permute-start | bytes 589832 | tf_op jit(solution)/shard_map/ppermute | solution.py:401
  72.7 4.2 %collective-permute-done.11.chip_received = f32[384,128]{1,0:T(8,128)S(1)} collective-permute-done((f32[384,128]{1,0:T(8,128)S(1)}, f32[384,128]{1,0:T(8,128)S(1)}, u32[]{:S(2)}, u32[]{:S(2)}) %collective-permute-start.11) | collective-permute-done | bytes 196640 | tf_op jit(solution)/shard_map/ppermute | solution.py:401
  76.9 0.1 shard_map.106
  77.0 0.1 collective-permute-start.12
  77.1 3.9 %collective-permute-start.13 = (f32[12,128]{1,0:T(8,128)S(1)}, f32[12,128]{1,0:T(8,128)S(1)}, u32[]{:S(2)}, u32[]{:S(2)}) collective-permute-start(f32[12,128]{1,0:T(8,128)S(1)} %slice.14), channel_id=1, source_target_pairs={{0,12},{1,13},{2,14},{3,15},{4,0},{5,1},{6,2},{7,3},{8,4},{9,5},{1... | collective-permute-start | bytes 18440 | tf_op jit(solution)/shard_map/ppermute | solution.py:406
  81.0 1.9 %shard_map.102 = (f32[256,1536]{1,0:T(8,128)S(1)}, f32[256,1536]{1,0:T(8,128)S(1)}) custom-call(bf16[256,1536]{1,0:T(8,128)(2,1)S(1)} %copy-done, bf16[256,1536]{1,0:T(8,128)(2,1)S(1)} %copy-done.2, f32[256,12]{1,0:T(8,128)S(1)} %copy.15.log_decay, bf16[3072,128]{1,0:T(8,128)(2,1)S(1)} %get-tuple-element.33.weights, ...), custom_call_target="tpu_custom_call" | custom-call | flops 301989888 | bytes 6303744 | tf_op jit(solution)/shard_map/pallas_call | solution.py:99
  83.0 0.6 fusion.2
  83.6 0.0 collective-permute-done.12.received
  83.6 2.9 %shard_map.107 = (bf16[256,1536]{1,0:T(8,128)(2,1)}, bf16[256,1536]{1,0:T(8,128)(2,1)}) custom-call(bf16[256,1536]{1,0:T(8,128)(2,1)S(1)} %copy-done.4, bf16[256,1536]{1,0:T(8,128)(2,1)S(1)} %copy-done.2, f32[256,12]{1,0:T(8,128)S(1)} %copy.15.log_decay, f32[32,128]{1,0:T(8,128)S(1)} %get-tuple-element.32.tail, f32[256,1536]{1,0:T(8,128)S(1)} %get-tuple-element.47.key_local, ...), custom_call_target="tpu_custom_call" | custom-call | flops 402653184 | bytes 7892992 | tf_op jit(solution)/shard_map/pallas_call | solution.py:99
  (15 shorter events, 0.1 us)
Async XLA Ops:
  2.2 1.1 %copy-start.1 = (bf16[256,1536]{1,0:T(8,128)(2,1)S(1)}, bf16[256,1536]{1,0:T(8,128)(2,1)}, u32[]{:S(2)}) copy-start(bf16[256,1536]{1,0:T(8,128)(2,1)} %values.7) | copy-start | bytes 2359300
  3.3 1.1 %copy-start.3 = (bf16[256,1536]{1,0:T(8,128)(2,1)S(1)}, bf16[256,1536]{1,0:T(8,128)(2,1)}, u32[]{:S(2)}) copy-start(bf16[256,1536]{1,0:T(8,128)(2,1)} %keys.5) | copy-start | bytes 2359300
  5.9 1.9 %collective-permute-start = (f32[800,128]{1,0:T(8,128)S(1)}, f32[800,128]{1,0:T(8,128)S(1)}, u32[]{:S(2)}, u32[]{:S(2)}) collective-permute-start(f32[800,128]{1,0:T(8,128)S(1)} %get-tuple-element.37), channel_id=1, source_target_pairs={{0,1},{1,0},{2,3},{3,2},{4,5},{5,4},{6,7},{7,6},{8,9},{9,8},{10,11... | collective-permute-start | bytes 1228808 | tf_op jit(solution)/shard_map/ppermute | solution.py:401
  7.9 30.9 %copy-start.6 = (f32[1536]{0:T(1024)S(1)}, f32[1536]{0:T(1024)}, u32[]{:S(2)}) copy-start(f32[1536]{0:T(1024)} %param.12) | copy-start | bytes 18436
  7.9 30.9 %copy-start = (bf16[256,1536]{1,0:T(8,128)(2,1)S(1)}, bf16[256,1536]{1,0:T(8,128)(2,1)}, u32[]{:S(2)}) copy-start(bf16[256,1536]{1,0:T(8,128)(2,1)} %queries.7) | copy-start | bytes 2359300
  7.9 30.9 %copy-start.2 = (bf16[256,1536]{1,0:T(8,128)(2,1)S(1)}, bf16[256,1536]{1,0:T(8,128)(2,1)}, u32[]{:S(2)}) copy-start(bf16[256,1536]{1,0:T(8,128)(2,1)} %values.7) | copy-start | bytes 2359300
  7.9 30.9 %copy-start.4 = (bf16[256,1536]{1,0:T(8,128)(2,1)S(1)}, bf16[256,1536]{1,0:T(8,128)(2,1)}, u32[]{:S(2)}) copy-start(bf16[256,1536]{1,0:T(8,128)(2,1)} %keys.5) | copy-start | bytes 2359300
  7.9 8.5 %collective-permute-start.1 = (f32[416,128]{1,0:T(8,128)S(1)}, f32[416,128]{1,0:T(8,128)S(1)}, u32[]{:S(2)}, u32[]{:S(2)}) collective-permute-start(f32[416,128]{1,0:T(8,128)S(1)} %get-tuple-element.39.sent), channel_id=1, source_target_pairs={{0,2},{1,3},{2,0},{3,1},{4,6},{5,7},{6,4},{7,5},{8,10},{9,11},{10,... | collective-permute-start | bytes 638984 | tf_op jit(solution)/shard_map/ppermute | solution.py:401
  16.5 8.6 %collective-permute-start.2 = (f32[416,128]{1,0:T(8,128)S(1)}, f32[416,128]{1,0:T(8,128)S(1)}, u32[]{:S(2)}, u32[]{:S(2)}) collective-permute-start(f32[416,128]{1,0:T(8,128)S(1)} %shard_map.97), channel_id=1, source_target_pairs={{0,4},{1,5},{2,6},{3,7},{4,8},{5,9},{6,10},{7,11},{8,12},{9,13},{1... | collective-permute-start | bytes 638984 | tf_op jit(solution)/shard_map/ppermute | solution.py:406
  25.1 7.6 %collective-permute-start.3 = (f32[416,128]{1,0:T(8,128)S(1)}, f32[416,128]{1,0:T(8,128)S(1)}, u32[]{:S(2)}, u32[]{:S(2)}) collective-permute-start(f32[416,128]{1,0:T(8,128)S(1)} %collective-permute-done.2.rest_0_), channel_id=1, source_target_pairs={{0,4},{1,5},{2,6},{3,7},{4,8},{5,9},{6,10},{7,11},{8,12},{9,13},{1... | collective-permute-start | bytes 638984 | tf_op jit(solution)/shard_map/ppermute | solution.py:406
  32.8 5.7 %collective-permute-start.4 = (f32[384,128]{1,0:T(8,128)S(1)}, f32[384,128]{1,0:T(8,128)S(1)}, u32[]{:S(2)}, u32[]{:S(2)}) collective-permute-start(f32[384,128]{1,0:T(8,128)S(1)} %get-tuple-element.41), channel_id=1, source_target_pairs={{0,2},{1,3},{2,0},{3,1},{4,6},{5,7},{6,4},{7,5},{8,10},{9,11},{10,... | collective-permute-start | bytes 589832 | tf_op jit(solution)/shard_map/ppermute | solution.py:401
  38.6 4.4 %copy-start.5 = (bf16[256,1536]{1,0:T(8,128)(2,1)S(1)}, bf16[256,1536]{1,0:T(8,128)(2,1)}, u32[]{:S(2)}) copy-start(bf16[256,1536]{1,0:T(8,128)(2,1)} %out_grad.3) | copy-start | bytes 2359300
  38.7 4.3 %collective-permute-start.5 = (f32[768,128]{1,0:T(8,128)S(1)}, f32[768,128]{1,0:T(8,128)S(1)}, u32[]{:S(2)}, u32[]{:S(2)}) collective-permute-start(f32[768,128]{1,0:T(8,128)S(1)} %get-tuple-element.43), channel_id=1, source_target_pairs={{0,1},{1,0},{2,3},{3,2},{4,5},{5,4},{6,7},{7,6},{8,9},{9,8},{10,11... | collective-permute-start | bytes 1179656 | tf_op jit(solution)/shard_map/ppermute | solution.py:401
  44.2 3.7 %collective-permute-start.6 = (f32[8,256]{1,0:T(8,128)S(1)}, f32[8,256]{1,0:T(8,128)S(1)}, u32[]{:S(2)}, u32[]{:S(2)}) collective-permute-start(f32[8,256]{1,0:T(8,128)S(1)} %get-tuple-element.45), channel_id=1, source_target_pairs={{0,16},{16,0},{1,17},{17,1},{2,18},{18,2},{3,19},{19,3},{4,20},{20... | collective-permute-start | bytes 24584 | tf_op jit(solution)/shard_map/ppermute | solution.py:401
  49.4 1.8 %collective-permute-start.7 = (f32[800,128]{1,0:T(8,128)S(1)}, f32[800,128]{1,0:T(8,128)S(1)}, u32[]{:S(2)}, u32[]{:S(2)}) collective-permute-start(f32[800,128]{1,0:T(8,128)S(1)} %get-tuple-element.51), channel_id=1, source_target_pairs={{0,1},{1,0},{2,3},{3,2},{4,5},{5,4},{6,7},{7,6},{8,9},{9,8},{10,11... | collective-permute-start | bytes 1228808 | tf_op jit(solution)/shard_map/ppermute | solution.py:401
  51.3 7.4 %collective-permute-start.8 = (f32[416,128]{1,0:T(8,128)S(1)}, f32[416,128]{1,0:T(8,128)S(1)}, u32[]{:S(2)}, u32[]{:S(2)}) collective-permute-start(f32[416,128]{1,0:T(8,128)S(1)} %get-tuple-element.54.sent), channel_id=1, source_target_pairs={{0,2},{1,3},{2,0},{3,1},{4,6},{5,7},{6,4},{7,5},{8,10},{9,11},{10,... | collective-permute-start | bytes 638984 | tf_op jit(solution)/shard_map/ppermute | solution.py:401
  58.7 6.5 %collective-permute-start.9 = (f32[416,128]{1,0:T(8,128)S(1)}, f32[416,128]{1,0:T(8,128)S(1)}, u32[]{:S(2)}, u32[]{:S(2)}) collective-permute-start(f32[416,128]{1,0:T(8,128)S(1)} %shard_map.104), channel_id=1, source_target_pairs={{0,12},{1,13},{2,14},{3,15},{4,0},{5,1},{6,2},{7,3},{8,4},{9,5},{1... | collective-permute-start | bytes 638984 | tf_op jit(solution)/shard_map/ppermute | solution.py:406
  65.2 5.8 %collective-permute-start.10 = (f32[416,128]{1,0:T(8,128)S(1)}, f32[416,128]{1,0:T(8,128)S(1)}, u32[]{:S(2)}, u32[]{:S(2)}) collective-permute-start(f32[416,128]{1,0:T(8,128)S(1)} %collective-permute-done.9.rest_0_), channel_id=1, source_target_pairs={{0,12},{1,13},{2,14},{3,15},{4,0},{5,1},{6,2},{7,3},{8,4},{9,5},{1... | collective-permute-start | bytes 638984 | tf_op jit(solution)/shard_map/ppermute | solution.py:406
  71.2 5.7 %collective-permute-start.11 = (f32[384,128]{1,0:T(8,128)S(1)}, f32[384,128]{1,0:T(8,128)S(1)}, u32[]{:S(2)}, u32[]{:S(2)}) collective-permute-start(f32[384,128]{1,0:T(8,128)S(1)} %get-tuple-element.56), channel_id=1, source_target_pairs={{0,2},{1,3},{2,0},{3,1},{4,6},{5,7},{6,4},{7,5},{8,10},{9,11},{10,... | collective-permute-start | bytes 589832 | tf_op jit(solution)/shard_map/ppermute | solution.py:401
  77.0 6.6 %collective-permute-start.12 = (f32[768,128]{1,0:T(8,128)S(1)}, f32[768,128]{1,0:T(8,128)S(1)}, u32[]{:S(2)}, u32[]{:S(2)}) collective-permute-start(f32[768,128]{1,0:T(8,128)S(1)} %get-tuple-element.58), channel_id=1, source_target_pairs={{0,1},{1,0},{2,3},{3,2},{4,5},{5,4},{6,7},{7,6},{8,9},{9,8},{10,11... | collective-permute-start | bytes 1179656 | tf_op jit(solution)/shard_map/ppermute | solution.py:401
  77.1 5.9 %collective-permute-start.13 = (f32[12,128]{1,0:T(8,128)S(1)}, f32[12,128]{1,0:T(8,128)S(1)}, u32[]{:S(2)}, u32[]{:S(2)}) collective-permute-start(f32[12,128]{1,0:T(8,128)S(1)} %slice.14), channel_id=1, source_target_pairs={{0,12},{1,13},{2,14},{3,15},{4,0},{5,1},{6,2},{7,3},{8,4},{9,5},{1... | collective-permute-start | bytes 18440 | tf_op jit(solution)/shard_map/ppermute | solution.py:406

commit v2 on v1

v2 whole, which is shorter than its diff:
```python
import functools

import jax
import jax.numpy as jnp
from jax import lax
from jax.experimental import pallas as pl
from jax.experimental.pallas import tpu as pltpu
from jax.sharding import PartitionSpec as P

C = 128
EPSILON = 1e-06
PLANE = 4
WAVES = (1,)
F32 = jnp.float32
BF16 = jnp.bfloat16
HIGHEST = lax.Precision.HIGHEST


def dot(a, b, contract_a, contract_b, precision=None):
    return lax.dot_general(
        a,
        b,
        (((contract_a,), (contract_b,)), ((), ())),
        precision=precision,
        preferred_element_type=F32,
    )


def two_parts(a):
    high = a.astype(BF16)
    return high, (a - high.astype(F32)).astype(BF16)


def far_dot(a, state, contract_state):
    high, low = two_parts(state)
    return dot(a, high, 1, contract_state) + dot(a, low, 1, contract_state)


def equal(a, b):
    return (a == b).astype(F32)


def place_bits(count, reverse):
    place = lax.axis_index("seq")
    place = count - 1 - place if reverse else place
    return lax.rem(place, 2), lax.rem(place // 2, 2), place // PLANE


def triangle():
    row = lax.broadcasted_iota(jnp.int32, (C, C), 0)
    column = lax.broadcasted_iota(jnp.int32, (C, C), 1)
    return row, column


def decay_columns(log_block):
    row, column = triangle()
    return dot((row >= column).astype(F32), log_block, 1, 1, HIGHEST)


def decay_rows(log_block):
    row, column = triangle()
    return dot(log_block, (row <= column).astype(F32), 1, 0, HIGHEST)


def total_rows(log_block):
    return dot(log_block, jnp.ones((C, C), F32), 1, 0, HIGHEST)


class Sizes:
    def __init__(self, tokens, features, all_heads, count, wave, waves):
        self.tokens, self.features, self.count = tokens, features, count
        self.heads = all_heads // waves
        self.first = wave * self.heads
        self.wave = wave
        self.blocks = tokens // C
        self.width = features // all_heads
        self.half = self.width // 2
        self.quarter = self.width // 4
        self.columns = self.heads * self.width
        self.planes = count // PLANE
        longest = self.blocks * count // 2
        per_plane = self.blocks * PLANE
        self.window = max(1, min(self.planes - 1, 1 + (longest - 2) // per_plane))
        self.gains = -(-self.heads // 8) * 8
        self.tail = -(-(self.heads + 2) // 8) * 8
        self.start, self.end = self.heads, self.heads + 1
        self.notes = -(-(self.heads + 2 + self.blocks) // 8) * 8

    def own(self, h):
        return slice(h * self.width, (h + 1) * self.width)

    def head(self, h):
        return self.own(self.first + h)

    def block(self, j):
        return slice(j * C, (j + 1) * C)

    def rows(self, h, size):
        return slice(h * size, (h + 1) * size)

    def carry(self, j):
        return slice(self.heads + 2 + j, self.heads + 3 + j)

    def logs(self, log_decay):
        return [
            log_decay[self.first : self.first + self.heads, self.block(j)]
            for j in range(self.blocks)
        ]


def call(kernel, outs, *args, flops=0, spaces=None, out_spaces=None, scratch=()):
    moved = sum(a.size * a.dtype.itemsize for a in args) + sum(
        o.size * o.dtype.itemsize for o in outs
    )
    spaces = spaces or [pltpu.VMEM] * len(args)
    out_spaces = out_spaces or [pltpu.VMEM] * len(outs)
    return pl.pallas_call(
        kernel,
        out_shape=outs,
        in_specs=[pl.BlockSpec(memory_space=p) for p in spaces],
        out_specs=[pl.BlockSpec(memory_space=p) for p in out_spaces],
        compiler_params=pltpu.CompilerParams(vmem_limit_bytes=2 * moved + (3 << 20)),
        cost_estimate=pl.CostEstimate(flops=flops, bytes_accessed=moved, transcendentals=0),
        scratch_shapes=scratch,
    )(*args)


def after(token, *values):
    return lax.optimization_barrier((token,) + values)[1:]


def shape(rows, columns, dtype=F32):
    return jax.ShapeDtypeStruct((rows, columns), dtype)


def put_tail(s, tail_ref, base, factors, start, end):
    tail_ref[base : base + s.heads, :] = factors
    tail_ref[base + s.start : base + s.start + 1, :] = start
    tail_ref[base + s.end : base + s.end + 1, :] = end


def put_parts(first, size, h, whole, keep_ref, send_ref):
    low, high = whole[:size], whole[size:]
    rows = slice(h * size, (h + 1) * size)
    keep_ref[rows, :] = lax.select(first, low, high)
    send_ref[rows, :] = lax.select(first, high, low)


def state_kernel(s, keys, values, log_decay, doc_ids, keep, send, notes, first_update, *near):
    each, waits, first = s.heads, [], s.first
    if near:
        near_keys, near_values, near_logs, near_ids, arrived, small = near
        few = [
            pltpu.make_async_copy(doc_ids, near_ids, small.at[0]),
            pltpu.make_async_copy(log_decay, near_logs, small.at[1]),
        ]
        each = s.heads // arrived.shape[1]
        for g in range(arrived.shape[1]):
            far_part = pl.ds((s.first + g * each) * s.width, each * s.width)
            part = pl.ds(g * each * s.width, each * s.width)
            waits.append(
                [
                    pltpu.make_async_copy(keys.at[:, far_part], near_keys.at[:, part], arrived.at[0, g]),
                    pltpu.make_async_copy(
                        values.at[:, far_part], near_values.at[:, part], arrived.at[1, g]
                    ),
                ]
            )
        for copy in few + sum(waits, []):
            copy.start()
        for copy in few:
            copy.wait()
        keys, values, log_decay, doc_ids, first = near_keys, near_values, near_logs, near_ids, 0
    core, _, _ = place_bits(s.count, False)
    lower = core == 0
    docs = [jnp.full((1, s.width), doc_ids[j].astype(F32)) for j in range(s.blocks)]
    carries = [None] + [equal(docs[j - 1], docs[j]) for j in range(1, s.blocks)]
    logs = s.logs(log_decay)
    totals = [total_rows(a) for a in logs]
    factors = [jnp.exp(t) for t in totals]
    whole_factor = factors[0]
    for j in range(1, s.blocks):
        whole_factor = whole_factor * factors[j] * carries[j]
    base = s.heads * s.half
    send[base:, :] = jnp.zeros((s.tail, s.width), F32)
    put_tail(s, send, base, whole_factor, docs[0], docs[-1])
    notes[...] = jnp.zeros(notes.shape, F32)
    put_tail(s, notes, 0, whole_factor, docs[0], docs[-1])
    for j in range(1, s.blocks):
        notes[s.carry(j), :] = carries[j]
    columns = [decay_columns(a) for a in logs]
    ends = [jnp.exp(a[C - 1 : C, :] - a) for a in columns]
    for h in range(s.heads):
        if waits and h % each == 0:
            for copy in waits[h // each]:
                copy.wait()
        place = slice((first + h) * s.width, (first + h + 1) * s.width)
        state = None
        for j in range(s.blocks):
            scaled = keys[s.block(j), place].astype(F32) * ends[j][:, h : h + 1]
            update = dot(scaled.astype(BF16), values[s.block(j), place], 0, 0)
            if j < s.blocks - 1:
                first_update[s.rows(j * s.heads + h, s.width), :] = update
            if state is None:
                state = update
            else:
                state = (carries[j] * factors[j][h : h + 1, :]) * state + update
        put_parts(lower, s.half, h, state, keep, send)


def sides(first, own, other):
    return lax.select(first, own, other), lax.select(first, other, own)


def linked(s, far, near):
    return equal(far[s.end : s.end + 1, :], near[s.start : s.start + 1, :])


def join_tail(s, out, base, far, near, factor):
    out[base : base + s.tail, :] = jnp.zeros((s.tail, s.width), F32)
    put_tail(
        s,
        out,
        base,
        far[: s.heads, :] * factor,
        far[s.start : s.start + 1, :],
        near[s.end : s.end + 1, :],
    )


def chip_kernel(s, reverse, keep, received, own_tail, *rest):
    out_keep, out_send = rest[-2:]
    core, chip, _ = place_bits(s.count, reverse)
    lower, left = core == 0, chip == 0
    base, top = s.heads * s.half, s.heads * s.quarter
    far, near = sides(lower, own_tail[: s.tail, :], received[base : base + s.tail, :])
    factor = near[: s.heads, :] * linked(s, far, near)
    join_tail(s, out_send, top, far, near, factor)
    if reverse:
        out_send[top + s.tail :, :] = rest[0][...] + received[base + s.tail :, :]
    for h in range(s.heads):
        rows = s.rows(h, s.half)
        far_state, near_state = sides(lower, keep[rows, :], received[rows, :])
        total = near_state + factor[h : h + 1, :] * far_state
        put_parts(left, s.quarter, h, total, out_keep, out_send)


def plane_kernel(s, reverse, keep, sent, received, *rest):
    out = rest[-2] if reverse else rest[0]
    _, chip, _ = place_bits(s.count, reverse)
    left = chip == 0
    top = s.heads * s.quarter
    far, near = sides(left, sent[top:, :], received[top:, :])
    factor = near[: s.heads, :] * linked(s, far, near)
    join_tail(s, out, top, far, near, factor)
    if reverse:
        gain = sent[top + s.tail :, :] + received[top + s.tail :, :]
        out[top + s.tail :, :] = gain
        every = rest[-1]
        if len(rest) > 2:
            every[: -s.gains, :] = rest[0][...]
        every[every.shape[0] - s.gains :, :] = gain
    for h in range(s.heads):
        rows = s.rows(h, s.quarter)
        far_state, near_state = sides(left, keep[rows, :], received[rows, :])
        out[rows, :] = near_state + factor[h : h + 1, :] * far_state


def spread_kernel(s, reverse, keep, sent, received, *rest):
    out_keep, out_send = rest[-3:-1] if reverse else rest[-2:]
    earlier = rest[: s.window]
    _, chip, plane = place_bits(s.count, reverse)
    left = chip == 0
    top = s.heads * s.quarter
    far, near = sides(left, sent[top:, :], received[top:, :])
    tails = [ref[top : top + s.tail, :] for ref in earlier]
    reach = [(plane >= w + 1).astype(F32) for w in range(s.window)]
    entry = linked(s, tails[0], far) * reach[0]
    inner = [
        linked(s, tails[w + 1], tails[w]) * reach[w + 1] * tails[w][: s.heads, :]
        for w in range(s.window - 1)
    ]
    link = linked(s, far, near)
    far_factor = far[: s.heads, :]
    if reverse:
        gain = rest[s.window][top + s.tail :, :]
        for other in earlier[: s.planes - 1]:
            gain = gain + other[top + s.tail :, :]
        rest[-1][...] = gain
    for h in range(s.heads):
        rows, one = s.rows(h, s.quarter), slice(h, h + 1)
        state = earlier[-1][rows, :]
        for w in reversed(range(s.window - 1)):
            state = earlier[w][rows, :] + inner[w][one] * state
        into_far = entry * state
        far_state = lax.select(left, keep[rows, :], received[rows, :])
        into_near = link * (far_state + far_factor[one] * into_far)
        out_keep[rows, :] = lax.select(left, into_far, into_near)
        out_send[rows, :] = lax.select(left, into_near, into_far)


def entry_kernel(
    s, reverse, chip_keep, chip_received, keep, received, own_tail, out_keep, out_send
):
    core, chip, _ = place_bits(s.count, reverse)
    lower, left = core == 0, chip == 0
    base = s.heads * s.half
    far, near = sides(lower, own_tail[: s.tail, :], received[base : base + s.tail, :])
    link = linked(s, far, near)
    far_factor = far[: s.heads, :]
    for h in range(s.heads):
        rows, quarter = s.rows(h, s.half), s.rows(h, s.quarter)
        into_far = jnp.concatenate(
            sides(left, chip_keep[quarter, :], chip_received[quarter, :]), axis=0
        )
        far_state = lax.select(lower, keep[rows, :], received[rows, :])
        into_near = link * (far_state + far_factor[h : h + 1, :] * into_far)
        out_keep[rows, :] = lax.select(lower, into_far, into_near)
        out_send[rows, :] = lax.select(lower, into_near, into_far)


def joined(s, lower, keep, received, h):
    rows = s.rows(h, s.half)
    return jnp.concatenate(sides(lower, keep[rows, :], received[rows, :]), axis=0)


def decay_mask(column, row):
    at, other = triangle()
    gap = jnp.minimum(column - row, 0.0)
    return jnp.where(at >= other, jnp.exp(gap), 0.0)


def local_kernel(s, queries, keys, values, log_decay, out, weights):
    for j, logs in enumerate(s.logs(log_decay)):
        columns, rows = decay_columns(logs), decay_rows(logs)
        for h in range(s.heads):
            mask = decay_mask(columns[:, h : h + 1], rows[h : h + 1, :])
            part = (s.block(j), s.head(h))
            scores = dot(queries[part], keys[part], 1, 1)
            weight = (scores * mask).astype(BF16)
            weights[s.rows(j * s.heads + h, C), :] = weight
            out[s.block(j), s.own(h)] = dot(weight, values[part], 1, 0)


def attention_kernel(
    s, queries, out_grad, gain, log_decay, notes, local, first_update, keep, received, *rest
):
    earlier_sums, (out, sums) = rest[:-2], rest[-2:]
    core, _, _ = place_bits(s.count, False)
    lower = core == 0
    logs = s.logs(log_decay)
    factors = [jnp.exp(total_rows(a)) for a in logs]
    decays = [jnp.exp(decay_columns(a)) for a in logs]
    squares = [jnp.zeros((C, s.width), F32) for _ in logs]
    inners = [jnp.zeros((C, s.width), F32) for _ in logs]
    for h in range(s.heads):
        state = joined(s, lower, keep, received, h)
        for j in range(s.blocks):
            part, own = (s.block(j), s.head(h)), (s.block(j), s.own(h))
            far = far_dot(queries[part], state, 0)
            attention = local[own] + decays[j][:, h : h + 1] * far
            out[own] = attention
            squares[j] = squares[j] + attention * attention
            inners[j] = inners[j] + out_grad[part].astype(F32) * gain[:, s.head(h)] * attention
            if j < s.blocks - 1:
                update = first_update[s.rows(j * s.heads + h, s.width), :]
                state = notes[s.carry(j + 1), :] * (factors[j][h : h + 1, :] * state + update)
    if earlier_sums:
        sums[...] = earlier_sums[0][...]
    else:
        sums[...] = jnp.zeros(sums.shape, F32)
    for j in range(s.blocks):
        for i, part in enumerate([squares[j], inners[j]]):
            row = (slice(i, i + 1), s.block(j))
            sums[row] = sums[row] + jnp.sum(part.T, axis=0, keepdims=True)


def grad_kernel(
    s, all_features, queries, out_grad, gain, log_decay, notes, attention, sums,
    attn_grad, keep, send, out_tail, out_gain, back_terms,
):
    core, _, _ = place_bits(s.count, True)
    lower = core == 0
    logs = s.logs(log_decay)
    factors = [jnp.exp(total_rows(a)) for a in logs]
    decays = [jnp.exp(decay_columns(a)) for a in logs]
    totals = sums[...] / all_features
    spread = lambda row: jnp.broadcast_to(row, (C, C)).T
    inverses, slopes = [], []
    for j in range(s.blocks):
        inverse = lax.rsqrt(totals[0:1, s.block(j)] + EPSILON)
        inverses.append(spread(inverse))
        slopes.append(spread(totals[1:2, s.block(j)] * inverse * inverse))
    base = s.heads * s.half
    out_tail[...] = jnp.zeros(out_tail.shape, F32)
    own = notes[: s.tail, :]
    put_tail(
        s, out_tail, 0, own[: s.heads], own[s.end : s.end + 1], own[s.start : s.start + 1]
    )
    out_gain[...] = jnp.zeros(out_gain.shape, F32)
    for h in range(s.heads):
        gain_row = gain[:, s.head(h)]
        gain_part = jnp.zeros((1, s.width), F32)
        terms = []
        for j in range(s.blocks):
            part, own = (s.block(j), s.head(h)), (s.block(j), s.own(h))
            cot = out_grad[part].astype(F32)
            att = attention[own]
            grad = ((cot * gain_row - att * slopes[j]) * inverses[j]).astype(BF16)
            attn_grad[own] = grad
            gain_part = gain_part + jnp.sum(cot * att * inverses[j], axis=0, keepdims=True)
            weighted = (queries[part].astype(F32) * decays[j][:, h : h + 1]).astype(BF16)
            term = dot(weighted, grad, 0, 0)
            terms.append(term)
            if j > 0:
                back_terms[s.rows((j - 1) * s.heads + h, s.width), :] = term
        state = terms[-1]
        for j in reversed(range(s.blocks - 1)):
            state = terms[j] + (notes[s.carry(j + 1), :] * factors[j][h : h + 1, :]) * state
        put_parts(lower, s.half, h, state, keep, send)
        out_gain[h : h + 1, :] = gain_part
    send[base : base + s.tail, :] = out_tail[...]
    send[base + s.tail :, :] = out_gain[...]


def local_grad_kernel(s, queries, values, log_decay, weights, attn_grad, key_out, value_out):
    for j, logs in enumerate(s.logs(log_decay)):
        columns, rows = decay_columns(logs), decay_rows(logs)
        for h in range(s.heads):
            mask = decay_mask(columns[:, h : h + 1], rows[h : h + 1, :])
            part, own = (s.block(j), s.head(h)), (s.block(j), s.own(h))
            grad = attn_grad[own]
            grad_weight = (dot(grad, values[part], 1, 1) * mask).astype(BF16)
            key_out[own] = dot(grad_weight, queries[part], 0, 0)
            value_out[own] = dot(weights[s.rows(j * s.heads + h, C), :], grad, 0, 0)


def final_kernel(
    s, last, keys, values, log_decay, notes, key_local, value_local, back_terms, keep, received,
    *rest,
):
    earlier, (key_out, value_out) = rest[:-2], rest[-2:]
    core, _, _ = place_bits(s.count, True)
    lower = core == 0
    logs = s.logs(log_decay)
    factors = [jnp.exp(total_rows(a)) for a in logs]
    columns = [decay_columns(a) for a in logs]
    ends = [jnp.exp(a[C - 1 : C, :] - a) for a in columns]
    for i in range(0, len(earlier), 2):
        place = slice(i // 2 * s.columns, (i // 2 + 1) * s.columns)
        key_out[:, place] = earlier[i][...]
        value_out[:, place] = earlier[i + 1][...]
    for h in range(s.heads):
        state = joined(s, lower, keep, received, h)
        for j in reversed(range(s.blocks)):
            part, own = (s.block(j), s.head(h)), (s.block(j), s.own(h))
            out = part if last else own
            end = ends[j][:, h : h + 1]
            key_far = end * far_dot(values[part], state, 1)
            value_far = end * far_dot(keys[part], state, 0)
            key_out[out] = (key_local[own] + key_far).astype(BF16)
            value_out[out] = (value_local[own] + value_far).astype(BF16)
            if j > 0:
                term = back_terms[s.rows((j - 1) * s.heads + h, s.width), :]
                state = notes[s.carry(j), :] * (term + factors[j][h : h + 1, :] * state)


def swap(value, axis, bit):
    count = lax.axis_size(axis)
    return lax.ppermute(value, axis, [(i, i ^ bit) for i in range(count)])


def next_plane(value, count, reverse):
    step = -PLANE if reverse else PLANE
    return lax.ppermute(value, "seq", [(i, (i + step) % count) for i in range(count)])


def scan_in(waves, parts, reverse, token, beside):
    bind = functools.partial
    gain_rows = lambda s: s.gains if reverse else 0
    received, chips, chip_received, local = [], [], [], []
    for s, (keep, send, tail, gain) in zip(waves, parts):
        received.append(swap(send, "seq", 1))
    for i, (s, (keep, send, tail, gain)) in enumerate(zip(waves, parts)):
        outs = [
            shape(s.heads * s.quarter, s.width),
            shape(s.heads * s.quarter + s.tail + gain_rows(s), s.width),
        ]
        (keep,) = after(token, keep)
        extra = [gain] if reverse else []
        chip = call(bind(chip_kernel, s, reverse), outs, keep, received[i], tail, *extra)
        token = chip[0]
        chips.append(chip)
        sent = chip[1]
        if chip_received:
            (sent,) = after(chip_received[-1], sent)
        chip_received.append(swap(sent, "seq", 2))
    planes, passed, gains, others = [], [], [], []
    for i, s in enumerate(waves):
        (keep,) = after(token, chips[i][0])
        outs = [shape(s.heads * s.quarter + s.tail + gain_rows(s), s.width)]
        if reverse:
            outs.append(shape((i + 1) * s.gains, s.width))
        plane, *gains = call(
            bind(plane_kernel, s, reverse), outs, keep, chips[i][1], chip_received[i], *gains
        )
        token = plane
        planes.append(plane)
        into = next_plane(plane, s.count, reverse)
        token, one = beside(token, i)
        local.append(one)
        if reverse and i == len(waves) - 1:
            others = list(after(token, *gains))
            for _ in range(s.planes - 1 - s.window):
                others.append(next_plane(others[-1], s.count, not reverse))
            (token,) = after(others[-1], token)
        passed.append(list(after(token, into)))
    for _ in range(waves[0].window - 1):
        for i, s in enumerate(waves):
            passed[i].append(next_plane(passed[i][-1], s.count, reverse))
    spreads, spread_received = [], []
    for i, s in enumerate(waves):
        (keep,) = after(token, chips[i][0])
        outs = [shape(s.heads * s.quarter, s.width)] * 2
        extra = []
        if reverse:
            outs.append(shape(s.gains, s.width))
            extra = [planes[i]]
        spread = call(
            bind(spread_kernel, s, reverse),
            outs,
            keep,
            chips[i][1],
            chip_received[i],
            *passed[i],
            *extra,
        )
        token = spread[0]
        spreads.append(spread)
        spread_received.append(swap(spread[1], "seq", 2))
    entries = []
    for i, s in enumerate(waves):
        (keep,) = after(token, spreads[i][0])
        entry = call(
            bind(entry_kernel, s, reverse),
            [shape(s.heads * s.half, s.width)] * 2,
            keep,
            spread_received[i],
            parts[i][0],
            received[i],
            parts[i][2],
        )
        token = entry[0]
        entries.append((entry[0], swap(entry[1], "seq", 1)))
    gain = None
    if reverse:
        pad = lambda a, s: a.reshape(-1, s.gains, s.width)[:, : s.heads].reshape(-1, s.width)
        gain = jnp.concatenate([pad(spread[2], s) for spread in spreads])
        for other in others[1:]:
            gain = gain + pad(other, s)
        gain = gain.reshape(-1)
    return entries, local, token, gain


def per_device(queries, keys, values, out_grad, log_decay, norm_gain, doc_ids):
    tokens, features = queries.shape
    heads = log_decay.shape[1]
    count, dp = lax.axis_size("seq"), lax.axis_size("dp")
    wave_count = max(w for w in WAVES if heads % w == 0)
    waves = [Sizes(tokens, features, heads, count, w, wave_count) for w in range(wave_count)]
    bind = functools.partial
    unit = 2 * C * C * C * waves[0].blocks * waves[0].heads
    gain = norm_gain.reshape(1, features)
    log_decay = log_decay.T
    states = []
    far = [pltpu.with_memory_space_constraint(a, pltpu.HBM) for a in (keys, values, log_decay, doc_ids)]
    for s in waves:
        groups = max(g for g in (2, 1) if s.heads % g == 0)
        given, options = (keys, values, log_decay, doc_ids), {}
        spaces = [pltpu.VMEM, pltpu.VMEM, pltpu.VMEM, pltpu.SMEM]
        scratch = []
        if not states:
            given, spaces = far, [pltpu.HBM] * 4
            scratch = [
                pltpu.VMEM((tokens, s.columns), BF16),
                pltpu.VMEM((tokens, s.columns), BF16),
                pltpu.VMEM(log_decay.shape, F32),
                pltpu.SMEM(doc_ids.shape, jnp.int32),
                pltpu.SemaphoreType.DMA((2, groups)),
                pltpu.SemaphoreType.DMA((2,)),
            ]
        else:
            given = given[:2] + after(token, log_decay) + given[3:]
        state = call(
            bind(state_kernel, s),
            [
                shape(s.heads * s.half, s.width),
                shape(s.heads * s.half + s.tail, s.width),
                shape(s.notes, s.width),
                shape(max(1, s.blocks - 1) * s.heads * s.width, s.width),
            ],
            *given,
            flops=unit,
            spaces=spaces,
            scratch=scratch,
        )
        token = state[0]
        states.append(state)
    queries, keys, values, out_grad, gain, log_decay = after(
        token, queries, keys, values, out_grad, gain, log_decay
    )

    def beside_forward(token, i):
        s = waves[i]
        (held,) = after(token, log_decay)
        local = call(
            bind(local_kernel, s),
            [shape(tokens, s.columns), shape(s.blocks * s.heads * C, C, BF16)],
            queries,
            keys,
            values,
            held,
            flops=2 * unit,
        )
        return local[0], local

    parts = [(state[0], state[1], state[2], None) for state in states]
    entries, local, token, _ = scan_in(waves, parts, False, token, beside_forward)
    attentions, sums = [], []
    for i, s in enumerate(waves):
        (held,) = after(token, log_decay)
        attention, total = call(
            bind(attention_kernel, s),
            [shape(tokens, s.columns), shape(8, tokens)],
            queries,
            out_grad,
            gain,
            held,
            states[i][2],
            local[i][0],
            states[i][3],
            *entries[i],
            *sums,
            flops=2 * unit,
        )
        token = attention
        attentions.append(attention)
        sums = [total]
    sums = sums[0]
    if dp & (dp - 1):
        sums = lax.psum(sums, "dp")
    else:
        bit = 1
        while bit < dp:
            sums = sums + swap(sums, "dp", bit)
            bit *= 2
    grads = []
    for i, s in enumerate(waves):
        (held,) = after(token, log_decay)
        grad = call(
            bind(grad_kernel, s, features * dp),
            [
                shape(tokens, s.columns, BF16),
                shape(s.heads * s.half, s.width),
                shape(s.heads * s.half + s.tail + s.gains, s.width),
                shape(s.tail, s.width),
                shape(s.gains, s.width),
                shape(max(1, s.blocks - 1) * s.heads * s.width, s.width),
            ],
            queries,
            out_grad,
            gain,
            held,
            states[i][2],
            attentions[i],
            sums,
            flops=unit,
        )
        token = grad[0]
        grads.append(grad)

    def beside_backward(token, i):
        s = waves[i]
        (held,) = after(token, log_decay)
        local_grad = call(
            bind(local_grad_kernel, s),
            [shape(tokens, s.columns), shape(tokens, s.columns)],
            queries,
            values,
            held,
            local[i][1],
            grads[i][0],
            flops=3 * unit,
        )
        return local_grad[0], local_grad

    parts = [(grad[1], grad[2], grad[3], grad[4]) for grad in grads]
    entries, local_grads, token, gain_grad = scan_in(waves, parts, True, token, beside_backward)
    (token,) = after(gain_grad, token)
    done = []
    for i, s in enumerate(waves):
        last = i == wave_count - 1
        (held,) = after(token, log_decay)
        done.extend(
            call(
                bind(final_kernel, s, last),
                [shape(tokens, features if last else s.columns, BF16)] * 2,
                keys,
                values,
                held,
                states[i][2],
                *local_grads[i],
                grads[i][5],
                *entries[i][:2],
                *(done if last else ()),
                flops=4 * unit,
            )
        )
        token = done[-1]
    return (done[-2], done[-1], gain_grad)


def solution(mesh):
    placed = (
        P("seq", "dp"),
        P("seq", "dp"),
        P("seq", "dp"),
        P("seq", "dp"),
        P("seq", "dp"),
        P("dp"),
        P("seq"),
    )
    return jax.shard_map(
        per_device,
        mesh=mesh,
        in_specs=placed,
        out_specs=(P("seq", "dp"), P("seq", "dp"), P("dp")),
        check_vma=False,
    )
```

time: 86.8 us -> 77.8 us (0.90)
  waiting for transfers between devices: 49.6 us -> 45.6 us
  local copies, waits for them, and re-layouts: 3.2 us -> 0.03 us
  starting transfers between devices: 17.9 us -> 15.2 us
  Pallas kernels: 13.8 us -> 15.4 us
    ppermute x5, waiting for transfers between devices: 24.6 us -> 17.9 us  [next_plane(): lax.ppermute(value, 'seq', [(i, (i + step) % count) for i in range(count)])]
    unnamed x15 -> x12, local copies, waits for them, and re-layouts: 3.12 us -> 0.03 us
    ppermute x9, waiting for transfers between devices: 25 us -> 27.6 us  [swap(): return lax.ppermute(value, axis, [(i, i ^ bit) for i in range(count)])]
    ppermute x5, starting transfers between devices: 7.96 us -> 5.3 us  [next_plane(): lax.ppermute(value, 'seq', [(i, (i + step) % count) for i in range(count)])]
    pallas_call x14, Pallas kernels: 13.8 us -> 15.4 us  [call(): pl.pallas_call(kernel, out_shape=outs, in_specs=[pl.BlockSpec(memory_spac...]
  transfers between devices with their start and end apart: 14 -> 14, of which waited for: 11 -> 13; matrix products, arithmetic and copies ran while one was open for 1% -> 1% of each run, Pallas kernels for 7% -> 8%
where the time goes in v2:
time: 77.8 us; the launch traced here: 77.6 us
  waiting for transfers between devices  45.6 us (59%)
  Pallas kernels  15.4 us (20%)
  starting transfers between devices  15.2 us (20%)
  between operations  0.82 us (1%)
    ppermute x9, waiting for transfers between devices, swap(): return lax.ppermute(value, axis, [(i, i ^ bit) for i in range(count)])  27.6 us
    ppermute x5, waiting for transfers between devices, next_plane(): lax.ppermute(value, 'seq', [(i, (i + step) % count) for i in range(count)])  17.9 us
    pallas_call x14, Pallas kernels, call(): pl.pallas_call(kernel, out_shape=outs, in_specs=[pl.BlockSpec(memory_spac...  15.4 us
    ppermute x9, starting transfers between devices, swap(): return lax.ppermute(value, axis, [(i, i ^ bit) for i in range(count)])  9.87 us
    ppermute x5, starting transfers between devices, next_plane(): lax.ppermute(value, 'seq', [(i, (i + step) % count) for i in range(count)])  5.3 us
  transfers between devices with their start and end apart: 14, of which 13 were waited for; matrix products, arithmetic and copies ran while one was open for 1% of the time, Pallas kernels for 8%

profile of v2, /device:TPU:0, one launch (start us, length us, event | category | flops | bytes accessed | tf_op | source)
XLA Modules:
  0.0 77.6 jit_solution(6079022083268061010)
XLA Ops:
  0.6 0.0 copy-start.5
  0.6 0.0 copy-start
  0.7 0.0 copy-start.1
  0.7 0.0 copy-start.2
  0.7 0.0 copy-start.4
  0.7 3.0 %shard_map.94 = (f32[768,128]{1,0:T(8,128)S(1)}, f32[784,128]{1,0:T(8,128)S(1)}, f32[16,128]{1,0:T(8,128)S(1)}, f32[1536,128]{1,0:T(8,128)S(1)}) custom-call(bf16[256,1536]{1,0:T(8,128)(2,1)} %keys.3, bf16[256,1536]{1,0:T(8,128)(2,1)} %values.4, f32[12,256]{1,0:T(8,128)} %bitcast.5, s32[2]{0:T(128)} %doc_ids.1), custom_call_target="tpu_custom_call" | custom-call | flops 100663296 | bytes 3174408 | tf_op jit(solution)/shard_map/pallas_call | solution.py:117
  3.7 0.5 collective-permute-start
  4.2 1.4 %collective-permute-done.received = f32[784,128]{1,0:T(8,128)S(1)} collective-permute-done((f32[784,128]{1,0:T(8,128)S(1)}, f32[784,128]{1,0:T(8,128)S(1)}, u32[]{:S(2)}, u32[]{:S(2)}) %collective-permute-start) | collective-permute-done | bytes 401440 | tf_op jit(solution)/shard_map/ppermute | solution.py:470
  5.6 0.1 shard_map.95
  5.7 2.9 %collective-permute-start.1 = (f32[400,128]{1,0:T(8,128)S(1)}, f32[400,128]{1,0:T(8,128)S(1)}, u32[]{:S(2)}, u32[]{:S(2)}) collective-permute-start(f32[400,128]{1,0:T(8,128)S(1)} %get-tuple-element.68.sent), channel_id=1, source_target_pairs={{0,2},{1,3},{2,0},{3,1},{4,6},{5,7},{6,4},{7,5},{8,10},{9,11},{10,... | collective-permute-start | bytes 614408 | tf_op jit(solution)/shard_map/ppermute | solution.py:470
  8.6 5.4 %collective-permute-done.1.received = f32[400,128]{1,0:T(8,128)S(1)} collective-permute-done((f32[400,128]{1,0:T(8,128)S(1)}, f32[400,128]{1,0:T(8,128)S(1)}, u32[]{:S(2)}, u32[]{:S(2)}) %collective-permute-start.1) | collective-permute-done | bytes 204832 | tf_op jit(solution)/shard_map/ppermute | solution.py:470
  14.0 1.9 %collective-permute-start.2 = (f32[400,128]{1,0:T(8,128)S(1)}, f32[400,128]{1,0:T(8,128)S(1)}, u32[]{:S(2)}, u32[]{:S(2)}) collective-permute-start(f32[400,128]{1,0:T(8,128)S(1)} %shard_map.96), channel_id=1, source_target_pairs={{0,4},{1,5},{2,6},{3,7},{4,8},{5,9},{6,10},{7,11},{8,12},{9,13},{1... | collective-permute-start | bytes 614408 | tf_op jit(solution)/shard_map/ppermute | solution.py:475
  15.9 0.0 copy-done.5
  15.9 4.1 %shard_map.97 = (f32[256,1536]{1,0:T(8,128)S(1)}, bf16[3072,128]{1,0:T(8,128)(2,1)S(1)}) custom-call(bf16[256,1536]{1,0:T(8,128)(2,1)S(1)} %copy-done.1, bf16[256,1536]{1,0:T(8,128)(2,1)S(1)} %copy-done.2, bf16[256,1536]{1,0:T(8,128)(2,1)S(1)} %copy-done, f32[12,256]{1,0:T(8,128)S(1)} %bitcast.6), custom_call_target="tpu_custom_call" | custom-call | flops 201326592 | bytes 4730880 | tf_op jit(solution)/shard_map/pallas_call | solution.py:117
  20.1 0.0 copy-start.3
  20.1 2.4 %collective-permute-done.2.rest_0_ = f32[400,128]{1,0:T(8,128)S(1)} collective-permute-done((f32[400,128]{1,0:T(8,128)S(1)}, f32[400,128]{1,0:T(8,128)S(1)}, u32[]{:S(2)}, u32[]{:S(2)}) %collective-permute-start.2) | collective-permute-done | bytes 204832 | tf_op jit(solution)/shard_map/ppermute | solution.py:475
  22.5 0.0 collective-permute-start.3
  22.5 7.6 %collective-permute-done.3.rest_1_ = f32[400,128]{1,0:T(8,128)S(1)} collective-permute-done((f32[400,128]{1,0:T(8,128)S(1)}, f32[400,128]{1,0:T(8,128)S(1)}, u32[]{:S(2)}, u32[]{:S(2)}) %collective-permute-start.3) | collective-permute-done | bytes 204832 | tf_op jit(solution)/shard_map/ppermute | solution.py:475
  30.0 0.1 shard_map.98
  30.1 1.5 %collective-permute-start.4 = (f32[384,128]{1,0:T(8,128)S(1)}, f32[384,128]{1,0:T(8,128)S(1)}, u32[]{:S(2)}, u32[]{:S(2)}) collective-permute-start(f32[384,128]{1,0:T(8,128)S(1)} %get-tuple-element.74), channel_id=1, source_target_pairs={{0,2},{1,3},{2,0},{3,1},{4,6},{5,7},{6,4},{7,5},{8,10},{9,11},{10,... | collective-permute-start | bytes 589832 | tf_op jit(solution)/shard_map/ppermute | solution.py:470
  31.7 4.2 %collective-permute-done.4.chip_received = f32[384,128]{1,0:T(8,128)S(1)} collective-permute-done((f32[384,128]{1,0:T(8,128)S(1)}, f32[384,128]{1,0:T(8,128)S(1)}, u32[]{:S(2)}, u32[]{:S(2)}) %collective-permute-start.4) | collective-permute-done | bytes 196640 | tf_op jit(solution)/shard_map/ppermute | solution.py:470
  35.9 0.1 shard_map.99
  36.0 0.1 collective-permute-start.5
  36.1 1.7 %collective-permute-done.5.received = f32[768,128]{1,0:T(8,128)S(1)} collective-permute-done((f32[768,128]{1,0:T(8,128)S(1)}, f32[768,128]{1,0:T(8,128)S(1)}, u32[]{:S(2)}, u32[]{:S(2)}) %collective-permute-start.5) | collective-permute-done | bytes 393248 | tf_op jit(solution)/shard_map/ppermute | solution.py:470
  37.8 1.3 %shard_map.100 = (f32[256,1536]{1,0:T(8,128)S(1)}, f32[8,256]{1,0:T(8,128)S(1)}) custom-call(bf16[256,1536]{1,0:T(8,128)(2,1)S(1)} %copy-done.1, bf16[256,1536]{1,0:T(8,128)(2,1)S(1)} %copy-done.3, f32[1,1536]{1,0:T(1,128)S(1)} %reshape.21.gain, f32[12,256]{1,0:T(8,128)S(1)} %bitcast.7, f32[16,128]{1,0:T(8,128)S(1)} %get-tuple-element.60.own_tail.notes, ...), custom_call_target="tpu_custom_call" | custom-call | flops 201326592 | bytes 6326272 | tf_op jit(solution)/shard_map/pallas_call | solution.py:117
  39.1 1.6 %collective-permute-start.6 = (f32[8,256]{1,0:T(8,128)S(1)}, f32[8,256]{1,0:T(8,128)S(1)}, u32[]{:S(2)}, u32[]{:S(2)}) collective-permute-start(f32[8,256]{1,0:T(8,128)S(1)} %get-tuple-element.81), channel_id=1, source_target_pairs={{0,16},{16,0},{1,17},{17,1},{2,18},{18,2},{3,19},{19,3},{4,20},{20... | collective-permute-start | bytes 24584 | tf_op jit(solution)/shard_map/ppermute | solution.py:470
  40.7 2.1 %collective-permute-done.6 = f32[8,256]{1,0:T(8,128)S(1)} collective-permute-done((f32[8,256]{1,0:T(8,128)S(1)}, f32[8,256]{1,0:T(8,128)S(1)}, u32[]{:S(2)}, u32[]{:S(2)}) %collective-permute-start.6) | collective-permute-done | bytes 8224 | tf_op jit(solution)/shard_map/ppermute | solution.py:470
  42.8 1.5 %shard_map.101 = (bf16[256,1536]{1,0:T(8,128)(2,1)S(1)}, f32[768,128]{1,0:T(8,128)S(1)}, f32[800,128]{1,0:T(8,128)S(1)}, f32[16,128]{1,0:T(8,128)S(1)}, f32[16,128]{1,0:T(8,128)S(1)}, /*index=5*/f32[1536,128]{1,0:T(8,128)S(1)}) custom-call(bf16[256,1536]{1,0:T(8,128)(2,1)S(1)} %copy-done.1, bf16[256,1536]{1,0:T(8,128)(2,1)S(1)} %copy-done.3, ...), custom_call_target="tpu_custom_call" | custom-call | flops 100663296 | bytes 5572608 | tf_op jit(solution)/shard_map/pallas_call | solution.py:117
  44.3 0.1 collective-permute-start.7
  44.4 1.7 %collective-permute-done.7.received = f32[800,128]{1,0:T(8,128)S(1)} collective-permute-done((f32[800,128]{1,0:T(8,128)S(1)}, f32[800,128]{1,0:T(8,128)S(1)}, u32[]{:S(2)}, u32[]{:S(2)}) %collective-permute-start.7) | collective-permute-done | bytes 409632 | tf_op jit(solution)/shard_map/ppermute | solution.py:470
  46.2 0.1 shard_map.102
  46.2 1.5 %collective-permute-start.8 = (f32[416,128]{1,0:T(8,128)S(1)}, f32[416,128]{1,0:T(8,128)S(1)}, u32[]{:S(2)}, u32[]{:S(2)}) collective-permute-start(f32[416,128]{1,0:T(8,128)S(1)} %get-tuple-element.90.sent), channel_id=1, source_target_pairs={{0,2},{1,3},{2,0},{3,1},{4,6},{5,7},{6,4},{7,5},{8,10},{9,11},{10,... | collective-permute-start | bytes 638984 | tf_op jit(solution)/shard_map/ppermute | solution.py:470
  47.8 5.8 %collective-permute-done.8.received = f32[416,128]{1,0:T(8,128)S(1)} collective-permute-done((f32[416,128]{1,0:T(8,128)S(1)}, f32[416,128]{1,0:T(8,128)S(1)}, u32[]{:S(2)}, u32[]{:S(2)}) %collective-permute-start.8) | collective-permute-done | bytes 213024 | tf_op jit(solution)/shard_map/ppermute | solution.py:470
  53.7 0.1 collective-permute-start.10
  53.7 1.9 %shard_map.104 = (f32[256,1536]{1,0:T(8,128)S(1)}, f32[256,1536]{1,0:T(8,128)S(1)}) custom-call(bf16[256,1536]{1,0:T(8,128)(2,1)S(1)} %copy-done.1, bf16[256,1536]{1,0:T(8,128)(2,1)S(1)} %copy-done, f32[12,256]{1,0:T(8,128)S(1)} %bitcast.9, bf16[3072,128]{1,0:T(8,128)(2,1)S(1)} %get-tuple-element.93.weights, bf16[256,1536]{1,0:T(8,128)(2,1)S(1)} %get-tuple-element.82.attn_grad), custom_call_target="tpu_custom_call" | custom-call | flops 301989888 | bytes 6303744 | tf_op jit(solution)/shard_map/pallas_call | solution.py:117
  55.6 2.1 %collective-permute-start.9 = (f32[16,128]{1,0:T(8,128)S(1)}, f32[16,128]{1,0:T(8,128)S(1)}, u32[]{:S(2)}, u32[]{:S(2)}) collective-permute-start(f32[16,128]{1,0:T(8,128)S(1)} %get-tuple-element.98), channel_id=1, source_target_pairs={{0,4},{1,5},{2,6},{3,7},{4,8},{5,9},{6,10},{7,11},{8,12},{9,13},{1... | collective-permute-start | bytes 24584 | tf_op jit(solution)/shard_map/ppermute | solution.py:475
  57.7 3.4 %collective-permute-done.9 = f32[16,128]{1,0:T(8,128)S(1)} collective-permute-done((f32[16,128]{1,0:T(8,128)S(1)}, f32[16,128]{1,0:T(8,128)S(1)}, u32[]{:S(2)}, u32[]{:S(2)}) %collective-permute-start.9) | collective-permute-done | bytes 8224 | tf_op jit(solution)/shard_map/ppermute | solution.py:475
  61.1 0.0 collective-permute-done.10.rest_0_
  61.1 1.3 %collective-permute-start.11 = (f32[416,128]{1,0:T(8,128)S(1)}, f32[416,128]{1,0:T(8,128)S(1)}, u32[]{:S(2)}, u32[]{:S(2)}) collective-permute-start(f32[416,128]{1,0:T(8,128)S(1)} %collective-permute-done.10.rest_0_), channel_id=1, source_target_pairs={{0,12},{1,13},{2,14},{3,15},{4,0},{5,1},{6,2},{7,3},{8,4},{9,5},{1... | collective-permute-start | bytes 638984 | tf_op jit(solution)/shard_map/ppermute | solution.py:475
  62.4 4.5 %collective-permute-done.11.rest_1_ = f32[416,128]{1,0:T(8,128)S(1)} collective-permute-done((f32[416,128]{1,0:T(8,128)S(1)}, f32[416,128]{1,0:T(8,128)S(1)}, u32[]{:S(2)}, u32[]{:S(2)}) %collective-permute-start.11) | collective-permute-done | bytes 213024 | tf_op jit(solution)/shard_map/ppermute | solution.py:475
  67.0 0.1 shard_map.105
  67.1 1.5 %collective-permute-start.12 = (f32[384,128]{1,0:T(8,128)S(1)}, f32[384,128]{1,0:T(8,128)S(1)}, u32[]{:S(2)}, u32[]{:S(2)}) collective-permute-start(f32[384,128]{1,0:T(8,128)S(1)} %get-tuple-element.103), channel_id=1, source_target_pairs={{0,2},{1,3},{2,0},{3,1},{4,6},{5,7},{6,4},{7,5},{8,10},{9,11},{10,... | collective-permute-start | bytes 589832 | tf_op jit(solution)/shard_map/ppermute | solution.py:470
  68.6 4.2 %collective-permute-done.12.chip_received = f32[384,128]{1,0:T(8,128)S(1)} collective-permute-done((f32[384,128]{1,0:T(8,128)S(1)}, f32[384,128]{1,0:T(8,128)S(1)}, u32[]{:S(2)}, u32[]{:S(2)}) %collective-permute-start.12) | collective-permute-done | bytes 196640 | tf_op jit(solution)/shard_map/ppermute | solution.py:470
  72.8 0.1 shard_map.106
  72.9 0.1 collective-permute-start.13
  73.0 0.6 fusion
  73.6 1.1 %collective-permute-done.13.received = f32[768,128]{1,0:T(8,128)S(1)} collective-permute-done((f32[768,128]{1,0:T(8,128)S(1)}, f32[768,128]{1,0:T(8,128)S(1)}, u32[]{:S(2)}, u32[]{:S(2)}) %collective-permute-start.13) | collective-permute-done | bytes 393248 | tf_op jit(solution)/shard_map/ppermute | solution.py:470
  74.7 2.9 %shard_map.107 = (bf16[256,1536]{1,0:T(8,128)(2,1)}, bf16[256,1536]{1,0:T(8,128)(2,1)}) custom-call(bf16[256,1536]{1,0:T(8,128)(2,1)S(1)} %copy-done.2, bf16[256,1536]{1,0:T(8,128)(2,1)S(1)} %copy-done, f32[12,256]{1,0:T(8,128)S(1)} %bitcast.10, f32[16,128]{1,0:T(8,128)S(1)} %get-tuple-element.60.own_tail.notes, ...), custom_call_target="tpu_custom_call" | custom-call | flops 402653184 | bytes 7884800 | tf_op jit(solution)/shard_map/pallas_call | solution.py:117
  (9 shorter events, 0.1 us)
Async XLA Ops:
  0.6 15.3 %copy-start.5 = (f32[1536]{0:T(1024)S(1)}, f32[1536]{0:T(1024)}, u32[]{:S(2)}) copy-start(f32[1536]{0:T(1024)} %param.12) | copy-start | bytes 18436
  0.6 15.3 %copy-start = (bf16[256,1536]{1,0:T(8,128)(2,1)S(1)}, bf16[256,1536]{1,0:T(8,128)(2,1)}, u32[]{:S(2)}) copy-start(bf16[256,1536]{1,0:T(8,128)(2,1)} %values.4) | copy-start | bytes 2359300
  0.7 15.3 %copy-start.1 = (bf16[256,1536]{1,0:T(8,128)(2,1)S(1)}, bf16[256,1536]{1,0:T(8,128)(2,1)}, u32[]{:S(2)}) copy-start(bf16[256,1536]{1,0:T(8,128)(2,1)} %queries.3) | copy-start | bytes 2359300
  0.7 15.3 %copy-start.2 = (bf16[256,1536]{1,0:T(8,128)(2,1)S(1)}, bf16[256,1536]{1,0:T(8,128)(2,1)}, u32[]{:S(2)}) copy-start(bf16[256,1536]{1,0:T(8,128)(2,1)} %keys.3) | copy-start | bytes 2359300
  0.7 15.3 %copy-start.4 = (f32[256,12]{0,1:T(8,128)S(1)}, f32[256,12]{0,1:T(8,128)}, u32[]{:S(2)}) copy-start(f32[256,12]{0,1:T(8,128)} %param.11) | copy-start | bytes 36868
  3.7 1.9 %collective-permute-start = (f32[784,128]{1,0:T(8,128)S(1)}, f32[784,128]{1,0:T(8,128)S(1)}, u32[]{:S(2)}, u32[]{:S(2)}) collective-permute-start(f32[784,128]{1,0:T(8,128)S(1)} %get-tuple-element.65), channel_id=1, source_target_pairs={{0,1},{1,0},{2,3},{3,2},{4,5},{5,4},{6,7},{7,6},{8,9},{9,8},{10,11... | collective-permute-start | bytes 1204232 | tf_op jit(solution)/shard_map/ppermute | solution.py:470
  5.7 8.3 %collective-permute-start.1 = (f32[400,128]{1,0:T(8,128)S(1)}, f32[400,128]{1,0:T(8,128)S(1)}, u32[]{:S(2)}, u32[]{:S(2)}) collective-permute-start(f32[400,128]{1,0:T(8,128)S(1)} %get-tuple-element.68.sent), channel_id=1, source_target_pairs={{0,2},{1,3},{2,0},{3,1},{4,6},{5,7},{6,4},{7,5},{8,10},{9,11},{10,... | collective-permute-start | bytes 614408 | tf_op jit(solution)/shard_map/ppermute | solution.py:470
  14.0 8.5 %collective-permute-start.2 = (f32[400,128]{1,0:T(8,128)S(1)}, f32[400,128]{1,0:T(8,128)S(1)}, u32[]{:S(2)}, u32[]{:S(2)}) collective-permute-start(f32[400,128]{1,0:T(8,128)S(1)} %shard_map.96), channel_id=1, source_target_pairs={{0,4},{1,5},{2,6},{3,7},{4,8},{5,9},{6,10},{7,11},{8,12},{9,13},{1... | collective-permute-start | bytes 614408 | tf_op jit(solution)/shard_map/ppermute | solution.py:475
  20.1 17.7 %copy-start.3 = (bf16[256,1536]{1,0:T(8,128)(2,1)S(1)}, bf16[256,1536]{1,0:T(8,128)(2,1)}, u32[]{:S(2)}) copy-start(bf16[256,1536]{1,0:T(8,128)(2,1)} %out_grad.1) | copy-start | bytes 2359300
  22.5 7.6 %collective-permute-start.3 = (f32[400,128]{1,0:T(8,128)S(1)}, f32[400,128]{1,0:T(8,128)S(1)}, u32[]{:S(2)}, u32[]{:S(2)}) collective-permute-start(f32[400,128]{1,0:T(8,128)S(1)} %collective-permute-done.2.rest_0_), channel_id=1, source_target_pairs={{0,4},{1,5},{2,6},{3,7},{4,8},{5,9},{6,10},{7,11},{8,12},{9,13},{1... | collective-permute-start | bytes 614408 | tf_op jit(solution)/shard_map/ppermute | solution.py:475
  30.1 5.7 %collective-permute-start.4 = (f32[384,128]{1,0:T(8,128)S(1)}, f32[384,128]{1,0:T(8,128)S(1)}, u32[]{:S(2)}, u32[]{:S(2)}) collective-permute-start(f32[384,128]{1,0:T(8,128)S(1)} %get-tuple-element.74), channel_id=1, source_target_pairs={{0,2},{1,3},{2,0},{3,1},{4,6},{5,7},{6,4},{7,5},{8,10},{9,11},{10,... | collective-permute-start | bytes 589832 | tf_op jit(solution)/shard_map/ppermute | solution.py:470
  36.0 1.8 %collective-permute-start.5 = (f32[768,128]{1,0:T(8,128)S(1)}, f32[768,128]{1,0:T(8,128)S(1)}, u32[]{:S(2)}, u32[]{:S(2)}) collective-permute-start(f32[768,128]{1,0:T(8,128)S(1)} %get-tuple-element.78), channel_id=1, source_target_pairs={{0,1},{1,0},{2,3},{3,2},{4,5},{5,4},{6,7},{7,6},{8,9},{9,8},{10,11... | collective-permute-start | bytes 1179656 | tf_op jit(solution)/shard_map/ppermute | solution.py:470
  39.1 3.7 %collective-permute-start.6 = (f32[8,256]{1,0:T(8,128)S(1)}, f32[8,256]{1,0:T(8,128)S(1)}, u32[]{:S(2)}, u32[]{:S(2)}) collective-permute-start(f32[8,256]{1,0:T(8,128)S(1)} %get-tuple-element.81), channel_id=1, source_target_pairs={{0,16},{16,0},{1,17},{17,1},{2,18},{18,2},{3,19},{19,3},{4,20},{20... | collective-permute-start | bytes 24584 | tf_op jit(solution)/shard_map/ppermute | solution.py:470
  44.3 1.8 %collective-permute-start.7 = (f32[800,128]{1,0:T(8,128)S(1)}, f32[800,128]{1,0:T(8,128)S(1)}, u32[]{:S(2)}, u32[]{:S(2)}) collective-permute-start(f32[800,128]{1,0:T(8,128)S(1)} %get-tuple-element.85), channel_id=1, source_target_pairs={{0,1},{1,0},{2,3},{3,2},{4,5},{5,4},{6,7},{7,6},{8,9},{9,8},{10,11... | collective-permute-start | bytes 1228808 | tf_op jit(solution)/shard_map/ppermute | solution.py:470
  46.2 7.4 %collective-permute-start.8 = (f32[416,128]{1,0:T(8,128)S(1)}, f32[416,128]{1,0:T(8,128)S(1)}, u32[]{:S(2)}, u32[]{:S(2)}) collective-permute-start(f32[416,128]{1,0:T(8,128)S(1)} %get-tuple-element.90.sent), channel_id=1, source_target_pairs={{0,2},{1,3},{2,0},{3,1},{4,6},{5,7},{6,4},{7,5},{8,10},{9,11},{10,... | collective-permute-start | bytes 638984 | tf_op jit(solution)/shard_map/ppermute | solution.py:470
  53.7 7.4 %collective-permute-start.10 = (f32[416,128]{1,0:T(8,128)S(1)}, f32[416,128]{1,0:T(8,128)S(1)}, u32[]{:S(2)}, u32[]{:S(2)}) collective-permute-start(f32[416,128]{1,0:T(8,128)S(1)} %get-tuple-element.91.rest_2_), channel_id=1, source_target_pairs={{0,12},{1,13},{2,14},{3,15},{4,0},{5,1},{6,2},{7,3},{8,4},{9,5},{1... | collective-permute-start | bytes 638984 | tf_op jit(solution)/shard_map/ppermute | solution.py:475
  55.6 5.5 %collective-permute-start.9 = (f32[16,128]{1,0:T(8,128)S(1)}, f32[16,128]{1,0:T(8,128)S(1)}, u32[]{:S(2)}, u32[]{:S(2)}) collective-permute-start(f32[16,128]{1,0:T(8,128)S(1)} %get-tuple-element.98), channel_id=1, source_target_pairs={{0,4},{1,5},{2,6},{3,7},{4,8},{5,9},{6,10},{7,11},{8,12},{9,13},{1... | collective-permute-start | bytes 24584 | tf_op jit(solution)/shard_map/ppermute | solution.py:475
  61.1 5.8 %collective-permute-start.11 = (f32[416,128]{1,0:T(8,128)S(1)}, f32[416,128]{1,0:T(8,128)S(1)}, u32[]{:S(2)}, u32[]{:S(2)}) collective-permute-start(f32[416,128]{1,0:T(8,128)S(1)} %collective-permute-done.10.rest_0_), channel_id=1, source_target_pairs={{0,12},{1,13},{2,14},{3,15},{4,0},{5,1},{6,2},{7,3},{8,4},{9,5},{1... | collective-permute-start | bytes 638984 | tf_op jit(solution)/shard_map/ppermute | solution.py:475
  67.1 5.7 %collective-permute-start.12 = (f32[384,128]{1,0:T(8,128)S(1)}, f32[384,128]{1,0:T(8,128)S(1)}, u32[]{:S(2)}, u32[]{:S(2)}) collective-permute-start(f32[384,128]{1,0:T(8,128)S(1)} %get-tuple-element.103), channel_id=1, source_target_pairs={{0,2},{1,3},{2,0},{3,1},{4,6},{5,7},{6,4},{7,5},{8,10},{9,11},{10,... | collective-permute-start | bytes 589832 | tf_op jit(solution)/shard_map/ppermute | solution.py:470
  72.9 1.8 %collective-permute-start.13 = (f32[768,128]{1,0:T(8,128)S(1)}, f32[768,128]{1,0:T(8,128)S(1)}, u32[]{:S(2)}, u32[]{:S(2)}) collective-permute-start(f32[768,128]{1,0:T(8,128)S(1)} %get-tuple-element.105), channel_id=1, source_target_pairs={{0,1},{1,0},{2,3},{3,2},{4,5},{5,4},{6,7},{7,6},{8,9},{9,8},{10,11... | collective-permute-start | bytes 1179656 | tf_op jit(solution)/shard_map/ppermute | solution.py:470

commit v3 on v2

--- a/solution.py
+++ b/solution.py
@@ -1,4 +1,5 @@
 import functools
+import math
 
 import jax
 import jax.numpy as jnp
@@ -10,7 +11,7 @@
 C = 128
 EPSILON = 1e-06
 PLANE = 4
-WAVES = (1,)
+WAVES = (2, 1)
 F32 = jnp.float32
 BF16 = jnp.bfloat16
 HIGHEST = lax.Precision.HIGHEST
@@ -108,21 +109,20 @@
         ]
 
 
-def call(kernel, outs, *args, flops=0, spaces=None, out_spaces=None, scratch=()):
-    moved = sum(a.size * a.dtype.itemsize for a in args) + sum(
-        o.size * o.dtype.itemsize for o in outs
-    )
+def call(kernel, outs, *args, flops=0, spaces=None, out_spaces=None, scratch=(), deps=()):
+    moved = sum(math.prod(a.shape) * a.dtype.itemsize for a in (*args, *outs))
     spaces = spaces or [pltpu.VMEM] * len(args)
     out_spaces = out_spaces or [pltpu.VMEM] * len(outs)
+    given = len(args)
     return pl.pallas_call(
-        kernel,
+        lambda *refs: kernel(*refs[:given], *refs[given + len(deps) :]),
         out_shape=outs,
-        in_specs=[pl.BlockSpec(memory_space=p) for p in spaces],
+        in_specs=[pl.BlockSpec(memory_space=p) for p in spaces + [pl.ANY] * len(deps)],
         out_specs=[pl.BlockSpec(memory_space=p) for p in out_spaces],
-        compiler_params=pltpu.CompilerParams(vmem_limit_bytes=2 * moved + (3 << 20)),
+        compiler_params=pltpu.CompilerParams(vmem_limit_bytes=moved + (4 << 20)),
         cost_estimate=pl.CostEstimate(flops=flops, bytes_accessed=moved, transcendentals=0),
         scratch_shapes=scratch,
-    )(*args)
+    )(*args, *deps)
 
 
 def after(token, *values):
@@ -229,7 +229,7 @@
 
 
 def chip_kernel(s, reverse, keep, received, own_tail, *rest):
-    out_keep, out_send = rest[-2:]
+    out_keep, out_send = rest[-3:-1] if reverse else rest
     core, chip, _ = place_bits(s.count, reverse)
     lower, left = core == 0, chip == 0
     base, top = s.heads * s.half, s.heads * s.quarter
@@ -237,7 +237,11 @@
     factor = near[: s.heads, :] * linked(s, far, near)
     join_tail(s, out_send, top, far, near, factor)
     if reverse:
-        out_send[top + s.tail :, :] = rest[0][...] + received[base + s.tail :, :]
+        gain = rest[0][...] + received[base + s.tail :, :]
+        every = rest[-1]
+        if s.wave:
+            every[: -s.gains, :] = rest[1][...]
+        every[every.shape[0] - s.gains :, :] = gain
     for h in range(s.heads):
         rows = s.rows(h, s.half)
         far_state, near_state = sides(lower, keep[rows, :], received[rows, :])
@@ -246,20 +250,15 @@
 
 
 def plane_kernel(s, reverse, keep, sent, received, *rest):
-    out = rest[-2] if reverse else rest[0]
+    columns, out = rest[:-1], rest[-1]
     _, chip, _ = place_bits(s.count, reverse)
     left = chip == 0
     top = s.heads * s.quarter
     far, near = sides(left, sent[top:, :], received[top:, :])
     factor = near[: s.heads, :] * linked(s, far, near)
     join_tail(s, out, top, far, near, factor)
-    if reverse:
-        gain = sent[top + s.tail :, :] + received[top + s.tail :, :]
-        out[top + s.tail :, :] = gain
-        every = rest[-1]
-        if len(rest) > 2:
-            every[: -s.gains, :] = rest[0][...]
-        every[every.shape[0] - s.gains :, :] = gain
+    if columns:
+        out[top + s.tail :, :] = sum([a[...] for a in columns[1:]], columns[0][...])
     for h in range(s.heads):
         rows = s.rows(h, s.quarter)
         far_state, near_state = sides(left, keep[rows, :], received[rows, :])
@@ -267,8 +266,8 @@
 
 
 def spread_kernel(s, reverse, keep, sent, received, *rest):
-    out_keep, out_send = rest[-3:-1] if reverse else rest[-2:]
-    earlier = rest[: s.window]
+    earlier, rest = rest[: s.window], rest[s.window :]
+    out_keep, out_send = rest[1:3] if rest[2:] else rest
     _, chip, plane = place_bits(s.count, reverse)
     left = chip == 0
     top = s.heads * s.quarter
@@ -282,11 +281,12 @@
     ]
     link = linked(s, far, near)
     far_factor = far[: s.heads, :]
-    if reverse:
-        gain = rest[s.window][top + s.tail :, :]
-        for other in earlier[: s.planes - 1]:
-            gain = gain + other[top + s.tail :, :]
-        rest[-1][...] = gain
+    if rest[2:]:
+        gain = rest[0][top + s.tail :, :]
+        if s.planes > 1:
+            gain = gain + earlier[0][top + s.tail :, :]
+        rest[3][...] = gain
+        out_send[top:, :] = gain
     for h in range(s.heads):
         rows, one = s.rows(h, s.quarter), slice(h, h + 1)
         state = earlier[-1][rows, :]
@@ -361,7 +361,7 @@
             attention = local[own] + decays[j][:, h : h + 1] * far
             out[own] = attention
             squares[j] = squares[j] + attention * attention
-            inners[j] = inners[j] + out_grad[part].astype(F32) * gain[:, s.head(h)] * attention
+            inners[j] = inners[j] + out_grad[part].astype(F32) * gain[s.head(h)].reshape(1, s.width) * attention
             if j < s.blocks - 1:
                 update = first_update[s.rows(j * s.heads + h, s.width), :]
                 state = notes[s.carry(j + 1), :] * (factors[j][h : h + 1, :] * state + update)
@@ -399,7 +399,7 @@
     )
     out_gain[...] = jnp.zeros(out_gain.shape, F32)
     for h in range(s.heads):
-        gain_row = gain[:, s.head(h)]
+        gain_row = gain[s.head(h)].reshape(1, s.width)
         gain_part = jnp.zeros((1, s.width), F32)
         terms = []
         for j in range(s.blocks):
@@ -435,34 +435,61 @@
             value_out[own] = dot(weights[s.rows(j * s.heads + h, C), :], grad, 0, 0)
 
 
-def final_kernel(
-    s, last, keys, values, log_decay, notes, key_local, value_local, back_terms, keep, received,
-    *rest,
-):
-    earlier, (key_out, value_out) = rest[:-2], rest[-2:]
+def final_kernel(s, waves, keys, values, log_decay, notes, key_local, value_local, back_terms, *rest):
+    keep, received = rest[:2]
+    last = s.wave == waves - 1
+    near_outs = rest[-2:]
+    copies = []
+    if last:
+        *far_outs, far_gain, near_gain, sent = rest[-7:-2]
+        groups = sent.shape[1] - s.wave
+        own, other = rest[2 + 2 * s.wave : 4 + 2 * s.wave]
+        base = s.heads * s.quarter
+        for w in range(waves):
+            for h in range(s.heads):
+                row = w * s.gains + h
+                total = own[row : row + 1, :] + other[base + row : base + row + 1, :]
+                place = (w * s.heads + h) * s.width
+                near_gain[place : place + s.width] = total.reshape(s.width)
+        copies.append(pltpu.make_async_copy(near_gain, far_gain, sent.at[2, 0]))
+        copies[-1].start()
+        for w in range(s.wave):
+            place = pl.ds(w * s.columns, s.columns)
+            for i, far in enumerate(far_outs):
+                near = rest[2 + 2 * w + i]
+                copies.append(
+                    pltpu.make_async_copy(near, far.at[:, place], sent.at[i, groups + w])
+                )
+                copies[-1].start()
     core, _, _ = place_bits(s.count, True)
     lower = core == 0
     logs = s.logs(log_decay)
     factors = [jnp.exp(total_rows(a)) for a in logs]
     columns = [decay_columns(a) for a in logs]
     ends = [jnp.exp(a[C - 1 : C, :] - a) for a in columns]
-    for i in range(0, len(earlier), 2):
-        place = slice(i // 2 * s.columns, (i // 2 + 1) * s.columns)
-        key_out[:, place] = earlier[i][...]
-        value_out[:, place] = earlier[i + 1][...]
     for h in range(s.heads):
         state = joined(s, lower, keep, received, h)
         for j in reversed(range(s.blocks)):
             part, own = (s.block(j), s.head(h)), (s.block(j), s.own(h))
-            out = part if last else own
             end = ends[j][:, h : h + 1]
             key_far = end * far_dot(values[part], state, 1)
             value_far = end * far_dot(keys[part], state, 0)
-            key_out[out] = (key_local[own] + key_far).astype(BF16)
-            value_out[out] = (value_local[own] + value_far).astype(BF16)
+            near_outs[0][own] = (key_local[own] + key_far).astype(BF16)
+            near_outs[1][own] = (value_local[own] + value_far).astype(BF16)
             if j > 0:
                 term = back_terms[s.rows((j - 1) * s.heads + h, s.width), :]
                 state = notes[s.carry(j), :] * (term + factors[j][h : h + 1, :] * state)
+        if last and (h + 1) * groups % s.heads == 0:
+            each, g = s.heads // groups, h * groups // s.heads
+            part = pl.ds(g * each * s.width, each * s.width)
+            far_part = pl.ds((s.first + g * each) * s.width, each * s.width)
+            for i, (near, far) in enumerate(zip(near_outs, far_outs)):
+                copies.append(
+                    pltpu.make_async_copy(near.at[:, part], far.at[:, far_part], sent.at[i, g])
+                )
+                copies[-1].start()
+    for copy in copies:
+        copy.wait()
 
 
 def swap(value, axis, bit):
@@ -477,54 +504,70 @@
 
 def scan_in(waves, parts, reverse, token, beside):
     bind = functools.partial
-    gain_rows = lambda s: s.gains if reverse else 0
-    received, chips, chip_received, local = [], [], [], []
+    last = waves[-1]
+    gain_rows = lambda s: len(waves) * s.gains if reverse and s is last else 0
+    received, chips, chip_received, local, gains, others = [], [], [], [], [], []
     for s, (keep, send, tail, gain) in zip(waves, parts):
         received.append(swap(send, "seq", 1))
     for i, (s, (keep, send, tail, gain)) in enumerate(zip(waves, parts)):
         outs = [
             shape(s.heads * s.quarter, s.width),
-            shape(s.heads * s.quarter + s.tail + gain_rows(s), s.width),
+            shape(s.heads * s.quarter + s.tail, s.width),
         ]
         (keep,) = after(token, keep)
-        extra = [gain] if reverse else []
-        chip = call(bind(chip_kernel, s, reverse), outs, keep, received[i], tail, *extra)
+        extra = []
+        if reverse:
+            extra = [gain, *gains]
+            outs.append(shape((i + 1) * s.gains, s.width))
+        *chip, = call(bind(chip_kernel, s, reverse), outs, keep, received[i], tail, *extra)
+        gains = chip[2:]
         token = chip[0]
         chips.append(chip)
-        sent = chip[1]
-        if chip_received:
-            (sent,) = after(chip_received[-1], sent)
-        chip_received.append(swap(sent, "seq", 2))
-    planes, passed, gains, others = [], [], [], []
+        chip_received.append(swap(chip[1], "seq", 2))
+    if reverse:
+        bit = last.count // 2
+        while bit > PLANE:
+            if others:
+                gains, others = [gains[0] + others[0]], []
+            others = [swap(gains[0], "seq", bit)]
+            bit //= 2
+    planes, passed = [], []
+    for i in range(len(waves) - 1):
+        token, one = beside(token, i)
+        local.append(one)
     for i, s in enumerate(waves):
         (keep,) = after(token, chips[i][0])
         outs = [shape(s.heads * s.quarter + s.tail + gain_rows(s), s.width)]
-        if reverse:
-            outs.append(shape((i + 1) * s.gains, s.width))
-        plane, *gains = call(
-            bind(plane_kernel, s, reverse), outs, keep, chips[i][1], chip_received[i], *gains
+        columns = gains + others if gain_rows(s) else []
+        (plane,) = call(
+            bind(plane_kernel, s, reverse),
+            outs,
+            keep,
+            chips[i][1],
+            chip_received[i],
+            *columns,
+            deps=planes[-1:],
         )
         token = plane
         planes.append(plane)
-        into = next_plane(plane, s.count, reverse)
+        passed.append([next_plane(plane, s.count, reverse)])
+    for i in range(len(local), len(waves)):
         token, one = beside(token, i)
         local.append(one)
-        if reverse and i == len(waves) - 1:
-            others = list(after(token, *gains))
-            for _ in range(s.planes - 1 - s.window):
-                others.append(next_plane(others[-1], s.count, not reverse))
-            (token,) = after(others[-1], token)
-        passed.append(list(after(token, into)))
+    passed = [list(after(token, one[0])) for one in passed]
     for _ in range(waves[0].window - 1):
         for i, s in enumerate(waves):
             passed[i].append(next_plane(passed[i][-1], s.count, reverse))
     spreads, spread_received = [], []
     for i, s in enumerate(waves):
         (keep,) = after(token, chips[i][0])
-        outs = [shape(s.heads * s.quarter, s.width)] * 2
+        outs = [
+            shape(s.heads * s.quarter, s.width),
+            shape(s.heads * s.quarter + gain_rows(s), s.width),
+        ]
         extra = []
-        if reverse:
-            outs.append(shape(s.gains, s.width))
+        if gain_rows(s):
+            outs.append(shape(gain_rows(s), s.width))
             extra = [planes[i]]
         spread = call(
             bind(spread_kernel, s, reverse),
@@ -552,14 +595,7 @@
         )
         token = entry[0]
         entries.append((entry[0], swap(entry[1], "seq", 1)))
-    gain = None
-    if reverse:
-        pad = lambda a, s: a.reshape(-1, s.gains, s.width)[:, : s.heads].reshape(-1, s.width)
-        gain = jnp.concatenate([pad(spread[2], s) for spread in spreads])
-        for other in others[1:]:
-            gain = gain + pad(other, s)
-        gain = gain.reshape(-1)
-    return entries, local, token, gain
+    return entries, local, token, [spreads[-1][-1], spread_received[-1]]
 
 
 def per_device(queries, keys, values, out_grad, log_decay, norm_gain, doc_ids):
@@ -570,7 +606,7 @@
     waves = [Sizes(tokens, features, heads, count, w, wave_count) for w in range(wave_count)]
     bind = functools.partial
     unit = 2 * C * C * C * waves[0].blocks * waves[0].heads
-    gain = norm_gain.reshape(1, features)
+    gain = norm_gain
     log_decay = log_decay.T
     states = []
     far = [pltpu.with_memory_space_constraint(a, pltpu.HBM) for a in (keys, values, log_decay, doc_ids)]
@@ -695,29 +731,40 @@
         return local_grad[0], local_grad
 
     parts = [(grad[1], grad[2], grad[3], grad[4]) for grad in grads]
-    entries, local_grads, token, gain_grad = scan_in(waves, parts, True, token, beside_backward)
-    (token,) = after(gain_grad, token)
+    entries, local_grads, token, gains = scan_in(waves, parts, True, token, beside_backward)
     done = []
     for i, s in enumerate(waves):
         last = i == wave_count - 1
         (held,) = after(token, log_decay)
-        done.extend(
-            call(
-                bind(final_kernel, s, last),
-                [shape(tokens, features if last else s.columns, BF16)] * 2,
-                keys,
-                values,
-                held,
-                states[i][2],
-                *local_grads[i],
-                grads[i][5],
-                *entries[i][:2],
-                *(done if last else ()),
-                flops=4 * unit,
-            )
-        )
-        token = done[-1]
-    return (done[-2], done[-1], gain_grad)
+        groups = max(g for g in (3, 2, 1) if s.heads % g == 0)
+        given = [
+            keys, values, held, states[i][2], *local_grads[i], grads[i][5], *entries[i], *done,
+        ]
+        scratch = []
+        if last:
+            given += gains
+            outs = [pltpu.HBM((tokens, features), BF16)] * 2 + [pltpu.HBM((features,), F32)]
+            out_spaces = [pltpu.HBM] * 3
+            scratch = [
+                pltpu.VMEM((features,), F32),
+                pltpu.SemaphoreType.DMA((3, groups + i)),
+                pltpu.VMEM((tokens, s.columns), BF16),
+                pltpu.VMEM((tokens, s.columns), BF16),
+            ]
+        else:
+            outs = [shape(tokens, s.columns, BF16)] * 2
+            out_spaces = [pltpu.VMEM] * 2
+        made = call(
+            bind(final_kernel, s, wave_count),
+            outs,
+            *given,
+            flops=4 * unit,
+            out_spaces=out_spaces,
+            scratch=scratch,
+        )
+        token = made[0]
+        done += made
+    return tuple(done[-3:])
 
 
 def solution(mesh):

time: 77.8 us -> 70.9 us (0.911)
  waiting for transfers between devices: 45.6 us -> 27.2 us
  starting transfers between devices: 15.2 us -> 24.1 us
  Pallas kernels: 15.4 us -> 17.9 us
    ppermute x9 -> x18, waiting for transfers between devices: 27.6 us -> 12.9 us  [swap(): return lax.ppermute(value, axis, [(i, i ^ bit) for i in range(count)])]
    ppermute x9 -> x18, starting transfers between devices: 9.87 us -> 15.8 us  [swap(): return lax.ppermute(value, axis, [(i, i ^ bit) for i in range(count)])]
    ppermute x5 -> x8, waiting for transfers between devices: 17.9 us -> 14.3 us  [next_plane(): lax.ppermute(value, 'seq', [(i, (i + step) % count) for i in range(count)])]
    ppermute x5 -> x8, starting transfers between devices: 5.3 us -> 8.32 us  [next_plane(): lax.ppermute(value, 'seq', [(i, (i + step) % count) for i in range(count)])]
    pallas_call x14 -> x28, Pallas kernels: 15.4 us -> 17.9 us  [call(): pl.pallas_call(lambda *refs: kernel(*refs[:given], *refs[given + len(deps...]
  transfers between devices with their start and end apart: 14 -> 26, of which waited for: 13 -> 16; matrix products, arithmetic and copies ran while one was open for 1% -> 0% of each run, Pallas kernels for 8% -> 17%
where the time goes in v3:
time: 70.9 us; the launch traced here: 70.8 us
  waiting for transfers between devices  27.2 us (38%)
  starting transfers between devices  24.1 us (34%)
  Pallas kernels  17.9 us (25%)
  between operations  0.9 us (1%)
    pallas_call x28, Pallas kernels, call(): pl.pallas_call(lambda *refs: kernel(*refs[:given], *refs[given + len(deps...  17.9 us
    ppermute x18, starting transfers between devices, swap(): return lax.ppermute(value, axis, [(i, i ^ bit) for i in range(count)])  15.8 us
    ppermute x8, waiting for transfers between devices, next_plane(): lax.ppermute(value, 'seq', [(i, (i + step) % count) for i in range(count)])  14.3 us
    ppermute x18, waiting for transfers between devices, swap(): return lax.ppermute(value, axis, [(i, i ^ bit) for i in range(count)])  12.9 us
    ppermute x8, starting transfers between devices, next_plane(): lax.ppermute(value, 'seq', [(i, (i + step) % count) for i in range(count)])  8.32 us
  transfers between devices with their start and end apart: 26, of which 16 were waited for; matrix products, arithmetic and copies ran while one was open for 0% of the time, Pallas kernels for 17%

profile of v3, /device:TPU:0, one launch (start us, length us, event | category | flops | bytes accessed | tf_op | source)
XLA Modules:
  0.0 70.8 jit_solution(16219094875654819060)
XLA Ops:
  0.7 2.4 %shard_map.94 = (f32[384,128]{1,0:T(8,128)S(1)}, f32[392,128]{1,0:T(8,128)S(1)}, f32[16,128]{1,0:T(8,128)S(1)}, f32[768,128]{1,0:T(8,128)S(1)}) custom-call(bf16[256,1536]{1,0:T(8,128)(2,1)} %refs_0_.13, bf16[256,1536]{1,0:T(8,128)(2,1)} %refs_1_.13, f32[12,256]{1,0:T(8,128)} %bitcast.1, s32[2]{0:T(128)} %refs_3_.3), custom_call_target="tpu_custom_call" | custom-call | flops 50331648 | bytes 2383880 | tf_op jit(solution)/shard_map/pallas_call | solution.py:117
  3.0 0.5 collective-permute-start
  3.6 0.1 copy-done.6
  3.7 1.4 %shard_map.95 = (f32[384,128]{1,0:T(8,128)S(1)}, f32[392,128]{1,0:T(8,128)S(1)}, f32[16,128]{1,0:T(8,128)S(1)}, f32[768,128]{1,0:T(8,128)S(1)}) custom-call(bf16[256,1536]{1,0:T(8,128)(2,1)S(1)} %copy-done.2, bf16[256,1536]{1,0:T(8,128)(2,1)S(1)} %copy-done, f32[12,256]{1,0:T(8,128)S(1)} %bitcast.2, s32[2]{0:T(128)S(1)} %copy-done.6), custom_call_target="tpu_custom_call" | custom-call | flops 50331648 | bytes 2383880 | tf_op jit(solution)/shard_map/pallas_call | solution.py:117
  5.1 0.5 collective-permute-start.1
  5.7 2.6 %collective-permute-start.2 = (f32[200,128]{1,0:T(8,128)S(1)}, f32[200,128]{1,0:T(8,128)S(1)}, u32[]{:S(2)}, u32[]{:S(2)}) collective-permute-start(f32[200,128]{1,0:T(8,128)S(1)} %get-tuple-element.121.refs_1_), channel_id=1, source_target_pairs={{0,2},{1,3},{2,0},{3,1},{4,6},{5,7},{6,4},{7,5},{8,10},{9,11},{10,... | collective-permute-start | bytes 307208 | tf_op jit(solution)/shard_map/ppermute | solution.py:497
  8.3 1.4 %collective-permute-start.3 = (f32[200,128]{1,0:T(8,128)S(1)}, f32[200,128]{1,0:T(8,128)S(1)}, u32[]{:S(2)}, u32[]{:S(2)}) collective-permute-start(f32[200,128]{1,0:T(8,128)S(1)} %get-tuple-element.123.refs_1_), channel_id=1, source_target_pairs={{0,2},{1,3},{2,0},{3,1},{4,6},{5,7},{6,4},{7,5},{8,10},{9,11},{10,... | collective-permute-start | bytes 307208 | tf_op jit(solution)/shard_map/ppermute | solution.py:497
  9.7 2.3 %shard_map.98 = (f32[256,768]{1,0:T(8,128)S(1)}, bf16[1536,128]{1,0:T(8,128)(2,1)S(1)}) custom-call(bf16[256,1536]{1,0:T(8,128)(2,1)S(1)} %copy-done.1, bf16[256,1536]{1,0:T(8,128)(2,1)S(1)} %copy-done.2, bf16[256,1536]{1,0:T(8,128)(2,1)S(1)} %copy-done, f32[12,256]{1,0:T(8,128)S(1)} %bitcast.3), custom_call_target="tpu_custom_call" | custom-call | flops 100663296 | bytes 3551232 | tf_op jit(solution)/shard_map/pallas_call | solution.py:117
  12.0 2.1 %collective-permute-start.4 = (f32[200,128]{1,0:T(8,128)S(1)}, f32[200,128]{1,0:T(8,128)S(1)}, u32[]{:S(2)}, u32[]{:S(2)}) collective-permute-start(f32[200,128]{1,0:T(8,128)S(1)} %shard_map.99.refs_3_), channel_id=1, source_target_pairs={{0,4},{1,5},{2,6},{3,7},{4,8},{5,9},{6,10},{7,11},{8,12},{9,13},{1... | collective-permute-start | bytes 307208 | tf_op jit(solution)/shard_map/ppermute | solution.py:502
  14.2 1.7 %collective-permute-start.6 = (f32[200,128]{1,0:T(8,128)S(1)}, f32[200,128]{1,0:T(8,128)S(1)}, u32[]{:S(2)}, u32[]{:S(2)}) collective-permute-start(f32[200,128]{1,0:T(8,128)S(1)} %shard_map.100), channel_id=1, source_target_pairs={{0,4},{1,5},{2,6},{3,7},{4,8},{5,9},{6,10},{7,11},{8,12},{9,13},{1... | collective-permute-start | bytes 307208 | tf_op jit(solution)/shard_map/ppermute | solution.py:502
  15.9 2.3 %shard_map.101 = (f32[256,768]{1,0:T(8,128)S(1)}, bf16[1536,128]{1,0:T(8,128)(2,1)S(1)}) custom-call(bf16[256,1536]{1,0:T(8,128)(2,1)S(1)} %copy-done.1, bf16[256,1536]{1,0:T(8,128)(2,1)S(1)} %copy-done.2, bf16[256,1536]{1,0:T(8,128)(2,1)S(1)} %copy-done, f32[12,256]{1,0:T(8,128)S(1)} %bitcast.4), custom_call_target="tpu_custom_call" | custom-call | flops 100663296 | bytes 3551232 | tf_op jit(solution)/shard_map/pallas_call | solution.py:117
  18.2 0.9 %collective-permute-done.4.refs_3_ = f32[200,128]{1,0:T(8,128)S(1)} collective-permute-done((f32[200,128]{1,0:T(8,128)S(1)}, f32[200,128]{1,0:T(8,128)S(1)}, u32[]{:S(2)}, u32[]{:S(2)}) %collective-permute-start.4) | collective-permute-done | bytes 102432 | tf_op jit(solution)/shard_map/ppermute | solution.py:502
  19.1 0.7 %collective-permute-start.5 = (f32[200,128]{1,0:T(8,128)S(1)}, f32[200,128]{1,0:T(8,128)S(1)}, u32[]{:S(2)}, u32[]{:S(2)}) collective-permute-start(f32[200,128]{1,0:T(8,128)S(1)} %collective-permute-done.4.refs_3_), channel_id=1, source_target_pairs={{0,4},{1,5},{2,6},{3,7},{4,8},{5,9},{6,10},{7,11},{8,12},{9,13},{1... | collective-permute-start | bytes 307208 | tf_op jit(solution)/shard_map/ppermute | solution.py:502
  19.8 1.2 %collective-permute-done.6.refs_3_ = f32[200,128]{1,0:T(8,128)S(1)} collective-permute-done((f32[200,128]{1,0:T(8,128)S(1)}, f32[200,128]{1,0:T(8,128)S(1)}, u32[]{:S(2)}, u32[]{:S(2)}) %collective-permute-start.6) | collective-permute-done | bytes 102432 | tf_op jit(solution)/shard_map/ppermute | solution.py:502
  21.0 0.4 collective-permute-start.7
  21.4 5.0 %collective-permute-done.5.refs_4_ = f32[200,128]{1,0:T(8,128)S(1)} collective-permute-done((f32[200,128]{1,0:T(8,128)S(1)}, f32[200,128]{1,0:T(8,128)S(1)}, u32[]{:S(2)}, u32[]{:S(2)}) %collective-permute-start.5) | collective-permute-done | bytes 102432 | tf_op jit(solution)/shard_map/ppermute | solution.py:502
  26.5 2.2 %collective-permute-start.8 = (f32[192,128]{1,0:T(8,128)S(1)}, f32[192,128]{1,0:T(8,128)S(1)}, u32[]{:S(2)}, u32[]{:S(2)}) collective-permute-start(f32[192,128]{1,0:T(8,128)S(1)} %get-tuple-element.133), channel_id=1, source_target_pairs={{0,2},{1,3},{2,0},{3,1},{4,6},{5,7},{6,4},{7,5},{8,10},{9,11},{10,... | collective-permute-start | bytes 294920 | tf_op jit(solution)/shard_map/ppermute | solution.py:497
  28.7 1.1 %collective-permute-start.9 = (f32[192,128]{1,0:T(8,128)S(1)}, f32[192,128]{1,0:T(8,128)S(1)}, u32[]{:S(2)}, u32[]{:S(2)}) collective-permute-start(f32[192,128]{1,0:T(8,128)S(1)} %get-tuple-element.136), channel_id=1, source_target_pairs={{0,2},{1,3},{2,0},{3,1},{4,6},{5,7},{6,4},{7,5},{8,10},{9,11},{10,... | collective-permute-start | bytes 294920 | tf_op jit(solution)/shard_map/ppermute | solution.py:497
  29.8 2.0 %collective-permute-done.8.refs_1_ = f32[192,128]{1,0:T(8,128)S(1)} collective-permute-done((f32[192,128]{1,0:T(8,128)S(1)}, f32[192,128]{1,0:T(8,128)S(1)}, u32[]{:S(2)}, u32[]{:S(2)}) %collective-permute-start.8) | collective-permute-done | bytes 98336 | tf_op jit(solution)/shard_map/ppermute | solution.py:497
  32.0 1.4 %collective-permute-done.9.refs_1_ = f32[192,128]{1,0:T(8,128)S(1)} collective-permute-done((f32[192,128]{1,0:T(8,128)S(1)}, f32[192,128]{1,0:T(8,128)S(1)}, u32[]{:S(2)}, u32[]{:S(2)}) %collective-permute-start.9) | collective-permute-done | bytes 98336 | tf_op jit(solution)/shard_map/ppermute | solution.py:497
  33.6 0.5 copy-done.5
  34.1 0.7 %shard_map.106 = (f32[256,768]{1,0:T(8,128)S(1)}, f32[8,256]{1,0:T(8,128)S(1)}) custom-call(bf16[256,1536]{1,0:T(8,128)(2,1)S(1)} %copy-done.1, bf16[256,1536]{1,0:T(8,128)(2,1)S(1)} %copy-done.3, f32[1536]{0:T(1024)S(1)} %copy-done.5, f32[12,256]{1,0:T(8,128)S(1)} %bitcast.5, f32[16,128]{1,0:T(8,128)S(1)} %get-tuple-element.111.refs_2_.refs_4_.refs_3_, ...), custom_call_target="tpu_custom_call" | custom-call | flops 100663296 | bytes 3966976 | tf_op jit(solution)/shard_map/pallas_call | solution.py:117
  34.9 0.1 collective-permute-done.11.refs_8_
  35.0 0.7 %shard_map.107 = (f32[256,768]{1,0:T(8,128)S(1)}, f32[8,256]{1,0:T(8,128)S(1)}) custom-call(bf16[256,1536]{1,0:T(8,128)(2,1)S(1)} %copy-done.1, bf16[256,1536]{1,0:T(8,128)(2,1)S(1)} %copy-done.3, f32[1536]{0:T(1024)S(1)} %copy-done.5, f32[12,256]{1,0:T(8,128)S(1)} %bitcast.6, f32[16,128]{1,0:T(8,128)S(1)} %get-tuple-element.115.refs_2_.refs_4_.refs_3_, ...), custom_call_target="tpu_custom_call" | custom-call | flops 100663296 | bytes 3975168 | tf_op jit(solution)/shard_map/pallas_call | solution.py:117
  35.8 1.6 %collective-permute-start.12 = (f32[8,256]{1,0:T(8,128)S(1)}, f32[8,256]{1,0:T(8,128)S(1)}, u32[]{:S(2)}, u32[]{:S(2)}) collective-permute-start(f32[8,256]{1,0:T(8,128)S(1)} %get-tuple-element.148), channel_id=1, source_target_pairs={{0,16},{16,0},{1,17},{17,1},{2,18},{18,2},{3,19},{19,3},{4,20},{20... | collective-permute-start | bytes 24584 | tf_op jit(solution)/shard_map/ppermute | solution.py:497
  37.3 2.1 %collective-permute-done.12 = f32[8,256]{1,0:T(8,128)S(1)} collective-permute-done((f32[8,256]{1,0:T(8,128)S(1)}, f32[8,256]{1,0:T(8,128)S(1)}, u32[]{:S(2)}, u32[]{:S(2)}) %collective-permute-start.12) | collective-permute-done | bytes 8224 | tf_op jit(solution)/shard_map/ppermute | solution.py:497
  39.5 0.8 %shard_map.108 = (bf16[256,768]{1,0:T(8,128)(2,1)S(1)}, f32[384,128]{1,0:T(8,128)S(1)}, f32[400,128]{1,0:T(8,128)S(1)}, f32[8,128]{1,0:T(8,128)S(1)}, f32[8,128]{1,0:T(8,128)S(1)}, /*index=5*/f32[768,128]{1,0:T(8,128)S(1)}) custom-call(bf16[256,1536]{1,0:T(8,128)(2,1)S(1)} %copy-done.1, bf16[256,1536]{1,0:T(8,128)(2,1)S(1)} %copy-done.3, ...), custom_call_target="tpu_custom_call" | custom-call | flops 50331648 | bytes 3590144 | tf_op jit(solution)/shard_map/pallas_call | solution.py:117
  40.4 0.8 %shard_map.109 = (bf16[256,768]{1,0:T(8,128)(2,1)S(1)}, f32[384,128]{1,0:T(8,128)S(1)}, f32[400,128]{1,0:T(8,128)S(1)}, f32[8,128]{1,0:T(8,128)S(1)}, f32[8,128]{1,0:T(8,128)S(1)}, /*index=5*/f32[768,128]{1,0:T(8,128)S(1)}) custom-call(bf16[256,1536]{1,0:T(8,128)(2,1)S(1)} %copy-done.1, bf16[256,1536]{1,0:T(8,128)(2,1)S(1)} %copy-done.3, ...), custom_call_target="tpu_custom_call" | custom-call | flops 50331648 | bytes 3590144 | tf_op jit(solution)/shard_map/pallas_call | solution.py:117
  41.3 0.6 collective-permute-start.14
  41.9 1.3 %collective-permute-start.15 = (f32[200,128]{1,0:T(8,128)S(1)}, f32[200,128]{1,0:T(8,128)S(1)}, u32[]{:S(2)}, u32[]{:S(2)}) collective-permute-start(f32[200,128]{1,0:T(8,128)S(1)} %get-tuple-element.169.refs_1_), channel_id=1, source_target_pairs={{0,2},{1,3},{2,0},{3,1},{4,6},{5,7},{6,4},{7,5},{8,10},{9,11},{10,... | collective-permute-start | bytes 307208 | tf_op jit(solution)/shard_map/ppermute | solution.py:497
  43.3 1.0 %collective-permute-start.16 = (f32[200,128]{1,0:T(8,128)S(1)}, f32[200,128]{1,0:T(8,128)S(1)}, u32[]{:S(2)}, u32[]{:S(2)}) collective-permute-start(f32[200,128]{1,0:T(8,128)S(1)} %get-tuple-element.171.refs_1_), channel_id=1, source_target_pairs={{0,2},{1,3},{2,0},{3,1},{4,6},{5,7},{6,4},{7,5},{8,10},{9,11},{10,... | collective-permute-start | bytes 307208 | tf_op jit(solution)/shard_map/ppermute | solution.py:497
  44.3 1.4 %shard_map.112 = (f32[256,768]{1,0:T(8,128)S(1)}, f32[256,768]{1,0:T(8,128)S(1)}) custom-call(bf16[256,1536]{1,0:T(8,128)(2,1)S(1)} %copy-done.1, bf16[256,1536]{1,0:T(8,128)(2,1)S(1)} %copy-done, f32[12,256]{1,0:T(8,128)S(1)} %bitcast.9, bf16[1536,128]{1,0:T(8,128)(2,1)S(1)} %get-tuple-element.166.refs_3_, bf16[256,768]{1,0:T(8,128)(2,1)S(1)} %get-tuple-element.149.refs_4_), custom_call_target="tpu_custom_call" | custom-call | flops 150994944 | bytes 3944448 | tf_op jit(solution)/shard_map/pallas_call | solution.py:117
  45.6 2.1 %collective-permute-done.15.refs_2_ = f32[200,128]{1,0:T(8,128)S(1)} collective-permute-done((f32[200,128]{1,0:T(8,128)S(1)}, f32[200,128]{1,0:T(8,128)S(1)}, u32[]{:S(2)}, u32[]{:S(2)}) %collective-permute-start.15) | collective-permute-done | bytes 102432 | tf_op jit(solution)/shard_map/ppermute | solution.py:497
  47.7 1.1 %collective-permute-done.17.refs_4_ = f32[16,128]{1,0:T(8,128)S(1)} collective-permute-done((f32[16,128]{1,0:T(8,128)S(1)}, f32[16,128]{1,0:T(8,128)S(1)}, u32[]{:S(2)}, u32[]{:S(2)}) %collective-permute-start.17) | collective-permute-done | bytes 8224 | tf_op jit(solution)/shard_map/ppermute | solution.py:497
  48.8 0.3 collective-permute-done.16.refs_2_
  49.1 0.2 collective-permute-start.20
  49.3 1.1 %collective-permute-start.18 = (f32[200,128]{1,0:T(8,128)S(1)}, f32[200,128]{1,0:T(8,128)S(1)}, u32[]{:S(2)}, u32[]{:S(2)}) collective-permute-start(f32[200,128]{1,0:T(8,128)S(1)} %shard_map.113.refs_5_), channel_id=1, source_target_pairs={{0,12},{1,13},{2,14},{3,15},{4,0},{5,1},{6,2},{7,3},{8,4},{9,5},{1... | collective-permute-start | bytes 307208 | tf_op jit(solution)/shard_map/ppermute | solution.py:502
  50.4 1.4 %shard_map.115 = (f32[256,768]{1,0:T(8,128)S(1)}, f32[256,768]{1,0:T(8,128)S(1)}) custom-call(bf16[256,1536]{1,0:T(8,128)(2,1)S(1)} %copy-done.1, bf16[256,1536]{1,0:T(8,128)(2,1)S(1)} %copy-done, f32[12,256]{1,0:T(8,128)S(1)} %bitcast.10, bf16[1536,128]{1,0:T(8,128)(2,1)S(1)} %get-tuple-element.174.refs_3_, bf16[256,768]{1,0:T(8,128)(2,1)S(1)} %get-tuple-element.151.refs_4_), custom_call_target="tpu_custom_call" | custom-call | flops 150994944 | bytes 3944448 | tf_op jit(solution)/shard_map/pallas_call | solution.py:117
  51.7 3.9 %collective-permute-done.18.refs_3_ = f32[200,128]{1,0:T(8,128)S(1)} collective-permute-done((f32[200,128]{1,0:T(8,128)S(1)}, f32[200,128]{1,0:T(8,128)S(1)}, u32[]{:S(2)}, u32[]{:S(2)}) %collective-permute-start.18) | collective-permute-done | bytes 102432 | tf_op jit(solution)/shard_map/ppermute | solution.py:502
  55.6 2.1 %collective-permute-start.19 = (f32[200,128]{1,0:T(8,128)S(1)}, f32[200,128]{1,0:T(8,128)S(1)}, u32[]{:S(2)}, u32[]{:S(2)}) collective-permute-start(f32[200,128]{1,0:T(8,128)S(1)} %collective-permute-done.18.refs_3_), channel_id=1, source_target_pairs={{0,12},{1,13},{2,14},{3,15},{4,0},{5,1},{6,2},{7,3},{8,4},{9,5},{1... | collective-permute-start | bytes 307208 | tf_op jit(solution)/shard_map/ppermute | solution.py:502
  57.8 3.1 %collective-permute-done.19.refs_4_ = f32[200,128]{1,0:T(8,128)S(1)} collective-permute-done((f32[200,128]{1,0:T(8,128)S(1)}, f32[200,128]{1,0:T(8,128)S(1)}, u32[]{:S(2)}, u32[]{:S(2)}) %collective-permute-start.19) | collective-permute-done | bytes 102432 | tf_op jit(solution)/shard_map/ppermute | solution.py:502
  60.9 1.4 %collective-permute-start.22 = (f32[192,128]{1,0:T(8,128)S(1)}, f32[192,128]{1,0:T(8,128)S(1)}, u32[]{:S(2)}, u32[]{:S(2)}) collective-permute-start(f32[192,128]{1,0:T(8,128)S(1)} %get-tuple-element.183), channel_id=1, source_target_pairs={{0,2},{1,3},{2,0},{3,1},{4,6},{5,7},{6,4},{7,5},{8,10},{9,11},{10,... | collective-permute-start | bytes 294920 | tf_op jit(solution)/shard_map/ppermute | solution.py:497
  62.5 1.3 %collective-permute-start.23 = (f32[208,128]{1,0:T(8,128)S(1)}, f32[208,128]{1,0:T(8,128)S(1)}, u32[]{:S(2)}, u32[]{:S(2)}) collective-permute-start(f32[208,128]{1,0:T(8,128)S(1)} %get-tuple-element.186), channel_id=1, source_target_pairs={{0,2},{1,3},{2,0},{3,1},{4,6},{5,7},{6,4},{7,5},{8,10},{9,11},{10,... | collective-permute-start | bytes 319496 | tf_op jit(solution)/shard_map/ppermute | solution.py:497
  63.8 1.8 %collective-permute-done.22.refs_1_ = f32[192,128]{1,0:T(8,128)S(1)} collective-permute-done((f32[192,128]{1,0:T(8,128)S(1)}, f32[192,128]{1,0:T(8,128)S(1)}, u32[]{:S(2)}, u32[]{:S(2)}) %collective-permute-start.22) | collective-permute-done | bytes 98336 | tf_op jit(solution)/shard_map/ppermute | solution.py:497
  65.8 1.5 %collective-permute-done.23.refs_1_.refs_12_ = f32[208,128]{1,0:T(8,128)S(1)} collective-permute-done((f32[208,128]{1,0:T(8,128)S(1)}, f32[208,128]{1,0:T(8,128)S(1)}, u32[]{:S(2)}, u32[]{:S(2)}) %collective-permute-start.23) | collective-permute-done | bytes 106528 | tf_op jit(solution)/shard_map/ppermute | solution.py:497
  67.5 1.1 %shard_map.120 = (bf16[256,768]{1,0:T(8,128)(2,1)S(1)}, bf16[256,768]{1,0:T(8,128)(2,1)S(1)}) custom-call(bf16[256,1536]{1,0:T(8,128)(2,1)S(1)} %copy-done.2, bf16[256,1536]{1,0:T(8,128)(2,1)S(1)} %copy-done, f32[12,256]{1,0:T(8,128)S(1)} %bitcast.11, f32[16,128]{1,0:T(8,128)S(1)} %get-tuple-element.111.refs_2_.refs_4_.refs_3_, ...), custom_call_target="tpu_custom_call" | custom-call | flops 201326592 | bytes 4739072 | tf_op jit(solution)/shard_map/pallas_call | solution.py:117
  68.5 0.4 collective-permute-done.25.refs_8_
  68.9 1.9 %shard_map.121 = (bf16[256,1536]{1,0:T(8,128)(2,1)}, bf16[256,1536]{1,0:T(8,128)(2,1)}, f32[1536]{0:T(1024)}) custom-call(bf16[256,1536]{1,0:T(8,128)(2,1)S(1)} %copy-done.2, bf16[256,1536]{1,0:T(8,128)(2,1)S(1)} %copy-done, f32[12,256]{1,0:T(8,128)S(1)} %bitcast.12, f32[16,128]{1,0:T(8,128)S(1)} %get-tuple-element.115.refs_2_.refs_4_.refs_3_, ...), custom_call_target="tpu_custom_call" | custom-call | flops 201326592 | bytes 6432768 | tf_op jit(solution)/shard_map/pallas_call | solution.py:117
  (47 shorter events, 1.5 us)
Async XLA Ops:
  0.6 2.9 %copy-start = (bf16[256,1536]{1,0:T(8,128)(2,1)S(1)}, bf16[256,1536]{1,0:T(8,128)(2,1)}, u32[]{:S(2)}) copy-start(bf16[256,1536]{1,0:T(8,128)(2,1)} %refs_1_.13) | copy-start | bytes 2359300
  0.6 2.9 %copy-start.2 = (bf16[256,1536]{1,0:T(8,128)(2,1)S(1)}, bf16[256,1536]{1,0:T(8,128)(2,1)}, u32[]{:S(2)}) copy-start(bf16[256,1536]{1,0:T(8,128)(2,1)} %refs_0_.13) | copy-start | bytes 2359300
  0.7 2.9 %copy-start.4 = (f32[256,12]{0,1:T(8,128)S(1)}, f32[256,12]{0,1:T(8,128)}, u32[]{:S(2)}) copy-start(f32[256,12]{0,1:T(8,128)} %param.11) | copy-start | bytes 36868
  3.0 0.7 copy-start.6
  3.0 2.6 %collective-permute-start = (f32[392,128]{1,0:T(8,128)S(1)}, f32[392,128]{1,0:T(8,128)S(1)}, u32[]{:S(2)}, u32[]{:S(2)}) collective-permute-start(f32[392,128]{1,0:T(8,128)S(1)} %get-tuple-element.110), channel_id=1, source_target_pairs={{0,1},{1,0},{2,3},{3,2},{4,5},{5,4},{6,7},{7,6},{8,9},{9,8},{10,11... | collective-permute-start | bytes 602120 | tf_op jit(solution)/shard_map/ppermute | solution.py:497
  5.1 4.6 %copy-start.1 = (bf16[256,1536]{1,0:T(8,128)(2,1)S(1)}, bf16[256,1536]{1,0:T(8,128)(2,1)}, u32[]{:S(2)}) copy-start(bf16[256,1536]{1,0:T(8,128)(2,1)} %refs_0_.11) | copy-start | bytes 2359300
  5.1 3.2 %collective-permute-start.1 = (f32[392,128]{1,0:T(8,128)S(1)}, f32[392,128]{1,0:T(8,128)S(1)}, u32[]{:S(2)}, u32[]{:S(2)}) collective-permute-start(f32[392,128]{1,0:T(8,128)S(1)} %get-tuple-element.114), channel_id=1, source_target_pairs={{0,1},{1,0},{2,3},{3,2},{4,5},{5,4},{6,7},{7,6},{8,9},{9,8},{10,11... | collective-permute-start | bytes 602120 | tf_op jit(solution)/shard_map/ppermute | solution.py:497
  5.7 6.3 %collective-permute-start.2 = (f32[200,128]{1,0:T(8,128)S(1)}, f32[200,128]{1,0:T(8,128)S(1)}, u32[]{:S(2)}, u32[]{:S(2)}) collective-permute-start(f32[200,128]{1,0:T(8,128)S(1)} %get-tuple-element.121.refs_1_), channel_id=1, source_target_pairs={{0,2},{1,3},{2,0},{3,1},{4,6},{5,7},{6,4},{7,5},{8,10},{9,11},{10,... | collective-permute-start | bytes 307208 | tf_op jit(solution)/shard_map/ppermute | solution.py:497
  8.3 5.8 %collective-permute-start.3 = (f32[200,128]{1,0:T(8,128)S(1)}, f32[200,128]{1,0:T(8,128)S(1)}, u32[]{:S(2)}, u32[]{:S(2)}) collective-permute-start(f32[200,128]{1,0:T(8,128)S(1)} %get-tuple-element.123.refs_1_), channel_id=1, source_target_pairs={{0,2},{1,3},{2,0},{3,1},{4,6},{5,7},{6,4},{7,5},{8,10},{9,11},{10,... | collective-permute-start | bytes 307208 | tf_op jit(solution)/shard_map/ppermute | solution.py:497
  12.0 7.1 %collective-permute-start.4 = (f32[200,128]{1,0:T(8,128)S(1)}, f32[200,128]{1,0:T(8,128)S(1)}, u32[]{:S(2)}, u32[]{:S(2)}) collective-permute-start(f32[200,128]{1,0:T(8,128)S(1)} %shard_map.99.refs_3_), channel_id=1, source_target_pairs={{0,4},{1,5},{2,6},{3,7},{4,8},{5,9},{6,10},{7,11},{8,12},{9,13},{1... | collective-permute-start | bytes 307208 | tf_op jit(solution)/shard_map/ppermute | solution.py:502
  14.2 6.8 %collective-permute-start.6 = (f32[200,128]{1,0:T(8,128)S(1)}, f32[200,128]{1,0:T(8,128)S(1)}, u32[]{:S(2)}, u32[]{:S(2)}) collective-permute-start(f32[200,128]{1,0:T(8,128)S(1)} %shard_map.100), channel_id=1, source_target_pairs={{0,4},{1,5},{2,6},{3,7},{4,8},{5,9},{6,10},{7,11},{8,12},{9,13},{1... | collective-permute-start | bytes 307208 | tf_op jit(solution)/shard_map/ppermute | solution.py:502
  19.1 7.3 %collective-permute-start.5 = (f32[200,128]{1,0:T(8,128)S(1)}, f32[200,128]{1,0:T(8,128)S(1)}, u32[]{:S(2)}, u32[]{:S(2)}) collective-permute-start(f32[200,128]{1,0:T(8,128)S(1)} %collective-permute-done.4.refs_3_), channel_id=1, source_target_pairs={{0,4},{1,5},{2,6},{3,7},{4,8},{5,9},{6,10},{7,11},{8,12},{9,13},{1... | collective-permute-start | bytes 307208 | tf_op jit(solution)/shard_map/ppermute | solution.py:502
  21.0 7.7 %collective-permute-start.7 = (f32[200,128]{1,0:T(8,128)S(1)}, f32[200,128]{1,0:T(8,128)S(1)}, u32[]{:S(2)}, u32[]{:S(2)}) collective-permute-start(f32[200,128]{1,0:T(8,128)S(1)} %collective-permute-done.6.refs_3_), channel_id=1, source_target_pairs={{0,4},{1,5},{2,6},{3,7},{4,8},{5,9},{6,10},{7,11},{8,12},{9,13},{1... | collective-permute-start | bytes 307208 | tf_op jit(solution)/shard_map/ppermute | solution.py:502
  26.5 5.4 %collective-permute-start.8 = (f32[192,128]{1,0:T(8,128)S(1)}, f32[192,128]{1,0:T(8,128)S(1)}, u32[]{:S(2)}, u32[]{:S(2)}) collective-permute-start(f32[192,128]{1,0:T(8,128)S(1)} %get-tuple-element.133), channel_id=1, source_target_pairs={{0,2},{1,3},{2,0},{3,1},{4,6},{5,7},{6,4},{7,5},{8,10},{9,11},{10,... | collective-permute-start | bytes 294920 | tf_op jit(solution)/shard_map/ppermute | solution.py:497
  28.7 4.9 %copy-start.3 = (bf16[256,1536]{1,0:T(8,128)(2,1)S(1)}, bf16[256,1536]{1,0:T(8,128)(2,1)}, u32[]{:S(2)}) copy-start(bf16[256,1536]{1,0:T(8,128)(2,1)} %refs_1_.9) | copy-start | bytes 2359300
  28.7 4.7 %collective-permute-start.9 = (f32[192,128]{1,0:T(8,128)S(1)}, f32[192,128]{1,0:T(8,128)S(1)}, u32[]{:S(2)}, u32[]{:S(2)}) collective-permute-start(f32[192,128]{1,0:T(8,128)S(1)} %get-tuple-element.136), channel_id=1, source_target_pairs={{0,2},{1,3},{2,0},{3,1},{4,6},{5,7},{6,4},{7,5},{8,10},{9,11},{10,... | collective-permute-start | bytes 294920 | tf_op jit(solution)/shard_map/ppermute | solution.py:497
  31.9 1.6 %collective-permute-start.10 = (f32[384,128]{1,0:T(8,128)S(1)}, f32[384,128]{1,0:T(8,128)S(1)}, u32[]{:S(2)}, u32[]{:S(2)}) collective-permute-start(f32[384,128]{1,0:T(8,128)S(1)} %get-tuple-element.140), channel_id=1, source_target_pairs={{0,1},{1,0},{2,3},{3,2},{4,5},{5,4},{6,7},{7,6},{8,9},{9,8},{10,11... | collective-permute-start | bytes 589832 | tf_op jit(solution)/shard_map/ppermute | solution.py:497
  33.4 0.7 copy-start.5
  33.5 1.5 %collective-permute-start.11 = (f32[384,128]{1,0:T(8,128)S(1)}, f32[384,128]{1,0:T(8,128)S(1)}, u32[]{:S(2)}, u32[]{:S(2)}) collective-permute-start(f32[384,128]{1,0:T(8,128)S(1)} %get-tuple-element.144), channel_id=1, source_target_pairs={{0,1},{1,0},{2,3},{3,2},{4,5},{5,4},{6,7},{7,6},{8,9},{9,8},{10,11... | collective-permute-start | bytes 589832 | tf_op jit(solution)/shard_map/ppermute | solution.py:497
  35.8 3.7 %collective-permute-start.12 = (f32[8,256]{1,0:T(8,128)S(1)}, f32[8,256]{1,0:T(8,128)S(1)}, u32[]{:S(2)}, u32[]{:S(2)}) collective-permute-start(f32[8,256]{1,0:T(8,128)S(1)} %get-tuple-element.148), channel_id=1, source_target_pairs={{0,16},{16,0},{1,17},{17,1},{2,18},{18,2},{3,19},{19,3},{4,20},{20... | collective-permute-start | bytes 24584 | tf_op jit(solution)/shard_map/ppermute | solution.py:497
  40.3 1.5 %collective-permute-start.13 = (f32[400,128]{1,0:T(8,128)S(1)}, f32[400,128]{1,0:T(8,128)S(1)}, u32[]{:S(2)}, u32[]{:S(2)}) collective-permute-start(f32[400,128]{1,0:T(8,128)S(1)} %get-tuple-element.154), channel_id=1, source_target_pairs={{0,1},{1,0},{2,3},{3,2},{4,5},{5,4},{6,7},{7,6},{8,9},{9,8},{10,11... | collective-permute-start | bytes 614408 | tf_op jit(solution)/shard_map/ppermute | solution.py:497
  41.3 1.9 %collective-permute-start.14 = (f32[400,128]{1,0:T(8,128)S(1)}, f32[400,128]{1,0:T(8,128)S(1)}, u32[]{:S(2)}, u32[]{:S(2)}) collective-permute-start(f32[400,128]{1,0:T(8,128)S(1)} %get-tuple-element.160), channel_id=1, source_target_pairs={{0,1},{1,0},{2,3},{3,2},{4,5},{5,4},{6,7},{7,6},{8,9},{9,8},{10,11... | collective-permute-start | bytes 614408 | tf_op jit(solution)/shard_map/ppermute | solution.py:497
  41.9 5.8 %collective-permute-start.15 = (f32[200,128]{1,0:T(8,128)S(1)}, f32[200,128]{1,0:T(8,128)S(1)}, u32[]{:S(2)}, u32[]{:S(2)}) collective-permute-start(f32[200,128]{1,0:T(8,128)S(1)} %get-tuple-element.169.refs_1_), channel_id=1, source_target_pairs={{0,2},{1,3},{2,0},{3,1},{4,6},{5,7},{6,4},{7,5},{8,10},{9,11},{10,... | collective-permute-start | bytes 307208 | tf_op jit(solution)/shard_map/ppermute | solution.py:497
  43.3 5.8 %collective-permute-start.16 = (f32[200,128]{1,0:T(8,128)S(1)}, f32[200,128]{1,0:T(8,128)S(1)}, u32[]{:S(2)}, u32[]{:S(2)}) collective-permute-start(f32[200,128]{1,0:T(8,128)S(1)} %get-tuple-element.171.refs_1_), channel_id=1, source_target_pairs={{0,2},{1,3},{2,0},{3,1},{4,6},{5,7},{6,4},{7,5},{8,10},{9,11},{10,... | collective-permute-start | bytes 307208 | tf_op jit(solution)/shard_map/ppermute | solution.py:497
  44.3 4.5 %collective-permute-start.17 = (f32[16,128]{1,0:T(8,128)S(1)}, f32[16,128]{1,0:T(8,128)S(1)}, u32[]{:S(2)}, u32[]{:S(2)}) collective-permute-start(f32[16,128]{1,0:T(8,128)S(1)} %get-tuple-element.172.refs_3_), channel_id=1, source_target_pairs={{0,8},{1,9},{2,10},{3,11},{4,12},{5,13},{6,14},{7,15},{8,0},{9,1},... | collective-permute-start | bytes 24584 | tf_op jit(solution)/shard_map/ppermute | solution.py:497
  49.1 8.6 %collective-permute-start.20 = (f32[216,128]{1,0:T(8,128)S(1)}, f32[216,128]{1,0:T(8,128)S(1)}, u32[]{:S(2)}, u32[]{:S(2)}) collective-permute-start(f32[216,128]{1,0:T(8,128)S(1)} %shard_map.114.refs_5_), channel_id=1, source_target_pairs={{0,12},{1,13},{2,14},{3,15},{4,0},{5,1},{6,2},{7,3},{8,4},{9,5},{1... | collective-permute-start | bytes 331784 | tf_op jit(solution)/shard_map/ppermute | solution.py:502
  49.3 6.3 %collective-permute-start.18 = (f32[200,128]{1,0:T(8,128)S(1)}, f32[200,128]{1,0:T(8,128)S(1)}, u32[]{:S(2)}, u32[]{:S(2)}) collective-permute-start(f32[200,128]{1,0:T(8,128)S(1)} %shard_map.113.refs_5_), channel_id=1, source_target_pairs={{0,12},{1,13},{2,14},{3,15},{4,0},{5,1},{6,2},{7,3},{8,4},{9,5},{1... | collective-permute-start | bytes 307208 | tf_op jit(solution)/shard_map/ppermute | solution.py:502
  55.6 5.2 %collective-permute-start.19 = (f32[200,128]{1,0:T(8,128)S(1)}, f32[200,128]{1,0:T(8,128)S(1)}, u32[]{:S(2)}, u32[]{:S(2)}) collective-permute-start(f32[200,128]{1,0:T(8,128)S(1)} %collective-permute-done.18.refs_3_), channel_id=1, source_target_pairs={{0,12},{1,13},{2,14},{3,15},{4,0},{5,1},{6,2},{7,3},{8,4},{9,5},{1... | collective-permute-start | bytes 307208 | tf_op jit(solution)/shard_map/ppermute | solution.py:502
  57.7 4.7 %collective-permute-start.21 = (f32[216,128]{1,0:T(8,128)S(1)}, f32[216,128]{1,0:T(8,128)S(1)}, u32[]{:S(2)}, u32[]{:S(2)}) collective-permute-start(f32[216,128]{1,0:T(8,128)S(1)} %collective-permute-done.20.refs_3_), channel_id=1, source_target_pairs={{0,12},{1,13},{2,14},{3,15},{4,0},{5,1},{6,2},{7,3},{8,4},{9,5},{1... | collective-permute-start | bytes 331784 | tf_op jit(solution)/shard_map/ppermute | solution.py:502
  60.9 4.7 %collective-permute-start.22 = (f32[192,128]{1,0:T(8,128)S(1)}, f32[192,128]{1,0:T(8,128)S(1)}, u32[]{:S(2)}, u32[]{:S(2)}) collective-permute-start(f32[192,128]{1,0:T(8,128)S(1)} %get-tuple-element.183), channel_id=1, source_target_pairs={{0,2},{1,3},{2,0},{3,1},{4,6},{5,7},{6,4},{7,5},{8,10},{9,11},{10,... | collective-permute-start | bytes 294920 | tf_op jit(solution)/shard_map/ppermute | solution.py:497
  62.5 4.8 %collective-permute-start.23 = (f32[208,128]{1,0:T(8,128)S(1)}, f32[208,128]{1,0:T(8,128)S(1)}, u32[]{:S(2)}, u32[]{:S(2)}) collective-permute-start(f32[208,128]{1,0:T(8,128)S(1)} %get-tuple-element.186), channel_id=1, source_target_pairs={{0,2},{1,3},{2,0},{3,1},{4,6},{5,7},{6,4},{7,5},{8,10},{9,11},{10,... | collective-permute-start | bytes 319496 | tf_op jit(solution)/shard_map/ppermute | solution.py:497
  65.7 1.8 %collective-permute-start.24 = (f32[384,128]{1,0:T(8,128)S(1)}, f32[384,128]{1,0:T(8,128)S(1)}, u32[]{:S(2)}, u32[]{:S(2)}) collective-permute-start(f32[384,128]{1,0:T(8,128)S(1)} %get-tuple-element.191), channel_id=1, source_target_pairs={{0,1},{1,0},{2,3},{3,2},{4,5},{5,4},{6,7},{7,6},{8,9},{9,8},{10,11... | collective-permute-start | bytes 589832 | tf_op jit(solution)/shard_map/ppermute | solution.py:497
  67.4 1.5 %collective-permute-start.25 = (f32[384,128]{1,0:T(8,128)S(1)}, f32[384,128]{1,0:T(8,128)S(1)}, u32[]{:S(2)}, u32[]{:S(2)}) collective-permute-start(f32[384,128]{1,0:T(8,128)S(1)} %get-tuple-element.196), channel_id=1, source_target_pairs={{0,1},{1,0},{2,3},{3,2},{4,5},{5,4},{6,7},{7,6},{8,9},{9,8},{10,11... | collective-permute-start | bytes 589832 | tf_op jit(solution)/shard_map/ppermute | solution.py:497

commit v4 on v3

--- a/solution.py
+++ b/solution.py
@@ -33,8 +33,8 @@
 
 
 def far_dot(a, state, contract_state):
-    high, low = two_parts(state)
-    return dot(a, high, 1, contract_state) + dot(a, low, 1, contract_state)
+    parts = jnp.concatenate(two_parts(state), axis=contract_state)
+    return dot(jnp.concatenate([a, a], axis=1), parts, 1, contract_state)
 
 
 def equal(a, b):
@@ -330,7 +330,7 @@
     return jnp.where(at >= other, jnp.exp(gap), 0.0)
 
 
-def local_kernel(s, queries, keys, values, log_decay, out, weights):
+def local_kernel(s, queries, keys, values, log_decay, gain, out, weights):
     for j, logs in enumerate(s.logs(log_decay)):
         columns, rows = decay_columns(logs), decay_rows(logs)
         for h in range(s.heads):
@@ -376,15 +376,15 @@
 
 
 def grad_kernel(
-    s, all_features, queries, out_grad, gain, log_decay, notes, attention, sums,
-    attn_grad, keep, send, out_tail, out_gain, back_terms,
+    s, all_features, queries, out_grad, gain, log_decay, notes, attention, *rest
 ):
+    sums, (attn_grad, keep, send, out_tail, out_gain, back_terms) = rest[:-6], rest[-6:]
     core, _, _ = place_bits(s.count, True)
     lower = core == 0
     logs = s.logs(log_decay)
     factors = [jnp.exp(total_rows(a)) for a in logs]
     decays = [jnp.exp(decay_columns(a)) for a in logs]
-    totals = sums[...] / all_features
+    totals = sum([a[...] for a in sums[1:]], sums[0][...]) / all_features
     spread = lambda row: jnp.broadcast_to(row, (C, C)).T
     inverses, slopes = [], []
     for j in range(s.blocks):
@@ -502,10 +502,23 @@
     return lax.ppermute(value, "seq", [(i, (i + step) % count) for i in range(count)])
 
 
+def pass_on(value, count, reverse, behind):
+    planes = count // PLANE
+    pairs = []
+    for source in range(count):
+        plane, place = divmod(source, PLANE)
+        if plane < behind:
+            target = source ^ 2
+        else:
+            target = (plane + 1 if plane < planes - 1 else behind) * PLANE + place
+        pair = (source, target)
+        pairs.append(tuple(count - 1 - a for a in pair) if reverse else pair)
+    return lax.ppermute(value, "seq", pairs)
+
+
 def scan_in(waves, parts, reverse, token, beside):
     bind = functools.partial
-    last = waves[-1]
-    gain_rows = lambda s: len(waves) * s.gains if reverse and s is last else 0
+    gain_rows = lambda s: len(waves) * s.gains if reverse and s.wave == 0 else 0
     received, chips, chip_received, local, gains, others = [], [], [], [], [], []
     for s, (keep, send, tail, gain) in zip(waves, parts):
         received.append(swap(send, "seq", 1))
@@ -525,11 +538,11 @@
         chips.append(chip)
         chip_received.append(swap(chip[1], "seq", 2))
     if reverse:
-        bit = last.count // 2
+        bit = waves[0].count // 2
         while bit > PLANE:
             if others:
                 gains, others = [gains[0] + others[0]], []
-            others = [swap(gains[0], "seq", bit)]
+            others = [swap(gains[0], "seq", bit + 1)]
             bit //= 2
     planes, passed = [], []
     for i in range(len(waves) - 1):
@@ -555,9 +568,9 @@
         token, one = beside(token, i)
         local.append(one)
     passed = [list(after(token, one[0])) for one in passed]
-    for _ in range(waves[0].window - 1):
+    for w in range(1, waves[0].window):
         for i, s in enumerate(waves):
-            passed[i].append(next_plane(passed[i][-1], s.count, reverse))
+            passed[i].append(pass_on(passed[i][-1], s.count, reverse, w))
     spreads, spread_received = [], []
     for i, s in enumerate(waves):
         (keep,) = after(token, chips[i][0])
@@ -595,7 +608,7 @@
         )
         token = entry[0]
         entries.append((entry[0], swap(entry[1], "seq", 1)))
-    return entries, local, token, [spreads[-1][-1], spread_received[-1]]
+    return entries, local, token, [spreads[0][-1], spread_received[0]]
 
 
 def per_device(queries, keys, values, out_grad, log_decay, norm_gain, doc_ids):
@@ -611,8 +624,8 @@
     states = []
     far = [pltpu.with_memory_space_constraint(a, pltpu.HBM) for a in (keys, values, log_decay, doc_ids)]
     for s in waves:
-        groups = max(g for g in (2, 1) if s.heads % g == 0)
-        given, options = (keys, values, log_decay, doc_ids), {}
+        groups = max(g for g in (3, 2, 1) if s.heads % g == 0)
+        given = (keys, values, log_decay, doc_ids)
         spaces = [pltpu.VMEM, pltpu.VMEM, pltpu.VMEM, pltpu.SMEM]
         scratch = []
         if not states:
@@ -656,6 +669,7 @@
             keys,
             values,
             held,
+            gain,
             flops=2 * unit,
         )
         return local[0], local
@@ -682,13 +696,13 @@
         token = attention
         attentions.append(attention)
         sums = [total]
-    sums = sums[0]
     if dp & (dp - 1):
-        sums = lax.psum(sums, "dp")
+        sums = [lax.psum(sums[0], "dp")]
     else:
         bit = 1
         while bit < dp:
-            sums = sums + swap(sums, "dp", bit)
+            total = sum(sums[1:], sums[0])
+            sums = [total, swap(total, "dp", bit)]
             bit *= 2
     grads = []
     for i, s in enumerate(waves):
@@ -709,7 +723,7 @@
             held,
             states[i][2],
             attentions[i],
-            sums,
+            *sums,
             flops=unit,
         )
         token = grad[0]

time: 70.9 us -> 68.2 us (0.962)
  waiting for transfers between devices: 27.2 us -> 23.1 us
  starting transfers between devices: 24.1 us -> 26.2 us
    ppermute x8 -> x4, waiting for transfers between devices: 14.3 us -> 5.17 us  [next_plane(): lax.ppermute(value, 'seq', [(i, (i + step) % count) for i in range(count)])]
    ppermute x0 -> x4, waiting for transfers between devices: none -> 6.49 us  [pass_on(): return lax.ppermute(value, 'seq', pairs)]
    ppermute x0 -> x4, starting transfers between devices: none -> 3.67 us  [pass_on(): return lax.ppermute(value, 'seq', pairs)]
    ppermute x8 -> x4, starting transfers between devices: 8.32 us -> 5.76 us  [next_plane(): lax.ppermute(value, 'seq', [(i, (i + step) % count) for i in range(count)])]
    ppermute x18, waiting for transfers between devices: 12.9 us -> 11.5 us  [swap(): return lax.ppermute(value, axis, [(i, i ^ bit) for i in range(count)])]
    ppermute x18, starting transfers between devices: 15.8 us -> 16.8 us  [swap(): return lax.ppermute(value, axis, [(i, i ^ bit) for i in range(count)])]
  transfers between devices with their start and end apart: 26 -> 26, of which waited for: 16 -> 15; matrix products, arithmetic and copies ran while one was open for 0% -> 0% of each run, Pallas kernels for 17% -> 17%
where the time goes in v4:
time: 68.2 us; the launch traced here: 68 us
  starting transfers between devices  26.2 us (38%)
  waiting for transfers between devices  23.1 us (34%)
  Pallas kernels  17.6 us (26%)
  between operations  0.89 us (1%)
    pallas_call x28, Pallas kernels, call(): pl.pallas_call(lambda *refs: kernel(*refs[:given], *refs[given + len(deps...  17.6 us
    ppermute x18, starting transfers between devices, swap(): return lax.ppermute(value, axis, [(i, i ^ bit) for i in range(count)])  16.8 us
    ppermute x18, waiting for transfers between devices, swap(): return lax.ppermute(value, axis, [(i, i ^ bit) for i in range(count)])  11.5 us
    ppermute x4, waiting for transfers between devices, pass_on(): return lax.ppermute(value, 'seq', pairs)  6.49 us
    ppermute x4, starting transfers between devices, next_plane(): lax.ppermute(value, 'seq', [(i, (i + step) % count) for i in range(count)])  5.76 us
    ppermute x4, waiting for transfers between devices, next_plane(): lax.ppermute(value, 'seq', [(i, (i + step) % count) for i in range(count)])  5.17 us
    ppermute x4, starting transfers between devices, pass_on(): return lax.ppermute(value, 'seq', pairs)  3.67 us
  transfers between devices with their start and end apart: 26, of which 15 were waited for; matrix products, arithmetic and copies ran while one was open for 0% of the time, Pallas kernels for 17%

profile of v4, /device:TPU:0, one launch (start us, length us, event | category | flops | bytes accessed | tf_op | source)
XLA Modules:
  0.0 68.0 jit_solution(5184610168925822256)
XLA Ops:
  0.7 2.5 %shard_map.94 = (f32[384,128]{1,0:T(8,128)S(1)}, f32[392,128]{1,0:T(8,128)S(1)}, f32[16,128]{1,0:T(8,128)S(1)}, f32[768,128]{1,0:T(8,128)S(1)}) custom-call(bf16[256,1536]{1,0:T(8,128)(2,1)} %refs_0_.13, bf16[256,1536]{1,0:T(8,128)(2,1)} %refs_1_.13, f32[12,256]{1,0:T(8,128)} %bitcast.1, s32[2]{0:T(128)} %refs_3_.3), custom_call_target="tpu_custom_call" | custom-call | flops 50331648 | bytes 2383880 | tf_op jit(solution)/shard_map/pallas_call | solution.py:117
  3.1 0.5 collective-permute-start
  3.7 0.1 copy-done.6
  3.8 1.4 %shard_map.95 = (f32[384,128]{1,0:T(8,128)S(1)}, f32[392,128]{1,0:T(8,128)S(1)}, f32[16,128]{1,0:T(8,128)S(1)}, f32[768,128]{1,0:T(8,128)S(1)}) custom-call(bf16[256,1536]{1,0:T(8,128)(2,1)S(1)} %copy-done.2, bf16[256,1536]{1,0:T(8,128)(2,1)S(1)} %copy-done, f32[12,256]{1,0:T(8,128)S(1)} %bitcast.2, s32[2]{0:T(128)S(1)} %copy-done.6), custom_call_target="tpu_custom_call" | custom-call | flops 50331648 | bytes 2383880 | tf_op jit(solution)/shard_map/pallas_call | solution.py:117
  5.2 0.5 collective-permute-start.1
  5.8 2.6 %collective-permute-start.2 = (f32[200,128]{1,0:T(8,128)S(1)}, f32[200,128]{1,0:T(8,128)S(1)}, u32[]{:S(2)}, u32[]{:S(2)}) collective-permute-start(f32[200,128]{1,0:T(8,128)S(1)} %get-tuple-element.121.refs_1_), channel_id=1, source_target_pairs={{0,2},{1,3},{2,0},{3,1},{4,6},{5,7},{6,4},{7,5},{8,10},{9,11},{10,... | collective-permute-start | bytes 307208 | tf_op jit(solution)/shard_map/ppermute | solution.py:497
  8.4 1.4 %collective-permute-start.3 = (f32[200,128]{1,0:T(8,128)S(1)}, f32[200,128]{1,0:T(8,128)S(1)}, u32[]{:S(2)}, u32[]{:S(2)}) collective-permute-start(f32[200,128]{1,0:T(8,128)S(1)} %get-tuple-element.123.refs_1_), channel_id=1, source_target_pairs={{0,2},{1,3},{2,0},{3,1},{4,6},{5,7},{6,4},{7,5},{8,10},{9,11},{10,... | collective-permute-start | bytes 307208 | tf_op jit(solution)/shard_map/ppermute | solution.py:497
  9.8 2.3 %shard_map.98 = (f32[256,768]{1,0:T(8,128)S(1)}, bf16[1536,128]{1,0:T(8,128)(2,1)S(1)}) custom-call(bf16[256,1536]{1,0:T(8,128)(2,1)S(1)} %copy-done.1, bf16[256,1536]{1,0:T(8,128)(2,1)S(1)} %copy-done.2, bf16[256,1536]{1,0:T(8,128)(2,1)S(1)} %copy-done, f32[12,256]{1,0:T(8,128)S(1)} %bitcast.3, f32[1536]{0:T(1024)S(1)} %copy-done.5), custom_call_target="tpu_custom_call" | custom-call | flops 100663296 | bytes 3557376 | tf_op jit(solution)/shard_map/pallas_call | solution.py:117
  12.1 2.1 %collective-permute-start.4 = (f32[200,128]{1,0:T(8,128)S(1)}, f32[200,128]{1,0:T(8,128)S(1)}, u32[]{:S(2)}, u32[]{:S(2)}) collective-permute-start(f32[200,128]{1,0:T(8,128)S(1)} %shard_map.99.refs_3_), channel_id=1, source_target_pairs={{0,4},{1,5},{2,6},{3,7},{4,8},{5,9},{6,10},{7,11},{8,12},{9,13},{1... | collective-permute-start | bytes 307208 | tf_op jit(solution)/shard_map/ppermute | solution.py:502
  14.3 1.7 %collective-permute-start.6 = (f32[200,128]{1,0:T(8,128)S(1)}, f32[200,128]{1,0:T(8,128)S(1)}, u32[]{:S(2)}, u32[]{:S(2)}) collective-permute-start(f32[200,128]{1,0:T(8,128)S(1)} %shard_map.100), channel_id=1, source_target_pairs={{0,4},{1,5},{2,6},{3,7},{4,8},{5,9},{6,10},{7,11},{8,12},{9,13},{1... | collective-permute-start | bytes 307208 | tf_op jit(solution)/shard_map/ppermute | solution.py:502
  16.0 2.3 %shard_map.101 = (f32[256,768]{1,0:T(8,128)S(1)}, bf16[1536,128]{1,0:T(8,128)(2,1)S(1)}) custom-call(bf16[256,1536]{1,0:T(8,128)(2,1)S(1)} %copy-done.1, bf16[256,1536]{1,0:T(8,128)(2,1)S(1)} %copy-done.2, bf16[256,1536]{1,0:T(8,128)(2,1)S(1)} %copy-done, f32[12,256]{1,0:T(8,128)S(1)} %bitcast.4, f32[1536]{0:T(1024)S(1)} %copy-done.5), custom_call_target="tpu_custom_call" | custom-call | flops 100663296 | bytes 3557376 | tf_op jit(solution)/shard_map/pallas_call | solution.py:117
  18.3 0.9 %collective-permute-done.4.refs_3_ = f32[200,128]{1,0:T(8,128)S(1)} collective-permute-done((f32[200,128]{1,0:T(8,128)S(1)}, f32[200,128]{1,0:T(8,128)S(1)}, u32[]{:S(2)}, u32[]{:S(2)}) %collective-permute-start.4) | collective-permute-done | bytes 102432 | tf_op jit(solution)/shard_map/ppermute | solution.py:502
  19.2 1.9 %collective-permute-start.5 = (f32[200,128]{1,0:T(8,128)S(1)}, f32[200,128]{1,0:T(8,128)S(1)}, u32[]{:S(2)}, u32[]{:S(2)}) collective-permute-start(f32[200,128]{1,0:T(8,128)S(1)} %collective-permute-done.4.refs_3_), channel_id=1, source_target_pairs={{0,2},{1,3},{2,0},{3,1},{4,8},{5,9},{6,10},{7,11},{8,12},{9,13},{1... | collective-permute-start | bytes 307208 | tf_op jit(solution)/shard_map/ppermute | solution.py:516
  21.2 1.6 %collective-permute-start.7 = (f32[200,128]{1,0:T(8,128)S(1)}, f32[200,128]{1,0:T(8,128)S(1)}, u32[]{:S(2)}, u32[]{:S(2)}) collective-permute-start(f32[200,128]{1,0:T(8,128)S(1)} %collective-permute-done.6.refs_3_), channel_id=1, source_target_pairs={{0,2},{1,3},{2,0},{3,1},{4,8},{5,9},{6,10},{7,11},{8,12},{9,13},{1... | collective-permute-start | bytes 307208 | tf_op jit(solution)/shard_map/ppermute | solution.py:516
  22.8 1.9 %collective-permute-done.5.refs_4_ = f32[200,128]{1,0:T(8,128)S(1)} collective-permute-done((f32[200,128]{1,0:T(8,128)S(1)}, f32[200,128]{1,0:T(8,128)S(1)}, u32[]{:S(2)}, u32[]{:S(2)}) %collective-permute-start.5) | collective-permute-done | bytes 102432 | tf_op jit(solution)/shard_map/ppermute | solution.py:516
  24.8 2.2 %collective-permute-start.8 = (f32[192,128]{1,0:T(8,128)S(1)}, f32[192,128]{1,0:T(8,128)S(1)}, u32[]{:S(2)}, u32[]{:S(2)}) collective-permute-start(f32[192,128]{1,0:T(8,128)S(1)} %get-tuple-element.133), channel_id=1, source_target_pairs={{0,2},{1,3},{2,0},{3,1},{4,6},{5,7},{6,4},{7,5},{8,10},{9,11},{10,... | collective-permute-start | bytes 294920 | tf_op jit(solution)/shard_map/ppermute | solution.py:497
  27.0 2.1 %collective-permute-start.9 = (f32[192,128]{1,0:T(8,128)S(1)}, f32[192,128]{1,0:T(8,128)S(1)}, u32[]{:S(2)}, u32[]{:S(2)}) collective-permute-start(f32[192,128]{1,0:T(8,128)S(1)} %get-tuple-element.136), channel_id=1, source_target_pairs={{0,2},{1,3},{2,0},{3,1},{4,6},{5,7},{6,4},{7,5},{8,10},{9,11},{10,... | collective-permute-start | bytes 294920 | tf_op jit(solution)/shard_map/ppermute | solution.py:497
  29.2 1.0 %collective-permute-done.8.refs_1_ = f32[192,128]{1,0:T(8,128)S(1)} collective-permute-done((f32[192,128]{1,0:T(8,128)S(1)}, f32[192,128]{1,0:T(8,128)S(1)}, u32[]{:S(2)}, u32[]{:S(2)}) %collective-permute-start.8) | collective-permute-done | bytes 98336 | tf_op jit(solution)/shard_map/ppermute | solution.py:497
  30.3 1.4 %collective-permute-done.9.refs_1_ = f32[192,128]{1,0:T(8,128)S(1)} collective-permute-done((f32[192,128]{1,0:T(8,128)S(1)}, f32[192,128]{1,0:T(8,128)S(1)}, u32[]{:S(2)}, u32[]{:S(2)}) %collective-permute-start.9) | collective-permute-done | bytes 98336 | tf_op jit(solution)/shard_map/ppermute | solution.py:497
  31.8 0.1 shard_map.105
  31.9 0.7 %shard_map.106 = (f32[256,768]{1,0:T(8,128)S(1)}, f32[8,256]{1,0:T(8,128)S(1)}) custom-call(bf16[256,1536]{1,0:T(8,128)(2,1)S(1)} %copy-done.1, bf16[256,1536]{1,0:T(8,128)(2,1)S(1)} %copy-done.3, f32[1536]{0:T(1024)S(1)} %copy-done.5, f32[12,256]{1,0:T(8,128)S(1)} %bitcast.5, f32[16,128]{1,0:T(8,128)S(1)} %get-tuple-element.111.refs_2_.refs_4_.refs_3_, ...), custom_call_target="tpu_custom_call" | custom-call | flops 100663296 | bytes 3966976 | tf_op jit(solution)/shard_map/pallas_call | solution.py:117
  32.7 0.7 collective-permute-done.11.refs_8_
  33.4 0.8 %shard_map.107 = (f32[256,768]{1,0:T(8,128)S(1)}, f32[8,256]{1,0:T(8,128)S(1)}) custom-call(bf16[256,1536]{1,0:T(8,128)(2,1)S(1)} %copy-done.1, bf16[256,1536]{1,0:T(8,128)(2,1)S(1)} %copy-done.3, f32[1536]{0:T(1024)S(1)} %copy-done.5, f32[12,256]{1,0:T(8,128)S(1)} %bitcast.6, f32[16,128]{1,0:T(8,128)S(1)} %get-tuple-element.115.refs_2_.refs_4_.refs_3_, ...), custom_call_target="tpu_custom_call" | custom-call | flops 100663296 | bytes 3975168 | tf_op jit(solution)/shard_map/pallas_call | solution.py:117
  34.1 2.1 %collective-permute-start.12 = (f32[8,256]{1,0:T(8,128)S(1)}, f32[8,256]{1,0:T(8,128)S(1)}, u32[]{:S(2)}, u32[]{:S(2)}) collective-permute-start(f32[8,256]{1,0:T(8,128)S(1)} %get-tuple-element.148.refs_6_), channel_id=1, source_target_pairs={{0,16},{16,0},{1,17},{17,1},{2,18},{18,2},{3,19},{19,3},{4,20},{20... | collective-permute-start | bytes 24584 | tf_op jit(solution)/shard_map/ppermute | solution.py:497
  36.2 1.6 %collective-permute-done.12.refs_7_ = f32[8,256]{1,0:T(8,128)S(1)} collective-permute-done((f32[8,256]{1,0:T(8,128)S(1)}, f32[8,256]{1,0:T(8,128)S(1)}, u32[]{:S(2)}, u32[]{:S(2)}) %collective-permute-start.12) | collective-permute-done | bytes 8224 | tf_op jit(solution)/shard_map/ppermute | solution.py:497
  37.9 0.8 %shard_map.108 = (bf16[256,768]{1,0:T(8,128)(2,1)S(1)}, f32[384,128]{1,0:T(8,128)S(1)}, f32[400,128]{1,0:T(8,128)S(1)}, f32[8,128]{1,0:T(8,128)S(1)}, f32[8,128]{1,0:T(8,128)S(1)}, /*index=5*/f32[768,128]{1,0:T(8,128)S(1)}) custom-call(bf16[256,1536]{1,0:T(8,128)(2,1)S(1)} %copy-done.1, bf16[256,1536]{1,0:T(8,128)(2,1)S(1)} %copy-done.3, ...), custom_call_target="tpu_custom_call" | custom-call | flops 50331648 | bytes 3598336 | tf_op jit(solution)/shard_map/pallas_call | solution.py:117
  38.8 0.8 %shard_map.109 = (bf16[256,768]{1,0:T(8,128)(2,1)S(1)}, f32[384,128]{1,0:T(8,128)S(1)}, f32[400,128]{1,0:T(8,128)S(1)}, f32[8,128]{1,0:T(8,128)S(1)}, f32[8,128]{1,0:T(8,128)S(1)}, /*index=5*/f32[768,128]{1,0:T(8,128)S(1)}) custom-call(bf16[256,1536]{1,0:T(8,128)(2,1)S(1)} %copy-done.1, bf16[256,1536]{1,0:T(8,128)(2,1)S(1)} %copy-done.3, ...), custom_call_target="tpu_custom_call" | custom-call | flops 50331648 | bytes 3598336 | tf_op jit(solution)/shard_map/pallas_call | solution.py:117
  39.6 0.6 collective-permute-start.14
  40.3 2.1 %collective-permute-start.15 = (f32[200,128]{1,0:T(8,128)S(1)}, f32[200,128]{1,0:T(8,128)S(1)}, u32[]{:S(2)}, u32[]{:S(2)}) collective-permute-start(f32[200,128]{1,0:T(8,128)S(1)} %get-tuple-element.169.refs_1_), channel_id=1, source_target_pairs={{0,2},{1,3},{2,0},{3,1},{4,6},{5,7},{6,4},{7,5},{8,10},{9,11},{10,... | collective-permute-start | bytes 307208 | tf_op jit(solution)/shard_map/ppermute | solution.py:497
  42.4 1.0 %collective-permute-start.17 = (f32[200,128]{1,0:T(8,128)S(1)}, f32[200,128]{1,0:T(8,128)S(1)}, u32[]{:S(2)}, u32[]{:S(2)}) collective-permute-start(f32[200,128]{1,0:T(8,128)S(1)} %get-tuple-element.172.refs_1_), channel_id=1, source_target_pairs={{0,2},{1,3},{2,0},{3,1},{4,6},{5,7},{6,4},{7,5},{8,10},{9,11},{10,... | collective-permute-start | bytes 307208 | tf_op jit(solution)/shard_map/ppermute | solution.py:497
  43.4 1.4 %shard_map.112 = (f32[256,768]{1,0:T(8,128)S(1)}, f32[256,768]{1,0:T(8,128)S(1)}) custom-call(bf16[256,1536]{1,0:T(8,128)(2,1)S(1)} %copy-done.1, bf16[256,1536]{1,0:T(8,128)(2,1)S(1)} %copy-done, f32[12,256]{1,0:T(8,128)S(1)} %bitcast.9, bf16[1536,128]{1,0:T(8,128)(2,1)S(1)} %get-tuple-element.166.refs_3_, bf16[256,768]{1,0:T(8,128)(2,1)S(1)} %get-tuple-element.149.refs_4_), custom_call_target="tpu_custom_call" | custom-call | flops 150994944 | bytes 3944448 | tf_op jit(solution)/shard_map/pallas_call | solution.py:117
  44.8 2.6 %collective-permute-done.16.refs_4_ = f32[16,128]{1,0:T(8,128)S(1)} collective-permute-done((f32[16,128]{1,0:T(8,128)S(1)}, f32[16,128]{1,0:T(8,128)S(1)}, u32[]{:S(2)}, u32[]{:S(2)}) %collective-permute-start.16) | collective-permute-done | bytes 8224 | tf_op jit(solution)/shard_map/ppermute | solution.py:497
  47.4 1.0 %collective-permute-start.18 = (f32[216,128]{1,0:T(8,128)S(1)}, f32[216,128]{1,0:T(8,128)S(1)}, u32[]{:S(2)}, u32[]{:S(2)}) collective-permute-start(f32[216,128]{1,0:T(8,128)S(1)} %shard_map.113.refs_3_.refs_5_), channel_id=1, source_target_pairs={{0,12},{1,13},{2,14},{3,15},{4,0},{5,1},{6,2},{7,3},{8,4},{9,5},{1... | collective-permute-start | bytes 331784 | tf_op jit(solution)/shard_map/ppermute | solution.py:502
  48.5 0.9 %collective-permute-start.20 = (f32[200,128]{1,0:T(8,128)S(1)}, f32[200,128]{1,0:T(8,128)S(1)}, u32[]{:S(2)}, u32[]{:S(2)}) collective-permute-start(f32[200,128]{1,0:T(8,128)S(1)} %shard_map.114), channel_id=1, source_target_pairs={{0,12},{1,13},{2,14},{3,15},{4,0},{5,1},{6,2},{7,3},{8,4},{9,5},{1... | collective-permute-start | bytes 307208 | tf_op jit(solution)/shard_map/ppermute | solution.py:502
  49.4 1.4 %shard_map.115 = (f32[256,768]{1,0:T(8,128)S(1)}, f32[256,768]{1,0:T(8,128)S(1)}) custom-call(bf16[256,1536]{1,0:T(8,128)(2,1)S(1)} %copy-done.1, bf16[256,1536]{1,0:T(8,128)(2,1)S(1)} %copy-done, f32[12,256]{1,0:T(8,128)S(1)} %bitcast.10, bf16[1536,128]{1,0:T(8,128)(2,1)S(1)} %get-tuple-element.174.refs_3_, bf16[256,768]{1,0:T(8,128)(2,1)S(1)} %get-tuple-element.151.refs_4_), custom_call_target="tpu_custom_call" | custom-call | flops 150994944 | bytes 3944448 | tf_op jit(solution)/shard_map/pallas_call | solution.py:117
  50.7 2.6 %collective-permute-done.18.refs_3_ = f32[216,128]{1,0:T(8,128)S(1)} collective-permute-done((f32[216,128]{1,0:T(8,128)S(1)}, f32[216,128]{1,0:T(8,128)S(1)}, u32[]{:S(2)}, u32[]{:S(2)}) %collective-permute-start.18) | collective-permute-done | bytes 110624 | tf_op jit(solution)/shard_map/ppermute | solution.py:502
  53.4 1.6 %collective-permute-done.20.refs_3_ = f32[200,128]{1,0:T(8,128)S(1)} collective-permute-done((f32[200,128]{1,0:T(8,128)S(1)}, f32[200,128]{1,0:T(8,128)S(1)}, u32[]{:S(2)}, u32[]{:S(2)}) %collective-permute-start.20) | collective-permute-done | bytes 102432 | tf_op jit(solution)/shard_map/ppermute | solution.py:502
  55.0 0.1 collective-permute-start.21
  55.1 3.8 %collective-permute-done.19.refs_4_ = f32[216,128]{1,0:T(8,128)S(1)} collective-permute-done((f32[216,128]{1,0:T(8,128)S(1)}, f32[216,128]{1,0:T(8,128)S(1)}, u32[]{:S(2)}, u32[]{:S(2)}) %collective-permute-start.19) | collective-permute-done | bytes 110624 | tf_op jit(solution)/shard_map/ppermute | solution.py:516
  59.0 0.3 collective-permute-start.22
  59.2 0.8 %collective-permute-done.21.refs_4_ = f32[200,128]{1,0:T(8,128)S(1)} collective-permute-done((f32[200,128]{1,0:T(8,128)S(1)}, f32[200,128]{1,0:T(8,128)S(1)}, u32[]{:S(2)}, u32[]{:S(2)}) %collective-permute-start.21) | collective-permute-done | bytes 102432 | tf_op jit(solution)/shard_map/ppermute | solution.py:516
  60.1 1.1 %collective-permute-start.23 = (f32[192,128]{1,0:T(8,128)S(1)}, f32[192,128]{1,0:T(8,128)S(1)}, u32[]{:S(2)}, u32[]{:S(2)}) collective-permute-start(f32[192,128]{1,0:T(8,128)S(1)} %get-tuple-element.186), channel_id=1, source_target_pairs={{0,2},{1,3},{2,0},{3,1},{4,6},{5,7},{6,4},{7,5},{8,10},{9,11},{10,... | collective-permute-start | bytes 294920 | tf_op jit(solution)/shard_map/ppermute | solution.py:497
  61.2 2.5 %collective-permute-done.22.refs_1_.refs_12_ = f32[208,128]{1,0:T(8,128)S(1)} collective-permute-done((f32[208,128]{1,0:T(8,128)S(1)}, f32[208,128]{1,0:T(8,128)S(1)}, u32[]{:S(2)}, u32[]{:S(2)}) %collective-permute-start.22) | collective-permute-done | bytes 106528 | tf_op jit(solution)/shard_map/ppermute | solution.py:497
  63.9 0.9 %collective-permute-done.23.refs_1_ = f32[192,128]{1,0:T(8,128)S(1)} collective-permute-done((f32[192,128]{1,0:T(8,128)S(1)}, f32[192,128]{1,0:T(8,128)S(1)}, u32[]{:S(2)}, u32[]{:S(2)}) %collective-permute-start.23) | collective-permute-done | bytes 98336 | tf_op jit(solution)/shard_map/ppermute | solution.py:497
  64.9 0.4 collective-permute-done.24.refs_8_
  65.3 0.8 %shard_map.120 = (bf16[256,768]{1,0:T(8,128)(2,1)S(1)}, bf16[256,768]{1,0:T(8,128)(2,1)S(1)}) custom-call(bf16[256,1536]{1,0:T(8,128)(2,1)S(1)} %copy-done.2, bf16[256,1536]{1,0:T(8,128)(2,1)S(1)} %copy-done, f32[12,256]{1,0:T(8,128)S(1)} %bitcast.11, f32[16,128]{1,0:T(8,128)S(1)} %get-tuple-element.111.refs_2_.refs_4_.refs_3_, ...), custom_call_target="tpu_custom_call" | custom-call | flops 201326592 | bytes 4739072 | tf_op jit(solution)/shard_map/pallas_call | solution.py:117
  66.1 0.2 collective-permute-done.25.refs_8_
  66.4 1.7 %shard_map.121 = (bf16[256,1536]{1,0:T(8,128)(2,1)}, bf16[256,1536]{1,0:T(8,128)(2,1)}, f32[1536]{0:T(1024)}) custom-call(bf16[256,1536]{1,0:T(8,128)(2,1)S(1)} %copy-done.2, bf16[256,1536]{1,0:T(8,128)(2,1)S(1)} %copy-done, f32[12,256]{1,0:T(8,128)S(1)} %bitcast.12, f32[16,128]{1,0:T(8,128)S(1)} %get-tuple-element.115.refs_2_.refs_4_.refs_3_, ...), custom_call_target="tpu_custom_call" | custom-call | flops 201326592 | bytes 6432768 | tf_op jit(solution)/shard_map/pallas_call | solution.py:117
  (46 shorter events, 1.3 us)
Async XLA Ops:
  0.6 3.0 %copy-start = (bf16[256,1536]{1,0:T(8,128)(2,1)S(1)}, bf16[256,1536]{1,0:T(8,128)(2,1)}, u32[]{:S(2)}) copy-start(bf16[256,1536]{1,0:T(8,128)(2,1)} %refs_1_.13) | copy-start | bytes 2359300
  0.6 3.0 %copy-start.2 = (bf16[256,1536]{1,0:T(8,128)(2,1)S(1)}, bf16[256,1536]{1,0:T(8,128)(2,1)}, u32[]{:S(2)}) copy-start(bf16[256,1536]{1,0:T(8,128)(2,1)} %refs_0_.13) | copy-start | bytes 2359300
  0.7 3.0 %copy-start.4 = (f32[256,12]{0,1:T(8,128)S(1)}, f32[256,12]{0,1:T(8,128)}, u32[]{:S(2)}) copy-start(f32[256,12]{0,1:T(8,128)} %param.11) | copy-start | bytes 36868
  3.1 0.7 copy-start.6
  3.1 2.6 %collective-permute-start = (f32[392,128]{1,0:T(8,128)S(1)}, f32[392,128]{1,0:T(8,128)S(1)}, u32[]{:S(2)}, u32[]{:S(2)}) collective-permute-start(f32[392,128]{1,0:T(8,128)S(1)} %get-tuple-element.110), channel_id=1, source_target_pairs={{0,1},{1,0},{2,3},{3,2},{4,5},{5,4},{6,7},{7,6},{8,9},{9,8},{10,11... | collective-permute-start | bytes 602120 | tf_op jit(solution)/shard_map/ppermute | solution.py:497
  5.2 4.6 %copy-start.1 = (bf16[256,1536]{1,0:T(8,128)(2,1)S(1)}, bf16[256,1536]{1,0:T(8,128)(2,1)}, u32[]{:S(2)}) copy-start(bf16[256,1536]{1,0:T(8,128)(2,1)} %refs_0_.11) | copy-start | bytes 2359300
  5.2 3.2 %collective-permute-start.1 = (f32[392,128]{1,0:T(8,128)S(1)}, f32[392,128]{1,0:T(8,128)S(1)}, u32[]{:S(2)}, u32[]{:S(2)}) collective-permute-start(f32[392,128]{1,0:T(8,128)S(1)} %get-tuple-element.114), channel_id=1, source_target_pairs={{0,1},{1,0},{2,3},{3,2},{4,5},{5,4},{6,7},{7,6},{8,9},{9,8},{10,11... | collective-permute-start | bytes 602120 | tf_op jit(solution)/shard_map/ppermute | solution.py:497
  5.8 6.3 %collective-permute-start.2 = (f32[200,128]{1,0:T(8,128)S(1)}, f32[200,128]{1,0:T(8,128)S(1)}, u32[]{:S(2)}, u32[]{:S(2)}) collective-permute-start(f32[200,128]{1,0:T(8,128)S(1)} %get-tuple-element.121.refs_1_), channel_id=1, source_target_pairs={{0,2},{1,3},{2,0},{3,1},{4,6},{5,7},{6,4},{7,5},{8,10},{9,11},{10,... | collective-permute-start | bytes 307208 | tf_op jit(solution)/shard_map/ppermute | solution.py:497
  8.4 1.4 %copy-start.5 = (f32[1536]{0:T(1024)S(1)}, f32[1536]{0:T(1024)}, u32[]{:S(2)}) copy-start(f32[1536]{0:T(1024)} %refs_2_.5) | copy-start | bytes 18436
  8.4 5.8 %collective-permute-start.3 = (f32[200,128]{1,0:T(8,128)S(1)}, f32[200,128]{1,0:T(8,128)S(1)}, u32[]{:S(2)}, u32[]{:S(2)}) collective-permute-start(f32[200,128]{1,0:T(8,128)S(1)} %get-tuple-element.123.refs_1_), channel_id=1, source_target_pairs={{0,2},{1,3},{2,0},{3,1},{4,6},{5,7},{6,4},{7,5},{8,10},{9,11},{10,... | collective-permute-start | bytes 307208 | tf_op jit(solution)/shard_map/ppermute | solution.py:497
  12.1 7.1 %collective-permute-start.4 = (f32[200,128]{1,0:T(8,128)S(1)}, f32[200,128]{1,0:T(8,128)S(1)}, u32[]{:S(2)}, u32[]{:S(2)}) collective-permute-start(f32[200,128]{1,0:T(8,128)S(1)} %shard_map.99.refs_3_), channel_id=1, source_target_pairs={{0,4},{1,5},{2,6},{3,7},{4,8},{5,9},{6,10},{7,11},{8,12},{9,13},{1... | collective-permute-start | bytes 307208 | tf_op jit(solution)/shard_map/ppermute | solution.py:502
  14.3 6.9 %collective-permute-start.6 = (f32[200,128]{1,0:T(8,128)S(1)}, f32[200,128]{1,0:T(8,128)S(1)}, u32[]{:S(2)}, u32[]{:S(2)}) collective-permute-start(f32[200,128]{1,0:T(8,128)S(1)} %shard_map.100), channel_id=1, source_target_pairs={{0,4},{1,5},{2,6},{3,7},{4,8},{5,9},{6,10},{7,11},{8,12},{9,13},{1... | collective-permute-start | bytes 307208 | tf_op jit(solution)/shard_map/ppermute | solution.py:502
  19.2 5.5 %collective-permute-start.5 = (f32[200,128]{1,0:T(8,128)S(1)}, f32[200,128]{1,0:T(8,128)S(1)}, u32[]{:S(2)}, u32[]{:S(2)}) collective-permute-start(f32[200,128]{1,0:T(8,128)S(1)} %collective-permute-done.4.refs_3_), channel_id=1, source_target_pairs={{0,2},{1,3},{2,0},{3,1},{4,8},{5,9},{6,10},{7,11},{8,12},{9,13},{1... | collective-permute-start | bytes 307208 | tf_op jit(solution)/shard_map/ppermute | solution.py:516
  21.2 5.8 %collective-permute-start.7 = (f32[200,128]{1,0:T(8,128)S(1)}, f32[200,128]{1,0:T(8,128)S(1)}, u32[]{:S(2)}, u32[]{:S(2)}) collective-permute-start(f32[200,128]{1,0:T(8,128)S(1)} %collective-permute-done.6.refs_3_), channel_id=1, source_target_pairs={{0,2},{1,3},{2,0},{3,1},{4,8},{5,9},{6,10},{7,11},{8,12},{9,13},{1... | collective-permute-start | bytes 307208 | tf_op jit(solution)/shard_map/ppermute | solution.py:516
  24.8 5.4 %collective-permute-start.8 = (f32[192,128]{1,0:T(8,128)S(1)}, f32[192,128]{1,0:T(8,128)S(1)}, u32[]{:S(2)}, u32[]{:S(2)}) collective-permute-start(f32[192,128]{1,0:T(8,128)S(1)} %get-tuple-element.133), channel_id=1, source_target_pairs={{0,2},{1,3},{2,0},{3,1},{4,6},{5,7},{6,4},{7,5},{8,10},{9,11},{10,... | collective-permute-start | bytes 294920 | tf_op jit(solution)/shard_map/ppermute | solution.py:497
  27.0 5.0 %copy-start.3 = (bf16[256,1536]{1,0:T(8,128)(2,1)S(1)}, bf16[256,1536]{1,0:T(8,128)(2,1)}, u32[]{:S(2)}) copy-start(bf16[256,1536]{1,0:T(8,128)(2,1)} %refs_1_.9) | copy-start | bytes 2359300
  27.0 4.7 %collective-permute-start.9 = (f32[192,128]{1,0:T(8,128)S(1)}, f32[192,128]{1,0:T(8,128)S(1)}, u32[]{:S(2)}, u32[]{:S(2)}) collective-permute-start(f32[192,128]{1,0:T(8,128)S(1)} %get-tuple-element.136), channel_id=1, source_target_pairs={{0,2},{1,3},{2,0},{3,1},{4,6},{5,7},{6,4},{7,5},{8,10},{9,11},{10,... | collective-permute-start | bytes 294920 | tf_op jit(solution)/shard_map/ppermute | solution.py:497
  30.2 1.7 %collective-permute-start.10 = (f32[384,128]{1,0:T(8,128)S(1)}, f32[384,128]{1,0:T(8,128)S(1)}, u32[]{:S(2)}, u32[]{:S(2)}) collective-permute-start(f32[384,128]{1,0:T(8,128)S(1)} %get-tuple-element.140), channel_id=1, source_target_pairs={{0,1},{1,0},{2,3},{3,2},{4,5},{5,4},{6,7},{7,6},{8,9},{9,8},{10,11... | collective-permute-start | bytes 589832 | tf_op jit(solution)/shard_map/ppermute | solution.py:497
  31.8 1.5 %collective-permute-start.11 = (f32[384,128]{1,0:T(8,128)S(1)}, f32[384,128]{1,0:T(8,128)S(1)}, u32[]{:S(2)}, u32[]{:S(2)}) collective-permute-start(f32[384,128]{1,0:T(8,128)S(1)} %get-tuple-element.144), channel_id=1, source_target_pairs={{0,1},{1,0},{2,3},{3,2},{4,5},{5,4},{6,7},{7,6},{8,9},{9,8},{10,11... | collective-permute-start | bytes 589832 | tf_op jit(solution)/shard_map/ppermute | solution.py:497
  34.1 3.7 %collective-permute-start.12 = (f32[8,256]{1,0:T(8,128)S(1)}, f32[8,256]{1,0:T(8,128)S(1)}, u32[]{:S(2)}, u32[]{:S(2)}) collective-permute-start(f32[8,256]{1,0:T(8,128)S(1)} %get-tuple-element.148.refs_6_), channel_id=1, source_target_pairs={{0,16},{16,0},{1,17},{17,1},{2,18},{18,2},{3,19},{19,3},{4,20},{20... | collective-permute-start | bytes 24584 | tf_op jit(solution)/shard_map/ppermute | solution.py:497
  38.7 1.5 %collective-permute-start.13 = (f32[400,128]{1,0:T(8,128)S(1)}, f32[400,128]{1,0:T(8,128)S(1)}, u32[]{:S(2)}, u32[]{:S(2)}) collective-permute-start(f32[400,128]{1,0:T(8,128)S(1)} %get-tuple-element.154), channel_id=1, source_target_pairs={{0,1},{1,0},{2,3},{3,2},{4,5},{5,4},{6,7},{7,6},{8,9},{9,8},{10,11... | collective-permute-start | bytes 614408 | tf_op jit(solution)/shard_map/ppermute | solution.py:497
  39.6 2.7 %collective-permute-start.14 = (f32[400,128]{1,0:T(8,128)S(1)}, f32[400,128]{1,0:T(8,128)S(1)}, u32[]{:S(2)}, u32[]{:S(2)}) collective-permute-start(f32[400,128]{1,0:T(8,128)S(1)} %get-tuple-element.160), channel_id=1, source_target_pairs={{0,1},{1,0},{2,3},{3,2},{4,5},{5,4},{6,7},{7,6},{8,9},{9,8},{10,11... | collective-permute-start | bytes 614408 | tf_op jit(solution)/shard_map/ppermute | solution.py:497
  40.3 7.1 %collective-permute-start.15 = (f32[200,128]{1,0:T(8,128)S(1)}, f32[200,128]{1,0:T(8,128)S(1)}, u32[]{:S(2)}, u32[]{:S(2)}) collective-permute-start(f32[200,128]{1,0:T(8,128)S(1)} %get-tuple-element.169.refs_1_), channel_id=1, source_target_pairs={{0,2},{1,3},{2,0},{3,1},{4,6},{5,7},{6,4},{7,5},{8,10},{9,11},{10,... | collective-permute-start | bytes 307208 | tf_op jit(solution)/shard_map/ppermute | solution.py:497
  42.4 6.0 %collective-permute-start.17 = (f32[200,128]{1,0:T(8,128)S(1)}, f32[200,128]{1,0:T(8,128)S(1)}, u32[]{:S(2)}, u32[]{:S(2)}) collective-permute-start(f32[200,128]{1,0:T(8,128)S(1)} %get-tuple-element.172.refs_1_), channel_id=1, source_target_pairs={{0,2},{1,3},{2,0},{3,1},{4,6},{5,7},{6,4},{7,5},{8,10},{9,11},{10,... | collective-permute-start | bytes 307208 | tf_op jit(solution)/shard_map/ppermute | solution.py:497
  43.4 4.0 %collective-permute-start.16 = (f32[16,128]{1,0:T(8,128)S(1)}, f32[16,128]{1,0:T(8,128)S(1)}, u32[]{:S(2)}, u32[]{:S(2)}) collective-permute-start(f32[16,128]{1,0:T(8,128)S(1)} %get-tuple-element.170.refs_3_), channel_id=1, source_target_pairs={{0,9},{1,8},{2,11},{3,10},{4,13},{5,12},{6,15},{7,14},{8,1},{9,0},... | collective-permute-start | bytes 24584 | tf_op jit(solution)/shard_map/ppermute | solution.py:497
  47.4 6.0 %collective-permute-start.18 = (f32[216,128]{1,0:T(8,128)S(1)}, f32[216,128]{1,0:T(8,128)S(1)}, u32[]{:S(2)}, u32[]{:S(2)}) collective-permute-start(f32[216,128]{1,0:T(8,128)S(1)} %shard_map.113.refs_3_.refs_5_), channel_id=1, source_target_pairs={{0,12},{1,13},{2,14},{3,15},{4,0},{5,1},{6,2},{7,3},{8,4},{9,5},{1... | collective-permute-start | bytes 331784 | tf_op jit(solution)/shard_map/ppermute | solution.py:502
  48.5 6.5 %collective-permute-start.20 = (f32[200,128]{1,0:T(8,128)S(1)}, f32[200,128]{1,0:T(8,128)S(1)}, u32[]{:S(2)}, u32[]{:S(2)}) collective-permute-start(f32[200,128]{1,0:T(8,128)S(1)} %shard_map.114), channel_id=1, source_target_pairs={{0,12},{1,13},{2,14},{3,15},{4,0},{5,1},{6,2},{7,3},{8,4},{9,5},{1... | collective-permute-start | bytes 307208 | tf_op jit(solution)/shard_map/ppermute | solution.py:502
  53.4 5.5 %collective-permute-start.19 = (f32[216,128]{1,0:T(8,128)S(1)}, f32[216,128]{1,0:T(8,128)S(1)}, u32[]{:S(2)}, u32[]{:S(2)}) collective-permute-start(f32[216,128]{1,0:T(8,128)S(1)} %collective-permute-done.18.refs_3_), channel_id=1, source_target_pairs={{15,13},{14,12},{13,15},{12,14},{11,7},{10,6},{9,5},{8,4},{7,3},{6... | collective-permute-start | bytes 331784 | tf_op jit(solution)/shard_map/ppermute | solution.py:516
  55.0 5.0 %collective-permute-start.21 = (f32[200,128]{1,0:T(8,128)S(1)}, f32[200,128]{1,0:T(8,128)S(1)}, u32[]{:S(2)}, u32[]{:S(2)}) collective-permute-start(f32[200,128]{1,0:T(8,128)S(1)} %collective-permute-done.20.refs_3_), channel_id=1, source_target_pairs={{15,13},{14,12},{13,15},{12,14},{11,7},{10,6},{9,5},{8,4},{7,3},{6... | collective-permute-start | bytes 307208 | tf_op jit(solution)/shard_map/ppermute | solution.py:516
  59.0 4.8 %collective-permute-start.22 = (f32[208,128]{1,0:T(8,128)S(1)}, f32[208,128]{1,0:T(8,128)S(1)}, u32[]{:S(2)}, u32[]{:S(2)}) collective-permute-start(f32[208,128]{1,0:T(8,128)S(1)} %get-tuple-element.183), channel_id=1, source_target_pairs={{0,2},{1,3},{2,0},{3,1},{4,6},{5,7},{6,4},{7,5},{8,10},{9,11},{10,... | collective-permute-start | bytes 319496 | tf_op jit(solution)/shard_map/ppermute | solution.py:497
  60.1 4.7 %collective-permute-start.23 = (f32[192,128]{1,0:T(8,128)S(1)}, f32[192,128]{1,0:T(8,128)S(1)}, u32[]{:S(2)}, u32[]{:S(2)}) collective-permute-start(f32[192,128]{1,0:T(8,128)S(1)} %get-tuple-element.186), channel_id=1, source_target_pairs={{0,2},{1,3},{2,0},{3,1},{4,6},{5,7},{6,4},{7,5},{8,10},{9,11},{10,... | collective-permute-start | bytes 294920 | tf_op jit(solution)/shard_map/ppermute | solution.py:497
  63.8 1.5 %collective-permute-start.24 = (f32[384,128]{1,0:T(8,128)S(1)}, f32[384,128]{1,0:T(8,128)S(1)}, u32[]{:S(2)}, u32[]{:S(2)}) collective-permute-start(f32[384,128]{1,0:T(8,128)S(1)} %get-tuple-element.191), channel_id=1, source_target_pairs={{0,1},{1,0},{2,3},{3,2},{4,5},{5,4},{6,7},{7,6},{8,9},{9,8},{10,11... | collective-permute-start | bytes 589832 | tf_op jit(solution)/shard_map/ppermute | solution.py:497
  64.9 1.5 %collective-permute-start.25 = (f32[384,128]{1,0:T(8,128)S(1)}, f32[384,128]{1,0:T(8,128)S(1)}, u32[]{:S(2)}, u32[]{:S(2)}) collective-permute-start(f32[384,128]{1,0:T(8,128)S(1)} %get-tuple-element.196), channel_id=1, source_target_pairs={{0,1},{1,0},{2,3},{3,2},{4,5},{5,4},{6,7},{7,6},{8,9},{9,8},{10,11... | collective-permute-start | bytes 589832 | tf_op jit(solution)/shard_map/ppermute | solution.py:497

commit v5 on v4

--- a/solution.py
+++ b/solution.py
@@ -14,15 +14,13 @@
 WAVES = (2, 1)
 F32 = jnp.float32
 BF16 = jnp.bfloat16
-HIGHEST = lax.Precision.HIGHEST
-
-
-def dot(a, b, contract_a, contract_b, precision=None):
+
+
+def dot(a, b, contract_a, contract_b):
     return lax.dot_general(
         a,
         b,
         (((contract_a,), (contract_b,)), ((), ())),
-        precision=precision,
         preferred_element_type=F32,
     )
 
@@ -53,18 +51,36 @@
     return row, column
 
 
+def sums_of(log_block, chosen, contract, log_first):
+    parts, left = [], log_block
+    for _ in range(3):
+        parts.append(left.astype(BF16))
+        left = left - parts[-1].astype(F32)
+    chosen = chosen.astype(BF16)
+    total = None
+    for some in (parts[2:], parts[:2]):
+        logs = jnp.concatenate(some, axis=1)
+        which = jnp.concatenate([chosen] * len(some), axis=contract)
+        if log_first:
+            one = dot(logs, which, 1, contract)
+        else:
+            one = dot(which, logs, contract, 1)
+        total = one if total is None else total + one
+    return total
+
+
 def decay_columns(log_block):
     row, column = triangle()
-    return dot((row >= column).astype(F32), log_block, 1, 1, HIGHEST)
+    return sums_of(log_block, (row >= column).astype(F32), 1, False)
 
 
 def decay_rows(log_block):
     row, column = triangle()
-    return dot(log_block, (row <= column).astype(F32), 1, 0, HIGHEST)
+    return sums_of(log_block, (row <= column).astype(F32), 0, True)
 
 
 def total_rows(log_block):
-    return dot(log_block, jnp.ones((C, C), F32), 1, 0, HIGHEST)
+    return sums_of(log_block, jnp.ones((C, C), F32), 0, True)
 
 
 class Sizes:
@@ -85,7 +101,8 @@
         self.gains = -(-self.heads // 8) * 8
         self.tail = -(-(self.heads + 2) // 8) * 8
         self.start, self.end = self.heads, self.heads + 1
-        self.notes = -(-(self.heads + 2 + self.blocks) // 8) * 8
+        self.factors = self.heads + 2 + self.blocks
+        self.notes = -(-(self.factors + self.blocks * self.heads) // 8) * 8
 
     def own(self, h):
         return slice(h * self.width, (h + 1) * self.width)
@@ -101,6 +118,10 @@
 
     def carry(self, j):
         return slice(self.heads + 2 + j, self.heads + 3 + j)
+
+    def factor(self, j, h):
+        row = self.factors + j * self.heads + h
+        return slice(row, row + 1)
 
     def logs(self, log_decay):
         return [
@@ -146,7 +167,9 @@
     send_ref[rows, :] = lax.select(first, high, low)
 
 
-def state_kernel(s, keys, values, log_decay, doc_ids, keep, send, notes, first_update, *near):
+def state_kernel(
+    s, keys, values, log_decay, doc_ids, keep, send, notes, cums, first_update, *near
+):
     each, waits, first = s.heads, [], s.first
     if near:
         near_keys, near_values, near_logs, near_ids, arrived, small = near
@@ -173,8 +196,12 @@
         keys, values, log_decay, doc_ids, first = near_keys, near_values, near_logs, near_ids, 0
     core, _, _ = place_bits(s.count, False)
     lower = core == 0
-    docs = [jnp.full((1, s.width), doc_ids[j].astype(F32)) for j in range(s.blocks)]
-    carries = [None] + [equal(docs[j - 1], docs[j]) for j in range(1, s.blocks)]
+    if near:
+        docs = [jnp.full((1, s.width), doc_ids[j].astype(F32)) for j in range(s.blocks)]
+        carries = [None] + [equal(docs[j - 1], docs[j]) for j in range(1, s.blocks)]
+    else:
+        docs = [doc_ids[s.start : s.start + 1, :], doc_ids[s.end : s.end + 1, :]]
+        carries = [doc_ids[s.carry(j), :] for j in range(s.blocks)]
     logs = s.logs(log_decay)
     totals = [total_rows(a) for a in logs]
     factors = [jnp.exp(t) for t in totals]
@@ -188,8 +215,12 @@
     put_tail(s, notes, 0, whole_factor, docs[0], docs[-1])
     for j in range(1, s.blocks):
         notes[s.carry(j), :] = carries[j]
+    for j, rows in enumerate(factors):
+        notes[s.factor(j, 0).start : s.factor(j, 0).start + s.heads, :] = rows
     columns = [decay_columns(a) for a in logs]
     ends = [jnp.exp(a[C - 1 : C, :] - a) for a in columns]
+    for j, column in enumerate(columns):
+        cums[s.block(j), :] = column
     for h in range(s.heads):
         if waits and h % each == 0:
             for copy in waits[h // each]:
@@ -330,9 +361,9 @@
     return jnp.where(at >= other, jnp.exp(gap), 0.0)
 
 
-def local_kernel(s, queries, keys, values, log_decay, gain, out, weights):
+def local_kernel(s, queries, keys, values, log_decay, cums, gain, out, weights):
     for j, logs in enumerate(s.logs(log_decay)):
-        columns, rows = decay_columns(logs), decay_rows(logs)
+        columns, rows = cums[s.block(j), :], decay_rows(logs)
         for h in range(s.heads):
             mask = decay_mask(columns[:, h : h + 1], rows[h : h + 1, :])
             part = (s.block(j), s.head(h))
@@ -343,16 +374,14 @@
 
 
 def attention_kernel(
-    s, queries, out_grad, gain, log_decay, notes, local, first_update, keep, received, *rest
+    s, queries, out_grad, gain, cums, notes, local, first_update, keep, received, *rest
 ):
     earlier_sums, (out, sums) = rest[:-2], rest[-2:]
     core, _, _ = place_bits(s.count, False)
     lower = core == 0
-    logs = s.logs(log_decay)
-    factors = [jnp.exp(total_rows(a)) for a in logs]
-    decays = [jnp.exp(decay_columns(a)) for a in logs]
-    squares = [jnp.zeros((C, s.width), F32) for _ in logs]
-    inners = [jnp.zeros((C, s.width), F32) for _ in logs]
+    decays = [jnp.exp(cums[s.block(j), :]) for j in range(s.blocks)]
+    squares = [jnp.zeros((C, s.width), F32) for _ in decays]
+    inners = [jnp.zeros((C, s.width), F32) for _ in decays]
     for h in range(s.heads):
         state = joined(s, lower, keep, received, h)
         for j in range(s.blocks):
@@ -364,7 +393,7 @@
             inners[j] = inners[j] + out_grad[part].astype(F32) * gain[s.head(h)].reshape(1, s.width) * attention
             if j < s.blocks - 1:
                 update = first_update[s.rows(j * s.heads + h, s.width), :]
-                state = notes[s.carry(j + 1), :] * (factors[j][h : h + 1, :] * state + update)
+                state = notes[s.carry(j + 1), :] * (notes[s.factor(j, h), :] * state + update)
     if earlier_sums:
         sums[...] = earlier_sums[0][...]
     else:
@@ -376,14 +405,12 @@
 
 
 def grad_kernel(
-    s, all_features, queries, out_grad, gain, log_decay, notes, attention, *rest
+    s, all_features, queries, out_grad, gain, cums, notes, attention, *rest
 ):
     sums, (attn_grad, keep, send, out_tail, out_gain, back_terms) = rest[:-6], rest[-6:]
     core, _, _ = place_bits(s.count, True)
     lower = core == 0
-    logs = s.logs(log_decay)
-    factors = [jnp.exp(total_rows(a)) for a in logs]
-    decays = [jnp.exp(decay_columns(a)) for a in logs]
+    decays = [jnp.exp(cums[s.block(j), :]) for j in range(s.blocks)]
     totals = sum([a[...] for a in sums[1:]], sums[0][...]) / all_features
     spread = lambda row: jnp.broadcast_to(row, (C, C)).T
     inverses, slopes = [], []
@@ -416,16 +443,18 @@
                 back_terms[s.rows((j - 1) * s.heads + h, s.width), :] = term
         state = terms[-1]
         for j in reversed(range(s.blocks - 1)):
-            state = terms[j] + (notes[s.carry(j + 1), :] * factors[j][h : h + 1, :]) * state
+            state = terms[j] + (notes[s.carry(j + 1), :] * notes[s.factor(j, h), :]) * state
         put_parts(lower, s.half, h, state, keep, send)
         out_gain[h : h + 1, :] = gain_part
     send[base : base + s.tail, :] = out_tail[...]
     send[base + s.tail :, :] = out_gain[...]
 
 
-def local_grad_kernel(s, queries, values, log_decay, weights, attn_grad, key_out, value_out):
+def local_grad_kernel(
+    s, queries, values, log_decay, cums, weights, attn_grad, key_out, value_out
+):
     for j, logs in enumerate(s.logs(log_decay)):
-        columns, rows = decay_columns(logs), decay_rows(logs)
+        columns, rows = cums[s.block(j), :], decay_rows(logs)
         for h in range(s.heads):
             mask = decay_mask(columns[:, h : h + 1], rows[h : h + 1, :])
             part, own = (s.block(j), s.head(h)), (s.block(j), s.own(h))
@@ -435,7 +464,7 @@
             value_out[own] = dot(weights[s.rows(j * s.heads + h, C), :], grad, 0, 0)
 
 
-def final_kernel(s, waves, keys, values, log_decay, notes, key_local, value_local, back_terms, *rest):
+def final_kernel(s, waves, keys, values, cums, notes, key_local, value_local, back_terms, *rest):
     keep, received = rest[:2]
     last = s.wave == waves - 1
     near_outs = rest[-2:]
@@ -463,9 +492,7 @@
                 copies[-1].start()
     core, _, _ = place_bits(s.count, True)
     lower = core == 0
-    logs = s.logs(log_decay)
-    factors = [jnp.exp(total_rows(a)) for a in logs]
-    columns = [decay_columns(a) for a in logs]
+    columns = [cums[s.block(j), :] for j in range(s.blocks)]
     ends = [jnp.exp(a[C - 1 : C, :] - a) for a in columns]
     for h in range(s.heads):
         state = joined(s, lower, keep, received, h)
@@ -478,7 +505,7 @@
             near_outs[1][own] = (value_local[own] + value_far).astype(BF16)
             if j > 0:
                 term = back_terms[s.rows((j - 1) * s.heads + h, s.width), :]
-                state = notes[s.carry(j), :] * (term + factors[j][h : h + 1, :] * state)
+                state = notes[s.carry(j), :] * (term + notes[s.factor(j, h), :] * state)
         if last and (h + 1) * groups % s.heads == 0:
             each, g = s.heads // groups, h * groups // s.heads
             part = pl.ds(g * each * s.width, each * s.width)
@@ -626,7 +653,7 @@
     for s in waves:
         groups = max(g for g in (3, 2, 1) if s.heads % g == 0)
         given = (keys, values, log_decay, doc_ids)
-        spaces = [pltpu.VMEM, pltpu.VMEM, pltpu.VMEM, pltpu.SMEM]
+        spaces = [pltpu.VMEM] * 4
         scratch = []
         if not states:
             given, spaces = far, [pltpu.HBM] * 4
@@ -639,13 +666,14 @@
                 pltpu.SemaphoreType.DMA((2,)),
             ]
         else:
-            given = given[:2] + after(token, log_decay) + given[3:]
+            given = (keys, values, log_decay, states[0][2])
         state = call(
             bind(state_kernel, s),
             [
                 shape(s.heads * s.half, s.width),
                 shape(s.heads * s.half + s.tail, s.width),
                 shape(s.notes, s.width),
+                shape(tokens, s.heads),
                 shape(max(1, s.blocks - 1) * s.heads * s.width, s.width),
             ],
             *given,
@@ -669,6 +697,7 @@
             keys,
             values,
             held,
+            states[i][3],
             gain,
             flops=2 * unit,
         )
@@ -678,17 +707,16 @@
     entries, local, token, _ = scan_in(waves, parts, False, token, beside_forward)
     attentions, sums = [], []
     for i, s in enumerate(waves):
-        (held,) = after(token, log_decay)
         attention, total = call(
             bind(attention_kernel, s),
             [shape(tokens, s.columns), shape(8, tokens)],
             queries,
             out_grad,
             gain,
-            held,
+            states[i][3],
             states[i][2],
             local[i][0],
-            states[i][3],
+            states[i][4],
             *entries[i],
             *sums,
             flops=2 * unit,
@@ -706,7 +734,6 @@
             bit *= 2
     grads = []
     for i, s in enumerate(waves):
-        (held,) = after(token, log_decay)
         grad = call(
             bind(grad_kernel, s, features * dp),
             [
@@ -720,7 +747,7 @@
             queries,
             out_grad,
             gain,
-            held,
+            states[i][3],
             states[i][2],
             attentions[i],
             *sums,
@@ -738,6 +765,7 @@
             queries,
             values,
             held,
+            states[i][3],
             local[i][1],
             grads[i][0],
             flops=3 * unit,
@@ -752,7 +780,7 @@
         (held,) = after(token, log_decay)
         groups = max(g for g in (3, 2, 1) if s.heads % g == 0)
         given = [
-            keys, values, held, states[i][2], *local_grads[i], grads[i][5], *entries[i], *done,
+            keys, values, states[i][3], states[i][2], *local_grads[i], grads[i][5], *entries[i], *done,
         ]
         scratch = []
         if last:

time: 68.2 us -> 66.9 us (0.981)
  waiting for transfers between devices: 23.1 us -> 27.5 us
  starting transfers between devices: 26.2 us -> 22.9 us
  Pallas kernels: 17.6 us -> 15.4 us
    ppermute x18, waiting for transfers between devices: 11.5 us -> 14 us  [swap(): return lax.ppermute(value, axis, [(i, i ^ bit) for i in range(count)])]
    ppermute x18, starting transfers between devices: 16.8 us -> 14.5 us  [swap(): return lax.ppermute(value, axis, [(i, i ^ bit) for i in range(count)])]
    pallas_call x28, Pallas kernels: 17.6 us -> 15.4 us  [call(): pl.pallas_call(lambda *refs: kernel(*refs[:given], *refs[given + len(deps...]
    ppermute x4, waiting for transfers between devices: 5.17 us -> 6.52 us  [next_plane(): lax.ppermute(value, 'seq', [(i, (i + step) % count) for i in range(count)])]
    ppermute x4, starting transfers between devices: 3.67 us -> 2.69 us  [pass_on(): return lax.ppermute(value, 'seq', pairs)]
  transfers between devices with their start and end apart: 26 -> 26, of which waited for: 15 -> 16; matrix products, arithmetic and copies ran while one was open for 0% -> 0% of each run, Pallas kernels for 17% -> 15%
where the time goes in v5:
time: 66.9 us; the launch traced here: 66.8 us
  waiting for transfers between devices  27.5 us (41%)
  starting transfers between devices  22.9 us (34%)
  Pallas kernels  15.4 us (23%)
  between operations  0.88 us (1%)
    pallas_call x28, Pallas kernels, call(): pl.pallas_call(lambda *refs: kernel(*refs[:given], *refs[given + len(deps...  15.4 us
    ppermute x18, starting transfers between devices, swap(): return lax.ppermute(value, axis, [(i, i ^ bit) for i in range(count)])  14.5 us
    ppermute x18, waiting for transfers between devices, swap(): return lax.ppermute(value, axis, [(i, i ^ bit) for i in range(count)])  14 us
    ppermute x4, waiting for transfers between devices, pass_on(): return lax.ppermute(value, 'seq', pairs)  6.95 us
    ppermute x4, waiting for transfers between devices, next_plane(): lax.ppermute(value, 'seq', [(i, (i + step) % count) for i in range(count)])  6.52 us
    ppermute x4, starting transfers between devices, next_plane(): lax.ppermute(value, 'seq', [(i, (i + step) % count) for i in range(count)])  5.75 us
    ppermute x4, starting transfers between devices, pass_on(): return lax.ppermute(value, 'seq', pairs)  2.69 us
  transfers between devices with their start and end apart: 26, of which 16 were waited for; matrix products, arithmetic and copies ran while one was open for 0% of the time, Pallas kernels for 15%

profile of v5, /device:TPU:0, one launch (start us, length us, event | category | flops | bytes accessed | tf_op | source)
XLA Modules:
  0.0 66.8 jit_solution(864562200695637679)
XLA Ops:
  0.7 2.4 %shard_map.94 = (f32[384,128]{1,0:T(8,128)S(1)}, f32[392,128]{1,0:T(8,128)S(1)}, f32[24,128]{1,0:T(8,128)S(1)}, f32[256,6]{1,0:T(8,128)S(1)}, f32[768,128]{1,0:T(8,128)S(1)}) custom-call(bf16[256,1536]{1,0:T(8,128)(2,1)} %refs_0_.13, bf16[256,1536]{1,0:T(8,128)(2,1)} %refs_1_.13, f32[12,256]{1,0:T(8,128)} %bitcast.1, s32[2]{0:T(128)} %refs_3_.1), custom_call_target="tpu_custom_call" | custom-call | flops 50331648 | bytes 2394120 | tf_op jit(solution)/shard_map/pallas_call | solution.py:138
  3.0 0.5 collective-permute-start
  3.6 0.8 %shard_map.95 = (f32[384,128]{1,0:T(8,128)S(1)}, f32[392,128]{1,0:T(8,128)S(1)}, f32[24,128]{1,0:T(8,128)S(1)}, f32[256,6]{1,0:T(8,128)S(1)}, f32[768,128]{1,0:T(8,128)S(1)}) custom-call(bf16[256,1536]{1,0:T(8,128)(2,1)S(1)} %copy-done.2, bf16[256,1536]{1,0:T(8,128)(2,1)S(1)} %copy-done.1, f32[12,256]{1,0:T(8,128)S(1)} %bitcast.2, ...), custom_call_target="tpu_custom_call" | custom-call | flops 50331648 | bytes 2406400 | tf_op jit(solution)/shard_map/pallas_call | solution.py:138
  4.3 0.1 collective-permute-start.1
  4.5 0.2 collective-permute-done.refs_1_.refs_3_
  4.7 2.9 %collective-permute-start.2 = (f32[200,128]{1,0:T(8,128)S(1)}, f32[200,128]{1,0:T(8,128)S(1)}, u32[]{:S(2)}, u32[]{:S(2)}) collective-permute-start(f32[200,128]{1,0:T(8,128)S(1)} %get-tuple-element.117.refs_1_), channel_id=1, source_target_pairs={{0,2},{1,3},{2,0},{3,1},{4,6},{5,7},{6,4},{7,5},{8,10},{9,11},{10,... | collective-permute-start | bytes 307208 | tf_op jit(solution)/shard_map/ppermute | solution.py:524
  7.7 0.9 %collective-permute-start.3 = (f32[200,128]{1,0:T(8,128)S(1)}, f32[200,128]{1,0:T(8,128)S(1)}, u32[]{:S(2)}, u32[]{:S(2)}) collective-permute-start(f32[200,128]{1,0:T(8,128)S(1)} %get-tuple-element.119.refs_1_), channel_id=1, source_target_pairs={{0,2},{1,3},{2,0},{3,1},{4,6},{5,7},{6,4},{7,5},{8,10},{9,11},{10,... | collective-permute-start | bytes 307208 | tf_op jit(solution)/shard_map/ppermute | solution.py:524
  8.6 2.0 %shard_map.98 = (f32[256,768]{1,0:T(8,128)S(1)}, bf16[1536,128]{1,0:T(8,128)(2,1)S(1)}) custom-call(bf16[256,1536]{1,0:T(8,128)(2,1)S(1)} %copy-done, bf16[256,1536]{1,0:T(8,128)(2,1)S(1)} %copy-done.2, bf16[256,1536]{1,0:T(8,128)(2,1)S(1)} %copy-done.1, f32[12,256]{1,0:T(8,128)S(1)} %bitcast.3, f32[256,6]{1,0:T(8,128)S(1)} %get-tuple-element.114.refs_4_.refs_3_.refs_2_, ...), custom_call_target="tpu_custom_call" | custom-call | flops 100663296 | bytes 3563520 | tf_op jit(solution)/shard_map/pallas_call | solution.py:138
  10.6 0.6 collective-permute-done.2.refs_2_
  11.3 2.2 %collective-permute-start.4 = (f32[200,128]{1,0:T(8,128)S(1)}, f32[200,128]{1,0:T(8,128)S(1)}, u32[]{:S(2)}, u32[]{:S(2)}) collective-permute-start(f32[200,128]{1,0:T(8,128)S(1)} %shard_map.99.refs_3_), channel_id=1, source_target_pairs={{0,4},{1,5},{2,6},{3,7},{4,8},{5,9},{6,10},{7,11},{8,12},{9,13},{1... | collective-permute-start | bytes 307208 | tf_op jit(solution)/shard_map/ppermute | solution.py:529
  13.5 1.6 %collective-permute-start.6 = (f32[200,128]{1,0:T(8,128)S(1)}, f32[200,128]{1,0:T(8,128)S(1)}, u32[]{:S(2)}, u32[]{:S(2)}) collective-permute-start(f32[200,128]{1,0:T(8,128)S(1)} %shard_map.100), channel_id=1, source_target_pairs={{0,4},{1,5},{2,6},{3,7},{4,8},{5,9},{6,10},{7,11},{8,12},{9,13},{1... | collective-permute-start | bytes 307208 | tf_op jit(solution)/shard_map/ppermute | solution.py:529
  15.2 2.0 %shard_map.101 = (f32[256,768]{1,0:T(8,128)S(1)}, bf16[1536,128]{1,0:T(8,128)(2,1)S(1)}) custom-call(bf16[256,1536]{1,0:T(8,128)(2,1)S(1)} %copy-done, bf16[256,1536]{1,0:T(8,128)(2,1)S(1)} %copy-done.2, bf16[256,1536]{1,0:T(8,128)(2,1)S(1)} %copy-done.1, f32[12,256]{1,0:T(8,128)S(1)} %bitcast.4, f32[256,6]{1,0:T(8,128)S(1)} %get-tuple-element.100.refs_4_.refs_3_.refs_2_, ...), custom_call_target="tpu_custom_call" | custom-call | flops 100663296 | bytes 3563520 | tf_op jit(solution)/shard_map/pallas_call | solution.py:138
  17.2 2.1 %collective-permute-done.4.refs_3_ = f32[200,128]{1,0:T(8,128)S(1)} collective-permute-done((f32[200,128]{1,0:T(8,128)S(1)}, f32[200,128]{1,0:T(8,128)S(1)}, u32[]{:S(2)}, u32[]{:S(2)}) %collective-permute-start.4) | collective-permute-done | bytes 102432 | tf_op jit(solution)/shard_map/ppermute | solution.py:529
  19.3 1.5 %collective-permute-start.5 = (f32[200,128]{1,0:T(8,128)S(1)}, f32[200,128]{1,0:T(8,128)S(1)}, u32[]{:S(2)}, u32[]{:S(2)}) collective-permute-start(f32[200,128]{1,0:T(8,128)S(1)} %collective-permute-done.4.refs_3_), channel_id=1, source_target_pairs={{0,2},{1,3},{2,0},{3,1},{4,8},{5,9},{6,10},{7,11},{8,12},{9,13},{1... | collective-permute-start | bytes 307208 | tf_op jit(solution)/shard_map/ppermute | solution.py:543
  20.8 1.1 %collective-permute-start.7 = (f32[200,128]{1,0:T(8,128)S(1)}, f32[200,128]{1,0:T(8,128)S(1)}, u32[]{:S(2)}, u32[]{:S(2)}) collective-permute-start(f32[200,128]{1,0:T(8,128)S(1)} %collective-permute-done.6.refs_3_), channel_id=1, source_target_pairs={{0,2},{1,3},{2,0},{3,1},{4,8},{5,9},{6,10},{7,11},{8,12},{9,13},{1... | collective-permute-start | bytes 307208 | tf_op jit(solution)/shard_map/ppermute | solution.py:543
  21.9 3.1 %collective-permute-done.5.refs_4_ = f32[200,128]{1,0:T(8,128)S(1)} collective-permute-done((f32[200,128]{1,0:T(8,128)S(1)}, f32[200,128]{1,0:T(8,128)S(1)}, u32[]{:S(2)}, u32[]{:S(2)}) %collective-permute-start.5) | collective-permute-done | bytes 102432 | tf_op jit(solution)/shard_map/ppermute | solution.py:543
  25.0 1.6 %collective-permute-start.8 = (f32[192,128]{1,0:T(8,128)S(1)}, f32[192,128]{1,0:T(8,128)S(1)}, u32[]{:S(2)}, u32[]{:S(2)}) collective-permute-start(f32[192,128]{1,0:T(8,128)S(1)} %get-tuple-element.130), channel_id=1, source_target_pairs={{0,2},{1,3},{2,0},{3,1},{4,6},{5,7},{6,4},{7,5},{8,10},{9,11},{10,... | collective-permute-start | bytes 294920 | tf_op jit(solution)/shard_map/ppermute | solution.py:524
  26.7 1.3 %collective-permute-start.9 = (f32[192,128]{1,0:T(8,128)S(1)}, f32[192,128]{1,0:T(8,128)S(1)}, u32[]{:S(2)}, u32[]{:S(2)}) collective-permute-start(f32[192,128]{1,0:T(8,128)S(1)} %get-tuple-element.133), channel_id=1, source_target_pairs={{0,2},{1,3},{2,0},{3,1},{4,6},{5,7},{6,4},{7,5},{8,10},{9,11},{10,... | collective-permute-start | bytes 294920 | tf_op jit(solution)/shard_map/ppermute | solution.py:524
  28.1 1.7 %collective-permute-done.8.refs_1_ = f32[192,128]{1,0:T(8,128)S(1)} collective-permute-done((f32[192,128]{1,0:T(8,128)S(1)}, f32[192,128]{1,0:T(8,128)S(1)}, u32[]{:S(2)}, u32[]{:S(2)}) %collective-permute-start.8) | collective-permute-done | bytes 98336 | tf_op jit(solution)/shard_map/ppermute | solution.py:524
  29.7 0.1 shard_map.104
  29.9 1.5 %collective-permute-done.9.refs_1_ = f32[192,128]{1,0:T(8,128)S(1)} collective-permute-done((f32[192,128]{1,0:T(8,128)S(1)}, f32[192,128]{1,0:T(8,128)S(1)}, u32[]{:S(2)}, u32[]{:S(2)}) %collective-permute-start.9) | collective-permute-done | bytes 98336 | tf_op jit(solution)/shard_map/ppermute | solution.py:524
  31.4 0.1 shard_map.105
  31.6 0.6 shard_map.106
  32.2 0.8 %collective-permute-done.10.refs_8_ = f32[384,128]{1,0:T(8,128)S(1)} collective-permute-done((f32[384,128]{1,0:T(8,128)S(1)}, f32[384,128]{1,0:T(8,128)S(1)}, u32[]{:S(2)}, u32[]{:S(2)}) %collective-permute-start.10) | collective-permute-done | bytes 196640 | tf_op jit(solution)/shard_map/ppermute | solution.py:524
  33.0 0.6 shard_map.107
  33.6 1.6 %collective-permute-start.12 = (f32[8,256]{1,0:T(8,128)S(1)}, f32[8,256]{1,0:T(8,128)S(1)}, u32[]{:S(2)}, u32[]{:S(2)}) collective-permute-start(f32[8,256]{1,0:T(8,128)S(1)} %get-tuple-element.140.refs_6_), channel_id=1, source_target_pairs={{0,16},{16,0},{1,17},{17,1},{2,18},{18,2},{3,19},{19,3},{4,20},{20... | collective-permute-start | bytes 24584 | tf_op jit(solution)/shard_map/ppermute | solution.py:524
  35.2 2.1 %collective-permute-done.12.refs_7_ = f32[8,256]{1,0:T(8,128)S(1)} collective-permute-done((f32[8,256]{1,0:T(8,128)S(1)}, f32[8,256]{1,0:T(8,128)S(1)}, u32[]{:S(2)}, u32[]{:S(2)}) %collective-permute-start.12) | collective-permute-done | bytes 8224 | tf_op jit(solution)/shard_map/ppermute | solution.py:524
  37.3 0.9 %shard_map.109 = (bf16[256,768]{1,0:T(8,128)(2,1)S(1)}, f32[384,128]{1,0:T(8,128)S(1)}, f32[400,128]{1,0:T(8,128)S(1)}, f32[8,128]{1,0:T(8,128)S(1)}, f32[8,128]{1,0:T(8,128)S(1)}, /*index=5*/f32[768,128]{1,0:T(8,128)S(1)}) custom-call(bf16[256,1536]{1,0:T(8,128)(2,1)S(1)} %copy-done, bf16[256,1536]{1,0:T(8,128)(2,1)S(1)} %copy-done.3, f32[1536]{0:T(1024)S(1)} %copy-done.5, ...), custom_call_target="tpu_custom_call" | custom-call | flops 50331648 | bytes 3596288 | tf_op jit(solution)/shard_map/pallas_call | solution.py:138
  38.3 0.9 %shard_map.108 = (bf16[256,768]{1,0:T(8,128)(2,1)S(1)}, f32[384,128]{1,0:T(8,128)S(1)}, f32[400,128]{1,0:T(8,128)S(1)}, f32[8,128]{1,0:T(8,128)S(1)}, f32[8,128]{1,0:T(8,128)S(1)}, /*index=5*/f32[768,128]{1,0:T(8,128)S(1)}) custom-call(bf16[256,1536]{1,0:T(8,128)(2,1)S(1)} %copy-done, bf16[256,1536]{1,0:T(8,128)(2,1)S(1)} %copy-done.3, f32[1536]{0:T(1024)S(1)} %copy-done.5, ...), custom_call_target="tpu_custom_call" | custom-call | flops 50331648 | bytes 3596288 | tf_op jit(solution)/shard_map/pallas_call | solution.py:138
  39.3 0.6 collective-permute-start.14
  39.9 1.3 %collective-permute-start.15 = (f32[200,128]{1,0:T(8,128)S(1)}, f32[200,128]{1,0:T(8,128)S(1)}, u32[]{:S(2)}, u32[]{:S(2)}) collective-permute-start(f32[200,128]{1,0:T(8,128)S(1)} %get-tuple-element.161.refs_1_), channel_id=1, source_target_pairs={{0,2},{1,3},{2,0},{3,1},{4,6},{5,7},{6,4},{7,5},{8,10},{9,11},{10,... | collective-permute-start | bytes 307208 | tf_op jit(solution)/shard_map/ppermute | solution.py:524
  41.3 1.0 %collective-permute-start.17 = (f32[200,128]{1,0:T(8,128)S(1)}, f32[200,128]{1,0:T(8,128)S(1)}, u32[]{:S(2)}, u32[]{:S(2)}) collective-permute-start(f32[200,128]{1,0:T(8,128)S(1)} %get-tuple-element.164.refs_1_), channel_id=1, source_target_pairs={{0,2},{1,3},{2,0},{3,1},{4,6},{5,7},{6,4},{7,5},{8,10},{9,11},{10,... | collective-permute-start | bytes 307208 | tf_op jit(solution)/shard_map/ppermute | solution.py:524
  42.3 1.1 %shard_map.112 = (f32[256,768]{1,0:T(8,128)S(1)}, f32[256,768]{1,0:T(8,128)S(1)}) custom-call(bf16[256,1536]{1,0:T(8,128)(2,1)S(1)} %copy-done, bf16[256,1536]{1,0:T(8,128)(2,1)S(1)} %copy-done.1, f32[12,256]{1,0:T(8,128)S(1)} %bitcast.5, f32[256,6]{1,0:T(8,128)S(1)} %get-tuple-element.114.refs_4_.refs_3_.refs_2_, ...), custom_call_target="tpu_custom_call" | custom-call | flops 150994944 | bytes 3950592 | tf_op jit(solution)/shard_map/pallas_call | solution.py:138
  43.5 2.8 %collective-permute-done.16.refs_4_ = f32[16,128]{1,0:T(8,128)S(1)} collective-permute-done((f32[16,128]{1,0:T(8,128)S(1)}, f32[16,128]{1,0:T(8,128)S(1)}, u32[]{:S(2)}, u32[]{:S(2)}) %collective-permute-start.16) | collective-permute-done | bytes 8224 | tf_op jit(solution)/shard_map/ppermute | solution.py:524
  46.3 1.5 %collective-permute-start.18 = (f32[216,128]{1,0:T(8,128)S(1)}, f32[216,128]{1,0:T(8,128)S(1)}, u32[]{:S(2)}, u32[]{:S(2)}) collective-permute-start(f32[216,128]{1,0:T(8,128)S(1)} %shard_map.113.refs_3_.refs_5_), channel_id=1, source_target_pairs={{0,12},{1,13},{2,14},{3,15},{4,0},{5,1},{6,2},{7,3},{8,4},{9,5},{1... | collective-permute-start | bytes 331784 | tf_op jit(solution)/shard_map/ppermute | solution.py:529
  47.9 0.4 collective-permute-start.20
  48.3 1.1 %shard_map.115 = (f32[256,768]{1,0:T(8,128)S(1)}, f32[256,768]{1,0:T(8,128)S(1)}) custom-call(bf16[256,1536]{1,0:T(8,128)(2,1)S(1)} %copy-done, bf16[256,1536]{1,0:T(8,128)(2,1)S(1)} %copy-done.1, f32[12,256]{1,0:T(8,128)S(1)} %bitcast.6, f32[256,6]{1,0:T(8,128)S(1)} %get-tuple-element.100.refs_4_.refs_3_.refs_2_, ...), custom_call_target="tpu_custom_call" | custom-call | flops 150994944 | bytes 3950592 | tf_op jit(solution)/shard_map/pallas_call | solution.py:138
  49.5 2.8 %collective-permute-done.18.refs_3_ = f32[216,128]{1,0:T(8,128)S(1)} collective-permute-done((f32[216,128]{1,0:T(8,128)S(1)}, f32[216,128]{1,0:T(8,128)S(1)}, u32[]{:S(2)}, u32[]{:S(2)}) %collective-permute-start.18) | collective-permute-done | bytes 110624 | tf_op jit(solution)/shard_map/ppermute | solution.py:529
  52.3 1.6 %collective-permute-done.20.refs_3_ = f32[200,128]{1,0:T(8,128)S(1)} collective-permute-done((f32[200,128]{1,0:T(8,128)S(1)}, f32[200,128]{1,0:T(8,128)S(1)}, u32[]{:S(2)}, u32[]{:S(2)}) %collective-permute-start.20) | collective-permute-done | bytes 102432 | tf_op jit(solution)/shard_map/ppermute | solution.py:529
  54.0 3.8 %collective-permute-done.19.refs_4_ = f32[216,128]{1,0:T(8,128)S(1)} collective-permute-done((f32[216,128]{1,0:T(8,128)S(1)}, f32[216,128]{1,0:T(8,128)S(1)}, u32[]{:S(2)}, u32[]{:S(2)}) %collective-permute-start.19) | collective-permute-done | bytes 110624 | tf_op jit(solution)/shard_map/ppermute | solution.py:543
  57.9 1.0 %collective-permute-start.22 = (f32[208,128]{1,0:T(8,128)S(1)}, f32[208,128]{1,0:T(8,128)S(1)}, u32[]{:S(2)}, u32[]{:S(2)}) collective-permute-start(f32[208,128]{1,0:T(8,128)S(1)} %get-tuple-element.177), channel_id=1, source_target_pairs={{0,2},{1,3},{2,0},{3,1},{4,6},{5,7},{6,4},{7,5},{8,10},{9,11},{10,... | collective-permute-start | bytes 319496 | tf_op jit(solution)/shard_map/ppermute | solution.py:524
  59.0 1.1 %collective-permute-start.23 = (f32[192,128]{1,0:T(8,128)S(1)}, f32[192,128]{1,0:T(8,128)S(1)}, u32[]{:S(2)}, u32[]{:S(2)}) collective-permute-start(f32[192,128]{1,0:T(8,128)S(1)} %get-tuple-element.180), channel_id=1, source_target_pairs={{0,2},{1,3},{2,0},{3,1},{4,6},{5,7},{6,4},{7,5},{8,10},{9,11},{10,... | collective-permute-start | bytes 294920 | tf_op jit(solution)/shard_map/ppermute | solution.py:524
  60.1 2.5 %collective-permute-done.22.refs_1_.refs_12_ = f32[208,128]{1,0:T(8,128)S(1)} collective-permute-done((f32[208,128]{1,0:T(8,128)S(1)}, f32[208,128]{1,0:T(8,128)S(1)}, u32[]{:S(2)}, u32[]{:S(2)}) %collective-permute-start.22) | collective-permute-done | bytes 106528 | tf_op jit(solution)/shard_map/ppermute | solution.py:524
  62.8 0.9 %collective-permute-done.23.refs_1_ = f32[192,128]{1,0:T(8,128)S(1)} collective-permute-done((f32[192,128]{1,0:T(8,128)S(1)}, f32[192,128]{1,0:T(8,128)S(1)}, u32[]{:S(2)}, u32[]{:S(2)}) %collective-permute-start.23) | collective-permute-done | bytes 98336 | tf_op jit(solution)/shard_map/ppermute | solution.py:524
  63.9 0.4 collective-permute-done.25.refs_8_
  64.2 0.6 shard_map.120
  64.8 0.4 collective-permute-done.24.refs_8_
  65.3 1.5 %shard_map.121 = (bf16[256,1536]{1,0:T(8,128)(2,1)}, bf16[256,1536]{1,0:T(8,128)(2,1)}, f32[1536]{0:T(1024)}) custom-call(bf16[256,1536]{1,0:T(8,128)(2,1)S(1)} %copy-done.2, bf16[256,1536]{1,0:T(8,128)(2,1)S(1)} %copy-done.1, f32[256,6]{1,0:T(8,128)S(1)} %get-tuple-element.100.refs_4_.refs_3_.refs_2_, ...), custom_call_target="tpu_custom_call" | custom-call | flops 201326592 | bytes 6430720 | tf_op jit(solution)/shard_map/pallas_call | solution.py:138
  (44 shorter events, 1.2 us)
Async XLA Ops:
  0.6 2.9 %copy-start.1 = (bf16[256,1536]{1,0:T(8,128)(2,1)S(1)}, bf16[256,1536]{1,0:T(8,128)(2,1)}, u32[]{:S(2)}) copy-start(bf16[256,1536]{1,0:T(8,128)(2,1)} %refs_1_.13) | copy-start | bytes 2359300
  0.6 2.9 %copy-start.2 = (bf16[256,1536]{1,0:T(8,128)(2,1)S(1)}, bf16[256,1536]{1,0:T(8,128)(2,1)}, u32[]{:S(2)}) copy-start(bf16[256,1536]{1,0:T(8,128)(2,1)} %refs_0_.13) | copy-start | bytes 2359300
  0.7 2.9 %copy-start.4 = (f32[256,12]{0,1:T(8,128)S(1)}, f32[256,12]{0,1:T(8,128)}, u32[]{:S(2)}) copy-start(f32[256,12]{0,1:T(8,128)} %param.11) | copy-start | bytes 36868
  3.0 1.6 %collective-permute-start = (f32[392,128]{1,0:T(8,128)S(1)}, f32[392,128]{1,0:T(8,128)S(1)}, u32[]{:S(2)}, u32[]{:S(2)}) collective-permute-start(f32[392,128]{1,0:T(8,128)S(1)} %get-tuple-element.107), channel_id=1, source_target_pairs={{0,1},{1,0},{2,3},{3,2},{4,5},{5,4},{6,7},{7,6},{8,9},{9,8},{10,11... | collective-permute-start | bytes 602120 | tf_op jit(solution)/shard_map/ppermute | solution.py:524
  4.3 4.3 %copy-start = (bf16[256,1536]{1,0:T(8,128)(2,1)S(1)}, bf16[256,1536]{1,0:T(8,128)(2,1)}, u32[]{:S(2)}) copy-start(bf16[256,1536]{1,0:T(8,128)(2,1)} %refs_0_.11) | copy-start | bytes 2359300
  4.3 3.3 %collective-permute-start.1 = (f32[392,128]{1,0:T(8,128)S(1)}, f32[392,128]{1,0:T(8,128)S(1)}, u32[]{:S(2)}, u32[]{:S(2)}) collective-permute-start(f32[392,128]{1,0:T(8,128)S(1)} %get-tuple-element.110), channel_id=1, source_target_pairs={{0,1},{1,0},{2,3},{3,2},{4,5},{5,4},{6,7},{7,6},{8,9},{9,8},{10,11... | collective-permute-start | bytes 602120 | tf_op jit(solution)/shard_map/ppermute | solution.py:524
  4.7 6.6 %collective-permute-start.2 = (f32[200,128]{1,0:T(8,128)S(1)}, f32[200,128]{1,0:T(8,128)S(1)}, u32[]{:S(2)}, u32[]{:S(2)}) collective-permute-start(f32[200,128]{1,0:T(8,128)S(1)} %get-tuple-element.117.refs_1_), channel_id=1, source_target_pairs={{0,2},{1,3},{2,0},{3,1},{4,6},{5,7},{6,4},{7,5},{8,10},{9,11},{10,... | collective-permute-start | bytes 307208 | tf_op jit(solution)/shard_map/ppermute | solution.py:524
  7.6 1.0 %copy-start.5 = (f32[1536]{0:T(1024)S(1)}, f32[1536]{0:T(1024)}, u32[]{:S(2)}) copy-start(f32[1536]{0:T(1024)} %refs_2_.5) | copy-start | bytes 18436
  7.7 5.8 %collective-permute-start.3 = (f32[200,128]{1,0:T(8,128)S(1)}, f32[200,128]{1,0:T(8,128)S(1)}, u32[]{:S(2)}, u32[]{:S(2)}) collective-permute-start(f32[200,128]{1,0:T(8,128)S(1)} %get-tuple-element.119.refs_1_), channel_id=1, source_target_pairs={{0,2},{1,3},{2,0},{3,1},{4,6},{5,7},{6,4},{7,5},{8,10},{9,11},{10,... | collective-permute-start | bytes 307208 | tf_op jit(solution)/shard_map/ppermute | solution.py:524
  11.3 7.9 %collective-permute-start.4 = (f32[200,128]{1,0:T(8,128)S(1)}, f32[200,128]{1,0:T(8,128)S(1)}, u32[]{:S(2)}, u32[]{:S(2)}) collective-permute-start(f32[200,128]{1,0:T(8,128)S(1)} %shard_map.99.refs_3_), channel_id=1, source_target_pairs={{0,4},{1,5},{2,6},{3,7},{4,8},{5,9},{6,10},{7,11},{8,12},{9,13},{1... | collective-permute-start | bytes 307208 | tf_op jit(solution)/shard_map/ppermute | solution.py:529
  13.5 7.2 %collective-permute-start.6 = (f32[200,128]{1,0:T(8,128)S(1)}, f32[200,128]{1,0:T(8,128)S(1)}, u32[]{:S(2)}, u32[]{:S(2)}) collective-permute-start(f32[200,128]{1,0:T(8,128)S(1)} %shard_map.100), channel_id=1, source_target_pairs={{0,4},{1,5},{2,6},{3,7},{4,8},{5,9},{6,10},{7,11},{8,12},{9,13},{1... | collective-permute-start | bytes 307208 | tf_op jit(solution)/shard_map/ppermute | solution.py:529
  19.3 5.7 %collective-permute-start.5 = (f32[200,128]{1,0:T(8,128)S(1)}, f32[200,128]{1,0:T(8,128)S(1)}, u32[]{:S(2)}, u32[]{:S(2)}) collective-permute-start(f32[200,128]{1,0:T(8,128)S(1)} %collective-permute-done.4.refs_3_), channel_id=1, source_target_pairs={{0,2},{1,3},{2,0},{3,1},{4,8},{5,9},{6,10},{7,11},{8,12},{9,13},{1... | collective-permute-start | bytes 307208 | tf_op jit(solution)/shard_map/ppermute | solution.py:543
  20.8 5.9 %collective-permute-start.7 = (f32[200,128]{1,0:T(8,128)S(1)}, f32[200,128]{1,0:T(8,128)S(1)}, u32[]{:S(2)}, u32[]{:S(2)}) collective-permute-start(f32[200,128]{1,0:T(8,128)S(1)} %collective-permute-done.6.refs_3_), channel_id=1, source_target_pairs={{0,2},{1,3},{2,0},{3,1},{4,8},{5,9},{6,10},{7,11},{8,12},{9,13},{1... | collective-permute-start | bytes 307208 | tf_op jit(solution)/shard_map/ppermute | solution.py:543
  25.0 4.7 %collective-permute-start.8 = (f32[192,128]{1,0:T(8,128)S(1)}, f32[192,128]{1,0:T(8,128)S(1)}, u32[]{:S(2)}, u32[]{:S(2)}) collective-permute-start(f32[192,128]{1,0:T(8,128)S(1)} %get-tuple-element.130), channel_id=1, source_target_pairs={{0,2},{1,3},{2,0},{3,1},{4,6},{5,7},{6,4},{7,5},{8,10},{9,11},{10,... | collective-permute-start | bytes 294920 | tf_op jit(solution)/shard_map/ppermute | solution.py:524
  26.7 4.9 %copy-start.3 = (bf16[256,1536]{1,0:T(8,128)(2,1)S(1)}, bf16[256,1536]{1,0:T(8,128)(2,1)}, u32[]{:S(2)}) copy-start(bf16[256,1536]{1,0:T(8,128)(2,1)} %refs_1_.9) | copy-start | bytes 2359300
  26.7 4.7 %collective-permute-start.9 = (f32[192,128]{1,0:T(8,128)S(1)}, f32[192,128]{1,0:T(8,128)S(1)}, u32[]{:S(2)}, u32[]{:S(2)}) collective-permute-start(f32[192,128]{1,0:T(8,128)S(1)} %get-tuple-element.133), channel_id=1, source_target_pairs={{0,2},{1,3},{2,0},{3,1},{4,6},{5,7},{6,4},{7,5},{8,10},{9,11},{10,... | collective-permute-start | bytes 294920 | tf_op jit(solution)/shard_map/ppermute | solution.py:524
  29.8 1.8 %collective-permute-start.11 = (f32[384,128]{1,0:T(8,128)S(1)}, f32[384,128]{1,0:T(8,128)S(1)}, u32[]{:S(2)}, u32[]{:S(2)}) collective-permute-start(f32[384,128]{1,0:T(8,128)S(1)} %get-tuple-element.137), channel_id=1, source_target_pairs={{0,1},{1,0},{2,3},{3,2},{4,5},{5,4},{6,7},{7,6},{8,9},{9,8},{10,11... | collective-permute-start | bytes 589832 | tf_op jit(solution)/shard_map/ppermute | solution.py:524
  31.5 1.5 %collective-permute-start.10 = (f32[384,128]{1,0:T(8,128)S(1)}, f32[384,128]{1,0:T(8,128)S(1)}, u32[]{:S(2)}, u32[]{:S(2)}) collective-permute-start(f32[384,128]{1,0:T(8,128)S(1)} %get-tuple-element.135), channel_id=1, source_target_pairs={{0,1},{1,0},{2,3},{3,2},{4,5},{5,4},{6,7},{7,6},{8,9},{9,8},{10,11... | collective-permute-start | bytes 589832 | tf_op jit(solution)/shard_map/ppermute | solution.py:524
  33.6 3.7 %collective-permute-start.12 = (f32[8,256]{1,0:T(8,128)S(1)}, f32[8,256]{1,0:T(8,128)S(1)}, u32[]{:S(2)}, u32[]{:S(2)}) collective-permute-start(f32[8,256]{1,0:T(8,128)S(1)} %get-tuple-element.140.refs_6_), channel_id=1, source_target_pairs={{0,16},{16,0},{1,17},{17,1},{2,18},{18,2},{3,19},{19,3},{4,20},{20... | collective-permute-start | bytes 24584 | tf_op jit(solution)/shard_map/ppermute | solution.py:524
  38.2 1.6 %collective-permute-start.13 = (f32[400,128]{1,0:T(8,128)S(1)}, f32[400,128]{1,0:T(8,128)S(1)}, u32[]{:S(2)}, u32[]{:S(2)}) collective-permute-start(f32[400,128]{1,0:T(8,128)S(1)} %get-tuple-element.145), channel_id=1, source_target_pairs={{0,1},{1,0},{2,3},{3,2},{4,5},{5,4},{6,7},{7,6},{8,9},{9,8},{10,11... | collective-permute-start | bytes 614408 | tf_op jit(solution)/shard_map/ppermute | solution.py:524
  39.3 2.0 %collective-permute-start.14 = (f32[400,128]{1,0:T(8,128)S(1)}, f32[400,128]{1,0:T(8,128)S(1)}, u32[]{:S(2)}, u32[]{:S(2)}) collective-permute-start(f32[400,128]{1,0:T(8,128)S(1)} %get-tuple-element.151), channel_id=1, source_target_pairs={{0,1},{1,0},{2,3},{3,2},{4,5},{5,4},{6,7},{7,6},{8,9},{9,8},{10,11... | collective-permute-start | bytes 614408 | tf_op jit(solution)/shard_map/ppermute | solution.py:524
  39.9 6.4 %collective-permute-start.15 = (f32[200,128]{1,0:T(8,128)S(1)}, f32[200,128]{1,0:T(8,128)S(1)}, u32[]{:S(2)}, u32[]{:S(2)}) collective-permute-start(f32[200,128]{1,0:T(8,128)S(1)} %get-tuple-element.161.refs_1_), channel_id=1, source_target_pairs={{0,2},{1,3},{2,0},{3,1},{4,6},{5,7},{6,4},{7,5},{8,10},{9,11},{10,... | collective-permute-start | bytes 307208 | tf_op jit(solution)/shard_map/ppermute | solution.py:524
  41.3 6.6 %collective-permute-start.17 = (f32[200,128]{1,0:T(8,128)S(1)}, f32[200,128]{1,0:T(8,128)S(1)}, u32[]{:S(2)}, u32[]{:S(2)}) collective-permute-start(f32[200,128]{1,0:T(8,128)S(1)} %get-tuple-element.164.refs_1_), channel_id=1, source_target_pairs={{0,2},{1,3},{2,0},{3,1},{4,6},{5,7},{6,4},{7,5},{8,10},{9,11},{10,... | collective-permute-start | bytes 307208 | tf_op jit(solution)/shard_map/ppermute | solution.py:524
  42.3 4.0 %collective-permute-start.16 = (f32[16,128]{1,0:T(8,128)S(1)}, f32[16,128]{1,0:T(8,128)S(1)}, u32[]{:S(2)}, u32[]{:S(2)}) collective-permute-start(f32[16,128]{1,0:T(8,128)S(1)} %get-tuple-element.162.refs_3_), channel_id=1, source_target_pairs={{0,9},{1,8},{2,11},{3,10},{4,13},{5,12},{6,15},{7,14},{8,1},{9,0},... | collective-permute-start | bytes 24584 | tf_op jit(solution)/shard_map/ppermute | solution.py:524
  46.3 6.0 %collective-permute-start.18 = (f32[216,128]{1,0:T(8,128)S(1)}, f32[216,128]{1,0:T(8,128)S(1)}, u32[]{:S(2)}, u32[]{:S(2)}) collective-permute-start(f32[216,128]{1,0:T(8,128)S(1)} %shard_map.113.refs_3_.refs_5_), channel_id=1, source_target_pairs={{0,12},{1,13},{2,14},{3,15},{4,0},{5,1},{6,2},{7,3},{8,4},{9,5},{1... | collective-permute-start | bytes 331784 | tf_op jit(solution)/shard_map/ppermute | solution.py:529
  47.9 6.0 %collective-permute-start.20 = (f32[200,128]{1,0:T(8,128)S(1)}, f32[200,128]{1,0:T(8,128)S(1)}, u32[]{:S(2)}, u32[]{:S(2)}) collective-permute-start(f32[200,128]{1,0:T(8,128)S(1)} %shard_map.114), channel_id=1, source_target_pairs={{0,12},{1,13},{2,14},{3,15},{4,0},{5,1},{6,2},{7,3},{8,4},{9,5},{1... | collective-permute-start | bytes 307208 | tf_op jit(solution)/shard_map/ppermute | solution.py:529
  52.3 5.5 %collective-permute-start.19 = (f32[216,128]{1,0:T(8,128)S(1)}, f32[216,128]{1,0:T(8,128)S(1)}, u32[]{:S(2)}, u32[]{:S(2)}) collective-permute-start(f32[216,128]{1,0:T(8,128)S(1)} %collective-permute-done.18.refs_3_), channel_id=1, source_target_pairs={{15,13},{14,12},{13,15},{12,14},{11,7},{10,6},{9,5},{8,4},{7,3},{6... | collective-permute-start | bytes 331784 | tf_op jit(solution)/shard_map/ppermute | solution.py:543
  53.9 5.0 %collective-permute-start.21 = (f32[200,128]{1,0:T(8,128)S(1)}, f32[200,128]{1,0:T(8,128)S(1)}, u32[]{:S(2)}, u32[]{:S(2)}) collective-permute-start(f32[200,128]{1,0:T(8,128)S(1)} %collective-permute-done.20.refs_3_), channel_id=1, source_target_pairs={{15,13},{14,12},{13,15},{12,14},{11,7},{10,6},{9,5},{8,4},{7,3},{6... | collective-permute-start | bytes 307208 | tf_op jit(solution)/shard_map/ppermute | solution.py:543
  57.9 4.8 %collective-permute-start.22 = (f32[208,128]{1,0:T(8,128)S(1)}, f32[208,128]{1,0:T(8,128)S(1)}, u32[]{:S(2)}, u32[]{:S(2)}) collective-permute-start(f32[208,128]{1,0:T(8,128)S(1)} %get-tuple-element.177), channel_id=1, source_target_pairs={{0,2},{1,3},{2,0},{3,1},{4,6},{5,7},{6,4},{7,5},{8,10},{9,11},{10,... | collective-permute-start | bytes 319496 | tf_op jit(solution)/shard_map/ppermute | solution.py:524
  59.0 4.7 %collective-permute-start.23 = (f32[192,128]{1,0:T(8,128)S(1)}, f32[192,128]{1,0:T(8,128)S(1)}, u32[]{:S(2)}, u32[]{:S(2)}) collective-permute-start(f32[192,128]{1,0:T(8,128)S(1)} %get-tuple-element.180), channel_id=1, source_target_pairs={{0,2},{1,3},{2,0},{3,1},{4,6},{5,7},{6,4},{7,5},{8,10},{9,11},{10,... | collective-permute-start | bytes 294920 | tf_op jit(solution)/shard_map/ppermute | solution.py:524
  62.7 1.5 %collective-permute-start.25 = (f32[384,128]{1,0:T(8,128)S(1)}, f32[384,128]{1,0:T(8,128)S(1)}, u32[]{:S(2)}, u32[]{:S(2)}) collective-permute-start(f32[384,128]{1,0:T(8,128)S(1)} %get-tuple-element.185), channel_id=1, source_target_pairs={{0,1},{1,0},{2,3},{3,2},{4,5},{5,4},{6,7},{7,6},{8,9},{9,8},{10,11... | collective-permute-start | bytes 589832 | tf_op jit(solution)/shard_map/ppermute | solution.py:524
  63.8 1.5 %collective-permute-start.24 = (f32[384,128]{1,0:T(8,128)S(1)}, f32[384,128]{1,0:T(8,128)S(1)}, u32[]{:S(2)}, u32[]{:S(2)}) collective-permute-start(f32[384,128]{1,0:T(8,128)S(1)} %get-tuple-element.182), channel_id=1, source_target_pairs={{0,1},{1,0},{2,3},{3,2},{4,5},{5,4},{6,7},{7,6},{8,9},{9,8},{10,11... | collective-permute-start | bytes 589832 | tf_op jit(solution)/shard_map/ppermute | solution.py:524

commit v6 on v5

--- a/solution.py
+++ b/solution.py
@@ -11,7 +11,8 @@
 C = 128
 EPSILON = 1e-06
 PLANE = 4
-WAVES = (2, 1)
+SECOND_WAVE = 0.5
+LOADED, STORED = 6, 3
 F32 = jnp.float32
 BF16 = jnp.bfloat16
 
@@ -84,11 +85,9 @@
 
 
 class Sizes:
-    def __init__(self, tokens, features, all_heads, count, wave, waves):
+    def __init__(self, tokens, features, all_heads, count, wave, first, heads):
         self.tokens, self.features, self.count = tokens, features, count
-        self.heads = all_heads // waves
-        self.first = wave * self.heads
-        self.wave = wave
+        self.heads, self.first, self.wave = heads, first, wave
         self.blocks = tokens // C
         self.width = features // all_heads
         self.half = self.width // 2
@@ -116,6 +115,12 @@
     def rows(self, h, size):
         return slice(h * size, (h + 1) * size)
 
+    def groups(self, most):
+        edges = [*range(0, self.heads, most), self.heads]
+        return [(a, b, pl.ds(a * self.width, (b - a) * self.width),
+                 pl.ds((self.first + a) * self.width, (b - a) * self.width))
+                for a, b in zip(edges[:-1], edges[1:])]
+
     def carry(self, j):
         return slice(self.heads + 2 + j, self.heads + 3 + j)
 
@@ -168,43 +173,38 @@
 
 
 def state_kernel(
-    s, keys, values, log_decay, doc_ids, keep, send, notes, cums, first_update, *near
+    s, told, keys, values, log_decay, doc_ids, keep, send, notes, cums, first_update, *near
 ):
-    each, waits, first = s.heads, [], s.first
+    waits, first = {}, s.first
     if near:
         near_keys, near_values, near_logs, near_ids, arrived, small = near
-        few = [
-            pltpu.make_async_copy(doc_ids, near_ids, small.at[0]),
-            pltpu.make_async_copy(log_decay, near_logs, small.at[1]),
-        ]
-        each = s.heads // arrived.shape[1]
-        for g in range(arrived.shape[1]):
-            far_part = pl.ds((s.first + g * each) * s.width, each * s.width)
-            part = pl.ds(g * each * s.width, each * s.width)
-            waits.append(
-                [
-                    pltpu.make_async_copy(keys.at[:, far_part], near_keys.at[:, part], arrived.at[0, g]),
-                    pltpu.make_async_copy(
-                        values.at[:, far_part], near_values.at[:, part], arrived.at[1, g]
-                    ),
-                ]
-            )
-        for copy in few + sum(waits, []):
+        ids_copy = pltpu.make_async_copy(doc_ids, near_ids, small.at[0])
+        logs_copy = pltpu.make_async_copy(log_decay, near_logs, small.at[1])
+        for g, (a, _, part, far_part) in enumerate(s.groups(LOADED)):
+            waits[a] = [
+                pltpu.make_async_copy(far.at[:, far_part], close.at[:, part], arrived.at[i, g])
+                for i, (far, close) in enumerate([(keys, near_keys), (values, near_values)])
+            ]
+        for copy in [logs_copy, ids_copy] + sum(waits.values(), []):
             copy.start()
-        for copy in few:
-            copy.wait()
+        logs_copy.wait()
         keys, values, log_decay, doc_ids, first = near_keys, near_values, near_logs, near_ids, 0
     core, _, _ = place_bits(s.count, False)
     lower = core == 0
+    logs = s.logs(log_decay)
+    totals = [total_rows(a) for a in logs]
+    factors = [jnp.exp(t) for t in totals]
+    columns = [decay_columns(a) for a in logs]
+    ends = [jnp.exp(a[C - 1 : C, :] - a) for a in columns]
+    for j, column in enumerate(columns):
+        cums[s.block(j), :] = column
     if near:
+        ids_copy.wait()
         docs = [jnp.full((1, s.width), doc_ids[j].astype(F32)) for j in range(s.blocks)]
         carries = [None] + [equal(docs[j - 1], docs[j]) for j in range(1, s.blocks)]
     else:
-        docs = [doc_ids[s.start : s.start + 1, :], doc_ids[s.end : s.end + 1, :]]
-        carries = [doc_ids[s.carry(j), :] for j in range(s.blocks)]
-    logs = s.logs(log_decay)
-    totals = [total_rows(a) for a in logs]
-    factors = [jnp.exp(t) for t in totals]
+        docs = [doc_ids[told.start : told.start + 1, :], doc_ids[told.end : told.end + 1, :]]
+        carries = [doc_ids[told.carry(j), :] for j in range(s.blocks)]
     whole_factor = factors[0]
     for j in range(1, s.blocks):
         whole_factor = whole_factor * factors[j] * carries[j]
@@ -217,14 +217,9 @@
         notes[s.carry(j), :] = carries[j]
     for j, rows in enumerate(factors):
         notes[s.factor(j, 0).start : s.factor(j, 0).start + s.heads, :] = rows
-    columns = [decay_columns(a) for a in logs]
-    ends = [jnp.exp(a[C - 1 : C, :] - a) for a in columns]
-    for j, column in enumerate(columns):
-        cums[s.block(j), :] = column
     for h in range(s.heads):
-        if waits and h % each == 0:
-            for copy in waits[h // each]:
-                copy.wait()
+        for copy in waits.get(h, ()):
+            copy.wait()
         place = slice((first + h) * s.width, (first + h + 1) * s.width)
         state = None
         for j in range(s.blocks):
@@ -466,28 +461,27 @@
 
 def final_kernel(s, waves, keys, values, cums, notes, key_local, value_local, back_terms, *rest):
     keep, received = rest[:2]
-    last = s.wave == waves - 1
+    last = s is waves[-1]
     near_outs = rest[-2:]
-    copies = []
+    copies, groups = [], []
     if last:
         *far_outs, far_gain, near_gain, sent = rest[-7:-2]
-        groups = sent.shape[1] - s.wave
+        groups = s.groups(STORED)
         own, other = rest[2 + 2 * s.wave : 4 + 2 * s.wave]
-        base = s.heads * s.quarter
-        for w in range(waves):
-            for h in range(s.heads):
-                row = w * s.gains + h
+        base = waves[0].heads * s.quarter
+        for wave in waves:
+            for h in range(wave.heads):
+                row = wave.wave * s.gains + h
                 total = own[row : row + 1, :] + other[base + row : base + row + 1, :]
-                place = (w * s.heads + h) * s.width
-                near_gain[place : place + s.width] = total.reshape(s.width)
+                near_gain[wave.head(h)] = total.reshape(s.width)
         copies.append(pltpu.make_async_copy(near_gain, far_gain, sent.at[2, 0]))
         copies[-1].start()
-        for w in range(s.wave):
-            place = pl.ds(w * s.columns, s.columns)
+        for w, wave in enumerate(waves[:-1]):
+            place = pl.ds(wave.first * s.width, wave.columns)
             for i, far in enumerate(far_outs):
                 near = rest[2 + 2 * w + i]
                 copies.append(
-                    pltpu.make_async_copy(near, far.at[:, place], sent.at[i, groups + w])
+                    pltpu.make_async_copy(near, far.at[:, place], sent.at[i, len(groups) + w])
                 )
                 copies[-1].start()
     core, _, _ = place_bits(s.count, True)
@@ -506,10 +500,9 @@
             if j > 0:
                 term = back_terms[s.rows((j - 1) * s.heads + h, s.width), :]
                 state = notes[s.carry(j), :] * (term + notes[s.factor(j, h), :] * state)
-        if last and (h + 1) * groups % s.heads == 0:
-            each, g = s.heads // groups, h * groups // s.heads
-            part = pl.ds(g * each * s.width, each * s.width)
-            far_part = pl.ds((s.first + g * each) * s.width, each * s.width)
+        for g, (_, stop, part, far_part) in enumerate(groups):
+            if h + 1 != stop:
+                continue
             for i, (near, far) in enumerate(zip(near_outs, far_outs)):
                 copies.append(
                     pltpu.make_async_copy(near.at[:, part], far.at[:, far_part], sent.at[i, g])
@@ -642,8 +635,9 @@
     tokens, features = queries.shape
     heads = log_decay.shape[1]
     count, dp = lax.axis_size("seq"), lax.axis_size("dp")
-    wave_count = max(w for w in WAVES if heads % w == 0)
-    waves = [Sizes(tokens, features, heads, count, w, wave_count) for w in range(wave_count)]
+    second = round(heads * SECOND_WAVE) if heads > 4 else 0
+    split = [(0, heads - second), (heads - second, second)][: 2 if second else 1]
+    waves = [Sizes(tokens, features, heads, count, w, *part) for w, part in enumerate(split)]
     bind = functools.partial
     unit = 2 * C * C * C * waves[0].blocks * waves[0].heads
     gain = norm_gain
@@ -651,7 +645,6 @@
     states = []
     far = [pltpu.with_memory_space_constraint(a, pltpu.HBM) for a in (keys, values, log_decay, doc_ids)]
     for s in waves:
-        groups = max(g for g in (3, 2, 1) if s.heads % g == 0)
         given = (keys, values, log_decay, doc_ids)
         spaces = [pltpu.VMEM] * 4
         scratch = []
@@ -662,13 +655,13 @@
                 pltpu.VMEM((tokens, s.columns), BF16),
                 pltpu.VMEM(log_decay.shape, F32),
                 pltpu.SMEM(doc_ids.shape, jnp.int32),
-                pltpu.SemaphoreType.DMA((2, groups)),
+                pltpu.SemaphoreType.DMA((2, len(s.groups(LOADED)))),
                 pltpu.SemaphoreType.DMA((2,)),
             ]
         else:
             given = (keys, values, log_decay, states[0][2])
         state = call(
-            bind(state_kernel, s),
+            bind(state_kernel, s, waves[0]),
             [
                 shape(s.heads * s.half, s.width),
                 shape(s.heads * s.half + s.tail, s.width),
@@ -752,6 +745,7 @@
             attentions[i],
             *sums,
             flops=unit,
+            deps=[token] if grads else [],
         )
         token = grad[0]
         grads.append(grad)
@@ -776,9 +770,8 @@
     entries, local_grads, token, gains = scan_in(waves, parts, True, token, beside_backward)
     done = []
     for i, s in enumerate(waves):
-        last = i == wave_count - 1
+        last = s is waves[-1]
         (held,) = after(token, log_decay)
-        groups = max(g for g in (3, 2, 1) if s.heads % g == 0)
         given = [
             keys, values, states[i][3], states[i][2], *local_grads[i], grads[i][5], *entries[i], *done,
         ]
@@ -789,7 +782,7 @@
             out_spaces = [pltpu.HBM] * 3
             scratch = [
                 pltpu.VMEM((features,), F32),
-                pltpu.SemaphoreType.DMA((3, groups + i)),
+                pltpu.SemaphoreType.DMA((3, len(s.groups(STORED)) + i)),
                 pltpu.VMEM((tokens, s.columns), BF16),
                 pltpu.VMEM((tokens, s.columns), BF16),
             ]
@@ -797,7 +790,7 @@
             outs = [shape(tokens, s.columns, BF16)] * 2
             out_spaces = [pltpu.VMEM] * 2
         made = call(
-            bind(final_kernel, s, wave_count),
+            bind(final_kernel, s, waves),
             outs,
             *given,
             flops=4 * unit,

time: 66.9 us -> 66.6 us (level)
  no operation moved by 1% of the time
where the time goes in v6:
time: 66.6 us; the launch traced here: 66.4 us
  waiting for transfers between devices  27.5 us (41%)
  starting transfers between devices  22.9 us (34%)
  Pallas kernels  15.1 us (23%)
  between operations  0.87 us (1%)
    pallas_call x28, Pallas kernels, call(): pl.pallas_call(lambda *refs: kernel(*refs[:given], *refs[given + len(deps...  15.1 us
    ppermute x18, starting transfers between devices, swap(): return lax.ppermute(value, axis, [(i, i ^ bit) for i in range(count)])  14.5 us
    ppermute x18, waiting for transfers between devices, swap(): return lax.ppermute(value, axis, [(i, i ^ bit) for i in range(count)])  14 us
    ppermute x4, waiting for transfers between devices, pass_on(): return lax.ppermute(value, 'seq', pairs)  6.94 us
    ppermute x4, waiting for transfers between devices, next_plane(): lax.ppermute(value, 'seq', [(i, (i + step) % count) for i in range(count)])  6.52 us
    ppermute x4, starting transfers between devices, next_plane(): lax.ppermute(value, 'seq', [(i, (i + step) % count) for i in range(count)])  5.75 us
    ppermute x4, starting transfers between devices, pass_on(): return lax.ppermute(value, 'seq', pairs)  2.69 us
  transfers between devices with their start and end apart: 26, of which 16 were waited for; matrix products, arithmetic and copies ran while one was open for 0% of the time, Pallas kernels for 15%

profile of v6, /device:TPU:0, one launch (start us, length us, event | category | flops | bytes accessed | tf_op | source)
XLA Modules:
  0.0 66.4 jit_solution(5345621029109838947)
XLA Ops:
  0.7 2.0 %shard_map.94 = (f32[384,128]{1,0:T(8,128)S(1)}, f32[392,128]{1,0:T(8,128)S(1)}, f32[24,128]{1,0:T(8,128)S(1)}, f32[256,6]{1,0:T(8,128)S(1)}, f32[768,128]{1,0:T(8,128)S(1)}) custom-call(bf16[256,1536]{1,0:T(8,128)(2,1)} %refs_0_.13, bf16[256,1536]{1,0:T(8,128)(2,1)} %refs_1_.13, f32[12,256]{1,0:T(8,128)} %bitcast.1, s32[2]{0:T(128)} %refs_3_.1), custom_call_target="tpu_custom_call" | custom-call | flops 50331648 | bytes 2394120 | tf_op jit(solution)/shard_map/pallas_call | solution.py:143
  2.6 0.5 collective-permute-start
  3.2 0.8 %shard_map.95 = (f32[384,128]{1,0:T(8,128)S(1)}, f32[392,128]{1,0:T(8,128)S(1)}, f32[24,128]{1,0:T(8,128)S(1)}, f32[256,6]{1,0:T(8,128)S(1)}, f32[768,128]{1,0:T(8,128)S(1)}) custom-call(bf16[256,1536]{1,0:T(8,128)(2,1)S(1)} %copy-done.2, bf16[256,1536]{1,0:T(8,128)(2,1)S(1)} %copy-done.1, f32[12,256]{1,0:T(8,128)S(1)} %bitcast.2, ...), custom_call_target="tpu_custom_call" | custom-call | flops 50331648 | bytes 2406400 | tf_op jit(solution)/shard_map/pallas_call | solution.py:143
  3.9 0.1 collective-permute-start.1
  4.1 0.2 collective-permute-done.refs_1_.refs_3_
  4.3 2.9 %collective-permute-start.2 = (f32[200,128]{1,0:T(8,128)S(1)}, f32[200,128]{1,0:T(8,128)S(1)}, u32[]{:S(2)}, u32[]{:S(2)}) collective-permute-start(f32[200,128]{1,0:T(8,128)S(1)} %get-tuple-element.117.refs_1_), channel_id=1, source_target_pairs={{0,2},{1,3},{2,0},{3,1},{4,6},{5,7},{6,4},{7,5},{8,10},{9,11},{10,... | collective-permute-start | bytes 307208 | tf_op jit(solution)/shard_map/ppermute | solution.py:517
  7.3 0.9 %collective-permute-start.3 = (f32[200,128]{1,0:T(8,128)S(1)}, f32[200,128]{1,0:T(8,128)S(1)}, u32[]{:S(2)}, u32[]{:S(2)}) collective-permute-start(f32[200,128]{1,0:T(8,128)S(1)} %get-tuple-element.119.refs_1_), channel_id=1, source_target_pairs={{0,2},{1,3},{2,0},{3,1},{4,6},{5,7},{6,4},{7,5},{8,10},{9,11},{10,... | collective-permute-start | bytes 307208 | tf_op jit(solution)/shard_map/ppermute | solution.py:517
  8.2 2.0 %shard_map.98 = (f32[256,768]{1,0:T(8,128)S(1)}, bf16[1536,128]{1,0:T(8,128)(2,1)S(1)}) custom-call(bf16[256,1536]{1,0:T(8,128)(2,1)S(1)} %copy-done, bf16[256,1536]{1,0:T(8,128)(2,1)S(1)} %copy-done.2, bf16[256,1536]{1,0:T(8,128)(2,1)S(1)} %copy-done.1, f32[12,256]{1,0:T(8,128)S(1)} %bitcast.3, f32[256,6]{1,0:T(8,128)S(1)} %get-tuple-element.114.refs_4_.refs_3_.refs_2_, ...), custom_call_target="tpu_custom_call" | custom-call | flops 100663296 | bytes 3563520 | tf_op jit(solution)/shard_map/pallas_call | solution.py:143
  10.2 0.6 collective-permute-done.2.refs_2_
  10.9 2.2 %collective-permute-start.4 = (f32[200,128]{1,0:T(8,128)S(1)}, f32[200,128]{1,0:T(8,128)S(1)}, u32[]{:S(2)}, u32[]{:S(2)}) collective-permute-start(f32[200,128]{1,0:T(8,128)S(1)} %shard_map.99.refs_3_), channel_id=1, source_target_pairs={{0,4},{1,5},{2,6},{3,7},{4,8},{5,9},{6,10},{7,11},{8,12},{9,13},{1... | collective-permute-start | bytes 307208 | tf_op jit(solution)/shard_map/ppermute | solution.py:522
  13.2 1.6 %collective-permute-start.6 = (f32[200,128]{1,0:T(8,128)S(1)}, f32[200,128]{1,0:T(8,128)S(1)}, u32[]{:S(2)}, u32[]{:S(2)}) collective-permute-start(f32[200,128]{1,0:T(8,128)S(1)} %shard_map.100), channel_id=1, source_target_pairs={{0,4},{1,5},{2,6},{3,7},{4,8},{5,9},{6,10},{7,11},{8,12},{9,13},{1... | collective-permute-start | bytes 307208 | tf_op jit(solution)/shard_map/ppermute | solution.py:522
  14.8 2.0 %shard_map.101 = (f32[256,768]{1,0:T(8,128)S(1)}, bf16[1536,128]{1,0:T(8,128)(2,1)S(1)}) custom-call(bf16[256,1536]{1,0:T(8,128)(2,1)S(1)} %copy-done, bf16[256,1536]{1,0:T(8,128)(2,1)S(1)} %copy-done.2, bf16[256,1536]{1,0:T(8,128)(2,1)S(1)} %copy-done.1, f32[12,256]{1,0:T(8,128)S(1)} %bitcast.4, f32[256,6]{1,0:T(8,128)S(1)} %get-tuple-element.100.refs_4_.refs_3_.refs_2_, ...), custom_call_target="tpu_custom_call" | custom-call | flops 100663296 | bytes 3563520 | tf_op jit(solution)/shard_map/pallas_call | solution.py:143
  16.8 2.1 %collective-permute-done.4.refs_3_ = f32[200,128]{1,0:T(8,128)S(1)} collective-permute-done((f32[200,128]{1,0:T(8,128)S(1)}, f32[200,128]{1,0:T(8,128)S(1)}, u32[]{:S(2)}, u32[]{:S(2)}) %collective-permute-start.4) | collective-permute-done | bytes 102432 | tf_op jit(solution)/shard_map/ppermute | solution.py:522
  18.9 1.5 %collective-permute-start.5 = (f32[200,128]{1,0:T(8,128)S(1)}, f32[200,128]{1,0:T(8,128)S(1)}, u32[]{:S(2)}, u32[]{:S(2)}) collective-permute-start(f32[200,128]{1,0:T(8,128)S(1)} %collective-permute-done.4.refs_3_), channel_id=1, source_target_pairs={{0,2},{1,3},{2,0},{3,1},{4,8},{5,9},{6,10},{7,11},{8,12},{9,13},{1... | collective-permute-start | bytes 307208 | tf_op jit(solution)/shard_map/ppermute | solution.py:536
  20.4 1.1 %collective-permute-start.7 = (f32[200,128]{1,0:T(8,128)S(1)}, f32[200,128]{1,0:T(8,128)S(1)}, u32[]{:S(2)}, u32[]{:S(2)}) collective-permute-start(f32[200,128]{1,0:T(8,128)S(1)} %collective-permute-done.6.refs_3_), channel_id=1, source_target_pairs={{0,2},{1,3},{2,0},{3,1},{4,8},{5,9},{6,10},{7,11},{8,12},{9,13},{1... | collective-permute-start | bytes 307208 | tf_op jit(solution)/shard_map/ppermute | solution.py:536
  21.5 3.1 %collective-permute-done.5.refs_4_ = f32[200,128]{1,0:T(8,128)S(1)} collective-permute-done((f32[200,128]{1,0:T(8,128)S(1)}, f32[200,128]{1,0:T(8,128)S(1)}, u32[]{:S(2)}, u32[]{:S(2)}) %collective-permute-start.5) | collective-permute-done | bytes 102432 | tf_op jit(solution)/shard_map/ppermute | solution.py:536
  24.6 1.6 %collective-permute-start.8 = (f32[192,128]{1,0:T(8,128)S(1)}, f32[192,128]{1,0:T(8,128)S(1)}, u32[]{:S(2)}, u32[]{:S(2)}) collective-permute-start(f32[192,128]{1,0:T(8,128)S(1)} %get-tuple-element.130), channel_id=1, source_target_pairs={{0,2},{1,3},{2,0},{3,1},{4,6},{5,7},{6,4},{7,5},{8,10},{9,11},{10,... | collective-permute-start | bytes 294920 | tf_op jit(solution)/shard_map/ppermute | solution.py:517
  26.3 1.3 %collective-permute-start.9 = (f32[192,128]{1,0:T(8,128)S(1)}, f32[192,128]{1,0:T(8,128)S(1)}, u32[]{:S(2)}, u32[]{:S(2)}) collective-permute-start(f32[192,128]{1,0:T(8,128)S(1)} %get-tuple-element.133), channel_id=1, source_target_pairs={{0,2},{1,3},{2,0},{3,1},{4,6},{5,7},{6,4},{7,5},{8,10},{9,11},{10,... | collective-permute-start | bytes 294920 | tf_op jit(solution)/shard_map/ppermute | solution.py:517
  27.7 1.7 %collective-permute-done.8.refs_1_ = f32[192,128]{1,0:T(8,128)S(1)} collective-permute-done((f32[192,128]{1,0:T(8,128)S(1)}, f32[192,128]{1,0:T(8,128)S(1)}, u32[]{:S(2)}, u32[]{:S(2)}) %collective-permute-start.8) | collective-permute-done | bytes 98336 | tf_op jit(solution)/shard_map/ppermute | solution.py:517
  29.3 0.1 shard_map.104
  29.5 1.5 %collective-permute-done.9.refs_1_ = f32[192,128]{1,0:T(8,128)S(1)} collective-permute-done((f32[192,128]{1,0:T(8,128)S(1)}, f32[192,128]{1,0:T(8,128)S(1)}, u32[]{:S(2)}, u32[]{:S(2)}) %collective-permute-start.9) | collective-permute-done | bytes 98336 | tf_op jit(solution)/shard_map/ppermute | solution.py:517
  31.2 0.6 shard_map.106
  31.8 0.8 %collective-permute-done.10.refs_8_ = f32[384,128]{1,0:T(8,128)S(1)} collective-permute-done((f32[384,128]{1,0:T(8,128)S(1)}, f32[384,128]{1,0:T(8,128)S(1)}, u32[]{:S(2)}, u32[]{:S(2)}) %collective-permute-start.10) | collective-permute-done | bytes 196640 | tf_op jit(solution)/shard_map/ppermute | solution.py:517
  32.6 0.6 shard_map.107
  33.2 1.6 %collective-permute-start.12 = (f32[8,256]{1,0:T(8,128)S(1)}, f32[8,256]{1,0:T(8,128)S(1)}, u32[]{:S(2)}, u32[]{:S(2)}) collective-permute-start(f32[8,256]{1,0:T(8,128)S(1)} %get-tuple-element.140.refs_6_), channel_id=1, source_target_pairs={{0,16},{16,0},{1,17},{17,1},{2,18},{18,2},{3,19},{19,3},{4,20},{20... | collective-permute-start | bytes 24584 | tf_op jit(solution)/shard_map/ppermute | solution.py:517
  34.8 2.1 %collective-permute-done.12.refs_7_ = f32[8,256]{1,0:T(8,128)S(1)} collective-permute-done((f32[8,256]{1,0:T(8,128)S(1)}, f32[8,256]{1,0:T(8,128)S(1)}, u32[]{:S(2)}, u32[]{:S(2)}) %collective-permute-start.12) | collective-permute-done | bytes 8224 | tf_op jit(solution)/shard_map/ppermute | solution.py:517
  36.9 0.9 %shard_map.108 = (bf16[256,768]{1,0:T(8,128)(2,1)S(1)}, f32[384,128]{1,0:T(8,128)S(1)}, f32[400,128]{1,0:T(8,128)S(1)}, f32[8,128]{1,0:T(8,128)S(1)}, f32[8,128]{1,0:T(8,128)S(1)}, /*index=5*/f32[768,128]{1,0:T(8,128)S(1)}) custom-call(bf16[256,1536]{1,0:T(8,128)(2,1)S(1)} %copy-done, bf16[256,1536]{1,0:T(8,128)(2,1)S(1)} %copy-done.3, f32[1536]{0:T(1024)S(1)} %copy-done.5, ...), custom_call_target="tpu_custom_call" | custom-call | flops 50331648 | bytes 3596288 | tf_op jit(solution)/shard_map/pallas_call | solution.py:143
  37.9 0.9 %shard_map.109 = (bf16[256,768]{1,0:T(8,128)(2,1)S(1)}, f32[384,128]{1,0:T(8,128)S(1)}, f32[400,128]{1,0:T(8,128)S(1)}, f32[8,128]{1,0:T(8,128)S(1)}, f32[8,128]{1,0:T(8,128)S(1)}, /*index=5*/f32[768,128]{1,0:T(8,128)S(1)}) custom-call(bf16[256,1536]{1,0:T(8,128)(2,1)S(1)} %copy-done, bf16[256,1536]{1,0:T(8,128)(2,1)S(1)} %copy-done.3, f32[1536]{0:T(1024)S(1)} %copy-done.5, ...), custom_call_target="tpu_custom_call" | custom-call | flops 50331648 | bytes 3596288 | tf_op jit(solution)/shard_map/pallas_call | solution.py:143
  38.9 0.6 collective-permute-start.14
  39.5 1.3 %collective-permute-start.15 = (f32[200,128]{1,0:T(8,128)S(1)}, f32[200,128]{1,0:T(8,128)S(1)}, u32[]{:S(2)}, u32[]{:S(2)}) collective-permute-start(f32[200,128]{1,0:T(8,128)S(1)} %get-tuple-element.161.refs_1_), channel_id=1, source_target_pairs={{0,2},{1,3},{2,0},{3,1},{4,6},{5,7},{6,4},{7,5},{8,10},{9,11},{10,... | collective-permute-start | bytes 307208 | tf_op jit(solution)/shard_map/ppermute | solution.py:517
  40.9 1.0 %collective-permute-start.17 = (f32[200,128]{1,0:T(8,128)S(1)}, f32[200,128]{1,0:T(8,128)S(1)}, u32[]{:S(2)}, u32[]{:S(2)}) collective-permute-start(f32[200,128]{1,0:T(8,128)S(1)} %get-tuple-element.164.refs_1_), channel_id=1, source_target_pairs={{0,2},{1,3},{2,0},{3,1},{4,6},{5,7},{6,4},{7,5},{8,10},{9,11},{10,... | collective-permute-start | bytes 307208 | tf_op jit(solution)/shard_map/ppermute | solution.py:517
  41.9 1.1 %shard_map.112 = (f32[256,768]{1,0:T(8,128)S(1)}, f32[256,768]{1,0:T(8,128)S(1)}) custom-call(bf16[256,1536]{1,0:T(8,128)(2,1)S(1)} %copy-done, bf16[256,1536]{1,0:T(8,128)(2,1)S(1)} %copy-done.1, f32[12,256]{1,0:T(8,128)S(1)} %bitcast.5, f32[256,6]{1,0:T(8,128)S(1)} %get-tuple-element.114.refs_4_.refs_3_.refs_2_, ...), custom_call_target="tpu_custom_call" | custom-call | flops 150994944 | bytes 3950592 | tf_op jit(solution)/shard_map/pallas_call | solution.py:143
  43.1 2.8 %collective-permute-done.16.refs_4_ = f32[16,128]{1,0:T(8,128)S(1)} collective-permute-done((f32[16,128]{1,0:T(8,128)S(1)}, f32[16,128]{1,0:T(8,128)S(1)}, u32[]{:S(2)}, u32[]{:S(2)}) %collective-permute-start.16) | collective-permute-done | bytes 8224 | tf_op jit(solution)/shard_map/ppermute | solution.py:517
  45.9 1.5 %collective-permute-start.18 = (f32[216,128]{1,0:T(8,128)S(1)}, f32[216,128]{1,0:T(8,128)S(1)}, u32[]{:S(2)}, u32[]{:S(2)}) collective-permute-start(f32[216,128]{1,0:T(8,128)S(1)} %shard_map.113.refs_3_.refs_5_), channel_id=1, source_target_pairs={{0,12},{1,13},{2,14},{3,15},{4,0},{5,1},{6,2},{7,3},{8,4},{9,5},{1... | collective-permute-start | bytes 331784 | tf_op jit(solution)/shard_map/ppermute | solution.py:522
  47.5 0.4 collective-permute-start.20
  47.9 1.1 %shard_map.115 = (f32[256,768]{1,0:T(8,128)S(1)}, f32[256,768]{1,0:T(8,128)S(1)}) custom-call(bf16[256,1536]{1,0:T(8,128)(2,1)S(1)} %copy-done, bf16[256,1536]{1,0:T(8,128)(2,1)S(1)} %copy-done.1, f32[12,256]{1,0:T(8,128)S(1)} %bitcast.6, f32[256,6]{1,0:T(8,128)S(1)} %get-tuple-element.100.refs_4_.refs_3_.refs_2_, ...), custom_call_target="tpu_custom_call" | custom-call | flops 150994944 | bytes 3950592 | tf_op jit(solution)/shard_map/pallas_call | solution.py:143
  49.1 2.8 %collective-permute-done.18.refs_3_ = f32[216,128]{1,0:T(8,128)S(1)} collective-permute-done((f32[216,128]{1,0:T(8,128)S(1)}, f32[216,128]{1,0:T(8,128)S(1)}, u32[]{:S(2)}, u32[]{:S(2)}) %collective-permute-start.18) | collective-permute-done | bytes 110624 | tf_op jit(solution)/shard_map/ppermute | solution.py:522
  51.9 1.6 %collective-permute-done.20.refs_3_ = f32[200,128]{1,0:T(8,128)S(1)} collective-permute-done((f32[200,128]{1,0:T(8,128)S(1)}, f32[200,128]{1,0:T(8,128)S(1)}, u32[]{:S(2)}, u32[]{:S(2)}) %collective-permute-start.20) | collective-permute-done | bytes 102432 | tf_op jit(solution)/shard_map/ppermute | solution.py:522
  53.5 0.1 collective-permute-start.21
  53.6 3.8 %collective-permute-done.19.refs_4_ = f32[216,128]{1,0:T(8,128)S(1)} collective-permute-done((f32[216,128]{1,0:T(8,128)S(1)}, f32[216,128]{1,0:T(8,128)S(1)}, u32[]{:S(2)}, u32[]{:S(2)}) %collective-permute-start.19) | collective-permute-done | bytes 110624 | tf_op jit(solution)/shard_map/ppermute | solution.py:536
  57.5 1.0 %collective-permute-start.22 = (f32[208,128]{1,0:T(8,128)S(1)}, f32[208,128]{1,0:T(8,128)S(1)}, u32[]{:S(2)}, u32[]{:S(2)}) collective-permute-start(f32[208,128]{1,0:T(8,128)S(1)} %get-tuple-element.177), channel_id=1, source_target_pairs={{0,2},{1,3},{2,0},{3,1},{4,6},{5,7},{6,4},{7,5},{8,10},{9,11},{10,... | collective-permute-start | bytes 319496 | tf_op jit(solution)/shard_map/ppermute | solution.py:517
  58.6 1.1 %collective-permute-start.23 = (f32[192,128]{1,0:T(8,128)S(1)}, f32[192,128]{1,0:T(8,128)S(1)}, u32[]{:S(2)}, u32[]{:S(2)}) collective-permute-start(f32[192,128]{1,0:T(8,128)S(1)} %get-tuple-element.180), channel_id=1, source_target_pairs={{0,2},{1,3},{2,0},{3,1},{4,6},{5,7},{6,4},{7,5},{8,10},{9,11},{10,... | collective-permute-start | bytes 294920 | tf_op jit(solution)/shard_map/ppermute | solution.py:517
  59.7 2.5 %collective-permute-done.22.refs_1_.refs_12_ = f32[208,128]{1,0:T(8,128)S(1)} collective-permute-done((f32[208,128]{1,0:T(8,128)S(1)}, f32[208,128]{1,0:T(8,128)S(1)}, u32[]{:S(2)}, u32[]{:S(2)}) %collective-permute-start.22) | collective-permute-done | bytes 106528 | tf_op jit(solution)/shard_map/ppermute | solution.py:517
  62.4 0.9 %collective-permute-done.23.refs_1_ = f32[192,128]{1,0:T(8,128)S(1)} collective-permute-done((f32[192,128]{1,0:T(8,128)S(1)}, f32[192,128]{1,0:T(8,128)S(1)}, u32[]{:S(2)}, u32[]{:S(2)}) %collective-permute-start.23) | collective-permute-done | bytes 98336 | tf_op jit(solution)/shard_map/ppermute | solution.py:517
  63.5 0.4 collective-permute-done.25.refs_8_
  63.8 0.6 shard_map.120
  64.5 0.4 collective-permute-done.24.refs_8_
  64.9 1.5 %shard_map.121 = (bf16[256,1536]{1,0:T(8,128)(2,1)}, bf16[256,1536]{1,0:T(8,128)(2,1)}, f32[1536]{0:T(1024)}) custom-call(bf16[256,1536]{1,0:T(8,128)(2,1)S(1)} %copy-done.2, bf16[256,1536]{1,0:T(8,128)(2,1)S(1)} %copy-done.1, f32[256,6]{1,0:T(8,128)S(1)} %get-tuple-element.100.refs_4_.refs_3_.refs_2_, ...), custom_call_target="tpu_custom_call" | custom-call | flops 201326592 | bytes 6430720 | tf_op jit(solution)/shard_map/pallas_call | solution.py:143
  (44 shorter events, 1.2 us)
Async XLA Ops:
  0.6 2.5 %copy-start.1 = (bf16[256,1536]{1,0:T(8,128)(2,1)S(1)}, bf16[256,1536]{1,0:T(8,128)(2,1)}, u32[]{:S(2)}) copy-start(bf16[256,1536]{1,0:T(8,128)(2,1)} %refs_1_.13) | copy-start | bytes 2359300
  0.6 2.5 %copy-start.2 = (bf16[256,1536]{1,0:T(8,128)(2,1)S(1)}, bf16[256,1536]{1,0:T(8,128)(2,1)}, u32[]{:S(2)}) copy-start(bf16[256,1536]{1,0:T(8,128)(2,1)} %refs_0_.13) | copy-start | bytes 2359300
  0.7 2.5 %copy-start.4 = (f32[256,12]{0,1:T(8,128)S(1)}, f32[256,12]{0,1:T(8,128)}, u32[]{:S(2)}) copy-start(f32[256,12]{0,1:T(8,128)} %param.11) | copy-start | bytes 36868
  2.6 1.6 %collective-permute-start = (f32[392,128]{1,0:T(8,128)S(1)}, f32[392,128]{1,0:T(8,128)S(1)}, u32[]{:S(2)}, u32[]{:S(2)}) collective-permute-start(f32[392,128]{1,0:T(8,128)S(1)} %get-tuple-element.107), channel_id=1, source_target_pairs={{0,1},{1,0},{2,3},{3,2},{4,5},{5,4},{6,7},{7,6},{8,9},{9,8},{10,11... | collective-permute-start | bytes 602120 | tf_op jit(solution)/shard_map/ppermute | solution.py:517
  3.9 4.3 %copy-start = (bf16[256,1536]{1,0:T(8,128)(2,1)S(1)}, bf16[256,1536]{1,0:T(8,128)(2,1)}, u32[]{:S(2)}) copy-start(bf16[256,1536]{1,0:T(8,128)(2,1)} %refs_0_.11) | copy-start | bytes 2359300
  3.9 3.3 %collective-permute-start.1 = (f32[392,128]{1,0:T(8,128)S(1)}, f32[392,128]{1,0:T(8,128)S(1)}, u32[]{:S(2)}, u32[]{:S(2)}) collective-permute-start(f32[392,128]{1,0:T(8,128)S(1)} %get-tuple-element.110), channel_id=1, source_target_pairs={{0,1},{1,0},{2,3},{3,2},{4,5},{5,4},{6,7},{7,6},{8,9},{9,8},{10,11... | collective-permute-start | bytes 602120 | tf_op jit(solution)/shard_map/ppermute | solution.py:517
  4.3 6.6 %collective-permute-start.2 = (f32[200,128]{1,0:T(8,128)S(1)}, f32[200,128]{1,0:T(8,128)S(1)}, u32[]{:S(2)}, u32[]{:S(2)}) collective-permute-start(f32[200,128]{1,0:T(8,128)S(1)} %get-tuple-element.117.refs_1_), channel_id=1, source_target_pairs={{0,2},{1,3},{2,0},{3,1},{4,6},{5,7},{6,4},{7,5},{8,10},{9,11},{10,... | collective-permute-start | bytes 307208 | tf_op jit(solution)/shard_map/ppermute | solution.py:517
  7.2 1.0 %copy-start.5 = (f32[1536]{0:T(1024)S(1)}, f32[1536]{0:T(1024)}, u32[]{:S(2)}) copy-start(f32[1536]{0:T(1024)} %refs_2_.5) | copy-start | bytes 18436
  7.3 5.8 %collective-permute-start.3 = (f32[200,128]{1,0:T(8,128)S(1)}, f32[200,128]{1,0:T(8,128)S(1)}, u32[]{:S(2)}, u32[]{:S(2)}) collective-permute-start(f32[200,128]{1,0:T(8,128)S(1)} %get-tuple-element.119.refs_1_), channel_id=1, source_target_pairs={{0,2},{1,3},{2,0},{3,1},{4,6},{5,7},{6,4},{7,5},{8,10},{9,11},{10,... | collective-permute-start | bytes 307208 | tf_op jit(solution)/shard_map/ppermute | solution.py:517
  10.9 7.9 %collective-permute-start.4 = (f32[200,128]{1,0:T(8,128)S(1)}, f32[200,128]{1,0:T(8,128)S(1)}, u32[]{:S(2)}, u32[]{:S(2)}) collective-permute-start(f32[200,128]{1,0:T(8,128)S(1)} %shard_map.99.refs_3_), channel_id=1, source_target_pairs={{0,4},{1,5},{2,6},{3,7},{4,8},{5,9},{6,10},{7,11},{8,12},{9,13},{1... | collective-permute-start | bytes 307208 | tf_op jit(solution)/shard_map/ppermute | solution.py:522
  13.2 7.2 %collective-permute-start.6 = (f32[200,128]{1,0:T(8,128)S(1)}, f32[200,128]{1,0:T(8,128)S(1)}, u32[]{:S(2)}, u32[]{:S(2)}) collective-permute-start(f32[200,128]{1,0:T(8,128)S(1)} %shard_map.100), channel_id=1, source_target_pairs={{0,4},{1,5},{2,6},{3,7},{4,8},{5,9},{6,10},{7,11},{8,12},{9,13},{1... | collective-permute-start | bytes 307208 | tf_op jit(solution)/shard_map/ppermute | solution.py:522
  18.9 5.7 %collective-permute-start.5 = (f32[200,128]{1,0:T(8,128)S(1)}, f32[200,128]{1,0:T(8,128)S(1)}, u32[]{:S(2)}, u32[]{:S(2)}) collective-permute-start(f32[200,128]{1,0:T(8,128)S(1)} %collective-permute-done.4.refs_3_), channel_id=1, source_target_pairs={{0,2},{1,3},{2,0},{3,1},{4,8},{5,9},{6,10},{7,11},{8,12},{9,13},{1... | collective-permute-start | bytes 307208 | tf_op jit(solution)/shard_map/ppermute | solution.py:536
  20.4 5.9 %collective-permute-start.7 = (f32[200,128]{1,0:T(8,128)S(1)}, f32[200,128]{1,0:T(8,128)S(1)}, u32[]{:S(2)}, u32[]{:S(2)}) collective-permute-start(f32[200,128]{1,0:T(8,128)S(1)} %collective-permute-done.6.refs_3_), channel_id=1, source_target_pairs={{0,2},{1,3},{2,0},{3,1},{4,8},{5,9},{6,10},{7,11},{8,12},{9,13},{1... | collective-permute-start | bytes 307208 | tf_op jit(solution)/shard_map/ppermute | solution.py:536
  24.6 4.7 %collective-permute-start.8 = (f32[192,128]{1,0:T(8,128)S(1)}, f32[192,128]{1,0:T(8,128)S(1)}, u32[]{:S(2)}, u32[]{:S(2)}) collective-permute-start(f32[192,128]{1,0:T(8,128)S(1)} %get-tuple-element.130), channel_id=1, source_target_pairs={{0,2},{1,3},{2,0},{3,1},{4,6},{5,7},{6,4},{7,5},{8,10},{9,11},{10,... | collective-permute-start | bytes 294920 | tf_op jit(solution)/shard_map/ppermute | solution.py:517
  26.3 4.9 %copy-start.3 = (bf16[256,1536]{1,0:T(8,128)(2,1)S(1)}, bf16[256,1536]{1,0:T(8,128)(2,1)}, u32[]{:S(2)}) copy-start(bf16[256,1536]{1,0:T(8,128)(2,1)} %refs_1_.9) | copy-start | bytes 2359300
  26.3 4.7 %collective-permute-start.9 = (f32[192,128]{1,0:T(8,128)S(1)}, f32[192,128]{1,0:T(8,128)S(1)}, u32[]{:S(2)}, u32[]{:S(2)}) collective-permute-start(f32[192,128]{1,0:T(8,128)S(1)} %get-tuple-element.133), channel_id=1, source_target_pairs={{0,2},{1,3},{2,0},{3,1},{4,6},{5,7},{6,4},{7,5},{8,10},{9,11},{10,... | collective-permute-start | bytes 294920 | tf_op jit(solution)/shard_map/ppermute | solution.py:517
  29.4 1.8 %collective-permute-start.11 = (f32[384,128]{1,0:T(8,128)S(1)}, f32[384,128]{1,0:T(8,128)S(1)}, u32[]{:S(2)}, u32[]{:S(2)}) collective-permute-start(f32[384,128]{1,0:T(8,128)S(1)} %get-tuple-element.137), channel_id=1, source_target_pairs={{0,1},{1,0},{2,3},{3,2},{4,5},{5,4},{6,7},{7,6},{8,9},{9,8},{10,11... | collective-permute-start | bytes 589832 | tf_op jit(solution)/shard_map/ppermute | solution.py:517
  31.1 1.5 %collective-permute-start.10 = (f32[384,128]{1,0:T(8,128)S(1)}, f32[384,128]{1,0:T(8,128)S(1)}, u32[]{:S(2)}, u32[]{:S(2)}) collective-permute-start(f32[384,128]{1,0:T(8,128)S(1)} %get-tuple-element.135), channel_id=1, source_target_pairs={{0,1},{1,0},{2,3},{3,2},{4,5},{5,4},{6,7},{7,6},{8,9},{9,8},{10,11... | collective-permute-start | bytes 589832 | tf_op jit(solution)/shard_map/ppermute | solution.py:517
  33.2 3.7 %collective-permute-start.12 = (f32[8,256]{1,0:T(8,128)S(1)}, f32[8,256]{1,0:T(8,128)S(1)}, u32[]{:S(2)}, u32[]{:S(2)}) collective-permute-start(f32[8,256]{1,0:T(8,128)S(1)} %get-tuple-element.140.refs_6_), channel_id=1, source_target_pairs={{0,16},{16,0},{1,17},{17,1},{2,18},{18,2},{3,19},{19,3},{4,20},{20... | collective-permute-start | bytes 24584 | tf_op jit(solution)/shard_map/ppermute | solution.py:517
  37.9 1.6 %collective-permute-start.13 = (f32[400,128]{1,0:T(8,128)S(1)}, f32[400,128]{1,0:T(8,128)S(1)}, u32[]{:S(2)}, u32[]{:S(2)}) collective-permute-start(f32[400,128]{1,0:T(8,128)S(1)} %get-tuple-element.146), channel_id=1, source_target_pairs={{0,1},{1,0},{2,3},{3,2},{4,5},{5,4},{6,7},{7,6},{8,9},{9,8},{10,11... | collective-permute-start | bytes 614408 | tf_op jit(solution)/shard_map/ppermute | solution.py:517
  38.9 2.0 %collective-permute-start.14 = (f32[400,128]{1,0:T(8,128)S(1)}, f32[400,128]{1,0:T(8,128)S(1)}, u32[]{:S(2)}, u32[]{:S(2)}) collective-permute-start(f32[400,128]{1,0:T(8,128)S(1)} %get-tuple-element.152), channel_id=1, source_target_pairs={{0,1},{1,0},{2,3},{3,2},{4,5},{5,4},{6,7},{7,6},{8,9},{9,8},{10,11... | collective-permute-start | bytes 614408 | tf_op jit(solution)/shard_map/ppermute | solution.py:517
  39.5 6.4 %collective-permute-start.15 = (f32[200,128]{1,0:T(8,128)S(1)}, f32[200,128]{1,0:T(8,128)S(1)}, u32[]{:S(2)}, u32[]{:S(2)}) collective-permute-start(f32[200,128]{1,0:T(8,128)S(1)} %get-tuple-element.161.refs_1_), channel_id=1, source_target_pairs={{0,2},{1,3},{2,0},{3,1},{4,6},{5,7},{6,4},{7,5},{8,10},{9,11},{10,... | collective-permute-start | bytes 307208 | tf_op jit(solution)/shard_map/ppermute | solution.py:517
  40.9 6.6 %collective-permute-start.17 = (f32[200,128]{1,0:T(8,128)S(1)}, f32[200,128]{1,0:T(8,128)S(1)}, u32[]{:S(2)}, u32[]{:S(2)}) collective-permute-start(f32[200,128]{1,0:T(8,128)S(1)} %get-tuple-element.164.refs_1_), channel_id=1, source_target_pairs={{0,2},{1,3},{2,0},{3,1},{4,6},{5,7},{6,4},{7,5},{8,10},{9,11},{10,... | collective-permute-start | bytes 307208 | tf_op jit(solution)/shard_map/ppermute | solution.py:517
  41.9 4.0 %collective-permute-start.16 = (f32[16,128]{1,0:T(8,128)S(1)}, f32[16,128]{1,0:T(8,128)S(1)}, u32[]{:S(2)}, u32[]{:S(2)}) collective-permute-start(f32[16,128]{1,0:T(8,128)S(1)} %get-tuple-element.162.refs_3_), channel_id=1, source_target_pairs={{0,9},{1,8},{2,11},{3,10},{4,13},{5,12},{6,15},{7,14},{8,1},{9,0},... | collective-permute-start | bytes 24584 | tf_op jit(solution)/shard_map/ppermute | solution.py:517
  45.9 6.0 %collective-permute-start.18 = (f32[216,128]{1,0:T(8,128)S(1)}, f32[216,128]{1,0:T(8,128)S(1)}, u32[]{:S(2)}, u32[]{:S(2)}) collective-permute-start(f32[216,128]{1,0:T(8,128)S(1)} %shard_map.113.refs_3_.refs_5_), channel_id=1, source_target_pairs={{0,12},{1,13},{2,14},{3,15},{4,0},{5,1},{6,2},{7,3},{8,4},{9,5},{1... | collective-permute-start | bytes 331784 | tf_op jit(solution)/shard_map/ppermute | solution.py:522
  47.5 6.0 %collective-permute-start.20 = (f32[200,128]{1,0:T(8,128)S(1)}, f32[200,128]{1,0:T(8,128)S(1)}, u32[]{:S(2)}, u32[]{:S(2)}) collective-permute-start(f32[200,128]{1,0:T(8,128)S(1)} %shard_map.114), channel_id=1, source_target_pairs={{0,12},{1,13},{2,14},{3,15},{4,0},{5,1},{6,2},{7,3},{8,4},{9,5},{1... | collective-permute-start | bytes 307208 | tf_op jit(solution)/shard_map/ppermute | solution.py:522
  51.9 5.5 %collective-permute-start.19 = (f32[216,128]{1,0:T(8,128)S(1)}, f32[216,128]{1,0:T(8,128)S(1)}, u32[]{:S(2)}, u32[]{:S(2)}) collective-permute-start(f32[216,128]{1,0:T(8,128)S(1)} %collective-permute-done.18.refs_3_), channel_id=1, source_target_pairs={{15,13},{14,12},{13,15},{12,14},{11,7},{10,6},{9,5},{8,4},{7,3},{6... | collective-permute-start | bytes 331784 | tf_op jit(solution)/shard_map/ppermute | solution.py:536
  53.5 5.0 %collective-permute-start.21 = (f32[200,128]{1,0:T(8,128)S(1)}, f32[200,128]{1,0:T(8,128)S(1)}, u32[]{:S(2)}, u32[]{:S(2)}) collective-permute-start(f32[200,128]{1,0:T(8,128)S(1)} %collective-permute-done.20.refs_3_), channel_id=1, source_target_pairs={{15,13},{14,12},{13,15},{12,14},{11,7},{10,6},{9,5},{8,4},{7,3},{6... | collective-permute-start | bytes 307208 | tf_op jit(solution)/shard_map/ppermute | solution.py:536
  57.5 4.8 %collective-permute-start.22 = (f32[208,128]{1,0:T(8,128)S(1)}, f32[208,128]{1,0:T(8,128)S(1)}, u32[]{:S(2)}, u32[]{:S(2)}) collective-permute-start(f32[208,128]{1,0:T(8,128)S(1)} %get-tuple-element.177), channel_id=1, source_target_pairs={{0,2},{1,3},{2,0},{3,1},{4,6},{5,7},{6,4},{7,5},{8,10},{9,11},{10,... | collective-permute-start | bytes 319496 | tf_op jit(solution)/shard_map/ppermute | solution.py:517
  58.6 4.7 %collective-permute-start.23 = (f32[192,128]{1,0:T(8,128)S(1)}, f32[192,128]{1,0:T(8,128)S(1)}, u32[]{:S(2)}, u32[]{:S(2)}) collective-permute-start(f32[192,128]{1,0:T(8,128)S(1)} %get-tuple-element.180), channel_id=1, source_target_pairs={{0,2},{1,3},{2,0},{3,1},{4,6},{5,7},{6,4},{7,5},{8,10},{9,11},{10,... | collective-permute-start | bytes 294920 | tf_op jit(solution)/shard_map/ppermute | solution.py:517
  62.3 1.5 %collective-permute-start.25 = (f32[384,128]{1,0:T(8,128)S(1)}, f32[384,128]{1,0:T(8,128)S(1)}, u32[]{:S(2)}, u32[]{:S(2)}) collective-permute-start(f32[384,128]{1,0:T(8,128)S(1)} %get-tuple-element.185), channel_id=1, source_target_pairs={{0,1},{1,0},{2,3},{3,2},{4,5},{5,4},{6,7},{7,6},{8,9},{9,8},{10,11... | collective-permute-start | bytes 589832 | tf_op jit(solution)/shard_map/ppermute | solution.py:517
  63.4 1.5 %collective-permute-start.24 = (f32[384,128]{1,0:T(8,128)S(1)}, f32[384,128]{1,0:T(8,128)S(1)}, u32[]{:S(2)}, u32[]{:S(2)}) collective-permute-start(f32[384,128]{1,0:T(8,128)S(1)} %get-tuple-element.182), channel_id=1, source_target_pairs={{0,1},{1,0},{2,3},{3,2},{4,5},{5,4},{6,7},{7,6},{8,9},{9,8},{10,11... | collective-permute-start | bytes 589832 | tf_op jit(solution)/shard_map/ppermute | solution.py:517

commit v7 on v6

--- a/solution.py
+++ b/solution.py
@@ -528,7 +528,7 @@
     for source in range(count):
         plane, place = divmod(source, PLANE)
         if plane < behind:
-            target = source ^ 2
+            target = source ^ 1
         else:
             target = (plane + 1 if plane < planes - 1 else behind) * PLANE + place
         pair = (source, target)

time: 66.6 us -> 65.7 us (0.986)
  waiting for transfers between devices: 27.5 us -> 22.5 us
  starting transfers between devices: 22.9 us -> 27.1 us
    ppermute x4, starting transfers between devices: 5.75 us -> 8.84 us  [next_plane(): lax.ppermute(value, 'seq', [(i, (i + step) % count) for i in range(count)])]
    ppermute x4, waiting for transfers between devices: 6.94 us -> 3.89 us  [pass_on(): return lax.ppermute(value, 'seq', pairs)]
    ppermute x18, starting transfers between devices: 14.5 us -> 16.8 us  [swap(): return lax.ppermute(value, axis, [(i, i ^ bit) for i in range(count)])]
    ppermute x18, waiting for transfers between devices: 14 us -> 12.4 us  [swap(): return lax.ppermute(value, axis, [(i, i ^ bit) for i in range(count)])]
    ppermute x4, starting transfers between devices: 2.69 us -> 1.47 us  [pass_on(): return lax.ppermute(value, 'seq', pairs)]
  transfers between devices with their start and end apart: 26 -> 26, of which waited for: 16 -> 18; matrix products, arithmetic and copies ran while one was open for 0% -> 0% of each run, Pallas kernels for 15% -> 15%
where the time goes in v7:
time: 65.7 us; the launch traced here: 65.6 us
  starting transfers between devices  27.1 us (41%)
  waiting for transfers between devices  22.5 us (34%)
  Pallas kernels  15.1 us (23%)
  between operations  0.87 us (1%)
    ppermute x18, starting transfers between devices, swap(): return lax.ppermute(value, axis, [(i, i ^ bit) for i in range(count)])  16.8 us
    pallas_call x28, Pallas kernels, call(): pl.pallas_call(lambda *refs: kernel(*refs[:given], *refs[given + len(deps...  15.1 us
    ppermute x18, waiting for transfers between devices, swap(): return lax.ppermute(value, axis, [(i, i ^ bit) for i in range(count)])  12.4 us
    ppermute x4, starting transfers between devices, next_plane(): lax.ppermute(value, 'seq', [(i, (i + step) % count) for i in range(count)])  8.84 us
    ppermute x4, waiting for transfers between devices, next_plane(): lax.ppermute(value, 'seq', [(i, (i + step) % count) for i in range(count)])  6.17 us
    ppermute x4, waiting for transfers between devices, pass_on(): return lax.ppermute(value, 'seq', pairs)  3.89 us
    ppermute x4, starting transfers between devices, pass_on(): return lax.ppermute(value, 'seq', pairs)  1.47 us
  transfers between devices with their start and end apart: 26, of which 18 were waited for; matrix products, arithmetic and copies ran while one was open for 0% of the time, Pallas kernels for 15%

profile of v7, /device:TPU:0, one launch (start us, length us, event | category | flops | bytes accessed | tf_op | source)
XLA Modules:
  0.0 65.6 jit_solution(12971620683581415488)
XLA Ops:
  0.7 2.0 %shard_map.94 = (f32[384,128]{1,0:T(8,128)S(1)}, f32[392,128]{1,0:T(8,128)S(1)}, f32[24,128]{1,0:T(8,128)S(1)}, f32[256,6]{1,0:T(8,128)S(1)}, f32[768,128]{1,0:T(8,128)S(1)}) custom-call(bf16[256,1536]{1,0:T(8,128)(2,1)} %refs_0_.13, bf16[256,1536]{1,0:T(8,128)(2,1)} %refs_1_.13, f32[12,256]{1,0:T(8,128)} %bitcast.1, s32[2]{0:T(128)} %refs_3_.1), custom_call_target="tpu_custom_call" | custom-call | flops 50331648 | bytes 2394120 | tf_op jit(solution)/shard_map/pallas_call | solution.py:143
  2.6 0.5 collective-permute-start
  3.2 0.8 %shard_map.95 = (f32[384,128]{1,0:T(8,128)S(1)}, f32[392,128]{1,0:T(8,128)S(1)}, f32[24,128]{1,0:T(8,128)S(1)}, f32[256,6]{1,0:T(8,128)S(1)}, f32[768,128]{1,0:T(8,128)S(1)}) custom-call(bf16[256,1536]{1,0:T(8,128)(2,1)S(1)} %copy-done.2, bf16[256,1536]{1,0:T(8,128)(2,1)S(1)} %copy-done.1, f32[12,256]{1,0:T(8,128)S(1)} %bitcast.2, ...), custom_call_target="tpu_custom_call" | custom-call | flops 50331648 | bytes 2406400 | tf_op jit(solution)/shard_map/pallas_call | solution.py:143
  4.1 0.2 collective-permute-done.refs_1_.refs_3_
  4.3 2.9 %collective-permute-start.2 = (f32[200,128]{1,0:T(8,128)S(1)}, f32[200,128]{1,0:T(8,128)S(1)}, u32[]{:S(2)}, u32[]{:S(2)}) collective-permute-start(f32[200,128]{1,0:T(8,128)S(1)} %get-tuple-element.117.refs_1_), channel_id=1, source_target_pairs={{0,2},{1,3},{2,0},{3,1},{4,6},{5,7},{6,4},{7,5},{8,10},{9,11},{10,... | collective-permute-start | bytes 307208 | tf_op jit(solution)/shard_map/ppermute | solution.py:517
  7.3 0.9 %collective-permute-start.3 = (f32[200,128]{1,0:T(8,128)S(1)}, f32[200,128]{1,0:T(8,128)S(1)}, u32[]{:S(2)}, u32[]{:S(2)}) collective-permute-start(f32[200,128]{1,0:T(8,128)S(1)} %get-tuple-element.119.refs_1_), channel_id=1, source_target_pairs={{0,2},{1,3},{2,0},{3,1},{4,6},{5,7},{6,4},{7,5},{8,10},{9,11},{10,... | collective-permute-start | bytes 307208 | tf_op jit(solution)/shard_map/ppermute | solution.py:517
  8.2 2.0 %shard_map.98 = (f32[256,768]{1,0:T(8,128)S(1)}, bf16[1536,128]{1,0:T(8,128)(2,1)S(1)}) custom-call(bf16[256,1536]{1,0:T(8,128)(2,1)S(1)} %copy-done, bf16[256,1536]{1,0:T(8,128)(2,1)S(1)} %copy-done.2, bf16[256,1536]{1,0:T(8,128)(2,1)S(1)} %copy-done.1, f32[12,256]{1,0:T(8,128)S(1)} %bitcast.3, f32[256,6]{1,0:T(8,128)S(1)} %get-tuple-element.114.refs_4_.refs_3_.refs_2_, ...), custom_call_target="tpu_custom_call" | custom-call | flops 100663296 | bytes 3563520 | tf_op jit(solution)/shard_map/pallas_call | solution.py:143
  10.2 0.6 collective-permute-done.2.refs_2_
  10.9 2.2 %collective-permute-start.4 = (f32[200,128]{1,0:T(8,128)S(1)}, f32[200,128]{1,0:T(8,128)S(1)}, u32[]{:S(2)}, u32[]{:S(2)}) collective-permute-start(f32[200,128]{1,0:T(8,128)S(1)} %shard_map.99.refs_3_), channel_id=1, source_target_pairs={{0,4},{1,5},{2,6},{3,7},{4,8},{5,9},{6,10},{7,11},{8,12},{9,13},{1... | collective-permute-start | bytes 307208 | tf_op jit(solution)/shard_map/ppermute | solution.py:522
  13.2 1.6 %collective-permute-start.6 = (f32[200,128]{1,0:T(8,128)S(1)}, f32[200,128]{1,0:T(8,128)S(1)}, u32[]{:S(2)}, u32[]{:S(2)}) collective-permute-start(f32[200,128]{1,0:T(8,128)S(1)} %shard_map.100), channel_id=1, source_target_pairs={{0,4},{1,5},{2,6},{3,7},{4,8},{5,9},{6,10},{7,11},{8,12},{9,13},{1... | collective-permute-start | bytes 307208 | tf_op jit(solution)/shard_map/ppermute | solution.py:522
  14.8 2.0 %shard_map.101 = (f32[256,768]{1,0:T(8,128)S(1)}, bf16[1536,128]{1,0:T(8,128)(2,1)S(1)}) custom-call(bf16[256,1536]{1,0:T(8,128)(2,1)S(1)} %copy-done, bf16[256,1536]{1,0:T(8,128)(2,1)S(1)} %copy-done.2, bf16[256,1536]{1,0:T(8,128)(2,1)S(1)} %copy-done.1, f32[12,256]{1,0:T(8,128)S(1)} %bitcast.4, f32[256,6]{1,0:T(8,128)S(1)} %get-tuple-element.100.refs_4_.refs_3_.refs_2_, ...), custom_call_target="tpu_custom_call" | custom-call | flops 100663296 | bytes 3563520 | tf_op jit(solution)/shard_map/pallas_call | solution.py:143
  16.8 2.1 %collective-permute-done.4.refs_3_ = f32[200,128]{1,0:T(8,128)S(1)} collective-permute-done((f32[200,128]{1,0:T(8,128)S(1)}, f32[200,128]{1,0:T(8,128)S(1)}, u32[]{:S(2)}, u32[]{:S(2)}) %collective-permute-start.4) | collective-permute-done | bytes 102432 | tf_op jit(solution)/shard_map/ppermute | solution.py:522
  18.9 1.1 %collective-permute-done.6.refs_3_ = f32[200,128]{1,0:T(8,128)S(1)} collective-permute-done((f32[200,128]{1,0:T(8,128)S(1)}, f32[200,128]{1,0:T(8,128)S(1)}, u32[]{:S(2)}, u32[]{:S(2)}) %collective-permute-start.6) | collective-permute-done | bytes 102432 | tf_op jit(solution)/shard_map/ppermute | solution.py:522
  20.0 0.2 collective-permute-done.5.refs_4_
  20.2 1.6 %collective-permute-start.8 = (f32[192,128]{1,0:T(8,128)S(1)}, f32[192,128]{1,0:T(8,128)S(1)}, u32[]{:S(2)}, u32[]{:S(2)}) collective-permute-start(f32[192,128]{1,0:T(8,128)S(1)} %get-tuple-element.130), channel_id=1, source_target_pairs={{0,2},{1,3},{2,0},{3,1},{4,6},{5,7},{6,4},{7,5},{8,10},{9,11},{10,... | collective-permute-start | bytes 294920 | tf_op jit(solution)/shard_map/ppermute | solution.py:517
  21.9 1.0 %collective-permute-start.9 = (f32[192,128]{1,0:T(8,128)S(1)}, f32[192,128]{1,0:T(8,128)S(1)}, u32[]{:S(2)}, u32[]{:S(2)}) collective-permute-start(f32[192,128]{1,0:T(8,128)S(1)} %get-tuple-element.133), channel_id=1, source_target_pairs={{0,2},{1,3},{2,0},{3,1},{4,6},{5,7},{6,4},{7,5},{8,10},{9,11},{10,... | collective-permute-start | bytes 294920 | tf_op jit(solution)/shard_map/ppermute | solution.py:517
  22.9 3.0 %collective-permute-done.8.refs_1_ = f32[192,128]{1,0:T(8,128)S(1)} collective-permute-done((f32[192,128]{1,0:T(8,128)S(1)}, f32[192,128]{1,0:T(8,128)S(1)}, u32[]{:S(2)}, u32[]{:S(2)}) %collective-permute-start.8) | collective-permute-done | bytes 98336 | tf_op jit(solution)/shard_map/ppermute | solution.py:517
  26.1 1.4 %collective-permute-done.9.refs_1_ = f32[192,128]{1,0:T(8,128)S(1)} collective-permute-done((f32[192,128]{1,0:T(8,128)S(1)}, f32[192,128]{1,0:T(8,128)S(1)}, u32[]{:S(2)}, u32[]{:S(2)}) %collective-permute-start.9) | collective-permute-done | bytes 98336 | tf_op jit(solution)/shard_map/ppermute | solution.py:517
  27.6 0.6 shard_map.106
  28.2 0.8 %collective-permute-done.10.refs_8_ = f32[384,128]{1,0:T(8,128)S(1)} collective-permute-done((f32[384,128]{1,0:T(8,128)S(1)}, f32[384,128]{1,0:T(8,128)S(1)}, u32[]{:S(2)}, u32[]{:S(2)}) %collective-permute-start.10) | collective-permute-done | bytes 196640 | tf_op jit(solution)/shard_map/ppermute | solution.py:517
  29.0 0.6 shard_map.107
  29.6 1.6 %collective-permute-start.12 = (f32[8,256]{1,0:T(8,128)S(1)}, f32[8,256]{1,0:T(8,128)S(1)}, u32[]{:S(2)}, u32[]{:S(2)}) collective-permute-start(f32[8,256]{1,0:T(8,128)S(1)} %get-tuple-element.140.refs_6_), channel_id=1, source_target_pairs={{0,16},{16,0},{1,17},{17,1},{2,18},{18,2},{3,19},{19,3},{4,20},{20... | collective-permute-start | bytes 24584 | tf_op jit(solution)/shard_map/ppermute | solution.py:517
  31.2 2.1 %collective-permute-done.12.refs_7_ = f32[8,256]{1,0:T(8,128)S(1)} collective-permute-done((f32[8,256]{1,0:T(8,128)S(1)}, f32[8,256]{1,0:T(8,128)S(1)}, u32[]{:S(2)}, u32[]{:S(2)}) %collective-permute-start.12) | collective-permute-done | bytes 8224 | tf_op jit(solution)/shard_map/ppermute | solution.py:517
  33.3 0.9 %shard_map.108 = (bf16[256,768]{1,0:T(8,128)(2,1)S(1)}, f32[384,128]{1,0:T(8,128)S(1)}, f32[400,128]{1,0:T(8,128)S(1)}, f32[8,128]{1,0:T(8,128)S(1)}, f32[8,128]{1,0:T(8,128)S(1)}, /*index=5*/f32[768,128]{1,0:T(8,128)S(1)}) custom-call(bf16[256,1536]{1,0:T(8,128)(2,1)S(1)} %copy-done, bf16[256,1536]{1,0:T(8,128)(2,1)S(1)} %copy-done.3, f32[1536]{0:T(1024)S(1)} %copy-done.5, ...), custom_call_target="tpu_custom_call" | custom-call | flops 50331648 | bytes 3596288 | tf_op jit(solution)/shard_map/pallas_call | solution.py:143
  34.3 0.9 %shard_map.109 = (bf16[256,768]{1,0:T(8,128)(2,1)S(1)}, f32[384,128]{1,0:T(8,128)S(1)}, f32[400,128]{1,0:T(8,128)S(1)}, f32[8,128]{1,0:T(8,128)S(1)}, f32[8,128]{1,0:T(8,128)S(1)}, /*index=5*/f32[768,128]{1,0:T(8,128)S(1)}) custom-call(bf16[256,1536]{1,0:T(8,128)(2,1)S(1)} %copy-done, bf16[256,1536]{1,0:T(8,128)(2,1)S(1)} %copy-done.3, f32[1536]{0:T(1024)S(1)} %copy-done.5, ...), custom_call_target="tpu_custom_call" | custom-call | flops 50331648 | bytes 3596288 | tf_op jit(solution)/shard_map/pallas_call | solution.py:143
  35.3 0.6 collective-permute-start.14
  35.9 1.6 %collective-permute-start.15 = (f32[200,128]{1,0:T(8,128)S(1)}, f32[200,128]{1,0:T(8,128)S(1)}, u32[]{:S(2)}, u32[]{:S(2)}) collective-permute-start(f32[200,128]{1,0:T(8,128)S(1)} %get-tuple-element.161.refs_1_), channel_id=1, source_target_pairs={{0,2},{1,3},{2,0},{3,1},{4,6},{5,7},{6,4},{7,5},{8,10},{9,11},{10,... | collective-permute-start | bytes 307208 | tf_op jit(solution)/shard_map/ppermute | solution.py:517
  37.5 1.0 %collective-permute-start.17 = (f32[200,128]{1,0:T(8,128)S(1)}, f32[200,128]{1,0:T(8,128)S(1)}, u32[]{:S(2)}, u32[]{:S(2)}) collective-permute-start(f32[200,128]{1,0:T(8,128)S(1)} %get-tuple-element.164.refs_1_), channel_id=1, source_target_pairs={{0,2},{1,3},{2,0},{3,1},{4,6},{5,7},{6,4},{7,5},{8,10},{9,11},{10,... | collective-permute-start | bytes 307208 | tf_op jit(solution)/shard_map/ppermute | solution.py:517
  38.6 2.9 %collective-permute-start.16 = (f32[16,128]{1,0:T(8,128)S(1)}, f32[16,128]{1,0:T(8,128)S(1)}, u32[]{:S(2)}, u32[]{:S(2)}) collective-permute-start(f32[16,128]{1,0:T(8,128)S(1)} %get-tuple-element.162.refs_3_), channel_id=1, source_target_pairs={{0,9},{1,8},{2,11},{3,10},{4,13},{5,12},{6,15},{7,14},{8,1},{9,0},... | collective-permute-start | bytes 24584 | tf_op jit(solution)/shard_map/ppermute | solution.py:517
  41.5 1.1 %shard_map.112 = (f32[256,768]{1,0:T(8,128)S(1)}, f32[256,768]{1,0:T(8,128)S(1)}) custom-call(bf16[256,1536]{1,0:T(8,128)(2,1)S(1)} %copy-done, bf16[256,1536]{1,0:T(8,128)(2,1)S(1)} %copy-done.1, f32[12,256]{1,0:T(8,128)S(1)} %bitcast.5, f32[256,6]{1,0:T(8,128)S(1)} %get-tuple-element.114.refs_4_.refs_3_.refs_2_, ...), custom_call_target="tpu_custom_call" | custom-call | flops 150994944 | bytes 3950592 | tf_op jit(solution)/shard_map/pallas_call | solution.py:143
  42.6 0.2 collective-permute-done.16.refs_4_
  42.9 4.6 %collective-permute-start.18 = (f32[216,128]{1,0:T(8,128)S(1)}, f32[216,128]{1,0:T(8,128)S(1)}, u32[]{:S(2)}, u32[]{:S(2)}) collective-permute-start(f32[216,128]{1,0:T(8,128)S(1)} %shard_map.113.refs_3_.refs_5_), channel_id=1, source_target_pairs={{0,12},{1,13},{2,14},{3,15},{4,0},{5,1},{6,2},{7,3},{8,4},{9,5},{1... | collective-permute-start | bytes 331784 | tf_op jit(solution)/shard_map/ppermute | solution.py:522
  47.5 0.4 collective-permute-start.20
  47.9 1.1 %shard_map.115 = (f32[256,768]{1,0:T(8,128)S(1)}, f32[256,768]{1,0:T(8,128)S(1)}) custom-call(bf16[256,1536]{1,0:T(8,128)(2,1)S(1)} %copy-done, bf16[256,1536]{1,0:T(8,128)(2,1)S(1)} %copy-done.1, f32[12,256]{1,0:T(8,128)S(1)} %bitcast.6, f32[256,6]{1,0:T(8,128)S(1)} %get-tuple-element.100.refs_4_.refs_3_.refs_2_, ...), custom_call_target="tpu_custom_call" | custom-call | flops 150994944 | bytes 3950592 | tf_op jit(solution)/shard_map/pallas_call | solution.py:143
  49.1 1.8 %collective-permute-done.18.refs_3_ = f32[216,128]{1,0:T(8,128)S(1)} collective-permute-done((f32[216,128]{1,0:T(8,128)S(1)}, f32[216,128]{1,0:T(8,128)S(1)}, u32[]{:S(2)}, u32[]{:S(2)}) %collective-permute-start.18) | collective-permute-done | bytes 110624 | tf_op jit(solution)/shard_map/ppermute | solution.py:522
  50.9 1.0 %collective-permute-start.19 = (f32[216,128]{1,0:T(8,128)S(1)}, f32[216,128]{1,0:T(8,128)S(1)}, u32[]{:S(2)}, u32[]{:S(2)}) collective-permute-start(f32[216,128]{1,0:T(8,128)S(1)} %collective-permute-done.18.refs_3_), channel_id=1, source_target_pairs={{15,14},{14,15},{13,12},{12,13},{11,7},{10,6},{9,5},{8,4},{7,3},{6... | collective-permute-start | bytes 331784 | tf_op jit(solution)/shard_map/ppermute | solution.py:536
  51.8 1.2 %collective-permute-done.20.refs_3_ = f32[200,128]{1,0:T(8,128)S(1)} collective-permute-done((f32[200,128]{1,0:T(8,128)S(1)}, f32[200,128]{1,0:T(8,128)S(1)}, u32[]{:S(2)}, u32[]{:S(2)}) %collective-permute-start.20) | collective-permute-done | bytes 102432 | tf_op jit(solution)/shard_map/ppermute | solution.py:522
  53.1 0.5 collective-permute-start.21
  53.5 2.9 %collective-permute-done.19.refs_4_ = f32[216,128]{1,0:T(8,128)S(1)} collective-permute-done((f32[216,128]{1,0:T(8,128)S(1)}, f32[216,128]{1,0:T(8,128)S(1)}, u32[]{:S(2)}, u32[]{:S(2)}) %collective-permute-start.19) | collective-permute-done | bytes 110624 | tf_op jit(solution)/shard_map/ppermute | solution.py:536
  56.4 0.4 collective-permute-start.22
  56.9 0.8 %collective-permute-done.21.refs_4_ = f32[200,128]{1,0:T(8,128)S(1)} collective-permute-done((f32[200,128]{1,0:T(8,128)S(1)}, f32[200,128]{1,0:T(8,128)S(1)}, u32[]{:S(2)}, u32[]{:S(2)}) %collective-permute-start.21) | collective-permute-done | bytes 102432 | tf_op jit(solution)/shard_map/ppermute | solution.py:536
  57.8 1.3 %collective-permute-start.23 = (f32[192,128]{1,0:T(8,128)S(1)}, f32[192,128]{1,0:T(8,128)S(1)}, u32[]{:S(2)}, u32[]{:S(2)}) collective-permute-start(f32[192,128]{1,0:T(8,128)S(1)} %get-tuple-element.180), channel_id=1, source_target_pairs={{0,2},{1,3},{2,0},{3,1},{4,6},{5,7},{6,4},{7,5},{8,10},{9,11},{10,... | collective-permute-start | bytes 294920 | tf_op jit(solution)/shard_map/ppermute | solution.py:517
  59.0 2.2 %collective-permute-done.22.refs_1_.refs_12_ = f32[208,128]{1,0:T(8,128)S(1)} collective-permute-done((f32[208,128]{1,0:T(8,128)S(1)}, f32[208,128]{1,0:T(8,128)S(1)}, u32[]{:S(2)}, u32[]{:S(2)}) %collective-permute-start.22) | collective-permute-done | bytes 106528 | tf_op jit(solution)/shard_map/ppermute | solution.py:517
  61.4 1.1 %collective-permute-done.23.refs_1_ = f32[192,128]{1,0:T(8,128)S(1)} collective-permute-done((f32[192,128]{1,0:T(8,128)S(1)}, f32[192,128]{1,0:T(8,128)S(1)}, u32[]{:S(2)}, u32[]{:S(2)}) %collective-permute-start.23) | collective-permute-done | bytes 98336 | tf_op jit(solution)/shard_map/ppermute | solution.py:517
  62.6 0.2 collective-permute-done.25.refs_8_
  62.8 0.6 shard_map.120
  63.4 0.6 collective-permute-done.24.refs_8_
  64.0 1.5 %shard_map.121 = (bf16[256,1536]{1,0:T(8,128)(2,1)}, bf16[256,1536]{1,0:T(8,128)(2,1)}, f32[1536]{0:T(1024)}) custom-call(bf16[256,1536]{1,0:T(8,128)(2,1)S(1)} %copy-done.2, bf16[256,1536]{1,0:T(8,128)(2,1)S(1)} %copy-done.1, f32[256,6]{1,0:T(8,128)S(1)} %get-tuple-element.100.refs_4_.refs_3_.refs_2_, ...), custom_call_target="tpu_custom_call" | custom-call | flops 201326592 | bytes 6430720 | tf_op jit(solution)/shard_map/pallas_call | solution.py:143
  (44 shorter events, 1.4 us)
Async XLA Ops:
  0.6 2.5 %copy-start.1 = (bf16[256,1536]{1,0:T(8,128)(2,1)S(1)}, bf16[256,1536]{1,0:T(8,128)(2,1)}, u32[]{:S(2)}) copy-start(bf16[256,1536]{1,0:T(8,128)(2,1)} %refs_1_.13) | copy-start | bytes 2359300
  0.6 2.5 %copy-start.2 = (bf16[256,1536]{1,0:T(8,128)(2,1)S(1)}, bf16[256,1536]{1,0:T(8,128)(2,1)}, u32[]{:S(2)}) copy-start(bf16[256,1536]{1,0:T(8,128)(2,1)} %refs_0_.13) | copy-start | bytes 2359300
  0.7 2.5 %copy-start.4 = (f32[256,12]{0,1:T(8,128)S(1)}, f32[256,12]{0,1:T(8,128)}, u32[]{:S(2)}) copy-start(f32[256,12]{0,1:T(8,128)} %param.11) | copy-start | bytes 36868
  2.6 1.6 %collective-permute-start = (f32[392,128]{1,0:T(8,128)S(1)}, f32[392,128]{1,0:T(8,128)S(1)}, u32[]{:S(2)}, u32[]{:S(2)}) collective-permute-start(f32[392,128]{1,0:T(8,128)S(1)} %get-tuple-element.107), channel_id=1, source_target_pairs={{0,1},{1,0},{2,3},{3,2},{4,5},{5,4},{6,7},{7,6},{8,9},{9,8},{10,11... | collective-permute-start | bytes 602120 | tf_op jit(solution)/shard_map/ppermute | solution.py:517
  3.9 4.3 %copy-start = (bf16[256,1536]{1,0:T(8,128)(2,1)S(1)}, bf16[256,1536]{1,0:T(8,128)(2,1)}, u32[]{:S(2)}) copy-start(bf16[256,1536]{1,0:T(8,128)(2,1)} %refs_0_.11) | copy-start | bytes 2359300
  3.9 3.3 %collective-permute-start.1 = (f32[392,128]{1,0:T(8,128)S(1)}, f32[392,128]{1,0:T(8,128)S(1)}, u32[]{:S(2)}, u32[]{:S(2)}) collective-permute-start(f32[392,128]{1,0:T(8,128)S(1)} %get-tuple-element.110), channel_id=1, source_target_pairs={{0,1},{1,0},{2,3},{3,2},{4,5},{5,4},{6,7},{7,6},{8,9},{9,8},{10,11... | collective-permute-start | bytes 602120 | tf_op jit(solution)/shard_map/ppermute | solution.py:517
  4.3 6.6 %collective-permute-start.2 = (f32[200,128]{1,0:T(8,128)S(1)}, f32[200,128]{1,0:T(8,128)S(1)}, u32[]{:S(2)}, u32[]{:S(2)}) collective-permute-start(f32[200,128]{1,0:T(8,128)S(1)} %get-tuple-element.117.refs_1_), channel_id=1, source_target_pairs={{0,2},{1,3},{2,0},{3,1},{4,6},{5,7},{6,4},{7,5},{8,10},{9,11},{10,... | collective-permute-start | bytes 307208 | tf_op jit(solution)/shard_map/ppermute | solution.py:517
  7.2 1.0 %copy-start.5 = (f32[1536]{0:T(1024)S(1)}, f32[1536]{0:T(1024)}, u32[]{:S(2)}) copy-start(f32[1536]{0:T(1024)} %refs_2_.5) | copy-start | bytes 18436
  7.3 5.8 %collective-permute-start.3 = (f32[200,128]{1,0:T(8,128)S(1)}, f32[200,128]{1,0:T(8,128)S(1)}, u32[]{:S(2)}, u32[]{:S(2)}) collective-permute-start(f32[200,128]{1,0:T(8,128)S(1)} %get-tuple-element.119.refs_1_), channel_id=1, source_target_pairs={{0,2},{1,3},{2,0},{3,1},{4,6},{5,7},{6,4},{7,5},{8,10},{9,11},{10,... | collective-permute-start | bytes 307208 | tf_op jit(solution)/shard_map/ppermute | solution.py:517
  10.9 7.9 %collective-permute-start.4 = (f32[200,128]{1,0:T(8,128)S(1)}, f32[200,128]{1,0:T(8,128)S(1)}, u32[]{:S(2)}, u32[]{:S(2)}) collective-permute-start(f32[200,128]{1,0:T(8,128)S(1)} %shard_map.99.refs_3_), channel_id=1, source_target_pairs={{0,4},{1,5},{2,6},{3,7},{4,8},{5,9},{6,10},{7,11},{8,12},{9,13},{1... | collective-permute-start | bytes 307208 | tf_op jit(solution)/shard_map/ppermute | solution.py:522
  13.2 6.8 %collective-permute-start.6 = (f32[200,128]{1,0:T(8,128)S(1)}, f32[200,128]{1,0:T(8,128)S(1)}, u32[]{:S(2)}, u32[]{:S(2)}) collective-permute-start(f32[200,128]{1,0:T(8,128)S(1)} %shard_map.100), channel_id=1, source_target_pairs={{0,4},{1,5},{2,6},{3,7},{4,8},{5,9},{6,10},{7,11},{8,12},{9,13},{1... | collective-permute-start | bytes 307208 | tf_op jit(solution)/shard_map/ppermute | solution.py:522
  18.9 1.3 %collective-permute-start.5 = (f32[200,128]{1,0:T(8,128)S(1)}, f32[200,128]{1,0:T(8,128)S(1)}, u32[]{:S(2)}, u32[]{:S(2)}) collective-permute-start(f32[200,128]{1,0:T(8,128)S(1)} %collective-permute-done.4.refs_3_), channel_id=1, source_target_pairs={{0,1},{1,0},{2,3},{3,2},{4,8},{5,9},{6,10},{7,11},{8,12},{9,13},{1... | collective-permute-start | bytes 307208 | tf_op jit(solution)/shard_map/ppermute | solution.py:536
  20.0 1.8 %collective-permute-start.7 = (f32[200,128]{1,0:T(8,128)S(1)}, f32[200,128]{1,0:T(8,128)S(1)}, u32[]{:S(2)}, u32[]{:S(2)}) collective-permute-start(f32[200,128]{1,0:T(8,128)S(1)} %collective-permute-done.6.refs_3_), channel_id=1, source_target_pairs={{0,1},{1,0},{2,3},{3,2},{4,8},{5,9},{6,10},{7,11},{8,12},{9,13},{1... | collective-permute-start | bytes 307208 | tf_op jit(solution)/shard_map/ppermute | solution.py:536
  20.2 5.7 %collective-permute-start.8 = (f32[192,128]{1,0:T(8,128)S(1)}, f32[192,128]{1,0:T(8,128)S(1)}, u32[]{:S(2)}, u32[]{:S(2)}) collective-permute-start(f32[192,128]{1,0:T(8,128)S(1)} %get-tuple-element.130), channel_id=1, source_target_pairs={{0,2},{1,3},{2,0},{3,1},{4,6},{5,7},{6,4},{7,5},{8,10},{9,11},{10,... | collective-permute-start | bytes 294920 | tf_op jit(solution)/shard_map/ppermute | solution.py:517
  21.8 5.8 %copy-start.3 = (bf16[256,1536]{1,0:T(8,128)(2,1)S(1)}, bf16[256,1536]{1,0:T(8,128)(2,1)}, u32[]{:S(2)}) copy-start(bf16[256,1536]{1,0:T(8,128)(2,1)} %refs_1_.9) | copy-start | bytes 2359300
  21.9 5.5 %collective-permute-start.9 = (f32[192,128]{1,0:T(8,128)S(1)}, f32[192,128]{1,0:T(8,128)S(1)}, u32[]{:S(2)}, u32[]{:S(2)}) collective-permute-start(f32[192,128]{1,0:T(8,128)S(1)} %get-tuple-element.133), channel_id=1, source_target_pairs={{0,2},{1,3},{2,0},{3,1},{4,6},{5,7},{6,4},{7,5},{8,10},{9,11},{10,... | collective-permute-start | bytes 294920 | tf_op jit(solution)/shard_map/ppermute | solution.py:517
  26.0 1.6 %collective-permute-start.11 = (f32[384,128]{1,0:T(8,128)S(1)}, f32[384,128]{1,0:T(8,128)S(1)}, u32[]{:S(2)}, u32[]{:S(2)}) collective-permute-start(f32[384,128]{1,0:T(8,128)S(1)} %get-tuple-element.137), channel_id=1, source_target_pairs={{0,1},{1,0},{2,3},{3,2},{4,5},{5,4},{6,7},{7,6},{8,9},{9,8},{10,11... | collective-permute-start | bytes 589832 | tf_op jit(solution)/shard_map/ppermute | solution.py:517
  27.5 1.5 %collective-permute-start.10 = (f32[384,128]{1,0:T(8,128)S(1)}, f32[384,128]{1,0:T(8,128)S(1)}, u32[]{:S(2)}, u32[]{:S(2)}) collective-permute-start(f32[384,128]{1,0:T(8,128)S(1)} %get-tuple-element.135), channel_id=1, source_target_pairs={{0,1},{1,0},{2,3},{3,2},{4,5},{5,4},{6,7},{7,6},{8,9},{9,8},{10,11... | collective-permute-start | bytes 589832 | tf_op jit(solution)/shard_map/ppermute | solution.py:517
  29.6 3.7 %collective-permute-start.12 = (f32[8,256]{1,0:T(8,128)S(1)}, f32[8,256]{1,0:T(8,128)S(1)}, u32[]{:S(2)}, u32[]{:S(2)}) collective-permute-start(f32[8,256]{1,0:T(8,128)S(1)} %get-tuple-element.140.refs_6_), channel_id=1, source_target_pairs={{0,16},{16,0},{1,17},{17,1},{2,18},{18,2},{3,19},{19,3},{4,20},{20... | collective-permute-start | bytes 24584 | tf_op jit(solution)/shard_map/ppermute | solution.py:517
  34.3 1.6 %collective-permute-start.13 = (f32[400,128]{1,0:T(8,128)S(1)}, f32[400,128]{1,0:T(8,128)S(1)}, u32[]{:S(2)}, u32[]{:S(2)}) collective-permute-start(f32[400,128]{1,0:T(8,128)S(1)} %get-tuple-element.146), channel_id=1, source_target_pairs={{0,1},{1,0},{2,3},{3,2},{4,5},{5,4},{6,7},{7,6},{8,9},{9,8},{10,11... | collective-permute-start | bytes 614408 | tf_op jit(solution)/shard_map/ppermute | solution.py:517
  35.3 2.2 %collective-permute-start.14 = (f32[400,128]{1,0:T(8,128)S(1)}, f32[400,128]{1,0:T(8,128)S(1)}, u32[]{:S(2)}, u32[]{:S(2)}) collective-permute-start(f32[400,128]{1,0:T(8,128)S(1)} %get-tuple-element.152), channel_id=1, source_target_pairs={{0,1},{1,0},{2,3},{3,2},{4,5},{5,4},{6,7},{7,6},{8,9},{9,8},{10,11... | collective-permute-start | bytes 614408 | tf_op jit(solution)/shard_map/ppermute | solution.py:517
  35.9 6.9 %collective-permute-start.15 = (f32[200,128]{1,0:T(8,128)S(1)}, f32[200,128]{1,0:T(8,128)S(1)}, u32[]{:S(2)}, u32[]{:S(2)}) collective-permute-start(f32[200,128]{1,0:T(8,128)S(1)} %get-tuple-element.161.refs_1_), channel_id=1, source_target_pairs={{0,2},{1,3},{2,0},{3,1},{4,6},{5,7},{6,4},{7,5},{8,10},{9,11},{10,... | collective-permute-start | bytes 307208 | tf_op jit(solution)/shard_map/ppermute | solution.py:517
  37.5 9.9 %collective-permute-start.17 = (f32[200,128]{1,0:T(8,128)S(1)}, f32[200,128]{1,0:T(8,128)S(1)}, u32[]{:S(2)}, u32[]{:S(2)}) collective-permute-start(f32[200,128]{1,0:T(8,128)S(1)} %get-tuple-element.164.refs_1_), channel_id=1, source_target_pairs={{0,2},{1,3},{2,0},{3,1},{4,6},{5,7},{6,4},{7,5},{8,10},{9,11},{10,... | collective-permute-start | bytes 307208 | tf_op jit(solution)/shard_map/ppermute | solution.py:517
  38.6 4.2 %collective-permute-start.16 = (f32[16,128]{1,0:T(8,128)S(1)}, f32[16,128]{1,0:T(8,128)S(1)}, u32[]{:S(2)}, u32[]{:S(2)}) collective-permute-start(f32[16,128]{1,0:T(8,128)S(1)} %get-tuple-element.162.refs_3_), channel_id=1, source_target_pairs={{0,9},{1,8},{2,11},{3,10},{4,13},{5,12},{6,15},{7,14},{8,1},{9,0},... | collective-permute-start | bytes 24584 | tf_op jit(solution)/shard_map/ppermute | solution.py:517
  42.9 8.0 %collective-permute-start.18 = (f32[216,128]{1,0:T(8,128)S(1)}, f32[216,128]{1,0:T(8,128)S(1)}, u32[]{:S(2)}, u32[]{:S(2)}) collective-permute-start(f32[216,128]{1,0:T(8,128)S(1)} %shard_map.113.refs_3_.refs_5_), channel_id=1, source_target_pairs={{0,12},{1,13},{2,14},{3,15},{4,0},{5,1},{6,2},{7,3},{8,4},{9,5},{1... | collective-permute-start | bytes 331784 | tf_op jit(solution)/shard_map/ppermute | solution.py:522
  47.5 5.6 %collective-permute-start.20 = (f32[200,128]{1,0:T(8,128)S(1)}, f32[200,128]{1,0:T(8,128)S(1)}, u32[]{:S(2)}, u32[]{:S(2)}) collective-permute-start(f32[200,128]{1,0:T(8,128)S(1)} %shard_map.114), channel_id=1, source_target_pairs={{0,12},{1,13},{2,14},{3,15},{4,0},{5,1},{6,2},{7,3},{8,4},{9,5},{1... | collective-permute-start | bytes 307208 | tf_op jit(solution)/shard_map/ppermute | solution.py:522
  50.9 5.5 %collective-permute-start.19 = (f32[216,128]{1,0:T(8,128)S(1)}, f32[216,128]{1,0:T(8,128)S(1)}, u32[]{:S(2)}, u32[]{:S(2)}) collective-permute-start(f32[216,128]{1,0:T(8,128)S(1)} %collective-permute-done.18.refs_3_), channel_id=1, source_target_pairs={{15,14},{14,15},{13,12},{12,13},{11,7},{10,6},{9,5},{8,4},{7,3},{6... | collective-permute-start | bytes 331784 | tf_op jit(solution)/shard_map/ppermute | solution.py:536
  53.1 4.7 %collective-permute-start.21 = (f32[200,128]{1,0:T(8,128)S(1)}, f32[200,128]{1,0:T(8,128)S(1)}, u32[]{:S(2)}, u32[]{:S(2)}) collective-permute-start(f32[200,128]{1,0:T(8,128)S(1)} %collective-permute-done.20.refs_3_), channel_id=1, source_target_pairs={{15,14},{14,15},{13,12},{12,13},{11,7},{10,6},{9,5},{8,4},{7,3},{6... | collective-permute-start | bytes 307208 | tf_op jit(solution)/shard_map/ppermute | solution.py:536
  56.4 4.8 %collective-permute-start.22 = (f32[208,128]{1,0:T(8,128)S(1)}, f32[208,128]{1,0:T(8,128)S(1)}, u32[]{:S(2)}, u32[]{:S(2)}) collective-permute-start(f32[208,128]{1,0:T(8,128)S(1)} %get-tuple-element.177), channel_id=1, source_target_pairs={{0,2},{1,3},{2,0},{3,1},{4,6},{5,7},{6,4},{7,5},{8,10},{9,11},{10,... | collective-permute-start | bytes 319496 | tf_op jit(solution)/shard_map/ppermute | solution.py:517
  57.8 4.7 %collective-permute-start.23 = (f32[192,128]{1,0:T(8,128)S(1)}, f32[192,128]{1,0:T(8,128)S(1)}, u32[]{:S(2)}, u32[]{:S(2)}) collective-permute-start(f32[192,128]{1,0:T(8,128)S(1)} %get-tuple-element.180), channel_id=1, source_target_pairs={{0,2},{1,3},{2,0},{3,1},{4,6},{5,7},{6,4},{7,5},{8,10},{9,11},{10,... | collective-permute-start | bytes 294920 | tf_op jit(solution)/shard_map/ppermute | solution.py:517
  61.3 1.5 %collective-permute-start.25 = (f32[384,128]{1,0:T(8,128)S(1)}, f32[384,128]{1,0:T(8,128)S(1)}, u32[]{:S(2)}, u32[]{:S(2)}) collective-permute-start(f32[384,128]{1,0:T(8,128)S(1)} %get-tuple-element.185), channel_id=1, source_target_pairs={{0,1},{1,0},{2,3},{3,2},{4,5},{5,4},{6,7},{7,6},{8,9},{9,8},{10,11... | collective-permute-start | bytes 589832 | tf_op jit(solution)/shard_map/ppermute | solution.py:517
  62.5 1.5 %collective-permute-start.24 = (f32[384,128]{1,0:T(8,128)S(1)}, f32[384,128]{1,0:T(8,128)S(1)}, u32[]{:S(2)}, u32[]{:S(2)}) collective-permute-start(f32[384,128]{1,0:T(8,128)S(1)} %get-tuple-element.182), channel_id=1, source_target_pairs={{0,1},{1,0},{2,3},{3,2},{4,5},{5,4},{6,7},{7,6},{8,9},{9,8},{10,11... | collective-permute-start | bytes 589832 | tf_op jit(solution)/shard_map/ppermute | solution.py:517

commit v8 on v7

--- a/solution.py
+++ b/solution.py
@@ -519,7 +519,8 @@
 
 def next_plane(value, count, reverse):
     step = -PLANE if reverse else PLANE
-    return lax.ppermute(value, "seq", [(i, (i + step) % count) for i in range(count)])
+    pairs = [(i, i + step) if 0 <= i + step < count else (i, (i + step) % count ^ 1) for i in range(count)]
+    return lax.ppermute(value, "seq", pairs)
 
 
 def pass_on(value, count, reverse, behind):

time: 65.7 us -> 64.8 us (0.986)
  waiting for transfers between devices: 22.5 us -> 19.2 us
  starting transfers between devices: 27.1 us -> 29.5 us
    ppermute x4, starting transfers between devices: 1.47 us -> 4.26 us  [pass_on(): return lax.ppermute(value, 'seq', pairs)]
    ppermute x4, waiting for transfers between devices: 6.17 us -> 4.29 us  [next_plane(): return lax.ppermute(value, 'seq', pairs)]
    ppermute x4, waiting for transfers between devices: 3.89 us -> 2.32 us  [pass_on(): return lax.ppermute(value, 'seq', pairs)]
    ppermute x4, starting transfers between devices: 8.84 us -> 7.55 us  [next_plane(): return lax.ppermute(value, 'seq', pairs)]
    ppermute x18, starting transfers between devices: 16.8 us -> 17.7 us  [swap(): return lax.ppermute(value, axis, [(i, i ^ bit) for i in range(count)])]
  transfers between devices with their start and end apart: 26 -> 26, of which waited for: 18 -> 17; matrix products, arithmetic and copies ran while one was open for 0% -> 0% of each run, Pallas kernels for 15% -> 16%
where the time goes in v8:
time: 64.8 us; the launch traced here: 64.7 us
  starting transfers between devices  29.5 us (46%)
  waiting for transfers between devices  19.2 us (30%)
  Pallas kernels  15.1 us (23%)
  between operations  0.87 us (1%)
    ppermute x18, starting transfers between devices, swap(): return lax.ppermute(value, axis, [(i, i ^ bit) for i in range(count)])  17.7 us
    pallas_call x28, Pallas kernels, call(): pl.pallas_call(lambda *refs: kernel(*refs[:given], *refs[given + len(deps...  15.1 us
    ppermute x18, waiting for transfers between devices, swap(): return lax.ppermute(value, axis, [(i, i ^ bit) for i in range(count)])  12.6 us
    ppermute x4, starting transfers between devices, next_plane(): return lax.ppermute(value, 'seq', pairs)  7.55 us
    ppermute x4, waiting for transfers between devices, next_plane(): return lax.ppermute(value, 'seq', pairs)  4.29 us
    ppermute x4, starting transfers between devices, pass_on(): return lax.ppermute(value, 'seq', pairs)  4.26 us
    ppermute x4, waiting for transfers between devices, pass_on(): return lax.ppermute(value, 'seq', pairs)  2.32 us
  transfers between devices with their start and end apart: 26, of which 17 were waited for; matrix products, arithmetic and copies ran while one was open for 0% of the time, Pallas kernels for 16%

profile of v8, /device:TPU:0, one launch (start us, length us, event | category | flops | bytes accessed | tf_op | source)
XLA Modules:
  0.0 64.7 jit_solution(16581927458698978052)
XLA Ops:
  0.7 2.0 %shard_map.94 = (f32[384,128]{1,0:T(8,128)S(1)}, f32[392,128]{1,0:T(8,128)S(1)}, f32[24,128]{1,0:T(8,128)S(1)}, f32[256,6]{1,0:T(8,128)S(1)}, f32[768,128]{1,0:T(8,128)S(1)}) custom-call(bf16[256,1536]{1,0:T(8,128)(2,1)} %refs_0_.13, bf16[256,1536]{1,0:T(8,128)(2,1)} %refs_1_.13, f32[12,256]{1,0:T(8,128)} %bitcast.1, s32[2]{0:T(128)} %refs_3_.1), custom_call_target="tpu_custom_call" | custom-call | flops 50331648 | bytes 2394120 | tf_op jit(solution)/shard_map/pallas_call | solution.py:143
  2.6 0.5 collective-permute-start
  3.2 0.8 %shard_map.95 = (f32[384,128]{1,0:T(8,128)S(1)}, f32[392,128]{1,0:T(8,128)S(1)}, f32[24,128]{1,0:T(8,128)S(1)}, f32[256,6]{1,0:T(8,128)S(1)}, f32[768,128]{1,0:T(8,128)S(1)}) custom-call(bf16[256,1536]{1,0:T(8,128)(2,1)S(1)} %copy-done.2, bf16[256,1536]{1,0:T(8,128)(2,1)S(1)} %copy-done.1, f32[12,256]{1,0:T(8,128)S(1)} %bitcast.2, ...), custom_call_target="tpu_custom_call" | custom-call | flops 50331648 | bytes 2406400 | tf_op jit(solution)/shard_map/pallas_call | solution.py:143
  3.9 0.1 collective-permute-start.1
  4.1 0.2 collective-permute-done.refs_1_.refs_3_
  4.3 2.9 %collective-permute-start.2 = (f32[200,128]{1,0:T(8,128)S(1)}, f32[200,128]{1,0:T(8,128)S(1)}, u32[]{:S(2)}, u32[]{:S(2)}) collective-permute-start(f32[200,128]{1,0:T(8,128)S(1)} %get-tuple-element.117.refs_1_), channel_id=1, source_target_pairs={{0,2},{1,3},{2,0},{3,1},{4,6},{5,7},{6,4},{7,5},{8,10},{9,11},{10,... | collective-permute-start | bytes 307208 | tf_op jit(solution)/shard_map/ppermute | solution.py:517
  7.3 0.9 %collective-permute-start.3 = (f32[200,128]{1,0:T(8,128)S(1)}, f32[200,128]{1,0:T(8,128)S(1)}, u32[]{:S(2)}, u32[]{:S(2)}) collective-permute-start(f32[200,128]{1,0:T(8,128)S(1)} %get-tuple-element.119.refs_1_), channel_id=1, source_target_pairs={{0,2},{1,3},{2,0},{3,1},{4,6},{5,7},{6,4},{7,5},{8,10},{9,11},{10,... | collective-permute-start | bytes 307208 | tf_op jit(solution)/shard_map/ppermute | solution.py:517
  8.2 2.0 %shard_map.98 = (f32[256,768]{1,0:T(8,128)S(1)}, bf16[1536,128]{1,0:T(8,128)(2,1)S(1)}) custom-call(bf16[256,1536]{1,0:T(8,128)(2,1)S(1)} %copy-done, bf16[256,1536]{1,0:T(8,128)(2,1)S(1)} %copy-done.2, bf16[256,1536]{1,0:T(8,128)(2,1)S(1)} %copy-done.1, f32[12,256]{1,0:T(8,128)S(1)} %bitcast.3, f32[256,6]{1,0:T(8,128)S(1)} %get-tuple-element.114.refs_4_.refs_3_.refs_2_, ...), custom_call_target="tpu_custom_call" | custom-call | flops 100663296 | bytes 3563520 | tf_op jit(solution)/shard_map/pallas_call | solution.py:143
  10.2 0.6 collective-permute-done.2.refs_2_
  10.9 2.2 %collective-permute-start.4 = (f32[200,128]{1,0:T(8,128)S(1)}, f32[200,128]{1,0:T(8,128)S(1)}, u32[]{:S(2)}, u32[]{:S(2)}) collective-permute-start(f32[200,128]{1,0:T(8,128)S(1)} %shard_map.99.refs_3_), channel_id=1, source_target_pairs={{0,4},{1,5},{2,6},{3,7},{4,8},{5,9},{6,10},{7,11},{8,12},{9,13},{1... | collective-permute-start | bytes 307208 | tf_op jit(solution)/shard_map/ppermute | solution.py:523
  13.2 1.6 %collective-permute-start.6 = (f32[200,128]{1,0:T(8,128)S(1)}, f32[200,128]{1,0:T(8,128)S(1)}, u32[]{:S(2)}, u32[]{:S(2)}) collective-permute-start(f32[200,128]{1,0:T(8,128)S(1)} %shard_map.100), channel_id=1, source_target_pairs={{0,4},{1,5},{2,6},{3,7},{4,8},{5,9},{6,10},{7,11},{8,12},{9,13},{1... | collective-permute-start | bytes 307208 | tf_op jit(solution)/shard_map/ppermute | solution.py:523
  14.8 2.0 %shard_map.101 = (f32[256,768]{1,0:T(8,128)S(1)}, bf16[1536,128]{1,0:T(8,128)(2,1)S(1)}) custom-call(bf16[256,1536]{1,0:T(8,128)(2,1)S(1)} %copy-done, bf16[256,1536]{1,0:T(8,128)(2,1)S(1)} %copy-done.2, bf16[256,1536]{1,0:T(8,128)(2,1)S(1)} %copy-done.1, f32[12,256]{1,0:T(8,128)S(1)} %bitcast.4, f32[256,6]{1,0:T(8,128)S(1)} %get-tuple-element.100.refs_4_.refs_3_.refs_2_, ...), custom_call_target="tpu_custom_call" | custom-call | flops 100663296 | bytes 3563520 | tf_op jit(solution)/shard_map/pallas_call | solution.py:143
  16.8 0.2 collective-permute-done.4.refs_3_
  17.0 0.7 %collective-permute-start.5 = (f32[200,128]{1,0:T(8,128)S(1)}, f32[200,128]{1,0:T(8,128)S(1)}, u32[]{:S(2)}, u32[]{:S(2)}) collective-permute-start(f32[200,128]{1,0:T(8,128)S(1)} %collective-permute-done.4.refs_3_), channel_id=1, source_target_pairs={{0,1},{1,0},{2,3},{3,2},{4,8},{5,9},{6,10},{7,11},{8,12},{9,13},{1... | collective-permute-start | bytes 307208 | tf_op jit(solution)/shard_map/ppermute | solution.py:537
  17.8 2.3 %collective-permute-done.6.refs_3_ = f32[200,128]{1,0:T(8,128)S(1)} collective-permute-done((f32[200,128]{1,0:T(8,128)S(1)}, f32[200,128]{1,0:T(8,128)S(1)}, u32[]{:S(2)}, u32[]{:S(2)}) %collective-permute-start.6) | collective-permute-done | bytes 102432 | tf_op jit(solution)/shard_map/ppermute | solution.py:523
  20.3 2.1 %collective-permute-start.8 = (f32[192,128]{1,0:T(8,128)S(1)}, f32[192,128]{1,0:T(8,128)S(1)}, u32[]{:S(2)}, u32[]{:S(2)}) collective-permute-start(f32[192,128]{1,0:T(8,128)S(1)} %get-tuple-element.130), channel_id=1, source_target_pairs={{0,2},{1,3},{2,0},{3,1},{4,6},{5,7},{6,4},{7,5},{8,10},{9,11},{10,... | collective-permute-start | bytes 294920 | tf_op jit(solution)/shard_map/ppermute | solution.py:517
  22.5 0.9 %collective-permute-start.9 = (f32[192,128]{1,0:T(8,128)S(1)}, f32[192,128]{1,0:T(8,128)S(1)}, u32[]{:S(2)}, u32[]{:S(2)}) collective-permute-start(f32[192,128]{1,0:T(8,128)S(1)} %get-tuple-element.133), channel_id=1, source_target_pairs={{0,2},{1,3},{2,0},{3,1},{4,6},{5,7},{6,4},{7,5},{8,10},{9,11},{10,... | collective-permute-start | bytes 294920 | tf_op jit(solution)/shard_map/ppermute | solution.py:517
  23.4 2.6 %collective-permute-done.8.refs_1_ = f32[192,128]{1,0:T(8,128)S(1)} collective-permute-done((f32[192,128]{1,0:T(8,128)S(1)}, f32[192,128]{1,0:T(8,128)S(1)}, u32[]{:S(2)}, u32[]{:S(2)}) %collective-permute-start.8) | collective-permute-done | bytes 98336 | tf_op jit(solution)/shard_map/ppermute | solution.py:517
  26.2 1.5 %collective-permute-done.9.refs_1_ = f32[192,128]{1,0:T(8,128)S(1)} collective-permute-done((f32[192,128]{1,0:T(8,128)S(1)}, f32[192,128]{1,0:T(8,128)S(1)}, u32[]{:S(2)}, u32[]{:S(2)}) %collective-permute-start.9) | collective-permute-done | bytes 98336 | tf_op jit(solution)/shard_map/ppermute | solution.py:517
  27.8 0.6 shard_map.106
  28.4 0.8 %collective-permute-done.10.refs_8_ = f32[384,128]{1,0:T(8,128)S(1)} collective-permute-done((f32[384,128]{1,0:T(8,128)S(1)}, f32[384,128]{1,0:T(8,128)S(1)}, u32[]{:S(2)}, u32[]{:S(2)}) %collective-permute-start.10) | collective-permute-done | bytes 196640 | tf_op jit(solution)/shard_map/ppermute | solution.py:517
  29.2 0.6 shard_map.107
  29.8 1.8 %collective-permute-start.12 = (f32[8,256]{1,0:T(8,128)S(1)}, f32[8,256]{1,0:T(8,128)S(1)}, u32[]{:S(2)}, u32[]{:S(2)}) collective-permute-start(f32[8,256]{1,0:T(8,128)S(1)} %get-tuple-element.140.refs_6_), channel_id=1, source_target_pairs={{0,16},{16,0},{1,17},{17,1},{2,18},{18,2},{3,19},{19,3},{4,20},{20... | collective-permute-start | bytes 24584 | tf_op jit(solution)/shard_map/ppermute | solution.py:517
  31.7 1.9 %collective-permute-done.12.refs_7_ = f32[8,256]{1,0:T(8,128)S(1)} collective-permute-done((f32[8,256]{1,0:T(8,128)S(1)}, f32[8,256]{1,0:T(8,128)S(1)}, u32[]{:S(2)}, u32[]{:S(2)}) %collective-permute-start.12) | collective-permute-done | bytes 8224 | tf_op jit(solution)/shard_map/ppermute | solution.py:517
  33.6 0.9 %shard_map.108 = (bf16[256,768]{1,0:T(8,128)(2,1)S(1)}, f32[384,128]{1,0:T(8,128)S(1)}, f32[400,128]{1,0:T(8,128)S(1)}, f32[8,128]{1,0:T(8,128)S(1)}, f32[8,128]{1,0:T(8,128)S(1)}, /*index=5*/f32[768,128]{1,0:T(8,128)S(1)}) custom-call(bf16[256,1536]{1,0:T(8,128)(2,1)S(1)} %copy-done, bf16[256,1536]{1,0:T(8,128)(2,1)S(1)} %copy-done.3, f32[1536]{0:T(1024)S(1)} %copy-done.5, ...), custom_call_target="tpu_custom_call" | custom-call | flops 50331648 | bytes 3596288 | tf_op jit(solution)/shard_map/pallas_call | solution.py:143
  34.6 0.9 %shard_map.109 = (bf16[256,768]{1,0:T(8,128)(2,1)S(1)}, f32[384,128]{1,0:T(8,128)S(1)}, f32[400,128]{1,0:T(8,128)S(1)}, f32[8,128]{1,0:T(8,128)S(1)}, f32[8,128]{1,0:T(8,128)S(1)}, /*index=5*/f32[768,128]{1,0:T(8,128)S(1)}) custom-call(bf16[256,1536]{1,0:T(8,128)(2,1)S(1)} %copy-done, bf16[256,1536]{1,0:T(8,128)(2,1)S(1)} %copy-done.3, f32[1536]{0:T(1024)S(1)} %copy-done.5, ...), custom_call_target="tpu_custom_call" | custom-call | flops 50331648 | bytes 3596288 | tf_op jit(solution)/shard_map/pallas_call | solution.py:143
  35.5 0.6 collective-permute-start.14
  36.1 1.8 %collective-permute-start.15 = (f32[200,128]{1,0:T(8,128)S(1)}, f32[200,128]{1,0:T(8,128)S(1)}, u32[]{:S(2)}, u32[]{:S(2)}) collective-permute-start(f32[200,128]{1,0:T(8,128)S(1)} %get-tuple-element.161.refs_1_), channel_id=1, source_target_pairs={{0,2},{1,3},{2,0},{3,1},{4,6},{5,7},{6,4},{7,5},{8,10},{9,11},{10,... | collective-permute-start | bytes 307208 | tf_op jit(solution)/shard_map/ppermute | solution.py:517
  38.0 1.0 %collective-permute-start.17 = (f32[200,128]{1,0:T(8,128)S(1)}, f32[200,128]{1,0:T(8,128)S(1)}, u32[]{:S(2)}, u32[]{:S(2)}) collective-permute-start(f32[200,128]{1,0:T(8,128)S(1)} %get-tuple-element.164.refs_1_), channel_id=1, source_target_pairs={{0,2},{1,3},{2,0},{3,1},{4,6},{5,7},{6,4},{7,5},{8,10},{9,11},{10,... | collective-permute-start | bytes 307208 | tf_op jit(solution)/shard_map/ppermute | solution.py:517
  39.0 2.4 %collective-permute-start.16 = (f32[16,128]{1,0:T(8,128)S(1)}, f32[16,128]{1,0:T(8,128)S(1)}, u32[]{:S(2)}, u32[]{:S(2)}) collective-permute-start(f32[16,128]{1,0:T(8,128)S(1)} %get-tuple-element.162.refs_3_), channel_id=1, source_target_pairs={{0,9},{1,8},{2,11},{3,10},{4,13},{5,12},{6,15},{7,14},{8,1},{9,0},... | collective-permute-start | bytes 24584 | tf_op jit(solution)/shard_map/ppermute | solution.py:517
  41.4 1.1 %shard_map.112 = (f32[256,768]{1,0:T(8,128)S(1)}, f32[256,768]{1,0:T(8,128)S(1)}) custom-call(bf16[256,1536]{1,0:T(8,128)(2,1)S(1)} %copy-done, bf16[256,1536]{1,0:T(8,128)(2,1)S(1)} %copy-done.1, f32[12,256]{1,0:T(8,128)S(1)} %bitcast.5, f32[256,6]{1,0:T(8,128)S(1)} %get-tuple-element.114.refs_4_.refs_3_.refs_2_, ...), custom_call_target="tpu_custom_call" | custom-call | flops 150994944 | bytes 3950592 | tf_op jit(solution)/shard_map/pallas_call | solution.py:143
  42.6 0.4 collective-permute-done.16.refs_4_
  43.1 3.1 %collective-permute-start.18 = (f32[216,128]{1,0:T(8,128)S(1)}, f32[216,128]{1,0:T(8,128)S(1)}, u32[]{:S(2)}, u32[]{:S(2)}) collective-permute-start(f32[216,128]{1,0:T(8,128)S(1)} %shard_map.113.refs_3_.refs_5_), channel_id=1, source_target_pairs={{0,13},{1,12},{2,15},{3,14},{4,0},{5,1},{6,2},{7,3},{8,4},{9,5},{1... | collective-permute-start | bytes 331784 | tf_op jit(solution)/shard_map/ppermute | solution.py:523
  46.2 0.6 collective-permute-start.20
  46.8 1.1 %shard_map.115 = (f32[256,768]{1,0:T(8,128)S(1)}, f32[256,768]{1,0:T(8,128)S(1)}) custom-call(bf16[256,1536]{1,0:T(8,128)(2,1)S(1)} %copy-done, bf16[256,1536]{1,0:T(8,128)(2,1)S(1)} %copy-done.1, f32[12,256]{1,0:T(8,128)S(1)} %bitcast.6, f32[256,6]{1,0:T(8,128)S(1)} %get-tuple-element.100.refs_4_.refs_3_.refs_2_, ...), custom_call_target="tpu_custom_call" | custom-call | flops 150994944 | bytes 3950592 | tf_op jit(solution)/shard_map/pallas_call | solution.py:143
  48.0 1.6 %collective-permute-done.18.refs_3_ = f32[216,128]{1,0:T(8,128)S(1)} collective-permute-done((f32[216,128]{1,0:T(8,128)S(1)}, f32[216,128]{1,0:T(8,128)S(1)}, u32[]{:S(2)}, u32[]{:S(2)}) %collective-permute-start.18) | collective-permute-done | bytes 110624 | tf_op jit(solution)/shard_map/ppermute | solution.py:523
  49.6 2.1 %collective-permute-start.19 = (f32[216,128]{1,0:T(8,128)S(1)}, f32[216,128]{1,0:T(8,128)S(1)}, u32[]{:S(2)}, u32[]{:S(2)}) collective-permute-start(f32[216,128]{1,0:T(8,128)S(1)} %collective-permute-done.18.refs_3_), channel_id=1, source_target_pairs={{15,14},{14,15},{13,12},{12,13},{11,7},{10,6},{9,5},{8,4},{7,3},{6... | collective-permute-start | bytes 331784 | tf_op jit(solution)/shard_map/ppermute | solution.py:537
  51.8 1.3 %collective-permute-start.21 = (f32[200,128]{1,0:T(8,128)S(1)}, f32[200,128]{1,0:T(8,128)S(1)}, u32[]{:S(2)}, u32[]{:S(2)}) collective-permute-start(f32[200,128]{1,0:T(8,128)S(1)} %collective-permute-done.20.refs_3_), channel_id=1, source_target_pairs={{15,14},{14,15},{13,12},{12,13},{11,7},{10,6},{9,5},{8,4},{7,3},{6... | collective-permute-start | bytes 307208 | tf_op jit(solution)/shard_map/ppermute | solution.py:537
  53.1 1.9 %collective-permute-done.19.refs_4_ = f32[216,128]{1,0:T(8,128)S(1)} collective-permute-done((f32[216,128]{1,0:T(8,128)S(1)}, f32[216,128]{1,0:T(8,128)S(1)}, u32[]{:S(2)}, u32[]{:S(2)}) %collective-permute-start.19) | collective-permute-done | bytes 110624 | tf_op jit(solution)/shard_map/ppermute | solution.py:537
  55.0 1.1 %collective-permute-start.22 = (f32[208,128]{1,0:T(8,128)S(1)}, f32[208,128]{1,0:T(8,128)S(1)}, u32[]{:S(2)}, u32[]{:S(2)}) collective-permute-start(f32[208,128]{1,0:T(8,128)S(1)} %get-tuple-element.177), channel_id=1, source_target_pairs={{0,2},{1,3},{2,0},{3,1},{4,6},{5,7},{6,4},{7,5},{8,10},{9,11},{10,... | collective-permute-start | bytes 319496 | tf_op jit(solution)/shard_map/ppermute | solution.py:517
  56.1 0.4 collective-permute-done.21.refs_4_
  56.6 1.1 %collective-permute-start.23 = (f32[192,128]{1,0:T(8,128)S(1)}, f32[192,128]{1,0:T(8,128)S(1)}, u32[]{:S(2)}, u32[]{:S(2)}) collective-permute-start(f32[192,128]{1,0:T(8,128)S(1)} %get-tuple-element.180), channel_id=1, source_target_pairs={{0,2},{1,3},{2,0},{3,1},{4,6},{5,7},{6,4},{7,5},{8,10},{9,11},{10,... | collective-permute-start | bytes 294920 | tf_op jit(solution)/shard_map/ppermute | solution.py:517
  57.7 2.8 %collective-permute-done.22.refs_1_.refs_12_ = f32[208,128]{1,0:T(8,128)S(1)} collective-permute-done((f32[208,128]{1,0:T(8,128)S(1)}, f32[208,128]{1,0:T(8,128)S(1)}, u32[]{:S(2)}, u32[]{:S(2)}) %collective-permute-start.22) | collective-permute-done | bytes 106528 | tf_op jit(solution)/shard_map/ppermute | solution.py:517
  60.7 0.9 %collective-permute-done.23.refs_1_ = f32[192,128]{1,0:T(8,128)S(1)} collective-permute-done((f32[192,128]{1,0:T(8,128)S(1)}, f32[192,128]{1,0:T(8,128)S(1)}, u32[]{:S(2)}, u32[]{:S(2)}) %collective-permute-start.23) | collective-permute-done | bytes 98336 | tf_op jit(solution)/shard_map/ppermute | solution.py:517
  61.7 0.4 collective-permute-done.25.refs_8_
  62.1 0.6 shard_map.120
  62.7 0.4 collective-permute-done.24.refs_8_
  63.1 1.5 %shard_map.121 = (bf16[256,1536]{1,0:T(8,128)(2,1)}, bf16[256,1536]{1,0:T(8,128)(2,1)}, f32[1536]{0:T(1024)}) custom-call(bf16[256,1536]{1,0:T(8,128)(2,1)S(1)} %copy-done.2, bf16[256,1536]{1,0:T(8,128)(2,1)S(1)} %copy-done.1, f32[256,6]{1,0:T(8,128)S(1)} %get-tuple-element.100.refs_4_.refs_3_.refs_2_, ...), custom_call_target="tpu_custom_call" | custom-call | flops 201326592 | bytes 6430720 | tf_op jit(solution)/shard_map/pallas_call | solution.py:143
  (44 shorter events, 1.4 us)
Async XLA Ops:
  0.6 2.5 %copy-start.1 = (bf16[256,1536]{1,0:T(8,128)(2,1)S(1)}, bf16[256,1536]{1,0:T(8,128)(2,1)}, u32[]{:S(2)}) copy-start(bf16[256,1536]{1,0:T(8,128)(2,1)} %refs_1_.13) | copy-start | bytes 2359300
  0.6 2.5 %copy-start.2 = (bf16[256,1536]{1,0:T(8,128)(2,1)S(1)}, bf16[256,1536]{1,0:T(8,128)(2,1)}, u32[]{:S(2)}) copy-start(bf16[256,1536]{1,0:T(8,128)(2,1)} %refs_0_.13) | copy-start | bytes 2359300
  0.7 2.5 %copy-start.4 = (f32[256,12]{0,1:T(8,128)S(1)}, f32[256,12]{0,1:T(8,128)}, u32[]{:S(2)}) copy-start(f32[256,12]{0,1:T(8,128)} %param.11) | copy-start | bytes 36868
  2.6 1.6 %collective-permute-start = (f32[392,128]{1,0:T(8,128)S(1)}, f32[392,128]{1,0:T(8,128)S(1)}, u32[]{:S(2)}, u32[]{:S(2)}) collective-permute-start(f32[392,128]{1,0:T(8,128)S(1)} %get-tuple-element.107), channel_id=1, source_target_pairs={{0,1},{1,0},{2,3},{3,2},{4,5},{5,4},{6,7},{7,6},{8,9},{9,8},{10,11... | collective-permute-start | bytes 602120 | tf_op jit(solution)/shard_map/ppermute | solution.py:517
  3.9 4.3 %copy-start = (bf16[256,1536]{1,0:T(8,128)(2,1)S(1)}, bf16[256,1536]{1,0:T(8,128)(2,1)}, u32[]{:S(2)}) copy-start(bf16[256,1536]{1,0:T(8,128)(2,1)} %refs_0_.11) | copy-start | bytes 2359300
  3.9 3.3 %collective-permute-start.1 = (f32[392,128]{1,0:T(8,128)S(1)}, f32[392,128]{1,0:T(8,128)S(1)}, u32[]{:S(2)}, u32[]{:S(2)}) collective-permute-start(f32[392,128]{1,0:T(8,128)S(1)} %get-tuple-element.110), channel_id=1, source_target_pairs={{0,1},{1,0},{2,3},{3,2},{4,5},{5,4},{6,7},{7,6},{8,9},{9,8},{10,11... | collective-permute-start | bytes 602120 | tf_op jit(solution)/shard_map/ppermute | solution.py:517
  4.3 6.6 %collective-permute-start.2 = (f32[200,128]{1,0:T(8,128)S(1)}, f32[200,128]{1,0:T(8,128)S(1)}, u32[]{:S(2)}, u32[]{:S(2)}) collective-permute-start(f32[200,128]{1,0:T(8,128)S(1)} %get-tuple-element.117.refs_1_), channel_id=1, source_target_pairs={{0,2},{1,3},{2,0},{3,1},{4,6},{5,7},{6,4},{7,5},{8,10},{9,11},{10,... | collective-permute-start | bytes 307208 | tf_op jit(solution)/shard_map/ppermute | solution.py:517
  7.2 1.0 %copy-start.5 = (f32[1536]{0:T(1024)S(1)}, f32[1536]{0:T(1024)}, u32[]{:S(2)}) copy-start(f32[1536]{0:T(1024)} %refs_2_.5) | copy-start | bytes 18436
  7.3 5.8 %collective-permute-start.3 = (f32[200,128]{1,0:T(8,128)S(1)}, f32[200,128]{1,0:T(8,128)S(1)}, u32[]{:S(2)}, u32[]{:S(2)}) collective-permute-start(f32[200,128]{1,0:T(8,128)S(1)} %get-tuple-element.119.refs_1_), channel_id=1, source_target_pairs={{0,2},{1,3},{2,0},{3,1},{4,6},{5,7},{6,4},{7,5},{8,10},{9,11},{10,... | collective-permute-start | bytes 307208 | tf_op jit(solution)/shard_map/ppermute | solution.py:517
  10.9 6.1 %collective-permute-start.4 = (f32[200,128]{1,0:T(8,128)S(1)}, f32[200,128]{1,0:T(8,128)S(1)}, u32[]{:S(2)}, u32[]{:S(2)}) collective-permute-start(f32[200,128]{1,0:T(8,128)S(1)} %shard_map.99.refs_3_), channel_id=1, source_target_pairs={{0,4},{1,5},{2,6},{3,7},{4,8},{5,9},{6,10},{7,11},{8,12},{9,13},{1... | collective-permute-start | bytes 307208 | tf_op jit(solution)/shard_map/ppermute | solution.py:523
  13.2 7.0 %collective-permute-start.6 = (f32[200,128]{1,0:T(8,128)S(1)}, f32[200,128]{1,0:T(8,128)S(1)}, u32[]{:S(2)}, u32[]{:S(2)}) collective-permute-start(f32[200,128]{1,0:T(8,128)S(1)} %shard_map.100), channel_id=1, source_target_pairs={{0,4},{1,5},{2,6},{3,7},{4,8},{5,9},{6,10},{7,11},{8,12},{9,13},{1... | collective-permute-start | bytes 307208 | tf_op jit(solution)/shard_map/ppermute | solution.py:523
  17.0 3.2 %collective-permute-start.5 = (f32[200,128]{1,0:T(8,128)S(1)}, f32[200,128]{1,0:T(8,128)S(1)}, u32[]{:S(2)}, u32[]{:S(2)}) collective-permute-start(f32[200,128]{1,0:T(8,128)S(1)} %collective-permute-done.4.refs_3_), channel_id=1, source_target_pairs={{0,1},{1,0},{2,3},{3,2},{4,8},{5,9},{6,10},{7,11},{8,12},{9,13},{1... | collective-permute-start | bytes 307208 | tf_op jit(solution)/shard_map/ppermute | solution.py:537
  20.1 2.3 %collective-permute-start.7 = (f32[200,128]{1,0:T(8,128)S(1)}, f32[200,128]{1,0:T(8,128)S(1)}, u32[]{:S(2)}, u32[]{:S(2)}) collective-permute-start(f32[200,128]{1,0:T(8,128)S(1)} %collective-permute-done.6.refs_3_), channel_id=1, source_target_pairs={{0,1},{1,0},{2,3},{3,2},{4,8},{5,9},{6,10},{7,11},{8,12},{9,13},{1... | collective-permute-start | bytes 307208 | tf_op jit(solution)/shard_map/ppermute | solution.py:537
  20.3 5.7 %collective-permute-start.8 = (f32[192,128]{1,0:T(8,128)S(1)}, f32[192,128]{1,0:T(8,128)S(1)}, u32[]{:S(2)}, u32[]{:S(2)}) collective-permute-start(f32[192,128]{1,0:T(8,128)S(1)} %get-tuple-element.130), channel_id=1, source_target_pairs={{0,2},{1,3},{2,0},{3,1},{4,6},{5,7},{6,4},{7,5},{8,10},{9,11},{10,... | collective-permute-start | bytes 294920 | tf_op jit(solution)/shard_map/ppermute | solution.py:517
  22.4 5.4 %copy-start.3 = (bf16[256,1536]{1,0:T(8,128)(2,1)S(1)}, bf16[256,1536]{1,0:T(8,128)(2,1)}, u32[]{:S(2)}) copy-start(bf16[256,1536]{1,0:T(8,128)(2,1)} %refs_1_.9) | copy-start | bytes 2359300
  22.5 5.2 %collective-permute-start.9 = (f32[192,128]{1,0:T(8,128)S(1)}, f32[192,128]{1,0:T(8,128)S(1)}, u32[]{:S(2)}, u32[]{:S(2)}) collective-permute-start(f32[192,128]{1,0:T(8,128)S(1)} %get-tuple-element.133), channel_id=1, source_target_pairs={{0,2},{1,3},{2,0},{3,1},{4,6},{5,7},{6,4},{7,5},{8,10},{9,11},{10,... | collective-permute-start | bytes 294920 | tf_op jit(solution)/shard_map/ppermute | solution.py:517
  26.1 1.7 %collective-permute-start.11 = (f32[384,128]{1,0:T(8,128)S(1)}, f32[384,128]{1,0:T(8,128)S(1)}, u32[]{:S(2)}, u32[]{:S(2)}) collective-permute-start(f32[384,128]{1,0:T(8,128)S(1)} %get-tuple-element.137), channel_id=1, source_target_pairs={{0,1},{1,0},{2,3},{3,2},{4,5},{5,4},{6,7},{7,6},{8,9},{9,8},{10,11... | collective-permute-start | bytes 589832 | tf_op jit(solution)/shard_map/ppermute | solution.py:517
  27.7 1.5 %collective-permute-start.10 = (f32[384,128]{1,0:T(8,128)S(1)}, f32[384,128]{1,0:T(8,128)S(1)}, u32[]{:S(2)}, u32[]{:S(2)}) collective-permute-start(f32[384,128]{1,0:T(8,128)S(1)} %get-tuple-element.135), channel_id=1, source_target_pairs={{0,1},{1,0},{2,3},{3,2},{4,5},{5,4},{6,7},{7,6},{8,9},{9,8},{10,11... | collective-permute-start | bytes 589832 | tf_op jit(solution)/shard_map/ppermute | solution.py:517
  29.8 3.7 %collective-permute-start.12 = (f32[8,256]{1,0:T(8,128)S(1)}, f32[8,256]{1,0:T(8,128)S(1)}, u32[]{:S(2)}, u32[]{:S(2)}) collective-permute-start(f32[8,256]{1,0:T(8,128)S(1)} %get-tuple-element.140.refs_6_), channel_id=1, source_target_pairs={{0,16},{16,0},{1,17},{17,1},{2,18},{18,2},{3,19},{19,3},{4,20},{20... | collective-permute-start | bytes 24584 | tf_op jit(solution)/shard_map/ppermute | solution.py:517
  34.5 1.6 %collective-permute-start.13 = (f32[400,128]{1,0:T(8,128)S(1)}, f32[400,128]{1,0:T(8,128)S(1)}, u32[]{:S(2)}, u32[]{:S(2)}) collective-permute-start(f32[400,128]{1,0:T(8,128)S(1)} %get-tuple-element.146), channel_id=1, source_target_pairs={{0,1},{1,0},{2,3},{3,2},{4,5},{5,4},{6,7},{7,6},{8,9},{9,8},{10,11... | collective-permute-start | bytes 614408 | tf_op jit(solution)/shard_map/ppermute | solution.py:517
  35.5 2.4 %collective-permute-start.14 = (f32[400,128]{1,0:T(8,128)S(1)}, f32[400,128]{1,0:T(8,128)S(1)}, u32[]{:S(2)}, u32[]{:S(2)}) collective-permute-start(f32[400,128]{1,0:T(8,128)S(1)} %get-tuple-element.152), channel_id=1, source_target_pairs={{0,1},{1,0},{2,3},{3,2},{4,5},{5,4},{6,7},{7,6},{8,9},{9,8},{10,11... | collective-permute-start | bytes 614408 | tf_op jit(solution)/shard_map/ppermute | solution.py:517
  36.1 6.9 %collective-permute-start.15 = (f32[200,128]{1,0:T(8,128)S(1)}, f32[200,128]{1,0:T(8,128)S(1)}, u32[]{:S(2)}, u32[]{:S(2)}) collective-permute-start(f32[200,128]{1,0:T(8,128)S(1)} %get-tuple-element.161.refs_1_), channel_id=1, source_target_pairs={{0,2},{1,3},{2,0},{3,1},{4,6},{5,7},{6,4},{7,5},{8,10},{9,11},{10,... | collective-permute-start | bytes 307208 | tf_op jit(solution)/shard_map/ppermute | solution.py:517
  38.0 8.2 %collective-permute-start.17 = (f32[200,128]{1,0:T(8,128)S(1)}, f32[200,128]{1,0:T(8,128)S(1)}, u32[]{:S(2)}, u32[]{:S(2)}) collective-permute-start(f32[200,128]{1,0:T(8,128)S(1)} %get-tuple-element.164.refs_1_), channel_id=1, source_target_pairs={{0,2},{1,3},{2,0},{3,1},{4,6},{5,7},{6,4},{7,5},{8,10},{9,11},{10,... | collective-permute-start | bytes 307208 | tf_op jit(solution)/shard_map/ppermute | solution.py:517
  39.0 4.0 %collective-permute-start.16 = (f32[16,128]{1,0:T(8,128)S(1)}, f32[16,128]{1,0:T(8,128)S(1)}, u32[]{:S(2)}, u32[]{:S(2)}) collective-permute-start(f32[16,128]{1,0:T(8,128)S(1)} %get-tuple-element.162.refs_3_), channel_id=1, source_target_pairs={{0,9},{1,8},{2,11},{3,10},{4,13},{5,12},{6,15},{7,14},{8,1},{9,0},... | collective-permute-start | bytes 24584 | tf_op jit(solution)/shard_map/ppermute | solution.py:517
  43.1 6.5 %collective-permute-start.18 = (f32[216,128]{1,0:T(8,128)S(1)}, f32[216,128]{1,0:T(8,128)S(1)}, u32[]{:S(2)}, u32[]{:S(2)}) collective-permute-start(f32[216,128]{1,0:T(8,128)S(1)} %shard_map.113.refs_3_.refs_5_), channel_id=1, source_target_pairs={{0,13},{1,12},{2,15},{3,14},{4,0},{5,1},{6,2},{7,3},{8,4},{9,5},{1... | collective-permute-start | bytes 331784 | tf_op jit(solution)/shard_map/ppermute | solution.py:523
  46.2 5.6 %collective-permute-start.20 = (f32[200,128]{1,0:T(8,128)S(1)}, f32[200,128]{1,0:T(8,128)S(1)}, u32[]{:S(2)}, u32[]{:S(2)}) collective-permute-start(f32[200,128]{1,0:T(8,128)S(1)} %shard_map.114), channel_id=1, source_target_pairs={{0,13},{1,12},{2,15},{3,14},{4,0},{5,1},{6,2},{7,3},{8,4},{9,5},{1... | collective-permute-start | bytes 307208 | tf_op jit(solution)/shard_map/ppermute | solution.py:523
  49.6 5.4 %collective-permute-start.19 = (f32[216,128]{1,0:T(8,128)S(1)}, f32[216,128]{1,0:T(8,128)S(1)}, u32[]{:S(2)}, u32[]{:S(2)}) collective-permute-start(f32[216,128]{1,0:T(8,128)S(1)} %collective-permute-done.18.refs_3_), channel_id=1, source_target_pairs={{15,14},{14,15},{13,12},{12,13},{11,7},{10,6},{9,5},{8,4},{7,3},{6... | collective-permute-start | bytes 331784 | tf_op jit(solution)/shard_map/ppermute | solution.py:537
  51.8 4.7 %collective-permute-start.21 = (f32[200,128]{1,0:T(8,128)S(1)}, f32[200,128]{1,0:T(8,128)S(1)}, u32[]{:S(2)}, u32[]{:S(2)}) collective-permute-start(f32[200,128]{1,0:T(8,128)S(1)} %collective-permute-done.20.refs_3_), channel_id=1, source_target_pairs={{15,14},{14,15},{13,12},{12,13},{11,7},{10,6},{9,5},{8,4},{7,3},{6... | collective-permute-start | bytes 307208 | tf_op jit(solution)/shard_map/ppermute | solution.py:537
  55.0 5.5 %collective-permute-start.22 = (f32[208,128]{1,0:T(8,128)S(1)}, f32[208,128]{1,0:T(8,128)S(1)}, u32[]{:S(2)}, u32[]{:S(2)}) collective-permute-start(f32[208,128]{1,0:T(8,128)S(1)} %get-tuple-element.177), channel_id=1, source_target_pairs={{0,2},{1,3},{2,0},{3,1},{4,6},{5,7},{6,4},{7,5},{8,10},{9,11},{10,... | collective-permute-start | bytes 319496 | tf_op jit(solution)/shard_map/ppermute | solution.py:517
  56.6 5.0 %collective-permute-start.23 = (f32[192,128]{1,0:T(8,128)S(1)}, f32[192,128]{1,0:T(8,128)S(1)}, u32[]{:S(2)}, u32[]{:S(2)}) collective-permute-start(f32[192,128]{1,0:T(8,128)S(1)} %get-tuple-element.180), channel_id=1, source_target_pairs={{0,2},{1,3},{2,0},{3,1},{4,6},{5,7},{6,4},{7,5},{8,10},{9,11},{10,... | collective-permute-start | bytes 294920 | tf_op jit(solution)/shard_map/ppermute | solution.py:517
  60.6 1.5 %collective-permute-start.25 = (f32[384,128]{1,0:T(8,128)S(1)}, f32[384,128]{1,0:T(8,128)S(1)}, u32[]{:S(2)}, u32[]{:S(2)}) collective-permute-start(f32[384,128]{1,0:T(8,128)S(1)} %get-tuple-element.185), channel_id=1, source_target_pairs={{0,1},{1,0},{2,3},{3,2},{4,5},{5,4},{6,7},{7,6},{8,9},{9,8},{10,11... | collective-permute-start | bytes 589832 | tf_op jit(solution)/shard_map/ppermute | solution.py:517
  61.6 1.5 %collective-permute-start.24 = (f32[384,128]{1,0:T(8,128)S(1)}, f32[384,128]{1,0:T(8,128)S(1)}, u32[]{:S(2)}, u32[]{:S(2)}) collective-permute-start(f32[384,128]{1,0:T(8,128)S(1)} %get-tuple-element.182), channel_id=1, source_target_pairs={{0,1},{1,0},{2,3},{3,2},{4,5},{5,4},{6,7},{7,6},{8,9},{9,8},{10,11... | collective-permute-start | bytes 589832 | tf_op jit(solution)/shard_map/ppermute | solution.py:517
